TPU v7x, 32 devices: a whole 2x2x4 slice. The times are simulated.
32 devices in a mesh: tiles: 8 (over z, y), probes: 4 (over x, core).
Axes of the slice: x: 2, y: 2, z: 4, core: 2. Of those that a mesh axis runs over, the one named last changes fastest.
Arguments:
- blocks: bfloat16 [512, 192, 192], P('tiles'), may hold values from -0.21875 to 0.21875
- connectivity: int32 [512, 64], P('tiles'), may hold values from 0 to 4607, as said below
- basal_map: int32 [512, 64], P('tiles'), may hold values from 0 to 383
- friction: float32 [512, 64, 3], P('tiles'), may hold values from 0.2 to 2
- elem_counts: int32 [8], P('tiles'), may hold values from 1 to 64, 384 in all
- obs_weight: float32 [32768, 3], P('tiles'), may hold values from 0.2 to 2
- sign_bits: int32 [2048, 32], P('tiles', 'probes'), may hold values from 0 to 1
- cluster_ids: int32 [2048], P('tiles'), may hold values from 0 to 7, never falling along the last dimension, each value on 1 to 512 neighbouring positions
Outputs:
- samples: float32 [2048, 32], P('tiles', 'probes')
- refined: float32 [2048, 32], P('tiles', 'probes')
- gram: float32 [8, 32, 32], P(None, 'probes')
Inputs may be any that keep to these rules, and one draw needn't show every extreme that they name: `connectivity`: about one reference in eight names a node of the next tile. `elem_counts`: some tile has all 64 slots live. `cluster_ids`: never falling along the cells; each cluster holds 1 to 512 cells.
All inputs are finite; a program needn't handle non-finite values. No bound on the sum of `elem_counts` on one device may be relied on, other than what follows from the above.
Results may differ from a plain program's by a relative error of at most 0.004.
Values may be sent and summed in bfloat16 or wider, within the bound.
No kernel may reach another device: no remote copies, remote signals or barrier semaphores. Data moves between devices by JAX's collectives and lax.ppermute only.
A program may use at most 64 MiB of HBM per device.

v0:
```python
import jax
import jax.numpy as jnp
from jax import lax
from jax.sharding import PartitionSpec as P

HALO = 512
POWER = 2
RIM = 64


def from_behind(block, axis, distance):
    devices = range(lax.axis_size(axis))
    route = [(i - distance, i) for i in devices if i - distance in devices]
    return lax.ppermute(block, axis, route)


def padded(x, sides, width):
    for axis, dim in sides:
        size, length = (lax.axis_size(axis), x.shape[dim])
        up = [(i, (i + 1) % size) for i in range(size - 1)]
        down = [(j, i) for i, j in up]
        last = lax.slice_in_dim(x, length - width, length, axis=dim)
        leading = lax.slice_in_dim(x, 0, width, axis=dim)
        before = lax.ppermute(last, axis, up)
        after = lax.ppermute(leading, axis, down)
        x = jnp.concatenate([before, x, after], axis=dim)
    return x


def shards(
    blocks, connectivity, basal_map, friction, elem_counts, obs_weight, sign_bits, cluster_ids
):
    elem_slots = blocks.shape[0]
    block_order = blocks.shape[1]
    node_slots = connectivity.shape[1]
    node_count = obs_weight.shape[0]
    halo_nodes = HALO
    rim_cells = RIM
    cell_count = sign_bits.shape[0]
    group_size = sign_bits.shape[1]
    tile_count = lax.axis_size("tiles")
    tile_index = lax.axis_index("tiles")
    alive_slots = jnp.arange(elem_slots, dtype=jnp.int32) < elem_counts[0]
    flat_nodes = connectivity.reshape(-1)
    flat_cells = basal_map.reshape(-1)
    weight_next = from_behind(obs_weight[:halo_nodes], "tiles", -1)

    def hessian(probe_field):
        window = padded(probe_field, (("tiles", 0),), rim_cells)
        picked = window[basal_map]
        inputs = (friction[:, :, :, None] * picked[:, :, None, :]).astype(jnp.bfloat16)
        inputs = inputs.reshape(elem_slots, block_order, group_size)
        forward = jnp.einsum("eij,ejp->eip", blocks, inputs, preferred_element_type=jnp.float32)
        forward = jnp.where(alive_slots[:, None, None], forward, jnp.float32(0.0))
        summed = jax.ops.segment_sum(
            forward.reshape(elem_slots * node_slots, 3 * group_size),
            flat_nodes,
            num_segments=node_count + halo_nodes,
        )
        owned_sum = summed[:node_count]
        spilled = summed[node_count:]
        from_earlier = from_behind(spilled, "tiles", 1)
        from_later = from_behind(owned_sum[:halo_nodes], "tiles", -1)
        rim_total = spilled + from_later
        owned_sum = jnp.concatenate(
            [owned_sum[:halo_nodes] + from_earlier, owned_sum[halo_nodes:]], 0
        )
        weighted = (obs_weight[:, :, None] * owned_sum.reshape(node_count, 3, group_size)).astype(
            jnp.bfloat16
        )
        weighted = weighted.reshape(node_count, 3 * group_size)
        rim_values = (
            weight_next[:, :, None] * rim_total.reshape(halo_nodes, 3, group_size)
        ).astype(jnp.bfloat16)
        inside = tile_index < tile_count - 1
        weighted_rim = jnp.where(
            inside, rim_values.reshape(halo_nodes, 3 * group_size), jnp.zeros((), jnp.bfloat16)
        )
        node_window = jnp.concatenate([weighted, weighted_rim], 0)
        adjoint_in = node_window[connectivity].reshape(elem_slots, block_order, group_size)
        adjoint_out = jnp.einsum(
            "eji,ejp->eip", blocks, adjoint_in, preferred_element_type=jnp.float32
        )
        partials = jnp.sum(
            friction[:, :, :, None] * adjoint_out.reshape(elem_slots, node_slots, 3, group_size),
            axis=2,
        )
        partials = jnp.where(alive_slots[:, None, None], partials, jnp.float32(0.0))
        basal = jax.ops.segment_sum(
            partials.reshape(elem_slots * node_slots, group_size),
            flat_cells,
            num_segments=cell_count + 2 * rim_cells,
        )
        from_next = from_behind(basal[:rim_cells], "tiles", -1)
        from_prev = from_behind(basal[cell_count + rim_cells :], "tiles", 1)
        middle = basal[rim_cells : cell_count + rim_cells]
        middle = middle + jnp.pad(from_prev, ((0, cell_count - rim_cells), (0, 0)))
        middle = middle + jnp.pad(from_next, ((cell_count - rim_cells, 0), (0, 0)))
        return middle

    parity = jnp.arange(group_size, dtype=jnp.int32) % 2
    same_colour = (cluster_ids % 2)[:, None] == parity[None, :]
    probe_start = jnp.where(same_colour, (2 * sign_bits - 1).astype(jnp.float32), jnp.float32(0.0))
    samples = jnp.where(same_colour, jnp.float32(0.0), hessian(probe_start))
    current = samples
    for power_step in range(POWER):
        squares = lax.psum(jnp.sum(current * current, axis=0), "tiles")
        rms_scale = jnp.sqrt(squares / (cell_count * tile_count) + 1e-06)
        applied = hessian(current / rms_scale)
        if power_step % 2 == 0:
            current = jnp.where(same_colour, applied, jnp.float32(0.0))
        else:
            current = jnp.where(same_colour, jnp.float32(0.0), applied)
    onehot = (cluster_ids[:, None] == jnp.arange(tile_count, dtype=jnp.int32)[None, :]).astype(
        jnp.float32
    )
    column_block = lax.all_gather(current, "probes", axis=1, tiled=True)
    outer = current[:, :, None] * column_block[:, None, :]
    width = column_block.shape[1]
    result = jnp.dot(
        onehot.T, outer.reshape(cell_count, group_size * width), precision=lax.Precision.HIGHEST
    )
    partial_gram = result.reshape(tile_count, group_size, width)
    gram = lax.psum(partial_gram, "tiles")
    return (samples, current, gram)


def solution(mesh):
    in_specs = (
        P("tiles", None, None),
        P("tiles", None),
        P("tiles", None),
        P("tiles", None, None),
        P("tiles"),
        P("tiles", None),
        P("tiles", "probes"),
        P("tiles"),
    )
    out_specs = (P("tiles", "probes"), P("tiles", "probes"), P(None, "probes", None))
    return jax.shard_map(shards, mesh=mesh, in_specs=in_specs, out_specs=out_specs, check_vma=False)
```

profile of v0, /device:TPU:0, one launch (start us, length us, event | category | flops | bytes accessed | tf_op | source)
XLA Modules:
  0.0 473.5 jit_solution(6626626156504258298)
XLA Ops:
  2.2 4.9 %collective-permute-start = (f32[64,8]{0,1:T(8,128)S(1)}, f32[64,8]{0,1:T(8,128)S(1)}, u32[]{:S(2)}, u32[]{:S(2)}) collective-permute-start(f32[64,8]{0,1:T(8,128)S(1)} %get-tuple-element.42), channel_id=1, source_target_pairs={{0,4},{4,8},{8,12},{12,16},{16,20},{20,24},{24,28},{1,5},{5,9},{9,... | collective-permute-start | bytes 6152 | tf_op jit(solution)/shard_map/ppermute | solution.py:24
  14.8 10.8 %gather_fusion = f32[4096,8]{1,0:T(8,128)S(1)} fusion(f32[384,8]{1,0:T(8,128)S(1)} %copy.228, s32[4096]{0:T(1024)S(1)} %broadcast_clamp_fusion.1), kind=kCustom, calls=%fused_computation | custom fusion | bytes 278528 | tf_op jit(solution)/shard_map/gather | solution.py:50
  27.1 4.5 fusion.2
  31.6 4.1 copy.231
  35.6 5.3 %reshape.161 = f32[4096,24]{1,0:T(8,128)} reshape(f32[64,192,8]{2,1,0:T(8,128)} %copy.231) | data formatting | bytes 786432 | tf_op jit(solution)/shard_map/reshape | solution.py:56
  40.9 23.2 %scatter_custom_fusion = f32[4608,24]{1,0:T(8,128)S(1)} fusion(s32[4096]{0:T(1024)S(1)} %reshape.159, f32[4096,24]{1,0:T(8,128)} %reshape.161, f32[]{:T(128)} %constant.45.clone.1), kind=kCustom, calls=%fused_computation.25 | custom fusion | flops 98304 | bytes 442880 | tf_op jit(solution)/shard_map/scatter-add | solution.py:55
  64.3 5.2 %collective-permute-start.2 = (f32[512,24]{0,1:T(8,128)S(1)}, f32[512,24]{0,1:T(8,128)S(1)}, u32[]{:S(2)}, u32[]{:S(2)}) collective-permute-start(f32[512,24]{0,1:T(8,128)S(1)} %copy.278), channel_id=1, source_target_pairs={{0,4},{4,8},{8,12},{12,16},{16,20},{20,24},{24,28},{1,5},{5,9},{9,... | collective-permute-start | bytes 147464 | tf_op jit(solution)/shard_map/ppermute | solution.py:14
  71.1 2.0 copy.279
  74.6 5.5 %collective-permute-done.4 = f32[512,24]{0,1:T(8,128)S(1)} collective-permute-done((f32[512,24]{0,1:T(8,128)S(1)}, f32[512,24]{0,1:T(8,128)S(1)}, u32[]{:S(2)}, u32[]{:S(2)}) %collective-permute-start.4) | collective-permute-done | bytes 49184 | tf_op jit(solution)/shard_map/ppermute | solution.py:14
  80.7 14.9 %gather_fusion.1 = bf16[4096,24]{1,0:T(8,128)(2,1)} fusion(bf16[4608,24]{1,0:T(8,128)(2,1)S(1)} %copy.235, s32[4096]{0:T(1024)S(1)} %broadcast_clamp_fusion), kind=kCustom, calls=%fused_computation.1 | custom fusion | bytes 409600 | tf_op jit(solution)/shard_map/gather | solution.py:80
  95.6 3.7 reshape.101
  99.3 4.6 convolution_bitcast_fusion.2
  106.2 22.4 %scatter_custom_fusion.1 = f32[384,8]{1,0:T(8,128)S(1)} fusion(s32[4096]{0:T(1024)S(1)} %reshape.167, f32[4096,8]{1,0:T(8,128)S(1)} %copy.239, f32[]{:T(128)} %constant.45.clone.1), kind=kCustom, calls=%fused_computation.57 | custom fusion | flops 32768 | bytes 12292 | tf_op jit(solution)/shard_map/scatter-add | solution.py:89
  130.1 5.4 %collective-permute-start.5 = (f32[64,8]{0,1:T(8,128)S(1)}, f32[64,8]{0,1:T(8,128)S(1)}, u32[]{:S(2)}, u32[]{:S(2)}) collective-permute-start(f32[64,8]{0,1:T(8,128)S(1)} %copy.281), channel_id=1, source_target_pairs={{0,4},{4,8},{8,12},{12,16},{16,20},{20,24},{24,28},{1,5},{5,9},{9,... | collective-permute-start | bytes 6152 | tf_op jit(solution)/shard_map/ppermute | solution.py:14
  137.1 22.3 %psum.21 = f32[8]{0:T(128)S(1)} all-reduce(f32[8]{0:T(128)S(1)} %get-tuple-element.24), channel_id=1, replica_groups=mesh['tiles'=8,'probes'=4] {'tiles'}, use_global_device_ids=true, to_apply=%region_4.5 | all-reduce | flops 8 | bytes 64 | tf_op jit(solution)/shard_map/psum | solution.py:107
  159.5 2.1 collective-permute-start.7
  163.2 4.0 collective-permute-done.8
  167.4 10.8 %gather_fusion.2 = f32[4096,8]{1,0:T(8,128)S(1)} fusion(f32[384,8]{1,0:T(8,128)S(1)} %copy.243, s32[4096]{0:T(1024)S(1)} %broadcast_clamp_fusion.1), kind=kCustom, calls=%fused_computation.2 | custom fusion | bytes 278528 | tf_op jit(solution)/shard_map/gather | solution.py:50
  179.7 4.5 fusion.1
  184.2 4.1 copy.246
  188.2 5.3 %reshape.177 = f32[4096,24]{1,0:T(8,128)} reshape(f32[64,192,8]{2,1,0:T(8,128)} %copy.246) | data formatting | bytes 786432 | tf_op jit(solution)/shard_map/reshape | solution.py:56
  193.5 23.2 %scatter_custom_fusion.2 = f32[4608,24]{1,0:T(8,128)S(1)} fusion(s32[4096]{0:T(1024)S(1)} %reshape.159, f32[4096,24]{1,0:T(8,128)} %reshape.177, f32[]{:T(128)} %constant.45.clone.1), kind=kCustom, calls=%fused_computation.23 | custom fusion | flops 98304 | bytes 442880 | tf_op jit(solution)/shard_map/scatter-add | solution.py:55
  216.9 2.8 collective-permute-start.9
  221.1 2.0 copy.285
  224.6 4.6 collective-permute-done.10
  229.7 14.9 %gather_fusion.3 = bf16[4096,24]{1,0:T(8,128)(2,1)} fusion(bf16[4608,24]{1,0:T(8,128)(2,1)S(1)} %copy.250, s32[4096]{0:T(1024)S(1)} %broadcast_clamp_fusion), kind=kCustom, calls=%fused_computation.3 | custom fusion | bytes 409600 | tf_op jit(solution)/shard_map/gather | solution.py:80
  244.6 3.7 reshape.104
  248.4 4.6 convolution_bitcast_fusion.1
  255.3 22.4 %scatter_custom_fusion.3 = f32[384,8]{1,0:T(8,128)S(1)} fusion(s32[4096]{0:T(1024)S(1)} %reshape.167, f32[4096,8]{1,0:T(8,128)S(1)} %copy.254, f32[]{:T(128)} %constant.45.clone.1), kind=kCustom, calls=%fused_computation.55 | custom fusion | flops 32768 | bytes 12292 | tf_op jit(solution)/shard_map/scatter-add | solution.py:89
  279.2 4.5 collective-permute-start.11
  285.2 20.3 %psum.22 = f32[8]{0:T(128)S(1)} all-reduce(f32[8]{0:T(128)S(1)} %multiply_reduce_fusion.3), channel_id=1, replica_groups=mesh['tiles'=8,'probes'=4] {'tiles'}, use_global_device_ids=true, to_apply=%region_9.10 | all-reduce | flops 8 | bytes 64 | tf_op jit(solution)/shard_map/psum | solution.py:107
  305.7 2.1 collective-permute-start.13
  309.3 4.0 collective-permute-done.14
  313.5 10.8 %gather_fusion.4 = f32[4096,8]{1,0:T(8,128)S(1)} fusion(f32[384,8]{1,0:T(8,128)S(1)} %copy.258, s32[4096]{0:T(1024)S(1)} %broadcast_clamp_fusion.1), kind=kCustom, calls=%fused_computation.4 | custom fusion | bytes 278528 | tf_op jit(solution)/shard_map/gather | solution.py:50
  325.8 4.5 fusion
  330.3 4.1 copy.261
  334.4 5.3 %reshape.193 = f32[4096,24]{1,0:T(8,128)} reshape(f32[64,192,8]{2,1,0:T(8,128)} %copy.261) | data formatting | bytes 786432 | tf_op jit(solution)/shard_map/reshape | solution.py:56
  339.6 23.2 %scatter_custom_fusion.4 = f32[4608,24]{1,0:T(8,128)S(1)} fusion(s32[4096]{0:T(1024)S(1)} %reshape.159, f32[4096,24]{1,0:T(8,128)} %reshape.193, f32[]{:T(128)} %constant.45.clone.1), kind=kCustom, calls=%fused_computation.21 | custom fusion | flops 98304 | bytes 442880 | tf_op jit(solution)/shard_map/scatter-add | solution.py:55
  363.0 2.8 collective-permute-start.15
  367.2 2.0 copy.291
  370.7 4.6 collective-permute-done.16
  375.9 14.9 %gather_fusion.5 = bf16[4096,24]{1,0:T(8,128)(2,1)} fusion(bf16[4608,24]{1,0:T(8,128)(2,1)S(1)} %copy.265, s32[4096]{0:T(1024)S(1)} %broadcast_clamp_fusion), kind=kCustom, calls=%fused_computation.5 | custom fusion | bytes 409600 | tf_op jit(solution)/shard_map/gather | solution.py:80
  390.8 3.7 reshape.107
  394.5 4.6 convolution_bitcast_fusion
  401.4 22.4 %scatter_custom_fusion.5 = f32[384,8]{1,0:T(8,128)S(1)} fusion(s32[4096]{0:T(1024)S(1)} %reshape.167, f32[4096,8]{1,0:T(8,128)S(1)} %copy.269, f32[]{:T(128)} %constant.45.clone.1), kind=kCustom, calls=%fused_computation.53 | custom fusion | flops 32768 | bytes 12292 | tf_op jit(solution)/shard_map/scatter-add | solution.py:89
  425.3 4.5 collective-permute-start.17
  431.2 5.2 %all_gather.3 = f32[256,32]{0,1:T(8,128)S(1)} all-gather(f32[256,8]{0,1:T(8,128)S(1)} %compare_select_fusion.2), channel_id=1, replica_groups=mesh['tiles'=8,'probes'=4] {'probes'}, dimensions={1}, use_global_device_ids=true | all-gather | bytes 40960 | tf_op jit(solution)/shard_map/all_gather | solution.py:117
  436.8 36.1 %psum.23 = f32[8,8,32]{2,0,1:T(8,128)S(1)} all-reduce(f32[8,8,32]{2,0,1:T(8,128)S(1)} %fusion.15), channel_id=1, replica_groups=mesh['tiles'=8,'probes'=4] {'tiles'}, use_global_device_ids=true, to_apply=%region_13.14 | all-reduce | flops 2048 | bytes 16384 | tf_op jit(solution)/shard_map/psum | solution.py:124
  (138 shorter events, 44.3 us)
Async XLA Ops:
  2.2 12.4 %collective-permute-start = (f32[64,8]{0,1:T(8,128)S(1)}, f32[64,8]{0,1:T(8,128)S(1)}, u32[]{:S(2)}, u32[]{:S(2)}) collective-permute-start(f32[64,8]{0,1:T(8,128)S(1)} %get-tuple-element.42), channel_id=1, source_target_pairs={{0,4},{4,8},{8,12},{12,16},{16,20},{20,24},{24,28},{1,5},{5,9},{9,... | collective-permute-start | bytes 6152 | tf_op jit(solution)/shard_map/ppermute | solution.py:24
  7.0 7.5 %collective-permute-start.1 = (f32[64,8]{0,1:T(8,128)S(1)}, f32[64,8]{0,1:T(8,128)S(1)}, u32[]{:S(2)}, u32[]{:S(2)}) collective-permute-start(f32[64,8]{0,1:T(8,128)S(1)} %get-tuple-element.43), channel_id=1, source_target_pairs={{4,0},{8,4},{12,8},{16,12},{20,16},{24,20},{28,24},{5,1},{9,5},{13... | collective-permute-start | bytes 6152 | tf_op jit(solution)/shard_map/ppermute | solution.py:25
  9.0 65.6 %collective-permute-start.3 = (f32[512,3]{0,1:T(4,128)S(1)}, f32[512,3]{0,1:T(4,128)S(1)}, u32[]{:S(2)}, u32[]{:S(2)}) collective-permute-start(f32[512,3]{0,1:T(4,128)S(1)} %slice.92), channel_id=1, source_target_pairs={{4,0},{8,4},{12,8},{16,12},{20,16},{24,20},{28,24},{5,1},{9,5},{13... | collective-permute-start | bytes 18440 | tf_op jit(solution)/shard_map/ppermute | solution.py:14
  40.9 28.6 %copy-start.1 = (s32[64,64]{1,0:T(8,128)S(1)}, s32[64,64]{1,0:T(8,128)}, u32[]{:S(2)}) copy-start(s32[64,64]{1,0:T(8,128)} %param.10) | copy-start | bytes 49156
  64.3 10.2 %collective-permute-start.2 = (f32[512,24]{0,1:T(8,128)S(1)}, f32[512,24]{0,1:T(8,128)S(1)}, u32[]{:S(2)}, u32[]{:S(2)}) collective-permute-start(f32[512,24]{0,1:T(8,128)S(1)} %copy.278), channel_id=1, source_target_pairs={{0,4},{4,8},{8,12},{12,16},{16,20},{20,24},{24,28},{1,5},{5,9},{9,... | collective-permute-start | bytes 147464 | tf_op jit(solution)/shard_map/ppermute | solution.py:14
  69.7 4.8 %copy-start = (f32[4096,3]{0,1:T(4,128)S(1)}, f32[4096,3]{0,1:T(4,128)}, u32[]{:S(2)}) copy-start(f32[4096,3]{0,1:T(4,128)} %param.13) | copy-start | bytes 147460
  73.2 6.9 %collective-permute-start.4 = (f32[512,24]{0,1:T(8,128)S(1)}, f32[512,24]{0,1:T(8,128)S(1)}, u32[]{:S(2)}, u32[]{:S(2)}) collective-permute-start(f32[512,24]{0,1:T(8,128)S(1)} %copy.277), channel_id=1, source_target_pairs={{4,0},{8,4},{12,8},{16,12},{20,16},{24,20},{28,24},{5,1},{9,5},{13... | collective-permute-start | bytes 147464 | tf_op jit(solution)/shard_map/ppermute | solution.py:14
  128.8 6.8 %collective-permute-start.6 = (f32[64,8]{0,1:T(8,128)S(1)}, f32[64,8]{0,1:T(8,128)S(1)}, u32[]{:S(2)}, u32[]{:S(2)}) collective-permute-start(f32[64,8]{0,1:T(8,128)S(1)} %copy.282), channel_id=1, source_target_pairs={{4,0},{8,4},{12,8},{16,12},{20,16},{24,20},{28,24},{5,1},{9,5},{13... | collective-permute-start | bytes 6152 | tf_op jit(solution)/shard_map/ppermute | solution.py:14
  130.1 6.8 %collective-permute-start.5 = (f32[64,8]{0,1:T(8,128)S(1)}, f32[64,8]{0,1:T(8,128)S(1)}, u32[]{:S(2)}, u32[]{:S(2)}) collective-permute-start(f32[64,8]{0,1:T(8,128)S(1)} %copy.281), channel_id=1, source_target_pairs={{0,4},{4,8},{8,12},{12,16},{16,20},{20,24},{24,28},{1,5},{5,9},{9,... | collective-permute-start | bytes 6152 | tf_op jit(solution)/shard_map/ppermute | solution.py:14
  137.0 41.1 %copy-start.3 = (f32[256,8]{0,1:T(8,128)}, f32[256,8]{0,1:T(8,128)S(1)}, u32[]{:S(2)}) copy-start(f32[256,8]{0,1:T(8,128)S(1)} %get-tuple-element.25) | copy-start | bytes 24580
  159.5 3.6 collective-permute-start.7
  161.7 5.5 %collective-permute-start.8 = (f32[64,8]{0,1:T(8,128)S(1)}, f32[64,8]{0,1:T(8,128)S(1)}, u32[]{:S(2)}, u32[]{:S(2)}) collective-permute-start(f32[64,8]{0,1:T(8,128)S(1)} %get-tuple-element.41), channel_id=1, source_target_pairs={{4,0},{8,4},{12,8},{16,12},{20,16},{24,20},{28,24},{5,1},{9,5},{13... | collective-permute-start | bytes 6152 | tf_op jit(solution)/shard_map/ppermute | solution.py:25
  216.9 7.6 %collective-permute-start.9 = (f32[512,24]{0,1:T(8,128)S(1)}, f32[512,24]{0,1:T(8,128)S(1)}, u32[]{:S(2)}, u32[]{:S(2)}) collective-permute-start(f32[512,24]{0,1:T(8,128)S(1)} %copy.284), channel_id=1, source_target_pairs={{0,4},{4,8},{8,12},{12,16},{16,20},{20,24},{24,28},{1,5},{5,9},{9,... | collective-permute-start | bytes 147464 | tf_op jit(solution)/shard_map/ppermute | solution.py:14
  223.2 6.0 %collective-permute-start.10 = (f32[512,24]{0,1:T(8,128)S(1)}, f32[512,24]{0,1:T(8,128)S(1)}, u32[]{:S(2)}, u32[]{:S(2)}) collective-permute-start(f32[512,24]{0,1:T(8,128)S(1)} %copy.283), channel_id=1, source_target_pairs={{4,0},{8,4},{12,8},{16,12},{20,16},{24,20},{28,24},{5,1},{9,5},{13... | collective-permute-start | bytes 147464 | tf_op jit(solution)/shard_map/ppermute | solution.py:14
  277.9 5.9 %collective-permute-start.12 = (f32[64,8]{0,1:T(8,128)S(1)}, f32[64,8]{0,1:T(8,128)S(1)}, u32[]{:S(2)}, u32[]{:S(2)}) collective-permute-start(f32[64,8]{0,1:T(8,128)S(1)} %copy.288), channel_id=1, source_target_pairs={{4,0},{8,4},{12,8},{16,12},{20,16},{24,20},{28,24},{5,1},{9,5},{13... | collective-permute-start | bytes 6152 | tf_op jit(solution)/shard_map/ppermute | solution.py:14
  279.2 5.9 %collective-permute-start.11 = (f32[64,8]{0,1:T(8,128)S(1)}, f32[64,8]{0,1:T(8,128)S(1)}, u32[]{:S(2)}, u32[]{:S(2)}) collective-permute-start(f32[64,8]{0,1:T(8,128)S(1)} %copy.287), channel_id=1, source_target_pairs={{0,4},{4,8},{8,12},{12,16},{16,20},{20,24},{24,28},{1,5},{5,9},{9,... | collective-permute-start | bytes 6152 | tf_op jit(solution)/shard_map/ppermute | solution.py:14
  305.7 3.6 collective-permute-start.13
  307.8 5.5 %collective-permute-start.14 = (f32[64,8]{0,1:T(8,128)S(1)}, f32[64,8]{0,1:T(8,128)S(1)}, u32[]{:S(2)}, u32[]{:S(2)}) collective-permute-start(f32[64,8]{0,1:T(8,128)S(1)} %get-tuple-element.39), channel_id=1, source_target_pairs={{4,0},{8,4},{12,8},{16,12},{20,16},{24,20},{28,24},{5,1},{9,5},{13... | collective-permute-start | bytes 6152 | tf_op jit(solution)/shard_map/ppermute | solution.py:25
  363.0 7.6 %collective-permute-start.15 = (f32[512,24]{0,1:T(8,128)S(1)}, f32[512,24]{0,1:T(8,128)S(1)}, u32[]{:S(2)}, u32[]{:S(2)}) collective-permute-start(f32[512,24]{0,1:T(8,128)S(1)} %copy.290), channel_id=1, source_target_pairs={{0,4},{4,8},{8,12},{12,16},{16,20},{20,24},{24,28},{1,5},{5,9},{9,... | collective-permute-start | bytes 147464 | tf_op jit(solution)/shard_map/ppermute | solution.py:14
  369.3 6.0 %collective-permute-start.16 = (f32[512,24]{0,1:T(8,128)S(1)}, f32[512,24]{0,1:T(8,128)S(1)}, u32[]{:S(2)}, u32[]{:S(2)}) collective-permute-start(f32[512,24]{0,1:T(8,128)S(1)} %copy.289), channel_id=1, source_target_pairs={{4,0},{8,4},{12,8},{16,12},{20,16},{24,20},{28,24},{5,1},{9,5},{13... | collective-permute-start | bytes 147464 | tf_op jit(solution)/shard_map/ppermute | solution.py:14
  400.5 35.9 %copy-start.4 = (s32[256]{0:T(256)S(1)}, s32[256]{0:T(256)}, u32[]{:S(2)}) copy-start(s32[256]{0:T(256)} %param.15) | copy-start | bytes 3076
  424.0 5.9 %collective-permute-start.18 = (f32[64,8]{0,1:T(8,128)S(1)}, f32[64,8]{0,1:T(8,128)S(1)}, u32[]{:S(2)}, u32[]{:S(2)}) collective-permute-start(f32[64,8]{0,1:T(8,128)S(1)} %copy.294), channel_id=1, source_target_pairs={{4,0},{8,4},{12,8},{16,12},{20,16},{24,20},{28,24},{5,1},{9,5},{13... | collective-permute-start | bytes 6152 | tf_op jit(solution)/shard_map/ppermute | solution.py:14
  425.3 5.9 %collective-permute-start.17 = (f32[64,8]{0,1:T(8,128)S(1)}, f32[64,8]{0,1:T(8,128)S(1)}, u32[]{:S(2)}, u32[]{:S(2)}) collective-permute-start(f32[64,8]{0,1:T(8,128)S(1)} %copy.293), channel_id=1, source_target_pairs={{0,4},{4,8},{8,12},{12,16},{16,20},{20,24},{24,28},{1,5},{5,9},{9,... | collective-permute-start | bytes 6152 | tf_op jit(solution)/shard_map/ppermute | solution.py:14
  431.2 42.2 %copy-start.2 = (f32[256,8]{0,1:T(8,128)}, f32[256,8]{0,1:T(8,128)S(1)}, u32[]{:S(2)}) copy-start(f32[256,8]{0,1:T(8,128)S(1)} %compare_select_fusion.2) | copy-start | bytes 24580
where the time goes:
time: 475 us; the launch traced here: 473 us
  local copies, waits for them, and re-layouts  144 us (30%)
  other arithmetic  142 us (30%)
  blocking collectives  83.9 us (18%)
  starting transfers between devices  47.8 us (10%)
  matrix products  27.6 us (6%)
  waiting for transfers between devices  26.4 us (6%)
    scatter-add x3, other arithmetic, hessian(): jax.ops.segment_sum(forward.reshape(elem_slots * node_slots, 3 * group_si...  69.7 us
    scatter-add x3, other arithmetic, hessian(): jax.ops.segment_sum(partials.reshape(elem_slots * node_slots, group_size)...  67.2 us
    gather x3, local copies, waits for them, and re-layouts, hessian(): node_window[connectivity].reshape(elem_slots, block_order, group_size)  44.7 us
    psum x2, blocking collectives, shards(): squares = lax.psum(jnp.sum(current * current, axis=0), 'tiles')  42.6 us
    psum x1, blocking collectives, shards(): gram = lax.psum(partial_gram, 'tiles')  36.1 us
    gather x6, local copies, waits for them, and re-layouts, hessian(): picked = window[basal_map]  35.6 us
    ppermute x13, starting transfers between devices, from_behind(): return lax.ppermute(block, axis, route)  34.4 us
    ppermute x13, waiting for transfers between devices, from_behind(): return lax.ppermute(block, axis, route)  18.4 us
  transfers between devices with their start and end apart: 19, of which 8 were waited for; matrix products, arithmetic and copies ran while one was open for 14% of the time, Pallas kernels for 0%

commit v1 on v0

v1 whole, which is shorter than its diff:
```python
import functools

import jax
import jax.numpy as jnp
from jax import lax
from jax.experimental import pallas as pl
from jax.experimental.pallas import tpu as pltpu
from jax.sharding import PartitionSpec as P

HALO = 512
POWER = 2
RIM = 64
LANES = 128
VMEM_BYTES = 48 * 1024 * 1024

F32 = jnp.float32
BF16 = jnp.bfloat16


def dot(a, b):
    return lax.dot_general(a, b, (((1,), (0,)), ((), ())), preferred_element_type=F32)


def dot_nt(a, b):
    return lax.dot_general(a, b, (((1,), (1,)), ((), ())), preferred_element_type=F32)


def split(x):
    hi = x.astype(BF16)
    return hi, (x - hi.astype(F32)).astype(BF16)


def from_behind(block, axis, distance):
    devices = range(lax.axis_size(axis))
    route = [(i - distance, i) for i in devices if i - distance in devices]
    return lax.ppermute(block, axis, route)


def rows_iota(shape):
    return lax.broadcasted_iota(jnp.int32, shape, 0)


def lanes_iota(shape):
    return lax.broadcasted_iota(jnp.int32, shape, 1)


def one_hot_columns(ids, depth):
    rows = rows_iota((depth, LANES))
    parts = [
        jnp.where(rows == ids[m : m + 1, :], F32(1), F32(0)).astype(BF16)
        for m in range(ids.shape[0])
    ]
    return jnp.concatenate(parts, axis=1)


def spread_matrix(node_slots, padded_order):
    shape = (2 * node_slots, 2 * padded_order)
    row = rows_iota(shape)
    start = (row // node_slots) * padded_order + 3 * (row % node_slots)
    gap = lanes_iota(shape) - start
    return jnp.where((gap >= 0) & (gap < 3), F32(1), F32(0)).astype(BF16)


def order_matrix(node_slots, padded_order):
    pair = 2 * node_slots
    shape = (2 * padded_order, 3 * pair)
    col = lanes_iota(shape)
    inner = col % pair
    source = (inner // node_slots) * padded_order + 3 * (inner % node_slots) + col // pair
    return jnp.where(rows_iota(shape) == source, F32(1), F32(0)).astype(BF16)


def same_colour(meta):
    ids = meta[8:, :]
    return (ids % 2) == (rows_iota(ids.shape) % 2)


def start_probes(meta):
    signs = (2 * meta[:8, :] - 1).astype(F32)
    return jnp.where(same_colour(meta), signs, F32(0))


def total_field(before, own, after):
    lane = lanes_iota((own.shape[0], LANES))
    first = own[:, :LANES] + jnp.where(lane < RIM, before[:, 2 * LANES :], F32(0))
    second = own[:, LANES : 2 * LANES] + jnp.where(lane >= RIM, after[:, 2 * LANES :], F32(0))
    return jnp.concatenate([first, second], axis=1)


def field_of(g_ref, t, tiles):
    zero = jnp.zeros(g_ref.shape[1:], F32)
    if isinstance(t, int):
        before = g_ref[t - 1] if t > 0 else zero
        after = g_ref[t + 1] if t < tiles - 1 else zero
    else:
        before = jnp.where(t > 0, g_ref[jnp.maximum(t - 1, 0)], zero)
        after = jnp.where(t < tiles - 1, g_ref[jnp.minimum(t + 1, tiles - 1)], zero)
    return total_field(before, g_ref[t], after)


def masked(field, meta, keep_same):
    same = same_colour(meta)
    return jnp.where(same if keep_same else ~same, field, F32(0))


def forward_kernel(first, keep_same, want_field, tiles, *refs):
    scalars, meta_ref, *refs = refs
    if not first:
        g_ref, *refs = refs
    conn_ref, cell_ref, fr_ref, blocks_hbm, *refs = refs
    nodes_ref, lead_ref, spill_ref, *refs = refs
    if want_field:
        field_ref, *refs = refs
    blocks, f_ref, v_ref, onehot_ref, sem = refs

    slots = blocks.shape[0]
    order = blocks.shape[1]
    node_slots = order // 3
    padded_order = f_ref.shape[1] // 2
    pairs = slots // 2

    load = pltpu.make_async_copy(blocks_hbm, blocks, sem)
    load.start()

    tile = scalars[0]
    count = scalars[1]

    if first:
        current = lambda t: start_probes(meta_ref[t])
        scale = F32(1)
    else:
        current = lambda t: masked(field_of(g_ref, t, tiles), meta_ref[t], keep_same)

        def add_squares(t, acc):
            part = current(t)
            part = part * part
            return acc + part[:, :LANES] + part[:, LANES:]

        squares = lax.fori_loop(0, tiles, add_squares, jnp.zeros((8, LANES), F32), unroll=tiles <= 8)
        squares = jnp.sum(squares, axis=1, keepdims=True)
        scale = jnp.sqrt(squares / (tiles * 2 * LANES) + F32(1e-06))

    own = current(tile)
    if want_field:
        field_ref[...] = own.T
    below = jnp.where(tile > 0, current(jnp.maximum(tile - 1, 0)), F32(0))
    above = jnp.where(tile < tiles - 1, current(jnp.minimum(tile + 1, tiles - 1)), F32(0))
    lane = lanes_iota((8, LANES))
    rims = jnp.where(lane < RIM, above[:, :LANES], below[:, LANES:])
    window = jnp.concatenate([own[:, :LANES], own[:, LANES:], rims], axis=0)
    if not first:
        window = window / jnp.concatenate([scale, scale, scale], axis=0)

    cells = cell_ref[...]
    hi, lo = split(window)
    picked = dot(jnp.concatenate([hi, lo], axis=0), one_hot_columns(cells % LANES, LANES))
    tops = []
    rests = []
    for m in range(pairs):
        part = picked[:, m * LANES : (m + 1) * LANES]
        which = cells[m : m + 1, :] // LANES
        for base, out in ((0, tops), (24, rests)):
            chosen = jnp.where(which == 0, part[base : base + 8], F32(0))
            for level in (1, 2):
                at = base + 8 * level
                chosen = jnp.where(which == level, part[at : at + 8], chosen)
            out.append(chosen)
    stacked = jnp.concatenate(tops + rests, axis=0).astype(BF16)
    spread = dot(stacked, spread_matrix(node_slots, padded_order))
    half = 8 * pairs
    spread = spread[:half] + spread[half:]

    conn = conn_ref[...]
    onehot_ref[...] = one_hot_columns(conn % HALO, HALO)
    f_ref[...] = jnp.zeros_like(f_ref)

    load.wait()
    for m in range(pairs):
        inputs = spread[8 * m : 8 * m + 8, :] * fr_ref[m : m + 1, :]
        for side in range(2):
            at = side * padded_order
            slot = 2 * m + side
            out = dot_nt(inputs[:, at : at + order].astype(BF16), blocks[slot])
            f_ref[8 * m : 8 * m + 8, at : at + order] = jnp.where(slot < count, out, F32(0))

    ordered = dot(f_ref[...].astype(BF16), order_matrix(node_slots, padded_order))
    levels = nodes_ref.shape[0] // 24
    for m in range(pairs):
        which = conn[m : m + 1, :] // HALO
        values = [
            ordered[8 * m : 8 * m + 8, c * LANES : (c + 1) * LANES] for c in range(3)
        ]
        rows = [
            jnp.where(which == level, values[c], F32(0)) for level in range(levels) for c in range(3)
        ]
        v_ref[:, m * LANES : (m + 1) * LANES] = jnp.concatenate(rows, axis=0).astype(BF16)
    nodes = dot_nt(v_ref[...], onehot_ref[...])
    nodes_ref[...] = nodes
    lead_ref[...] = nodes[:24]
    spill_ref[...] = nodes[24 * (levels - 1) :]


def adjoint_kernel(
    scalars,
    nodes_ref,
    lead_ref,
    rim_ref,
    weight_ref,
    conn_ref,
    cell_ref,
    fr_ref,
    blocks_hbm,
    out_ref,
    blocks,
    p_ref,
    a_ref,
    v_ref,
    sem,
):
    slots = blocks.shape[0]
    order = blocks.shape[1]
    node_slots = order // 3
    padded_order = p_ref.shape[1] // 2
    pairs = slots // 2
    levels = nodes_ref.shape[0] // 24
    load = pltpu.make_async_copy(blocks_hbm, blocks, sem)
    load.start()
    count = scalars[1]

    rows = []
    for level in range(levels):
        for c in range(3):
            at = 24 * level + 8 * c
            value = nodes_ref[at : at + 8, :]
            if level == 0:
                value = value + lead_ref[8 * c : 8 * c + 8, :]
            if level == levels - 1:
                value = value + rim_ref[8 * c : 8 * c + 8, :]
            rows.append(value * weight_ref[3 * level + c : 3 * level + c + 1, :])
    weighted = jnp.concatenate(rows, axis=0).astype(BF16)

    conn = conn_ref[...]
    step = 2
    for start in range(0, pairs, step):
        here = conn[start : start + step, :]
        found = dot(weighted, one_hot_columns(here % HALO, HALO))
        for i in range(step):
            m = start + i
            which = here[i : i + 1, :] // HALO
            part = found[:, i * LANES : (i + 1) * LANES]
            chosen = jnp.where(which == 0, part[:24], F32(0))
            for level in range(1, levels):
                chosen = jnp.where(which == level, part[24 * level : 24 * level + 24], chosen)
            for c in range(3):
                a_ref[8 * m : 8 * m + 8, c * LANES : (c + 1) * LANES] = chosen[8 * c : 8 * c + 8]
    natural = dot_nt(a_ref[...].astype(BF16), order_matrix(node_slots, padded_order))
    p_ref[...] = jnp.zeros_like(p_ref)

    load.wait()
    for m in range(pairs):
        for side in range(2):
            at = side * padded_order
            slot = 2 * m + side
            out = dot(natural[8 * m : 8 * m + 8, at : at + order].astype(BF16), blocks[slot])
            out = out * fr_ref[m : m + 1, at : at + order]
            p_ref[8 * m : 8 * m + 8, at : at + order] = jnp.where(slot < count, out, F32(0))

    hi, lo = split(p_ref[...])
    partial = dot_nt(jnp.concatenate([hi, lo], axis=0), spread_matrix(node_slots, padded_order))
    half = 8 * pairs
    partial = partial[:half] + partial[half:]
    cells = cell_ref[...]
    for m in range(pairs):
        which = cells[m : m + 1, :] // LANES
        value = partial[8 * m : 8 * m + 8, :]
        rows = jnp.concatenate([jnp.where(which == level, value, F32(0)) for level in range(3)], axis=0)
        hi = rows.astype(BF16).astype(F32)
        both = jnp.concatenate([hi, rows - hi], axis=0)
        v_ref[:, m * LANES : (m + 1) * LANES] = both.astype(BF16)
    basal = dot_nt(v_ref[...], one_hot_columns(cells % LANES, LANES))
    basal = basal[:24] + basal[24:]
    for level in range(3):
        out_ref[:, level * LANES : (level + 1) * LANES] = basal[8 * level : 8 * level + 8]


def gram_kernel(keep_same, tiles, groups, scalars, meta_ref, g_ref, field_ref, gram_ref):
    tile = scalars[0]
    group = scalars[2]
    clusters = gram_ref.shape[0]

    def field(t, p):
        zero = jnp.zeros(g_ref.shape[2:], F32)
        if isinstance(t, int):
            before = g_ref[t - 1, p] if t > 0 else zero
            after = g_ref[t + 1, p] if t < tiles - 1 else zero
        else:
            before = jnp.where(t > 0, g_ref[jnp.maximum(t - 1, 0), p], zero)
            after = jnp.where(t < tiles - 1, g_ref[jnp.minimum(t + 1, tiles - 1), p], zero)
        return masked(total_field(before, g_ref[t, p], after), meta_ref[t], keep_same)

    field_ref[...] = field(tile, group).T

    def add_tile(t, acc):
        ids = meta_ref[t][8:, :]
        mine = field(t, group)
        every = jnp.concatenate([field(t, p) for p in range(groups)], axis=0)
        left = jnp.concatenate(
            [jnp.where(ids == k, mine, F32(0)) for k in range(clusters)], axis=0
        )
        return acc + lax.dot_general(
            left,
            every,
            (((1,), (1,)), ((), ())),
            precision=lax.Precision.HIGHEST,
            preferred_element_type=F32,
        )

    acc = jnp.zeros((8 * clusters, 8 * groups), F32)
    acc = lax.fori_loop(0, tiles, add_tile, acc, unroll=tiles <= 8)
    gram_ref[...] = acc.reshape(gram_ref.shape)


def shards(
    blocks, connectivity, basal_map, friction, elem_counts, obs_weight, sign_bits, cluster_ids
):
    slots, order, _ = blocks.shape
    node_slots = connectivity.shape[1]
    node_count = obs_weight.shape[0]
    cell_count, group_size = sign_bits.shape
    tiles = lax.axis_size("tiles")
    groups = lax.axis_size("probes")
    pairs = slots * node_slots // LANES
    levels = node_count // HALO + 1
    padded_order = 2 * LANES
    window = cell_count + 2 * RIM

    meta = jnp.concatenate(
        [sign_bits.T, jnp.broadcast_to(cluster_ids[None, :], (8, cell_count))], axis=0
    )
    meta = lax.all_gather(meta, "tiles", axis=0)
    weight = obs_weight.reshape(node_count // HALO, HALO, 3).transpose(0, 2, 1)
    weight_next = from_behind(weight[0], "tiles", -1)
    weight = jnp.concatenate([weight.reshape(-1, HALO), weight_next], axis=0)
    conn = connectivity.reshape(pairs, LANES)
    cells = ((basal_map + (window - RIM)) % window).reshape(pairs, LANES)
    fr = jnp.pad(friction.reshape(slots, order), ((0, 0), (0, padded_order - order)))
    fr = fr.reshape(pairs, 2 * padded_order)
    scalars = jnp.stack(
        [lax.axis_index("tiles"), elem_counts[0], lax.axis_index("probes")]
    ).astype(jnp.int32)

    smem = pl.BlockSpec(memory_space=pltpu.SMEM)
    vmem = pl.BlockSpec(memory_space=pltpu.VMEM)
    anywhere = pl.BlockSpec(memory_space=pl.ANY)
    params = pltpu.CompilerParams(vmem_limit_bytes=VMEM_BYTES)

    def forward(gathered, keep_same, want_field):
        first = gathered is None
        out_shape = [
            jax.ShapeDtypeStruct((24 * levels, HALO), F32),
            jax.ShapeDtypeStruct((24, HALO), F32),
            jax.ShapeDtypeStruct((24, HALO), F32),
        ]
        if want_field:
            out_shape.append(jax.ShapeDtypeStruct((cell_count, group_size), F32))
        operands = [scalars, meta] + ([] if first else [gathered]) + [conn, cells, fr, blocks]
        return pl.pallas_call(
            functools.partial(forward_kernel, first, keep_same, want_field, tiles),
            out_shape=out_shape,
            in_specs=[smem] + [vmem] * (len(operands) - 2) + [anywhere],
            out_specs=[vmem] * len(out_shape),
            scratch_shapes=[
                pltpu.VMEM(blocks.shape, BF16),
                pltpu.VMEM((8 * pairs, 2 * padded_order), F32),
                pltpu.VMEM((24 * levels, pairs * LANES), BF16),
                pltpu.VMEM((HALO, pairs * LANES), BF16),
                pltpu.SemaphoreType.DMA,
            ],
            compiler_params=params,
            name="forward",
        )(*operands)

    def adjoint(nodes, lead, rim):
        return pl.pallas_call(
            adjoint_kernel,
            out_shape=jax.ShapeDtypeStruct((group_size, window), F32),
            in_specs=[smem] + [vmem] * 7 + [anywhere],
            out_specs=vmem,
            scratch_shapes=[
                pltpu.VMEM(blocks.shape, BF16),
                pltpu.VMEM((8 * pairs, 2 * padded_order), F32),
                pltpu.VMEM((8 * pairs, 3 * LANES), F32),
                pltpu.VMEM((48, pairs * LANES), BF16),
                pltpu.SemaphoreType.DMA,
            ],
            compiler_params=params,
            name="adjoint",
        )(scalars, nodes, lead, rim, weight, conn, cells, fr, blocks)

    gathered = None
    samples = None
    for step in range(POWER + 1):
        nodes, lead, spill, *field = forward(gathered, step % 2 == 0, step == 1)
        if field:
            samples = field[0]
        from_earlier = from_behind(spill, "tiles", 1)
        from_later = from_behind(lead, "tiles", -1)
        basal = adjoint(nodes, from_earlier, from_later)
        axes = "tiles" if step < POWER else ("tiles", "probes")
        gathered = lax.all_gather(basal, axes, axis=0)

    gathered = gathered.reshape(tiles, groups, group_size, window)
    refined, gram = pl.pallas_call(
        functools.partial(gram_kernel, POWER % 2 == 1, tiles, groups),
        out_shape=[
            jax.ShapeDtypeStruct((cell_count, group_size), F32),
            jax.ShapeDtypeStruct((tiles, group_size, groups * group_size), F32),
        ],
        in_specs=[smem, vmem, vmem],
        out_specs=[vmem, vmem],
        compiler_params=params,
        name="gram",
    )(scalars, meta, gathered)
    return (samples, refined, gram)


def solution(mesh):
    in_specs = (
        P("tiles", None, None),
        P("tiles", None),
        P("tiles", None),
        P("tiles", None, None),
        P("tiles"),
        P("tiles", None),
        P("tiles", "probes"),
        P("tiles"),
    )
    out_specs = (P("tiles", "probes"), P("tiles", "probes"), P(None, "probes", None))
    return jax.shard_map(shards, mesh=mesh, in_specs=in_specs, out_specs=out_specs, check_vma=False)
```

time: 475 us -> 213 us (0.45)
  other arithmetic: 142 us -> 1.56 us
  local copies, waits for them, and re-layouts: 144 us -> 4.88 us
  blocking collectives: 83.9 us -> 137 us
  Pallas kernels: 0 us -> 44 us
  starting transfers between devices: 47.8 us -> 10.8 us
  matrix products: 27.6 us -> 0 us
  waiting for transfers between devices: 26.4 us -> 13.1 us
    scatter-add x6 -> x0, other arithmetic: 137 us -> none  [the longest x3 69.7 us: hessian(): jax.ops.segment_sum(forward.reshape(elem_slots * node_slots, 3 * group_si...]
    all_gather x1 -> x4, blocking collectives: 5.18 us -> 137 us  [the longest x3 102 us: shards(): gathered = lax.all_gather(basal, axes, axis=0)]
    gather x9 -> x0, local copies, waits for them, and re-layouts: 80.3 us -> none  [the longest x3 44.7 us: hessian(): node_window[connectivity].reshape(elem_slots, block_order, group_size)]
    psum x3 -> x0, blocking collectives: 78.7 us -> none  [the longest x2 42.6 us: shards(): squares = lax.psum(jnp.sum(current * current, axis=0), 'tiles')]
    pallas_call x0 -> x7, Pallas kernels: none -> 44 us  [the longest x3 22.7 us: forward(): pl.pallas_call(functools.partial(forward_kernel, first, keep_same, want_f...]
    dot_general x7 -> x0, matrix products: 27.6 us -> none  [the longest x3 13.7 us: hessian(): jnp.einsum('eji,ejp->eip', blocks, adjoint_in, preferred_element_type=jnp...]
    reshape x6 -> x5, local copies, waits for them, and re-layouts: 26.9 us -> 1 us  [the longest x1 0.83 us: shards(): conn = connectivity.reshape(pairs, LANES)]
    ppermute x13 -> x7, starting transfers between devices: 34.4 us -> 10.8 us  [from_behind(): return lax.ppermute(block, axis, route)]
  transfers between devices with their start and end apart: 19 -> 7, of which waited for: 8 -> 5; matrix products, arithmetic and copies ran while one was open for 14% -> 2% of each run, Pallas kernels for 0% -> 3%
where the time goes in v1:
time: 213 us; the launch traced here: 212 us
  blocking collectives  137 us (64%)
  Pallas kernels  44 us (21%)
  waiting for transfers between devices  13.1 us (6%)
  starting transfers between devices  10.8 us (5%)
  local copies, waits for them, and re-layouts  4.88 us (2%)
    all_gather x3, blocking collectives, shards(): gathered = lax.all_gather(basal, axes, axis=0)  102 us
    all_gather x1, blocking collectives, shards(): meta = lax.all_gather(meta, 'tiles', axis=0)  34.4 us
    pallas_call x3, Pallas kernels, forward(): pl.pallas_call(functools.partial(forward_kernel, first, keep_same, want_f...  22.7 us
    pallas_call x3, Pallas kernels, adjoint(): pl.pallas_call(adjoint_kernel, out_shape=jax.ShapeDtypeStruct((group_size...  19.6 us
    ppermute x7, waiting for transfers between devices, from_behind(): return lax.ppermute(block, axis, route)  13.1 us
    ppermute x7, starting transfers between devices, from_behind(): return lax.ppermute(block, axis, route)  10.8 us
  transfers between devices with their start and end apart: 7, of which 5 were waited for; matrix products, arithmetic and copies ran while one was open for 2% of the time, Pallas kernels for 3%

profile of v1, /device:TPU:0, one launch (start us, length us, event | category | flops | bytes accessed | tf_op | source)
XLA Modules:
  0.0 212.4 jit_solution(17816390277283343026)
XLA Ops:
  0.6 0.0 copy-start
  0.6 0.8 slice_bitcast_fusion
  1.4 1.3 collective-permute-start.2
  3.3 0.8 reshape.28.refs_2_.conn_ref.refs_3_
  4.2 0.8 add_select_fusion
  5.0 0.1 reshape.29.refs_3_.cell_ref.refs_4_
  5.0 0.7 broadcast_in_dim.2
  5.7 0.7 pad_add_fusion
  6.4 34.4 %all-gather = s32[128,256]{1,0:T(8,128)S(1)} all-gather(s32[16,256]{1,0:T(8,128)S(1)} %pad_add_fusion), channel_id=2, replica_groups=mesh['tiles'=8,'probes'=4] {'tiles'}, dimensions={0}, use_global_device_ids=true | all-gather | bytes 147456 | tf_op jit(solution)/shard_map/all_gather | solution.py:340
  40.8 1.0 copy.13
  41.9 0.1 copy.17
  42.0 0.1 pad_add_fusion.1.refs_0_.scalars
  42.1 7.4 %forward.3 = (f32[216,512]{1,0:T(8,128)S(1)}, f32[24,512]{1,0:T(8,128)S(1)}, f32[24,512]{1,0:T(8,128)S(1)}) custom-call(s32[3]{0:T(128)S(1)} %pad_add_fusion.1.refs_0_.scalars, s32[8,16,256]{2,1,0:T(8,128)S(1)} %bitcast.14, s32[32,128]{1,0:T(8,128)S(1)} %reshape.28.refs_2_.conn_ref.refs_3_, s32[32,128]{1,0:T(8,128)S(1)} %reshape.29.refs_3_.cell_ref.refs_4_, ...), custom_call_target="tpu_custom_call" | custom-call | tf_op jit(solution)/shard_map/forward/pallas_call | solution.py:367
  49.5 2.5 %collective-permute-start = (f32[24,512]{1,0:T(8,128)S(1)}, f32[24,512]{1,0:T(8,128)S(1)}, u32[]{:S(2)}, u32[]{:S(2)}) collective-permute-start(f32[24,512]{1,0:T(8,128)S(1)} %get-tuple-element.16), channel_id=1, source_target_pairs={{0,4},{4,8},{8,12},{12,16},{16,20},{20,24},{24,28},{1,5},{5,9},{9,... | collective-permute-start | bytes 147464 | tf_op jit(solution)/shard_map/ppermute | solution.py:36
  52.0 1.3 collective-permute-start.1
  53.3 0.0 copy-done
  53.3 0.0 collective-permute-done.2
  53.3 0.3 collective-permute-done.lead_ref
  53.7 4.3 %collective-permute-done.1.rim_ref = f32[24,512]{1,0:T(8,128)S(1)} collective-permute-done((f32[24,512]{1,0:T(8,128)S(1)}, f32[24,512]{1,0:T(8,128)S(1)}, u32[]{:S(2)}, u32[]{:S(2)}) %collective-permute-start.1) | collective-permute-done | bytes 49184 | tf_op jit(solution)/shard_map/ppermute | solution.py:36
  57.9 6.5 %adjoint.3 = f32[8,384]{1,0:T(8,128)S(1)} custom-call(s32[3]{0:T(128)S(1)} %pad_add_fusion.1.refs_0_.scalars, f32[216,512]{1,0:T(8,128)S(1)} %get-tuple-element.15.nodes_ref, f32[24,512]{1,0:T(8,128)S(1)} %collective-permute-done.lead_ref, f32[24,512]{1,0:T(8,128)S(1)} %collective-permute-done.1.rim_ref, ...), custom_call_target="tpu_custom_call" | custom-call | tf_op jit(solution)/shard_map/adjoint/pallas_call | solution.py:384
  64.5 30.8 %all-gather.1 = f32[64,384]{1,0:T(8,128)S(1)} all-gather(f32[8,384]{1,0:T(8,128)S(1)} %adjoint.3), channel_id=3, replica_groups=mesh['tiles'=8,'probes'=4] {'tiles'}, dimensions={0}, use_global_device_ids=true | all-gather | bytes 110592 | tf_op jit(solution)/shard_map/all_gather | solution.py:410
  95.3 7.6 %forward.4 = (f32[216,512]{1,0:T(8,128)S(1)}, f32[24,512]{1,0:T(8,128)S(1)}, f32[24,512]{1,0:T(8,128)S(1)}, f32[256,8]{1,0:T(8,128)S(1)}) custom-call(s32[3]{0:T(128)S(1)} %pad_add_fusion.1.refs_0_.scalars, s32[8,16,256]{2,1,0:T(8,128)S(1)} %bitcast.15, f32[8,8,384]{2,1,0:T(8,128)S(1)} %bitcast.19, s32[32,128]{1,0:T(8,128)S(1)} %reshape.28.refs_2_.conn_ref.refs_3_, ...), custom_call_target="tpu_custom_call" | custom-call | tf_op jit(solution)/shard_map/forward/pallas_call | solution.py:367
  102.9 1.5 collective-permute-start.3
  104.4 1.3 collective-permute-start.4
  105.7 0.4 collective-permute-done.3.lead_ref
  106.1 4.3 %collective-permute-done.4.rim_ref = f32[24,512]{1,0:T(8,128)S(1)} collective-permute-done((f32[24,512]{1,0:T(8,128)S(1)}, f32[24,512]{1,0:T(8,128)S(1)}, u32[]{:S(2)}, u32[]{:S(2)}) %collective-permute-start.4) | collective-permute-done | bytes 49184 | tf_op jit(solution)/shard_map/ppermute | solution.py:36
  110.4 6.5 %adjoint.4 = f32[8,384]{1,0:T(8,128)S(1)} custom-call(s32[3]{0:T(128)S(1)} %pad_add_fusion.1.refs_0_.scalars, f32[216,512]{1,0:T(8,128)S(1)} %get-tuple-element.19.nodes_ref, f32[24,512]{1,0:T(8,128)S(1)} %collective-permute-done.3.lead_ref, f32[24,512]{1,0:T(8,128)S(1)} %collective-permute-done.4.rim_ref, ...), custom_call_target="tpu_custom_call" | custom-call | tf_op jit(solution)/shard_map/adjoint/pallas_call | solution.py:384
  116.9 30.7 %all-gather.2 = f32[64,384]{1,0:T(8,128)S(1)} all-gather(f32[8,384]{1,0:T(8,128)S(1)} %adjoint.4), channel_id=4, replica_groups=mesh['tiles'=8,'probes'=4] {'tiles'}, dimensions={0}, use_global_device_ids=true | all-gather | bytes 110592 | tf_op jit(solution)/shard_map/all_gather | solution.py:410
  147.6 7.7 %forward.5 = (f32[216,512]{1,0:T(8,128)S(1)}, f32[24,512]{1,0:T(8,128)S(1)}, f32[24,512]{1,0:T(8,128)S(1)}) custom-call(s32[3]{0:T(128)S(1)} %pad_add_fusion.1.refs_0_.scalars, s32[8,16,256]{2,1,0:T(8,128)S(1)} %bitcast.16, f32[8,8,384]{2,1,0:T(8,128)S(1)} %bitcast.20, s32[32,128]{1,0:T(8,128)S(1)} %reshape.28.refs_2_.conn_ref.refs_3_, ...), custom_call_target="tpu_custom_call" | custom-call | tf_op jit(solution)/shard_map/forward/pallas_call | solution.py:367
  155.3 1.4 collective-permute-start.5
  156.8 1.5 collective-permute-start.6
  158.3 0.7 copy.15
  158.9 0.0 collective-permute-done.5.lead_ref
  158.9 3.8 %collective-permute-done.6.rim_ref = f32[24,512]{1,0:T(8,128)S(1)} collective-permute-done((f32[24,512]{1,0:T(8,128)S(1)}, f32[24,512]{1,0:T(8,128)S(1)}, u32[]{:S(2)}, u32[]{:S(2)}) %collective-permute-start.6) | collective-permute-done | bytes 49184 | tf_op jit(solution)/shard_map/ppermute | solution.py:36
  162.7 6.5 %adjoint.5 = f32[8,384]{1,0:T(8,128)S(1)} custom-call(s32[3]{0:T(128)S(1)} %pad_add_fusion.1.refs_0_.scalars, f32[216,512]{1,0:T(8,128)S(1)} %get-tuple-element.22.nodes_ref, f32[24,512]{1,0:T(8,128)S(1)} %collective-permute-done.5.lead_ref, f32[24,512]{1,0:T(8,128)S(1)} %collective-permute-done.6.rim_ref, ...), custom_call_target="tpu_custom_call" | custom-call | tf_op jit(solution)/shard_map/adjoint/pallas_call | solution.py:384
  169.3 40.7 %all-gather.3 = f32[256,384]{1,0:T(8,128)S(1)} all-gather(f32[8,384]{1,0:T(8,128)S(1)} %adjoint.5), channel_id=5, replica_groups=mesh['tiles'=8,'probes'=4] {'tiles','probes'}, dimensions={0}, use_global_device_ids=true | all-gather | bytes 405504 | tf_op jit(solution)/shard_map/all_gather | solution.py:410
  210.0 1.7 gram.1
  211.7 0.7 copy.16
  (6 shorter events, 0.1 us)
Async XLA Ops:
  0.6 52.6 %copy-start = (f32[4096,3]{0,1:T(4,128)S(1)}, f32[4096,3]{0,1:T(4,128)}, u32[]{:S(2)}) copy-start(f32[4096,3]{0,1:T(4,128)} %param.13) | copy-start | bytes 147460
  1.4 51.9 %collective-permute-start.2 = (f32[3,512]{1,0:T(4,128)S(1)}, f32[3,512]{1,0:T(4,128)S(1)}, u32[]{:S(2)}, u32[]{:S(2)}) collective-permute-start(f32[3,512]{1,0:T(4,128)S(1)} %slice_bitcast_fusion), channel_id=1, source_target_pairs={{4,0},{8,4},{12,8},{16,12},{20,16},{24,20},{28,24},{5,1},{9,5},{13... | collective-permute-start | bytes 18440 | tf_op jit(solution)/shard_map/ppermute | solution.py:36
  49.5 4.2 %collective-permute-start = (f32[24,512]{1,0:T(8,128)S(1)}, f32[24,512]{1,0:T(8,128)S(1)}, u32[]{:S(2)}, u32[]{:S(2)}) collective-permute-start(f32[24,512]{1,0:T(8,128)S(1)} %get-tuple-element.16), channel_id=1, source_target_pairs={{0,4},{4,8},{8,12},{12,16},{16,20},{20,24},{24,28},{1,5},{5,9},{9,... | collective-permute-start | bytes 147464 | tf_op jit(solution)/shard_map/ppermute | solution.py:36
  52.0 6.0 %collective-permute-start.1 = (f32[24,512]{1,0:T(8,128)S(1)}, f32[24,512]{1,0:T(8,128)S(1)}, u32[]{:S(2)}, u32[]{:S(2)}) collective-permute-start(f32[24,512]{1,0:T(8,128)S(1)} %get-tuple-element.17), channel_id=1, source_target_pairs={{4,0},{8,4},{12,8},{16,12},{20,16},{24,20},{28,24},{5,1},{9,5},{13... | collective-permute-start | bytes 147464 | tf_op jit(solution)/shard_map/ppermute | solution.py:36
  102.9 3.3 %collective-permute-start.3 = (f32[24,512]{1,0:T(8,128)S(1)}, f32[24,512]{1,0:T(8,128)S(1)}, u32[]{:S(2)}, u32[]{:S(2)}) collective-permute-start(f32[24,512]{1,0:T(8,128)S(1)} %get-tuple-element.20), channel_id=1, source_target_pairs={{0,4},{4,8},{8,12},{12,16},{16,20},{20,24},{24,28},{1,5},{5,9},{9,... | collective-permute-start | bytes 147464 | tf_op jit(solution)/shard_map/ppermute | solution.py:36
  104.4 6.0 %collective-permute-start.4 = (f32[24,512]{1,0:T(8,128)S(1)}, f32[24,512]{1,0:T(8,128)S(1)}, u32[]{:S(2)}, u32[]{:S(2)}) collective-permute-start(f32[24,512]{1,0:T(8,128)S(1)} %get-tuple-element.21), channel_id=1, source_target_pairs={{4,0},{8,4},{12,8},{16,12},{20,16},{24,20},{28,24},{5,1},{9,5},{13... | collective-permute-start | bytes 147464 | tf_op jit(solution)/shard_map/ppermute | solution.py:36
  155.3 3.6 %collective-permute-start.5 = (f32[24,512]{1,0:T(8,128)S(1)}, f32[24,512]{1,0:T(8,128)S(1)}, u32[]{:S(2)}, u32[]{:S(2)}) collective-permute-start(f32[24,512]{1,0:T(8,128)S(1)} %get-tuple-element.23), channel_id=1, source_target_pairs={{0,4},{4,8},{8,12},{12,16},{16,20},{20,24},{24,28},{1,5},{5,9},{9,... | collective-permute-start | bytes 147464 | tf_op jit(solution)/shard_map/ppermute | solution.py:36
  156.8 6.0 %collective-permute-start.6 = (f32[24,512]{1,0:T(8,128)S(1)}, f32[24,512]{1,0:T(8,128)S(1)}, u32[]{:S(2)}, u32[]{:S(2)}) collective-permute-start(f32[24,512]{1,0:T(8,128)S(1)} %get-tuple-element.24), channel_id=1, source_target_pairs={{4,0},{8,4},{12,8},{16,12},{20,16},{24,20},{28,24},{5,1},{9,5},{13... | collective-permute-start | bytes 147464 | tf_op jit(solution)/shard_map/ppermute | solution.py:36

commit v2 on v1

--- a/solution.py
+++ b/solution.py
@@ -279,8 +279,9 @@
         v_ref[:, m * LANES : (m + 1) * LANES] = both.astype(BF16)
     basal = dot_nt(v_ref[...], one_hot_columns(cells % LANES, LANES))
     basal = basal[:24] + basal[24:]
-    for level in range(3):
-        out_ref[:, level * LANES : (level + 1) * LANES] = basal[8 * level : 8 * level + 8]
+    basal = jnp.concatenate([basal[:8], basal[8:16], basal[16:]], axis=1)
+    for t in range(out_ref.shape[0]):
+        out_ref[t] = basal
 
 
 def gram_kernel(keep_same, tiles, groups, scalars, meta_ref, g_ref, field_ref, gram_ref):
@@ -337,7 +338,7 @@
     meta = jnp.concatenate(
         [sign_bits.T, jnp.broadcast_to(cluster_ids[None, :], (8, cell_count))], axis=0
     )
-    meta = lax.all_gather(meta, "tiles", axis=0)
+    meta = lax.all_to_all(jnp.broadcast_to(meta, (tiles, *meta.shape)), "tiles", 0, 0)
     weight = obs_weight.reshape(node_count // HALO, HALO, 3).transpose(0, 2, 1)
     weight_next = from_behind(weight[0], "tiles", -1)
     weight = jnp.concatenate([weight.reshape(-1, HALO), weight_next], axis=0)
@@ -380,10 +381,10 @@
             name="forward",
         )(*operands)
 
-    def adjoint(nodes, lead, rim):
+    def adjoint(nodes, lead, rim, copies):
         return pl.pallas_call(
             adjoint_kernel,
-            out_shape=jax.ShapeDtypeStruct((group_size, window), F32),
+            out_shape=jax.ShapeDtypeStruct((copies, group_size, window), F32),
             in_specs=[smem] + [vmem] * 7 + [anywhere],
             out_specs=vmem,
             scratch_shapes=[
@@ -405,9 +406,9 @@
             samples = field[0]
         from_earlier = from_behind(spill, "tiles", 1)
         from_later = from_behind(lead, "tiles", -1)
-        basal = adjoint(nodes, from_earlier, from_later)
         axes = "tiles" if step < POWER else ("tiles", "probes")
-        gathered = lax.all_gather(basal, axes, axis=0)
+        basal = adjoint(nodes, from_earlier, from_later, lax.axis_size(axes))
+        gathered = lax.all_to_all(basal, axes, 0, 0)
 
     gathered = gathered.reshape(tiles, groups, group_size, window)
     refined, gram = pl.pallas_call(

time: 213 us -> 131 us (0.62)
  blocking collectives: 137 us -> 22.2 us
  waiting for transfers between devices: 13.1 us -> 29.2 us
  starting transfers between devices: 10.8 us -> 24.2 us
    all_gather x4 -> x0, blocking collectives: 137 us -> none  [the longest x3 102 us: shards(): gathered = lax.all_gather(basal, axes, axis=0)]
    all_to_all x0 -> x2, blocking collectives: none -> 22.2 us  [shards(): gathered = lax.all_to_all(basal, axes, 0, 0)]
    all_to_all x0 -> x2, waiting for transfers between devices: none -> 15.4 us  [the longest x1 12.5 us: shards(): gathered = lax.all_to_all(basal, axes, 0, 0)]
    all_to_all x0 -> x2, starting transfers between devices: none -> 12.3 us  [the longest x1 8.4 us: shards(): lax.all_to_all(jnp.broadcast_to(meta, (tiles, *meta.shape)), 'tiles', 0, 0)]
  transfers between devices with their start and end apart: 7 -> 9, of which waited for: 5 -> 8; matrix products, arithmetic and copies ran while one was open for 2% -> 5% of each run, Pallas kernels for 3% -> 6%
where the time goes in v2:
time: 131 us; the launch traced here: 130 us
  Pallas kernels  44.8 us (34%)
  waiting for transfers between devices  29.2 us (22%)
  starting transfers between devices  24.2 us (18%)
  blocking collectives  22.2 us (17%)
  local copies, waits for them, and re-layouts  6.31 us (5%)
  other arithmetic  1.56 us (1%)
  between operations  1.47 us (1%)
    pallas_call x3, Pallas kernels, forward(): pl.pallas_call(functools.partial(forward_kernel, first, keep_same, want_f...  22.7 us
    all_to_all x2, blocking collectives, shards(): gathered = lax.all_to_all(basal, axes, 0, 0)  22.2 us
    pallas_call x3, Pallas kernels, adjoint(): pl.pallas_call(adjoint_kernel, out_shape=jax.ShapeDtypeStruct((copies, gr...  20.4 us
    ppermute x7, waiting for transfers between devices, from_behind(): return lax.ppermute(block, axis, route)  13.8 us
    all_to_all x1, waiting for transfers between devices, shards(): gathered = lax.all_to_all(basal, axes, 0, 0)  12.5 us
    ppermute x7, starting transfers between devices, from_behind(): return lax.ppermute(block, axis, route)  11.9 us
    all_to_all x1, starting transfers between devices, shards(): lax.all_to_all(jnp.broadcast_to(meta, (tiles, *meta.shape)), 'tiles', 0, 0)  8.4 us
    all_to_all x1, starting transfers between devices, shards(): gathered = lax.all_to_all(basal, axes, 0, 0)  3.94 us
  transfers between devices with their start and end apart: 9, of which 8 were waited for; matrix products, arithmetic and copies ran while one was open for 5% of the time, Pallas kernels for 6%

profile of v2, /device:TPU:0, one launch (start us, length us, event | category | flops | bytes accessed | tf_op | source)
XLA Modules:
  0.0 129.7 jit_solution(9430320973718200811)
XLA Ops:
  0.6 0.7 slice_bitcast_fusion
  1.3 1.3 collective-permute-start.2
  2.6 0.7 broadcast_in_dim.4
  3.3 0.7 pad_add_fusion
  4.0 0.7 broadcast_in_dim.10
  4.7 8.4 %all-to-all-start = ((s32[8,16,256]{2,1,0:T(8,128)}), s32[8,16,256]{2,1,0:T(8,128)S(1)}, u32[]{:S(2)}, u32[]{:S(2)}) async-start(s32[8,16,256]{2,1,0:T(8,128)} %broadcast_in_dim.10), calls=%async_computation | async-start | bytes 262144 | tf_op jit(solution)/shard_map/all_to_all | solution.py:341
  13.1 0.8 add_select_fusion
  13.8 0.9 reshape.33
  15.4 0.1 pad_add_fusion.1.refs_0_.scalars
  15.5 0.8 reshape.28.refs_2_.conn_ref.refs_3_
  16.3 0.1 reshape.29.refs_3_.cell_ref.refs_4_
  16.4 1.0 copy.13
  17.4 0.1 copy.17
  17.6 2.8 %all-to-all-done.refs_1_.meta_ref = s32[8,16,256]{2,1,0:T(8,128)S(1)} async-done(((s32[8,16,256]{2,1,0:T(8,128)}), s32[8,16,256]{2,1,0:T(8,128)S(1)}, u32[]{:S(2)}, u32[]{:S(2)}) %all-to-all-start) | async-done | bytes 131104 | tf_op jit(solution)/shard_map/all_to_all | solution.py:341
  20.4 7.4 %forward.3 = (f32[216,512]{1,0:T(8,128)S(1)}, f32[24,512]{1,0:T(8,128)S(1)}, f32[24,512]{1,0:T(8,128)S(1)}) custom-call(s32[3]{0:T(128)S(1)} %pad_add_fusion.1.refs_0_.scalars, s32[8,16,256]{2,1,0:T(8,128)S(1)} %all-to-all-done.refs_1_.meta_ref, s32[32,128]{1,0:T(8,128)S(1)} %reshape.28.refs_2_.conn_ref.refs_3_, ...), custom_call_target="tpu_custom_call" | custom-call | tf_op jit(solution)/shard_map/forward/pallas_call | solution.py:368
  27.8 2.1 %collective-permute-start = (f32[24,512]{1,0:T(8,128)S(1)}, f32[24,512]{1,0:T(8,128)S(1)}, u32[]{:S(2)}, u32[]{:S(2)}) collective-permute-start(f32[24,512]{1,0:T(8,128)S(1)} %get-tuple-element.16), channel_id=1, source_target_pairs={{0,4},{4,8},{8,12},{12,16},{16,20},{20,24},{24,28},{1,5},{5,9},{9,... | collective-permute-start | bytes 147464 | tf_op jit(solution)/shard_map/ppermute | solution.py:36
  30.0 1.3 collective-permute-start.1
  31.3 0.0 collective-permute-done.2
  31.3 0.4 collective-permute-done.lead_ref
  31.7 4.3 %collective-permute-done.1.rim_ref = f32[24,512]{1,0:T(8,128)S(1)} collective-permute-done((f32[24,512]{1,0:T(8,128)S(1)}, f32[24,512]{1,0:T(8,128)S(1)}, u32[]{:S(2)}, u32[]{:S(2)}) %collective-permute-start.1) | collective-permute-done | bytes 49184 | tf_op jit(solution)/shard_map/ppermute | solution.py:36
  35.9 6.5 %adjoint.3 = f32[8,8,384]{2,1,0:T(8,128)S(1)} custom-call(s32[3]{0:T(128)S(1)} %pad_add_fusion.1.refs_0_.scalars, f32[216,512]{1,0:T(8,128)S(1)} %get-tuple-element.15.nodes_ref, f32[24,512]{1,0:T(8,128)S(1)} %collective-permute-done.lead_ref, f32[24,512]{1,0:T(8,128)S(1)} %collective-permute-done.1.rim_ref, ...), custom_call_target="tpu_custom_call" | custom-call | tf_op jit(solution)/shard_map/adjoint/pallas_call | solution.py:385
  42.5 11.3 %all_to_all.20.refs_2_ = f32[8,8,384]{2,1,0:T(8,128)S(1)} all-to-all(f32[8,8,384]{2,1,0:T(8,128)S(1)} %adjoint.3), channel_id=1, replica_groups=mesh['tiles'=8,'probes'=4] {'tiles'}, dimensions={0} | all-to-all | bytes 196608 | tf_op jit(solution)/shard_map/all_to_all | solution.py:411
  53.8 7.6 %forward.4 = (f32[216,512]{1,0:T(8,128)S(1)}, f32[24,512]{1,0:T(8,128)S(1)}, f32[24,512]{1,0:T(8,128)S(1)}, f32[256,8]{1,0:T(8,128)S(1)}) custom-call(s32[3]{0:T(128)S(1)} %pad_add_fusion.1.refs_0_.scalars, s32[8,16,256]{2,1,0:T(8,128)S(1)} %all-to-all-done.refs_1_.meta_ref, f32[8,8,384]{2,1,0:T(8,128)S(1)} %all_to_all.20.refs_2_, ...), custom_call_target="tpu_custom_call" | custom-call | tf_op jit(solution)/shard_map/forward/pallas_call | solution.py:368
  61.4 2.2 %collective-permute-start.3 = (f32[24,512]{1,0:T(8,128)S(1)}, f32[24,512]{1,0:T(8,128)S(1)}, u32[]{:S(2)}, u32[]{:S(2)}) collective-permute-start(f32[24,512]{1,0:T(8,128)S(1)} %get-tuple-element.20), channel_id=1, source_target_pairs={{0,4},{4,8},{8,12},{12,16},{16,20},{20,24},{24,28},{1,5},{5,9},{9,... | collective-permute-start | bytes 147464 | tf_op jit(solution)/shard_map/ppermute | solution.py:36
  63.6 1.3 collective-permute-start.4
  64.9 0.4 collective-permute-done.3.lead_ref
  65.4 4.3 %collective-permute-done.4.rim_ref = f32[24,512]{1,0:T(8,128)S(1)} collective-permute-done((f32[24,512]{1,0:T(8,128)S(1)}, f32[24,512]{1,0:T(8,128)S(1)}, u32[]{:S(2)}, u32[]{:S(2)}) %collective-permute-start.4) | collective-permute-done | bytes 49184 | tf_op jit(solution)/shard_map/ppermute | solution.py:36
  69.6 6.5 %adjoint.4 = f32[8,8,384]{2,1,0:T(8,128)S(1)} custom-call(s32[3]{0:T(128)S(1)} %pad_add_fusion.1.refs_0_.scalars, f32[216,512]{1,0:T(8,128)S(1)} %get-tuple-element.19.nodes_ref, f32[24,512]{1,0:T(8,128)S(1)} %collective-permute-done.3.lead_ref, f32[24,512]{1,0:T(8,128)S(1)} %collective-permute-done.4.rim_ref, ...), custom_call_target="tpu_custom_call" | custom-call | tf_op jit(solution)/shard_map/adjoint/pallas_call | solution.py:385
  76.2 10.8 %all_to_all.21.refs_2_ = f32[8,8,384]{2,1,0:T(8,128)S(1)} all-to-all(f32[8,8,384]{2,1,0:T(8,128)S(1)} %adjoint.4), channel_id=1, replica_groups=mesh['tiles'=8,'probes'=4] {'tiles'}, dimensions={0} | all-to-all | bytes 196608 | tf_op jit(solution)/shard_map/all_to_all | solution.py:411
  87.0 7.7 %forward.5 = (f32[216,512]{1,0:T(8,128)S(1)}, f32[24,512]{1,0:T(8,128)S(1)}, f32[24,512]{1,0:T(8,128)S(1)}) custom-call(s32[3]{0:T(128)S(1)} %pad_add_fusion.1.refs_0_.scalars, s32[8,16,256]{2,1,0:T(8,128)S(1)} %all-to-all-done.refs_1_.meta_ref, f32[8,8,384]{2,1,0:T(8,128)S(1)} %all_to_all.21.refs_2_, s32[32,128]{1,0:T(8,128)S(1)} %reshape.28.refs_2_.conn_ref.refs_3_, ...), custom_call_target="tpu_custom_call" | custom-call | tf_op jit(solution)/shard_map/forward/pallas_call | solution.py:368
  94.7 2.2 %collective-permute-start.5 = (f32[24,512]{1,0:T(8,128)S(1)}, f32[24,512]{1,0:T(8,128)S(1)}, u32[]{:S(2)}, u32[]{:S(2)}) collective-permute-start(f32[24,512]{1,0:T(8,128)S(1)} %get-tuple-element.23), channel_id=1, source_target_pairs={{0,4},{4,8},{8,12},{12,16},{16,20},{20,24},{24,28},{1,5},{5,9},{9,... | collective-permute-start | bytes 147464 | tf_op jit(solution)/shard_map/ppermute | solution.py:36
  96.9 1.5 %collective-permute-start.6 = (f32[24,512]{1,0:T(8,128)S(1)}, f32[24,512]{1,0:T(8,128)S(1)}, u32[]{:S(2)}, u32[]{:S(2)}) collective-permute-start(f32[24,512]{1,0:T(8,128)S(1)} %get-tuple-element.24), channel_id=1, source_target_pairs={{4,0},{8,4},{12,8},{16,12},{20,16},{24,20},{28,24},{5,1},{9,5},{13... | collective-permute-start | bytes 147464 | tf_op jit(solution)/shard_map/ppermute | solution.py:36
  98.4 0.2 collective-permute-done.5.lead_ref
  98.6 4.3 %collective-permute-done.6.rim_ref = f32[24,512]{1,0:T(8,128)S(1)} collective-permute-done((f32[24,512]{1,0:T(8,128)S(1)}, f32[24,512]{1,0:T(8,128)S(1)}, u32[]{:S(2)}, u32[]{:S(2)}) %collective-permute-start.6) | collective-permute-done | bytes 49184 | tf_op jit(solution)/shard_map/ppermute | solution.py:36
  102.8 7.3 %adjoint.5 = f32[32,8,384]{2,1,0:T(8,128)} custom-call(s32[3]{0:T(128)S(1)} %pad_add_fusion.1.refs_0_.scalars, f32[216,512]{1,0:T(8,128)S(1)} %get-tuple-element.22.nodes_ref, f32[24,512]{1,0:T(8,128)S(1)} %collective-permute-done.5.lead_ref, f32[24,512]{1,0:T(8,128)S(1)} %collective-permute-done.6.rim_ref, ...), custom_call_target="tpu_custom_call" | custom-call | tf_op jit(solution)/shard_map/adjoint/pallas_call | solution.py:385
  110.1 3.9 %all-to-all-start.3 = ((f32[32,8,384]{2,1,0:T(8,128)}), f32[32,8,384]{2,1,0:T(8,128)S(1)}, u32[]{:S(2)}, u32[]{:S(2)}) async-start(f32[32,8,384]{2,1,0:T(8,128)} %adjoint.5), calls=%async_computation.3 | async-start | bytes 786432 | tf_op jit(solution)/shard_map/all_to_all | solution.py:411
  114.1 0.7 copy.15
  114.8 12.5 %all-to-all-done.3 = f32[32,8,384]{2,1,0:T(8,128)S(1)} async-done(((f32[32,8,384]{2,1,0:T(8,128)}), f32[32,8,384]{2,1,0:T(8,128)S(1)}, u32[]{:S(2)}, u32[]{:S(2)}) %all-to-all-start.3) | async-done | bytes 393248 | tf_op jit(solution)/shard_map/all_to_all | solution.py:411
  127.3 1.7 %gram.1 = (f32[256,8]{1,0:T(8,128)S(1)}, f32[8,8,32]{2,1,0:T(8,128)}) custom-call(s32[3]{0:T(128)S(1)} %pad_add_fusion.1.refs_0_.scalars, s32[8,16,256]{2,1,0:T(8,128)S(1)} %all-to-all-done.refs_1_.meta_ref, f32[8,4,8,384]{3,2,1,0:T(8,128)S(1)} %bitcast.11), custom_call_target="tpu_custom_call" | custom-call | tf_op jit(solution)/shard_map/gram/pallas_call | solution.py:414
  129.0 0.7 copy.16
  (5 shorter events, 0.1 us)
Async XLA Ops:
  1.3 29.9 %collective-permute-start.2 = (f32[3,512]{1,0:T(4,128)S(1)}, f32[3,512]{1,0:T(4,128)S(1)}, u32[]{:S(2)}, u32[]{:S(2)}) collective-permute-start(f32[3,512]{1,0:T(4,128)S(1)} %slice_bitcast_fusion), channel_id=1, source_target_pairs={{4,0},{8,4},{12,8},{16,12},{20,16},{24,20},{28,24},{5,1},{9,5},{13... | collective-permute-start | bytes 18440 | tf_op jit(solution)/shard_map/ppermute | solution.py:36
  4.7 15.7 %all-to-all-start = ((s32[8,16,256]{2,1,0:T(8,128)}), s32[8,16,256]{2,1,0:T(8,128)S(1)}, u32[]{:S(2)}, u32[]{:S(2)}) async-start(s32[8,16,256]{2,1,0:T(8,128)} %broadcast_in_dim.10), calls=%async_computation | async-start | bytes 262144 | tf_op jit(solution)/shard_map/all_to_all | solution.py:341
  27.8 3.9 %collective-permute-start = (f32[24,512]{1,0:T(8,128)S(1)}, f32[24,512]{1,0:T(8,128)S(1)}, u32[]{:S(2)}, u32[]{:S(2)}) collective-permute-start(f32[24,512]{1,0:T(8,128)S(1)} %get-tuple-element.16), channel_id=1, source_target_pairs={{0,4},{4,8},{8,12},{12,16},{16,20},{20,24},{24,28},{1,5},{5,9},{9,... | collective-permute-start | bytes 147464 | tf_op jit(solution)/shard_map/ppermute | solution.py:36
  30.0 6.0 %collective-permute-start.1 = (f32[24,512]{1,0:T(8,128)S(1)}, f32[24,512]{1,0:T(8,128)S(1)}, u32[]{:S(2)}, u32[]{:S(2)}) collective-permute-start(f32[24,512]{1,0:T(8,128)S(1)} %get-tuple-element.17), channel_id=1, source_target_pairs={{4,0},{8,4},{12,8},{16,12},{20,16},{24,20},{28,24},{5,1},{9,5},{13... | collective-permute-start | bytes 147464 | tf_op jit(solution)/shard_map/ppermute | solution.py:36
  61.4 3.9 %collective-permute-start.3 = (f32[24,512]{1,0:T(8,128)S(1)}, f32[24,512]{1,0:T(8,128)S(1)}, u32[]{:S(2)}, u32[]{:S(2)}) collective-permute-start(f32[24,512]{1,0:T(8,128)S(1)} %get-tuple-element.20), channel_id=1, source_target_pairs={{0,4},{4,8},{8,12},{12,16},{16,20},{20,24},{24,28},{1,5},{5,9},{9,... | collective-permute-start | bytes 147464 | tf_op jit(solution)/shard_map/ppermute | solution.py:36
  63.6 6.0 %collective-permute-start.4 = (f32[24,512]{1,0:T(8,128)S(1)}, f32[24,512]{1,0:T(8,128)S(1)}, u32[]{:S(2)}, u32[]{:S(2)}) collective-permute-start(f32[24,512]{1,0:T(8,128)S(1)} %get-tuple-element.21), channel_id=1, source_target_pairs={{4,0},{8,4},{12,8},{16,12},{20,16},{24,20},{28,24},{5,1},{9,5},{13... | collective-permute-start | bytes 147464 | tf_op jit(solution)/shard_map/ppermute | solution.py:36
  94.7 3.9 %collective-permute-start.5 = (f32[24,512]{1,0:T(8,128)S(1)}, f32[24,512]{1,0:T(8,128)S(1)}, u32[]{:S(2)}, u32[]{:S(2)}) collective-permute-start(f32[24,512]{1,0:T(8,128)S(1)} %get-tuple-element.23), channel_id=1, source_target_pairs={{0,4},{4,8},{8,12},{12,16},{16,20},{20,24},{24,28},{1,5},{5,9},{9,... | collective-permute-start | bytes 147464 | tf_op jit(solution)/shard_map/ppermute | solution.py:36
  96.9 6.0 %collective-permute-start.6 = (f32[24,512]{1,0:T(8,128)S(1)}, f32[24,512]{1,0:T(8,128)S(1)}, u32[]{:S(2)}, u32[]{:S(2)}) collective-permute-start(f32[24,512]{1,0:T(8,128)S(1)} %get-tuple-element.24), channel_id=1, source_target_pairs={{4,0},{8,4},{12,8},{16,12},{20,16},{24,20},{28,24},{5,1},{9,5},{13... | collective-permute-start | bytes 147464 | tf_op jit(solution)/shard_map/ppermute | solution.py:36
  110.1 17.1 %all-to-all-start.3 = ((f32[32,8,384]{2,1,0:T(8,128)}), f32[32,8,384]{2,1,0:T(8,128)S(1)}, u32[]{:S(2)}, u32[]{:S(2)}) async-start(f32[32,8,384]{2,1,0:T(8,128)} %adjoint.5), calls=%async_computation.3 | async-start | bytes 786432 | tf_op jit(solution)/shard_map/all_to_all | solution.py:411

commit v3 on v2

v3 whole, which is shorter than its diff:
```python
import functools

import jax
import jax.numpy as jnp
from jax import lax
from jax.experimental import pallas as pl
from jax.experimental.pallas import tpu as pltpu
from jax.sharding import PartitionSpec as P

HALO = 512
POWER = 2
RIM = 64
LANES = 128
VMEM_BYTES = 30 * 1024 * 1024

F32 = jnp.float32
BF16 = jnp.bfloat16


def dot(a, b):
    return lax.dot_general(a, b, (((1,), (0,)), ((), ())), preferred_element_type=F32)


def dot_nt(a, b):
    return lax.dot_general(a, b, (((1,), (1,)), ((), ())), preferred_element_type=F32)


def split(x):
    hi = x.astype(BF16)
    return hi, (x - hi.astype(F32)).astype(BF16)


def rows_iota(shape):
    return lax.broadcasted_iota(jnp.int32, shape, 0)


def lanes_iota(shape):
    return lax.broadcasted_iota(jnp.int32, shape, 1)


def spread_matrix(node_slots, padded_order):
    shape = (2 * node_slots, 2 * padded_order)
    row = rows_iota(shape)
    start = (row // node_slots) * padded_order + 3 * (row % node_slots)
    gap = lanes_iota(shape) - start
    return jnp.where((gap >= 0) & (gap < 3), F32(1), F32(0)).astype(BF16)


def order_matrix(node_slots, padded_order):
    pair = 2 * node_slots
    shape = (2 * padded_order, 3 * pair)
    col = lanes_iota(shape)
    inner = col % pair
    source = (inner // node_slots) * padded_order + 3 * (inner % node_slots) + col // pair
    return jnp.where(rows_iota(shape) == source, F32(1), F32(0)).astype(BF16)


def same_colour(meta):
    ids = meta[8:16, :].astype(jnp.int32)
    return (ids % 2) == (rows_iota(ids.shape) % 2)


def start_probes(meta):
    signs = 2 * meta[:8, :] - 1
    return jnp.where(same_colour(meta), signs, F32(0))


def total_field(before, own, after):
    lane = lanes_iota((own.shape[0], LANES))
    first = own[:, :LANES] + jnp.where(lane < RIM, before[:, 2 * LANES :], F32(0))
    second = own[:, LANES : 2 * LANES] + jnp.where(lane >= RIM, after[:, 2 * LANES :], F32(0))
    return jnp.concatenate([first, second], axis=1)


def field_of(g_ref, t, tiles):
    zero = jnp.zeros(g_ref.shape[1:], F32)
    if isinstance(t, int):
        before = g_ref[t - 1] if t > 0 else zero
        after = g_ref[t + 1] if t < tiles - 1 else zero
    else:
        before = jnp.where(t > 0, g_ref[jnp.maximum(t - 1, 0)], zero)
        after = jnp.where(t < tiles - 1, g_ref[jnp.minimum(t + 1, tiles - 1)], zero)
    return total_field(before, g_ref[t], after)


def masked(field, meta, keep_same):
    same = same_colour(meta)
    return jnp.where(same if keep_same else ~same, field, F32(0))


def announce_kernel(signs_ref, ids_ref, weight_hbm, out_ref, lead, sem):
    load = pltpu.make_async_copy(weight_hbm.at[pl.ds(0, HALO)], lead, sem)
    load.start()
    half = HALO // 2
    out_ref[0, :8, :] = signs_ref[...].astype(F32).T
    out_ref[0, 8:16, :] = jnp.broadcast_to(ids_ref[...].astype(F32), (8, half))
    load.wait()
    turned = lead[...].T
    out_ref[0, 16:24, :] = jnp.zeros((8, half), F32)
    out_ref[0, 16:19, :] = turned[:, :half]
    out_ref[0, 19:22, :] = turned[:, half:]
    block = out_ref[0]
    for t in range(1, out_ref.shape[0]):
        out_ref[t] = block


def setup_kernel(
    node_slots,
    padded_order,
    conn_in,
    cell_in,
    conn_ref,
    cell_ref,
    node_hot_ref,
    cell_hot_ref,
    spread_ref,
    order_ref,
):
    pairs = conn_ref.shape[0]
    window = 3 * LANES

    def paired(ref):
        return jnp.concatenate(
            [ref[pl.ds(0, pairs, stride=2), :], ref[pl.ds(1, pairs, stride=2), :]], axis=1
        )

    conn = paired(conn_in)
    cells = paired(cell_in)
    cells = jnp.where(cells < RIM, cells + (window - RIM), cells - RIM)
    conn_ref[...] = conn
    cell_ref[...] = cells
    rows = rows_iota((HALO, LANES))
    for m in range(pairs):
        at = pl.ds(m * LANES, LANES)
        hot = rows == conn[m : m + 1, :] % HALO
        node_hot_ref[:, at] = jnp.where(hot, F32(1), F32(0)).astype(BF16)
        hot = rows[:LANES] == cells[m : m + 1, :] % LANES
        cell_hot_ref[:, at] = jnp.where(hot, F32(1), F32(0)).astype(BF16)
    spread_ref[...] = spread_matrix(node_slots, padded_order)
    order_ref[...] = order_matrix(node_slots, padded_order)


def forward_kernel(first, keep_same, want_field, tiles, levels, *refs):
    scalars, meta_ref, *refs = refs
    if not first:
        g_ref, *refs = refs
    conn_ref, cell_ref, fr_ref, blocks, node_hot, cell_hot, spread_ref, order_ref, *refs = refs
    ordered_ref, a_ref, b_ref, *refs = refs
    if want_field:
        field_ref, *refs = refs
    f_ref, v_ref = refs

    order = blocks.shape[1]
    padded_order = f_ref.shape[1] // 2
    pairs = blocks.shape[0] // 2
    tile = scalars[0]
    count = scalars[1]

    if first:
        current = lambda t: start_probes(meta_ref[t])
    else:
        current = lambda t: masked(field_of(g_ref, t, tiles), meta_ref[t], keep_same)

    own = current(tile)
    if want_field:
        field_ref[...] = own.T
    below = jnp.where(tile > 0, current(jnp.maximum(tile - 1, 0)), F32(0))
    above = jnp.where(tile < tiles - 1, current(jnp.minimum(tile + 1, tiles - 1)), F32(0))
    lane = lanes_iota((8, LANES))
    rims = jnp.where(lane < RIM, above[:, :LANES], below[:, LANES:])
    window = jnp.concatenate([own[:, :LANES], own[:, LANES:], rims], axis=0)
    if not first:

        def add_squares(t, acc):
            part = current(t)
            part = part * part
            return acc + part[:, :LANES] + part[:, LANES:]

        squares = lax.fori_loop(0, tiles, add_squares, jnp.zeros((8, LANES), F32), unroll=tiles <= 8)
        squares = jnp.sum(squares, axis=1, keepdims=True)
        scale = jnp.sqrt(squares / (tiles * 2 * LANES) + F32(1e-06))
        window = window / jnp.concatenate([scale, scale, scale], axis=0)

    cells = cell_ref[...]
    hi, lo = split(window)
    picked = dot(jnp.concatenate([hi, lo], axis=0), cell_hot[...])
    tops = []
    rests = []
    for m in range(pairs):
        part = picked[:, m * LANES : (m + 1) * LANES]
        which = cells[m : m + 1, :] // LANES
        for base, out in ((0, tops), (24, rests)):
            chosen = jnp.where(which == 0, part[base : base + 8], F32(0))
            for level in (1, 2):
                at = base + 8 * level
                chosen = jnp.where(which == level, part[at : at + 8], chosen)
            out.append(chosen)
    stacked = jnp.concatenate(tops + rests, axis=0).astype(BF16)
    spread = dot(stacked, spread_ref[...])
    half = 8 * pairs
    spread = spread[:half] + spread[half:]

    f_ref[...] = jnp.zeros_like(f_ref)
    for m in range(pairs):
        inputs = spread[8 * m : 8 * m + 8, :] * fr_ref[m : m + 1, :]
        for side in range(2):
            at = side * padded_order
            slot = 2 * m + side
            out = dot_nt(inputs[:, at : at + order].astype(BF16), blocks[slot])
            out = jnp.where(slot < count, out, F32(0))
            hi = out.astype(BF16).astype(F32)
            f_ref[16 * m : 16 * m + 8, at : at + order] = hi
            f_ref[16 * m + 8 : 16 * m + 16, at : at + order] = out - hi

    ordered = dot(f_ref[...].astype(BF16), order_ref[...])
    ordered_ref[...] = ordered
    conn = conn_ref[...]
    for m in range(pairs):
        which = conn[m : m + 1, :] // HALO
        rows = [
            jnp.where(
                which == level,
                ordered[16 * m : 16 * m + 16, c * LANES : (c + 1) * LANES],
                F32(0),
            )
            for level in (0, levels - 1)
            for c in range(3)
        ]
        v_ref[:, m * LANES : (m + 1) * LANES] = jnp.concatenate(rows, axis=0).astype(BF16)
    rim = dot_nt(v_ref[...], node_hot[...])
    even = tile % 2 == 0
    for c in range(3):
        lead = rim[16 * c : 16 * c + 8] + rim[16 * c + 8 : 16 * c + 16]
        at = 48 + 16 * c
        spill = rim[at : at + 8] + rim[at + 8 : at + 16]
        a_ref[8 * c : 8 * c + 8, :] = jnp.where(even, spill, lead)
        b_ref[8 * c : 8 * c + 8, :] = jnp.where(even, lead, spill)


def inner_kernel(levels, ordered_ref, weight_ref, conn_ref, node_hot, picked_ref, v_ref):
    pairs = conn_ref.shape[0]
    conn = conn_ref[...]
    for m in range(pairs):
        which = conn[m : m + 1, :] // HALO
        rows = [
            jnp.where(
                which == level,
                ordered_ref[16 * m : 16 * m + 16, c * LANES : (c + 1) * LANES],
                F32(0),
            )
            for level in range(1, levels - 1)
            for c in range(3)
        ]
        v_ref[:, m * LANES : (m + 1) * LANES] = jnp.concatenate(rows, axis=0).astype(BF16)
    nodes = dot_nt(v_ref[...], node_hot[...])
    rows = []
    for i in range(3 * (levels - 2)):
        value = nodes[16 * i : 16 * i + 8] + nodes[16 * i + 8 : 16 * i + 16]
        rows.append(value * weight_ref[i + 3 : i + 4, :])
    weighted = jnp.concatenate(rows, axis=0).astype(BF16)
    step = 2
    for start in range(0, pairs, step):
        found = dot(weighted, node_hot[:, start * LANES : (start + step) * LANES])
        for i in range(step):
            m = start + i
            which = conn[m : m + 1, :] // HALO
            part = found[:, i * LANES : (i + 1) * LANES]
            chosen = jnp.zeros((24, LANES), F32)
            for level in range(1, levels - 1):
                at = 24 * (level - 1)
                chosen = jnp.where(which == level, part[at : at + 24], chosen)
            for c in range(3):
                picked_ref[8 * m : 8 * m + 8, c * LANES : (c + 1) * LANES] = chosen[8 * c : 8 * c + 8]


def adjoint_kernel(
    tiles,
    levels,
    scalars,
    meta_ref,
    own_a,
    own_b,
    new_a,
    new_b,
    inner_ref,
    weight_ref,
    conn_ref,
    cell_ref,
    fr_ref,
    blocks,
    node_hot,
    cell_hot,
    spread_ref,
    order_ref,
    out_ref,
    p_ref,
    n_ref,
    v_ref,
):
    order = blocks.shape[1]
    padded_order = p_ref.shape[1] // 2
    pairs = blocks.shape[0] // 2
    tile = scalars[0]
    count = scalars[1]

    even = tile % 2 == 0
    lead = jnp.where(even, own_b[...] + new_b[...], own_a[...] + new_a[...])
    spill = jnp.where(even, own_a[...] + new_a[...], own_b[...] + new_b[...])
    after = meta_ref[jnp.minimum(tile + 1, tiles - 1)]
    after = jnp.where(tile < tiles - 1, after, F32(0))
    rows = [lead[8 * c : 8 * c + 8] * weight_ref[c : c + 1, :] for c in range(3)]
    for c in range(3):
        weight = jnp.concatenate([after[16 + c : 17 + c, :], after[19 + c : 20 + c, :]], axis=1)
        rows.append(spill[8 * c : 8 * c + 8] * weight)
    weighted = jnp.concatenate(rows, axis=0).astype(BF16)

    conn = conn_ref[...]
    step = 2
    for start in range(0, pairs, step):
        found = dot(weighted, node_hot[:, start * LANES : (start + step) * LANES])
        for i in range(step):
            m = start + i
            which = conn[m : m + 1, :] // HALO
            part = found[:, i * LANES : (i + 1) * LANES]
            for c in range(3):
                value = inner_ref[8 * m : 8 * m + 8, c * LANES : (c + 1) * LANES]
                value = jnp.where(which == 0, part[8 * c : 8 * c + 8], value)
                value = jnp.where(which == levels - 1, part[24 + 8 * c : 32 + 8 * c], value)
                n_ref[8 * m : 8 * m + 8, c * LANES : (c + 1) * LANES] = value
    natural = dot_nt(n_ref[...].astype(BF16), order_ref[...])
    p_ref[...] = jnp.zeros_like(p_ref)
    for m in range(pairs):
        for side in range(2):
            at = side * padded_order
            slot = 2 * m + side
            out = dot(natural[8 * m : 8 * m + 8, at : at + order].astype(BF16), blocks[slot])
            out = out * fr_ref[m : m + 1, at : at + order]
            p_ref[8 * m : 8 * m + 8, at : at + order] = jnp.where(slot < count, out, F32(0))

    hi, lo = split(p_ref[...])
    partial = dot_nt(jnp.concatenate([hi, lo], axis=0), spread_ref[...])
    half = 8 * pairs
    partial = partial[:half] + partial[half:]
    cells = cell_ref[...]
    for m in range(pairs):
        which = cells[m : m + 1, :] // LANES
        value = partial[8 * m : 8 * m + 8, :]
        rows = jnp.concatenate([jnp.where(which == level, value, F32(0)) for level in range(3)], axis=0)
        hi = rows.astype(BF16).astype(F32)
        both = jnp.concatenate([hi, rows - hi], axis=0)
        v_ref[:, m * LANES : (m + 1) * LANES] = both.astype(BF16)
    basal = dot_nt(v_ref[...], cell_hot[...])
    basal = basal[:24] + basal[24:]
    basal = jnp.concatenate([basal[:8], basal[8:16], basal[16:]], axis=1)
    for t in range(out_ref.shape[0]):
        out_ref[t] = basal


def gram_kernel(keep_same, tiles, groups, scalars, meta_ref, g_ref, field_ref, gram_ref):
    tile = scalars[0]
    group = scalars[2]
    clusters = gram_ref.shape[0]

    def field(t, p):
        zero = jnp.zeros(g_ref.shape[2:], F32)
        if isinstance(t, int):
            before = g_ref[t - 1, p] if t > 0 else zero
            after = g_ref[t + 1, p] if t < tiles - 1 else zero
        else:
            before = jnp.where(t > 0, g_ref[jnp.maximum(t - 1, 0), p], zero)
            after = jnp.where(t < tiles - 1, g_ref[jnp.minimum(t + 1, tiles - 1), p], zero)
        return masked(total_field(before, g_ref[t, p], after), meta_ref[t], keep_same)

    field_ref[...] = field(tile, group).T

    def add_tile(t, acc):
        ids = meta_ref[t][8:16, :].astype(jnp.int32)
        mine = field(t, group)
        every = jnp.concatenate([field(t, p) for p in range(groups)], axis=0)
        left = jnp.concatenate(
            [jnp.where(ids == k, mine, F32(0)) for k in range(clusters)], axis=0
        )
        return acc + lax.dot_general(
            left,
            every,
            (((1,), (1,)), ((), ())),
            precision=lax.Precision.HIGHEST,
            preferred_element_type=F32,
        )

    acc = jnp.zeros((8 * clusters, 8 * groups), F32)
    acc = lax.fori_loop(0, tiles, add_tile, acc, unroll=tiles <= 8)
    gram_ref[...] = acc.reshape(gram_ref.shape)


def shards(
    blocks, connectivity, basal_map, friction, elem_counts, obs_weight, sign_bits, cluster_ids
):
    slots, order, _ = blocks.shape
    node_slots = connectivity.shape[1]
    node_count = obs_weight.shape[0]
    cell_count, group_size = sign_bits.shape
    tiles = lax.axis_size("tiles")
    groups = lax.axis_size("probes")
    pairs = slots * node_slots // LANES
    refs = pairs * LANES
    levels = node_count // HALO + 1
    padded_order = 2 * LANES
    window = cell_count + 2 * RIM

    smem = pl.BlockSpec(memory_space=pltpu.SMEM)
    vmem = pl.BlockSpec(memory_space=pltpu.VMEM)
    anywhere = pl.BlockSpec(memory_space=pl.ANY)
    params = pltpu.CompilerParams(vmem_limit_bytes=VMEM_BYTES)
    shaped = jax.ShapeDtypeStruct

    def call(kernel, name, out_shape, operands, in_specs=None, scratch=()):
        return pl.pallas_call(
            kernel,
            out_shape=out_shape,
            in_specs=in_specs or [vmem] * len(operands),
            out_specs=jax.tree.map(lambda _: vmem, out_shape),
            scratch_shapes=list(scratch),
            compiler_params=params,
            name=name,
        )(*operands)

    meta = call(
        announce_kernel,
        "announce",
        shaped((tiles, 24, cell_count), F32),
        [sign_bits, cluster_ids.reshape(1, cell_count), obs_weight],
        [vmem, vmem, anywhere],
        [pltpu.VMEM((HALO, 3), F32), pltpu.SemaphoreType.DMA],
    )
    meta = lax.all_to_all(meta, "tiles", 0, 0)
    conn, cells, node_hot, cell_hot, spread, order_map = call(
        functools.partial(setup_kernel, node_slots, padded_order),
        "setup",
        [
            shaped((pairs, LANES), jnp.int32),
            shaped((pairs, LANES), jnp.int32),
            shaped((HALO, refs), BF16),
            shaped((LANES, refs), BF16),
            shaped((LANES, 2 * padded_order), BF16),
            shaped((2 * padded_order, 3 * LANES), BF16),
        ],
        [connectivity, basal_map],
    )
    weight = obs_weight.reshape(node_count // HALO, HALO, 3).transpose(0, 2, 1).reshape(-1, HALO)
    fr = jnp.pad(friction.reshape(slots, order), ((0, 0), (0, padded_order - order)))
    fr = fr.reshape(pairs, 2 * padded_order)
    scalars = jnp.stack(
        [lax.axis_index("tiles"), elem_counts[0], lax.axis_index("probes")]
    ).astype(jnp.int32)
    shared = [conn, cells, fr, blocks, node_hot, cell_hot, spread, order_map]

    evens = range(0, tiles - 1, 2)
    odds = range(1, tiles - 1, 2)
    swap_a = [(i, i + 1) for i in evens] + [(i + 1, i) for i in evens]
    swap_b = [(i, i + 1) for i in odds] + [(i + 1, i) for i in odds]

    def forward(gathered, keep_same, want_field):
        first = gathered is None
        out_shape = [
            shaped((16 * pairs, 3 * LANES), F32),
            shaped((24, HALO), F32),
            shaped((24, HALO), F32),
        ]
        if want_field:
            out_shape.append(shaped((cell_count, group_size), F32))
        operands = [scalars, meta] + ([] if first else [gathered]) + shared
        return call(
            functools.partial(forward_kernel, first, keep_same, want_field, tiles, levels),
            "forward",
            out_shape,
            operands,
            [smem] + [vmem] * (len(operands) - 1),
            [pltpu.VMEM((16 * pairs, 2 * padded_order), F32), pltpu.VMEM((96, refs), BF16)],
        )

    gathered = None
    samples = None
    for step in range(POWER + 1):
        ordered, own_a, own_b, *field = forward(gathered, step % 2 == 0, step == 1)
        if field:
            samples = field[0]
        new_b = lax.ppermute(own_b, "tiles", swap_b)
        new_a = lax.ppermute(own_a, "tiles", swap_a)
        inner = call(
            functools.partial(inner_kernel, levels),
            "inner",
            shaped((8 * pairs, 3 * LANES), F32),
            [ordered, weight, conn, node_hot],
            scratch=[pltpu.VMEM((48 * (levels - 2), refs), BF16)],
        )
        axes = "tiles" if step < POWER else ("tiles", "probes")
        operands = [scalars, meta, own_a, own_b, new_a, new_b, inner, weight] + shared
        basal = call(
            functools.partial(adjoint_kernel, tiles, levels),
            "adjoint",
            shaped((lax.axis_size(axes), group_size, window), F32),
            operands,
            [smem] + [vmem] * (len(operands) - 1),
            [
                pltpu.VMEM((8 * pairs, 2 * padded_order), F32),
                pltpu.VMEM((8 * pairs, 3 * LANES), F32),
                pltpu.VMEM((48, refs), BF16),
            ],
        )
        gathered = lax.all_to_all(basal, axes, 0, 0)

    gathered = gathered.reshape(tiles, groups, group_size, window)
    refined, gram = call(
        functools.partial(gram_kernel, POWER % 2 == 1, tiles, groups),
        "gram",
        [
            shaped((cell_count, group_size), F32),
            shaped((tiles, group_size, groups * group_size), F32),
        ],
        [scalars, meta, gathered],
        [smem, vmem, vmem],
    )
    return (samples, refined, gram)


def solution(mesh):
    in_specs = (
        P("tiles", None, None),
        P("tiles", None),
        P("tiles", None),
        P("tiles", None, None),
        P("tiles"),
        P("tiles", None),
        P("tiles", "probes"),
        P("tiles"),
    )
    out_specs = (P("tiles", "probes"), P("tiles", "probes"), P(None, "probes", None))
    return jax.shard_map(shards, mesh=mesh, in_specs=in_specs, out_specs=out_specs, check_vma=False)
```

time: 131 us -> 115 us (0.88)
  waiting for transfers between devices: 29.2 us -> 15.6 us
  local copies, waits for them, and re-layouts: 6.31 us -> 16.5 us
  Pallas kernels: 44.8 us -> 37.4 us
  starting transfers between devices: 24.2 us -> 17.4 us
  blocking collectives: 22.2 us -> 26 us
  other arithmetic: 1.56 us -> 0.08 us
    unnamed x5 -> x28, local copies, waits for them, and re-layouts: 2.41 us -> 16.4 us
    ppermute x7 -> x6, waiting for transfers between devices: 13.8 us -> 1.01 us  [the longest x3 1 us: shards(): new_a = lax.ppermute(own_a, 'tiles', swap_a)]
    ppermute x7 -> x6, starting transfers between devices: 11.9 us -> 4.06 us  [the longest x3 2.18 us: shards(): new_b = lax.ppermute(own_b, 'tiles', swap_b)]
    pallas_call x7 -> x12, Pallas kernels: 44.8 us -> 37.4 us  [call(): pl.pallas_call(kernel, out_shape=out_shape, in_specs=in_specs or [vmem] *...]
    all_to_all x2, blocking collectives: 22.2 us -> 26 us  [shards(): gathered = lax.all_to_all(basal, axes, 0, 0)]
    all_to_all x1, starting transfers between devices: 3.94 us -> 6.09 us  [shards(): gathered = lax.all_to_all(basal, axes, 0, 0)]
    reshape x3 -> x1, local copies, waits for them, and re-layouts: 1.77 us -> 0.03 us  [shards(): obs_weight.reshape(node_count // HALO, HALO, 3).transpose(0, 2, 1)]
    broadcast_in_dim x2 -> x0, local copies, waits for them, and re-layouts: 1.34 us -> none  [the longest x1 0.68 us: shards(): jnp.broadcast_to(cluster_ids[None, :], (8, cell_count))]
  transfers between devices with their start and end apart: 9 -> 8, of which waited for: 8 -> 4; matrix products, arithmetic and copies ran while one was open for 5% -> 1% of each run, Pallas kernels for 6% -> 9%
where the time goes in v3:
time: 115 us
  Pallas kernels  37.4 us (33%)
  blocking collectives  26 us (23%)
  starting transfers between devices  17.4 us (15%)
  local copies, waits for them, and re-layouts  16.5 us (14%)
  waiting for transfers between devices  15.6 us (14%)
  between operations  1.57 us (1%)
    pallas_call x12, Pallas kernels, call(): pl.pallas_call(kernel, out_shape=out_shape, in_specs=in_specs or [vmem] *...  37.4 us
    all_to_all x2, blocking collectives, shards(): gathered = lax.all_to_all(basal, axes, 0, 0)  26 us
    unnamed x28, local copies, waits for them, and re-layouts  16.4 us
    all_to_all x1, waiting for transfers between devices, shards(): gathered = lax.all_to_all(basal, axes, 0, 0)  12.5 us
    all_to_all x1, starting transfers between devices, shards(): meta = lax.all_to_all(meta, 'tiles', 0, 0)  7.29 us
    all_to_all x1, starting transfers between devices, shards(): gathered = lax.all_to_all(basal, axes, 0, 0)  6.09 us
  transfers between devices with their start and end apart: 8, of which 4 were waited for; matrix products, arithmetic and copies ran while one was open for 1% of the time, Pallas kernels for 9%

profile of v3, /device:TPU:0, one launch (start us, length us, event | category | flops | bytes accessed | tf_op | source)
XLA Modules:
  0.0 114.7 jit_solution(17677000238761640322)
XLA Ops:
  0.6 0.0 copy-start.10
  0.6 0.0 copy-start.7
  0.7 0.0 copy-start.6
  0.7 0.9 copy.16.signs_ref
  1.5 1.5 %copy.17.weight_hbm = f32[4096,3]{1,0:T(8,128)S(1)} copy(f32[4096,3]{0,1:T(4,128)} %param.13) | data formatting | bytes 98304 | tf_op args[5]
  3.0 0.0 copy-start.8
  3.0 0.7 copy-done.8
  3.7 0.9 announce.1
  4.6 7.3 %all-to-all-start = ((f32[8,24,256]{2,1,0:T(8,128)}), f32[8,24,256]{2,1,0:T(8,128)S(1)}, u32[]{:S(2)}, u32[]{:S(2)}) async-start(f32[8,24,256]{2,1,0:T(8,128)} %announce.1), calls=%async_computation | async-start | bytes 393216 | tf_op jit(solution)/shard_map/all_to_all | solution.py:436
  12.6 0.1 copy.18
  12.7 0.1 copy.23
  12.9 2.9 %setup.1 = (s32[32,128]{1,0:T(8,128)S(1)}, s32[32,128]{1,0:T(8,128)S(1)}, bf16[512,4096]{1,0:T(8,128)(2,1)S(1)}, bf16[128,4096]{1,0:T(8,128)(2,1)S(1)}, bf16[128...) custom-call(s32[64,64]{1,0:T(8,128)S(1)} %copy-done.6, s32[64,64]{1,0:T(8,128)S(1)} %copy-done.7), custom_call_target="tpu_custom_call" | custom-call | tf_op jit(solution)/shard_map/setup/pallas_call | solution.py:418
  15.8 1.9 %copy-done = bf16[512,4096]{1,0:T(8,128)(2,1)} copy-done((bf16[512,4096]{1,0:T(8,128)(2,1)}, bf16[512,4096]{1,0:T(8,128)(2,1)S(1)}, u32[]{:S(2)}) %copy-start) | copy-done | bytes 4194328
  17.7 0.1 pad_add_fusion.refs_0_.scalars
  17.8 2.1 %all-to-all-done.refs_1_.meta_ref = f32[8,24,256]{2,1,0:T(8,128)S(1)} async-done(((f32[8,24,256]{2,1,0:T(8,128)}), f32[8,24,256]{2,1,0:T(8,128)S(1)}, u32[]{:S(2)}, u32[]{:S(2)}) %all-to-all-start) | async-done | bytes 196640 | tf_op jit(solution)/shard_map/all_to_all | solution.py:436
  19.9 2.2 %copy-done.1 = bf16[512,4096]{1,0:T(8,128)(2,1)S(1)} copy-done((bf16[512,4096]{1,0:T(8,128)(2,1)S(1)}, bf16[512,4096]{1,0:T(8,128)(2,1)}, u32[]{:S(2)}) %copy-start.1) | copy-done | bytes 4194328
  22.0 2.8 %copy-done.4 = bf16[64,192,192]{2,1,0:T(8,128)(2,1)S(1)} copy-done((bf16[64,192,192]{2,1,0:T(8,128)(2,1)S(1)}, bf16[64,192,192]{2,1,0:T(8,128)(2,1)}, u32[]{:S(2)}) %copy-start.4) | copy-done | bytes 4718616
  24.8 4.3 %forward.3 = (f32[512,384]{1,0:T(8,128)S(1)}, f32[24,512]{1,0:T(8,128)S(1)}, f32[24,512]{1,0:T(8,128)S(1)}) custom-call(s32[3]{0:T(128)S(1)} %pad_add_fusion.refs_0_.scalars, f32[8,24,256]{2,1,0:T(8,128)S(1)} %all-to-all-done.refs_1_.meta_ref, s32[32,128]{1,0:T(8,128)S(1)} %get-tuple-element.21.refs_2_.conn_ref.refs_3_, ...), custom_call_target="tpu_custom_call" | custom-call | tf_op jit(solution)/shard_map/forward/pallas_call | solution.py:418
  29.1 1.1 %collective-permute-start = (f32[24,512]{1,0:T(8,128)S(1)}, f32[24,512]{1,0:T(8,128)S(1)}, u32[]{:S(2)}, u32[]{:S(2)}) collective-permute-start(f32[24,512]{1,0:T(8,128)S(1)} %get-tuple-element.27.own_a), channel_id=1, source_target_pairs={{0,4},{8,12},{16,20},{24,28},{4,0},{12,8},{20,16},{28,24},{1,5},{9... | collective-permute-start | bytes 147464 | tf_op jit(solution)/shard_map/ppermute | solution.py:489
  30.3 0.7 collective-permute-start.1
  31.0 2.2 %copy-done.2 = bf16[512,4096]{1,0:T(8,128)(2,1)S(1)} copy-done((bf16[512,4096]{1,0:T(8,128)(2,1)S(1)}, bf16[512,4096]{1,0:T(8,128)(2,1)}, u32[]{:S(2)}) %copy-start.2) | copy-done | bytes 4194328
  33.2 2.5 %inner.3.inner_ref = f32[256,384]{1,0:T(8,128)S(1)} custom-call(f32[512,384]{1,0:T(8,128)S(1)} %get-tuple-element.29.ordered_ref, f32[24,512]{1,0:T(8,128)S(1)} %reshape.28.weight_ref, s32[32,128]{1,0:T(8,128)S(1)} %get-tuple-element.21.refs_2_.conn_ref.refs_3_, bf16[512,4096]{1,0:T(8,128)(2,1)S(1)} %copy-done.2), custom_call_target="tpu_custom_call" | custom-call | tf_op jit(solution)/shard_map/inner/pallas_call | solution.py:418
  35.6 0.0 collective-permute-done.new_a
  35.6 0.0 collective-permute-done.1.new_b
  35.7 0.0 copy-start.5
  35.7 2.8 %copy-done.5 = bf16[64,192,192]{2,1,0:T(8,128)(2,1)S(1)} copy-done((bf16[64,192,192]{2,1,0:T(8,128)(2,1)S(1)}, bf16[64,192,192]{2,1,0:T(8,128)(2,1)}, u32[]{:S(2)}) %copy-start.5) | copy-done | bytes 4718616
  38.5 3.5 %adjoint.3 = f32[8,8,384]{2,1,0:T(8,128)S(1)} custom-call(s32[3]{0:T(128)S(1)} %pad_add_fusion.refs_0_.scalars, f32[8,24,256]{2,1,0:T(8,128)S(1)} %all-to-all-done.refs_1_.meta_ref, f32[24,512]{1,0:T(8,128)S(1)} %get-tuple-element.27.own_a, f32[24,512]{1,0:T(8,128)S(1)} %get-tuple-element.28.own_b, f32[24,512]{1,0:T(8,128)S(1)} %collective-permute-done.new_a, ...), custom_call_target="tpu_custom_call" | custom-call | tf_op jit(solution)/shard_map/adjoint/pallas_call | solution.py:418
  41.9 13.0 %all_to_all.20.refs_2_ = f32[8,8,384]{2,1,0:T(8,128)S(1)} all-to-all(f32[8,8,384]{2,1,0:T(8,128)S(1)} %adjoint.3), channel_id=1, replica_groups=mesh['tiles'=8,'probes'=4] {'tiles'}, dimensions={0} | all-to-all | bytes 196608 | tf_op jit(solution)/shard_map/all_to_all | solution.py:511
  55.0 4.5 %forward.4 = (f32[512,384]{1,0:T(8,128)S(1)}, f32[24,512]{1,0:T(8,128)S(1)}, f32[24,512]{1,0:T(8,128)S(1)}, f32[256,8]{1,0:T(8,128)S(1)}) custom-call(s32[3]{0:T(128)S(1)} %pad_add_fusion.refs_0_.scalars, f32[8,24,256]{2,1,0:T(8,128)S(1)} %all-to-all-done.refs_1_.meta_ref, f32[8,8,384]{2,1,0:T(8,128)S(1)} %all_to_all.20.refs_2_, ...), custom_call_target="tpu_custom_call" | custom-call | tf_op jit(solution)/shard_map/forward/pallas_call | solution.py:418
  59.5 0.4 collective-permute-start.2
  59.8 0.7 collective-permute-start.3
  60.5 2.5 %inner.4.inner_ref = f32[256,384]{1,0:T(8,128)S(1)} custom-call(f32[512,384]{1,0:T(8,128)S(1)} %get-tuple-element.33.ordered_ref, f32[24,512]{1,0:T(8,128)S(1)} %reshape.28.weight_ref, s32[32,128]{1,0:T(8,128)S(1)} %get-tuple-element.21.refs_2_.conn_ref.refs_3_, bf16[512,4096]{1,0:T(8,128)(2,1)S(1)} %copy-done.3), custom_call_target="tpu_custom_call" | custom-call | tf_op jit(solution)/shard_map/inner/pallas_call | solution.py:418
  63.0 0.6 collective-permute-done.2.new_a
  63.6 0.0 collective-permute-done.3.new_b
  63.6 3.5 %adjoint.4 = f32[8,8,384]{2,1,0:T(8,128)S(1)} custom-call(s32[3]{0:T(128)S(1)} %pad_add_fusion.refs_0_.scalars, f32[8,24,256]{2,1,0:T(8,128)S(1)} %all-to-all-done.refs_1_.meta_ref, f32[24,512]{1,0:T(8,128)S(1)} %get-tuple-element.31.own_a, f32[24,512]{1,0:T(8,128)S(1)} %get-tuple-element.32.own_b, f32[24,512]{1,0:T(8,128)S(1)} %collective-permute-done.2.new_a, ...), custom_call_target="tpu_custom_call" | custom-call | tf_op jit(solution)/shard_map/adjoint/pallas_call | solution.py:418
  67.1 13.0 %all_to_all.21.refs_2_ = f32[8,8,384]{2,1,0:T(8,128)S(1)} all-to-all(f32[8,8,384]{2,1,0:T(8,128)S(1)} %adjoint.4), channel_id=1, replica_groups=mesh['tiles'=8,'probes'=4] {'tiles'}, dimensions={0} | all-to-all | bytes 196608 | tf_op jit(solution)/shard_map/all_to_all | solution.py:511
  80.1 4.5 %forward.5 = (f32[512,384]{1,0:T(8,128)S(1)}, f32[24,512]{1,0:T(8,128)S(1)}, f32[24,512]{1,0:T(8,128)S(1)}) custom-call(s32[3]{0:T(128)S(1)} %pad_add_fusion.refs_0_.scalars, f32[8,24,256]{2,1,0:T(8,128)S(1)} %all-to-all-done.refs_1_.meta_ref, f32[8,8,384]{2,1,0:T(8,128)S(1)} %all_to_all.21.refs_2_, ...), custom_call_target="tpu_custom_call" | custom-call | tf_op jit(solution)/shard_map/forward/pallas_call | solution.py:418
  84.6 0.4 collective-permute-start.4
  85.0 0.9 collective-permute-start.5
  85.9 2.5 %inner.5.inner_ref = f32[256,384]{1,0:T(8,128)S(1)} custom-call(f32[512,384]{1,0:T(8,128)S(1)} %get-tuple-element.36.ordered_ref, f32[24,512]{1,0:T(8,128)S(1)} %reshape.28.weight_ref, s32[32,128]{1,0:T(8,128)S(1)} %get-tuple-element.21.refs_2_.conn_ref.refs_3_, bf16[512,4096]{1,0:T(8,128)(2,1)S(1)} %copy-done.3), custom_call_target="tpu_custom_call" | custom-call | tf_op jit(solution)/shard_map/inner/pallas_call | solution.py:418
  88.4 0.4 collective-permute-done.4.new_a
  88.8 0.0 collective-permute-done.5.new_b
  88.8 4.2 %adjoint.5 = f32[32,8,384]{2,1,0:T(8,128)} custom-call(s32[3]{0:T(128)S(1)} %pad_add_fusion.refs_0_.scalars, f32[8,24,256]{2,1,0:T(8,128)S(1)} %all-to-all-done.refs_1_.meta_ref, f32[24,512]{1,0:T(8,128)S(1)} %get-tuple-element.34.own_a, f32[24,512]{1,0:T(8,128)S(1)} %get-tuple-element.35.own_b, f32[24,512]{1,0:T(8,128)S(1)} %collective-permute-done.4.new_a, ...), custom_call_target="tpu_custom_call" | custom-call | tf_op jit(solution)/shard_map/adjoint/pallas_call | solution.py:418
  93.0 6.1 %all-to-all-start.3 = ((f32[32,8,384]{2,1,0:T(8,128)}), f32[32,8,384]{2,1,0:T(8,128)S(1)}, u32[]{:S(2)}, u32[]{:S(2)}) async-start(f32[32,8,384]{2,1,0:T(8,128)} %adjoint.5), calls=%async_computation.3 | async-start | bytes 786432 | tf_op jit(solution)/shard_map/all_to_all | solution.py:511
  99.1 0.7 copy.21
  99.8 12.5 %all-to-all-done.3 = f32[32,8,384]{2,1,0:T(8,128)S(1)} async-done(((f32[32,8,384]{2,1,0:T(8,128)}), f32[32,8,384]{2,1,0:T(8,128)S(1)}, u32[]{:S(2)}, u32[]{:S(2)}) %all-to-all-start.3) | async-done | bytes 393248 | tf_op jit(solution)/shard_map/all_to_all | solution.py:511
  112.3 1.7 %gram.1 = (f32[256,8]{1,0:T(8,128)S(1)}, f32[8,8,32]{2,1,0:T(8,128)}) custom-call(s32[3]{0:T(128)S(1)} %pad_add_fusion.refs_0_.scalars, f32[8,24,256]{2,1,0:T(8,128)S(1)} %all-to-all-done.refs_1_.meta_ref, f32[8,4,8,384]{3,2,1,0:T(8,128)S(1)} %bitcast.9), custom_call_target="tpu_custom_call" | custom-call | tf_op jit(solution)/shard_map/gram/pallas_call | solution.py:418
  114.0 0.7 copy.22
  (15 shorter events, 0.1 us)
Async XLA Ops:
  0.6 11.9 %copy-start.10 = (f32[64,64,3]{1,0,2:T(8,128)S(1)}, f32[64,64,3]{1,0,2:T(8,128)}, u32[]{:S(2)}) copy-start(f32[64,64,3]{1,0,2:T(8,128)} %param.11) | copy-start | bytes 147460
  0.6 12.2 %copy-start.7 = (s32[64,64]{1,0:T(8,128)S(1)}, s32[64,64]{1,0:T(8,128)}, u32[]{:S(2)}) copy-start(s32[64,64]{1,0:T(8,128)} %cell_in.1) | copy-start | bytes 49156
  0.7 12.2 %copy-start.6 = (s32[64,64]{1,0:T(8,128)S(1)}, s32[64,64]{1,0:T(8,128)}, u32[]{:S(2)}) copy-start(s32[64,64]{1,0:T(8,128)} %conn_in.1) | copy-start | bytes 49156
  3.0 0.7 copy-start.8
  4.6 15.2 %all-to-all-start = ((f32[8,24,256]{2,1,0:T(8,128)}), f32[8,24,256]{2,1,0:T(8,128)S(1)}, u32[]{:S(2)}, u32[]{:S(2)}) async-start(f32[8,24,256]{2,1,0:T(8,128)} %announce.1), calls=%async_computation | async-start | bytes 393216 | tf_op jit(solution)/shard_map/all_to_all | solution.py:436
  15.8 1.9 %copy-start = (bf16[512,4096]{1,0:T(8,128)(2,1)}, bf16[512,4096]{1,0:T(8,128)(2,1)S(1)}, u32[]{:S(2)}) copy-start(bf16[512,4096]{1,0:T(8,128)(2,1)S(1)} %get-tuple-element.23.refs_6_.node_hot.refs_7_) | copy-start | bytes 12582916
  19.9 2.2 %copy-start.1 = (bf16[512,4096]{1,0:T(8,128)(2,1)S(1)}, bf16[512,4096]{1,0:T(8,128)(2,1)}, u32[]{:S(2)}) copy-start(bf16[512,4096]{1,0:T(8,128)(2,1)} %copy-done) | copy-start | bytes 12582916
  22.0 2.8 %copy-start.4 = (bf16[64,192,192]{2,1,0:T(8,128)(2,1)S(1)}, bf16[64,192,192]{2,1,0:T(8,128)(2,1)}, u32[]{:S(2)}) copy-start(bf16[64,192,192]{2,1,0:T(8,128)(2,1)} %blocks.5) | copy-start | bytes 14155780
  24.8 6.1 %copy-start.9 = (f32[4096,3]{0,1:T(4,128)S(1)}, f32[4096,3]{0,1:T(4,128)}, u32[]{:S(2)}) copy-start(f32[4096,3]{0,1:T(4,128)} %param.13) | copy-start | bytes 147460
  29.1 6.5 %collective-permute-start = (f32[24,512]{1,0:T(8,128)S(1)}, f32[24,512]{1,0:T(8,128)S(1)}, u32[]{:S(2)}, u32[]{:S(2)}) collective-permute-start(f32[24,512]{1,0:T(8,128)S(1)} %get-tuple-element.27.own_a), channel_id=1, source_target_pairs={{0,4},{8,12},{16,20},{24,28},{4,0},{12,8},{20,16},{28,24},{1,5},{9... | collective-permute-start | bytes 147464 | tf_op jit(solution)/shard_map/ppermute | solution.py:489
  30.3 5.4 %collective-permute-start.1 = (f32[24,512]{1,0:T(8,128)S(1)}, f32[24,512]{1,0:T(8,128)S(1)}, u32[]{:S(2)}, u32[]{:S(2)}) collective-permute-start(f32[24,512]{1,0:T(8,128)S(1)} %get-tuple-element.28.own_b), channel_id=1, source_target_pairs={{4,8},{12,16},{20,24},{8,4},{16,12},{24,20},{5,9},{13,17},{21,25},... | collective-permute-start | bytes 147464 | tf_op jit(solution)/shard_map/ppermute | solution.py:488
  31.0 2.2 %copy-start.2 = (bf16[512,4096]{1,0:T(8,128)(2,1)S(1)}, bf16[512,4096]{1,0:T(8,128)(2,1)}, u32[]{:S(2)}) copy-start(bf16[512,4096]{1,0:T(8,128)(2,1)} %copy-done) | copy-start | bytes 12582916
  33.2 2.5 %copy-start.3 = (bf16[512,4096]{1,0:T(8,128)(2,1)S(1)}, bf16[512,4096]{1,0:T(8,128)(2,1)}, u32[]{:S(2)}) copy-start(bf16[512,4096]{1,0:T(8,128)(2,1)} %copy-done) | copy-start | bytes 12582916
  35.7 2.8 %copy-start.5 = (bf16[64,192,192]{2,1,0:T(8,128)(2,1)S(1)}, bf16[64,192,192]{2,1,0:T(8,128)(2,1)}, u32[]{:S(2)}) copy-start(bf16[64,192,192]{2,1,0:T(8,128)(2,1)} %blocks.5) | copy-start | bytes 14155780
  59.5 4.2 %collective-permute-start.2 = (f32[24,512]{1,0:T(8,128)S(1)}, f32[24,512]{1,0:T(8,128)S(1)}, u32[]{:S(2)}, u32[]{:S(2)}) collective-permute-start(f32[24,512]{1,0:T(8,128)S(1)} %get-tuple-element.31.own_a), channel_id=1, source_target_pairs={{0,4},{8,12},{16,20},{24,28},{4,0},{12,8},{20,16},{28,24},{1,5},{9... | collective-permute-start | bytes 147464 | tf_op jit(solution)/shard_map/ppermute | solution.py:489
  59.8 3.8 %collective-permute-start.3 = (f32[24,512]{1,0:T(8,128)S(1)}, f32[24,512]{1,0:T(8,128)S(1)}, u32[]{:S(2)}, u32[]{:S(2)}) collective-permute-start(f32[24,512]{1,0:T(8,128)S(1)} %get-tuple-element.32.own_b), channel_id=1, source_target_pairs={{4,8},{12,16},{20,24},{8,4},{16,12},{24,20},{5,9},{13,17},{21,25},... | collective-permute-start | bytes 147464 | tf_op jit(solution)/shard_map/ppermute | solution.py:488
  84.6 4.2 %collective-permute-start.4 = (f32[24,512]{1,0:T(8,128)S(1)}, f32[24,512]{1,0:T(8,128)S(1)}, u32[]{:S(2)}, u32[]{:S(2)}) collective-permute-start(f32[24,512]{1,0:T(8,128)S(1)} %get-tuple-element.34.own_a), channel_id=1, source_target_pairs={{0,4},{8,12},{16,20},{24,28},{4,0},{12,8},{20,16},{28,24},{1,5},{9... | collective-permute-start | bytes 147464 | tf_op jit(solution)/shard_map/ppermute | solution.py:489
  85.0 3.8 %collective-permute-start.5 = (f32[24,512]{1,0:T(8,128)S(1)}, f32[24,512]{1,0:T(8,128)S(1)}, u32[]{:S(2)}, u32[]{:S(2)}) collective-permute-start(f32[24,512]{1,0:T(8,128)S(1)} %get-tuple-element.35.own_b), channel_id=1, source_target_pairs={{4,8},{12,16},{20,24},{8,4},{16,12},{24,20},{5,9},{13,17},{21,25},... | collective-permute-start | bytes 147464 | tf_op jit(solution)/shard_map/ppermute | solution.py:488
  93.0 19.3 %all-to-all-start.3 = ((f32[32,8,384]{2,1,0:T(8,128)}), f32[32,8,384]{2,1,0:T(8,128)S(1)}, u32[]{:S(2)}, u32[]{:S(2)}) async-start(f32[32,8,384]{2,1,0:T(8,128)} %adjoint.5), calls=%async_computation.3 | async-start | bytes 786432 | tf_op jit(solution)/shard_map/all_to_all | solution.py:511

commit v4 on v3

--- a/solution.py
+++ b/solution.py
@@ -11,7 +11,7 @@
 POWER = 2
 RIM = 64
 LANES = 128
-VMEM_BYTES = 30 * 1024 * 1024
+VMEM_BYTES = 16 * 1024 * 1024
 
 F32 = jnp.float32
 BF16 = jnp.bfloat16
@@ -88,35 +88,33 @@
     return jnp.where(same if keep_same else ~same, field, F32(0))
 
 
-def announce_kernel(signs_ref, ids_ref, weight_hbm, out_ref, lead, sem):
-    load = pltpu.make_async_copy(weight_hbm.at[pl.ds(0, HALO)], lead, sem)
-    load.start()
+def announce_kernel(signs_ref, ids_ref, weight_ref, out_ref):
     half = HALO // 2
-    out_ref[0, :8, :] = signs_ref[...].astype(F32).T
+    out_ref[0, :8, :] = signs_ref[...].astype(F32)
     out_ref[0, 8:16, :] = jnp.broadcast_to(ids_ref[...].astype(F32), (8, half))
-    load.wait()
-    turned = lead[...].T
     out_ref[0, 16:24, :] = jnp.zeros((8, half), F32)
-    out_ref[0, 16:19, :] = turned[:, :half]
-    out_ref[0, 19:22, :] = turned[:, half:]
+    out_ref[0, 16:19, :] = weight_ref[:, :half]
+    out_ref[0, 19:22, :] = weight_ref[:, half:HALO]
     block = out_ref[0]
     for t in range(1, out_ref.shape[0]):
         out_ref[t] = block
 
 
 def setup_kernel(
-    node_slots,
-    padded_order,
     conn_in,
     cell_in,
+    friction_ref,
     conn_ref,
     cell_ref,
+    fr_ref,
     node_hot_ref,
     cell_hot_ref,
     spread_ref,
     order_ref,
 ):
     pairs = conn_ref.shape[0]
+    slots, padded_order = fr_ref.shape
+    node_slots = conn_in.shape[1]
     window = 3 * LANES
 
     def paired(ref):
@@ -138,6 +136,18 @@
         cell_hot_ref[:, at] = jnp.where(hot, F32(1), F32(0)).astype(BF16)
     spread_ref[...] = spread_matrix(node_slots, padded_order)
     order_ref[...] = order_matrix(node_slots, padded_order)
+
+    shape = (node_slots, padded_order)
+    total = jnp.zeros((slots, padded_order), F32)
+    for c in range(3):
+        place = lanes_iota(shape) == 3 * rows_iota(shape) + c
+        place = jnp.where(place, F32(1), F32(0)).astype(BF16)
+        rest = friction_ref[c]
+        for _ in range(3):
+            part = rest.astype(BF16)
+            total = total + dot(part, place)
+            rest = rest - part.astype(F32)
+    fr_ref[...] = total
 
 
 def forward_kernel(first, keep_same, want_field, tiles, levels, *refs):
@@ -163,7 +173,7 @@
 
     own = current(tile)
     if want_field:
-        field_ref[...] = own.T
+        field_ref[...] = own
     below = jnp.where(tile > 0, current(jnp.maximum(tile - 1, 0)), F32(0))
     above = jnp.where(tile < tiles - 1, current(jnp.minimum(tile + 1, tiles - 1)), F32(0))
     lane = lanes_iota((8, LANES))
@@ -202,11 +212,11 @@
 
     f_ref[...] = jnp.zeros_like(f_ref)
     for m in range(pairs):
-        inputs = spread[8 * m : 8 * m + 8, :] * fr_ref[m : m + 1, :]
         for side in range(2):
             at = side * padded_order
             slot = 2 * m + side
-            out = dot_nt(inputs[:, at : at + order].astype(BF16), blocks[slot])
+            inputs = spread[8 * m : 8 * m + 8, at : at + order] * fr_ref[slot : slot + 1, :order]
+            out = dot_nt(inputs.astype(BF16), blocks[slot])
             out = jnp.where(slot < count, out, F32(0))
             hi = out.astype(BF16).astype(F32)
             f_ref[16 * m : 16 * m + 8, at : at + order] = hi
@@ -256,7 +266,8 @@
     rows = []
     for i in range(3 * (levels - 2)):
         value = nodes[16 * i : 16 * i + 8] + nodes[16 * i + 8 : 16 * i + 16]
-        rows.append(value * weight_ref[i + 3 : i + 4, :])
+        at = (i // 3 + 1) * HALO
+        rows.append(value * weight_ref[i % 3 : i % 3 + 1, at : at + HALO])
     weighted = jnp.concatenate(rows, axis=0).astype(BF16)
     step = 2
     for start in range(0, pairs, step):
@@ -293,10 +304,9 @@
     spread_ref,
     order_ref,
     out_ref,
-    p_ref,
-    n_ref,
-    v_ref,
+    *refs,
 ):
+    *own_ref, p_ref, n_ref, v_ref = refs
     order = blocks.shape[1]
     padded_order = p_ref.shape[1] // 2
     pairs = blocks.shape[0] // 2
@@ -308,7 +318,7 @@
     spill = jnp.where(even, own_a[...] + new_a[...], own_b[...] + new_b[...])
     after = meta_ref[jnp.minimum(tile + 1, tiles - 1)]
     after = jnp.where(tile < tiles - 1, after, F32(0))
-    rows = [lead[8 * c : 8 * c + 8] * weight_ref[c : c + 1, :] for c in range(3)]
+    rows = [lead[8 * c : 8 * c + 8] * weight_ref[c : c + 1, :HALO] for c in range(3)]
     for c in range(3):
         weight = jnp.concatenate([after[16 + c : 17 + c, :], after[19 + c : 20 + c, :]], axis=1)
         rows.append(spill[8 * c : 8 * c + 8] * weight)
@@ -334,7 +344,7 @@
             at = side * padded_order
             slot = 2 * m + side
             out = dot(natural[8 * m : 8 * m + 8, at : at + order].astype(BF16), blocks[slot])
-            out = out * fr_ref[m : m + 1, at : at + order]
+            out = out * fr_ref[slot : slot + 1, :order]
             p_ref[8 * m : 8 * m + 8, at : at + order] = jnp.where(slot < count, out, F32(0))
 
     hi, lo = split(p_ref[...])
@@ -352,26 +362,32 @@
     basal = dot_nt(v_ref[...], cell_hot[...])
     basal = basal[:24] + basal[24:]
     basal = jnp.concatenate([basal[:8], basal[8:16], basal[16:]], axis=1)
+    if own_ref:
+        own_ref[0][...] = basal
+    basal = basal.astype(out_ref.dtype)
     for t in range(out_ref.shape[0]):
         out_ref[t] = basal
 
 
-def gram_kernel(keep_same, tiles, groups, scalars, meta_ref, g_ref, field_ref, gram_ref):
+def gram_kernel(keep_same, tiles, groups, scalars, meta_ref, g_ref, own_ref, field_ref, gram_ref):
     tile = scalars[0]
     group = scalars[2]
     clusters = gram_ref.shape[0]
 
-    def field(t, p):
+    def field(t, p, own=None):
         zero = jnp.zeros(g_ref.shape[2:], F32)
         if isinstance(t, int):
-            before = g_ref[t - 1, p] if t > 0 else zero
-            after = g_ref[t + 1, p] if t < tiles - 1 else zero
+            before = g_ref[t - 1, p].astype(F32) if t > 0 else zero
+            after = g_ref[t + 1, p].astype(F32) if t < tiles - 1 else zero
         else:
-            before = jnp.where(t > 0, g_ref[jnp.maximum(t - 1, 0), p], zero)
-            after = jnp.where(t < tiles - 1, g_ref[jnp.minimum(t + 1, tiles - 1), p], zero)
-        return masked(total_field(before, g_ref[t, p], after), meta_ref[t], keep_same)
-
-    field_ref[...] = field(tile, group).T
+            before = jnp.where(t > 0, g_ref[jnp.maximum(t - 1, 0), p].astype(F32), zero)
+            after = g_ref[jnp.minimum(t + 1, tiles - 1), p].astype(F32)
+            after = jnp.where(t < tiles - 1, after, zero)
+        if own is None:
+            own = g_ref[t, p].astype(F32)
+        return masked(total_field(before, own, after), meta_ref[t], keep_same)
+
+    field_ref[...] = field(tile, group, own_ref[...])
 
     def add_tile(t, acc):
         ids = meta_ref[t][8:16, :].astype(jnp.int32)
@@ -396,7 +412,7 @@
 def shards(
     blocks, connectivity, basal_map, friction, elem_counts, obs_weight, sign_bits, cluster_ids
 ):
-    slots, order, _ = blocks.shape
+    slots = blocks.shape[0]
     node_slots = connectivity.shape[1]
     node_count = obs_weight.shape[0]
     cell_count, group_size = sign_bits.shape
@@ -410,7 +426,6 @@
 
     smem = pl.BlockSpec(memory_space=pltpu.SMEM)
     vmem = pl.BlockSpec(memory_space=pltpu.VMEM)
-    anywhere = pl.BlockSpec(memory_space=pl.ANY)
     params = pltpu.CompilerParams(vmem_limit_bytes=VMEM_BYTES)
     shaped = jax.ShapeDtypeStruct
 
@@ -425,31 +440,28 @@
             name=name,
         )(*operands)
 
+    weight = obs_weight.T
     meta = call(
         announce_kernel,
         "announce",
         shaped((tiles, 24, cell_count), F32),
-        [sign_bits, cluster_ids.reshape(1, cell_count), obs_weight],
-        [vmem, vmem, anywhere],
-        [pltpu.VMEM((HALO, 3), F32), pltpu.SemaphoreType.DMA],
+        [sign_bits.T, cluster_ids.reshape(1, cell_count), weight],
     )
     meta = lax.all_to_all(meta, "tiles", 0, 0)
-    conn, cells, node_hot, cell_hot, spread, order_map = call(
-        functools.partial(setup_kernel, node_slots, padded_order),
+    conn, cells, fr, node_hot, cell_hot, spread, order_map = call(
+        setup_kernel,
         "setup",
         [
             shaped((pairs, LANES), jnp.int32),
             shaped((pairs, LANES), jnp.int32),
+            shaped((slots, padded_order), F32),
             shaped((HALO, refs), BF16),
             shaped((LANES, refs), BF16),
             shaped((LANES, 2 * padded_order), BF16),
             shaped((2 * padded_order, 3 * LANES), BF16),
         ],
-        [connectivity, basal_map],
+        [connectivity, basal_map, friction.transpose(2, 0, 1)],
     )
-    weight = obs_weight.reshape(node_count // HALO, HALO, 3).transpose(0, 2, 1).reshape(-1, HALO)
-    fr = jnp.pad(friction.reshape(slots, order), ((0, 0), (0, padded_order - order)))
-    fr = fr.reshape(pairs, 2 * padded_order)
     scalars = jnp.stack(
         [lax.axis_index("tiles"), elem_counts[0], lax.axis_index("probes")]
     ).astype(jnp.int32)
@@ -468,7 +480,7 @@
             shaped((24, HALO), F32),
         ]
         if want_field:
-            out_shape.append(shaped((cell_count, group_size), F32))
+            out_shape.append(shaped((group_size, cell_count), F32))
         operands = [scalars, meta] + ([] if first else [gathered]) + shared
         return call(
             functools.partial(forward_kernel, first, keep_same, want_field, tiles, levels),
@@ -484,7 +496,7 @@
     for step in range(POWER + 1):
         ordered, own_a, own_b, *field = forward(gathered, step % 2 == 0, step == 1)
         if field:
-            samples = field[0]
+            samples = field[0].T
         new_b = lax.ppermute(own_b, "tiles", swap_b)
         new_a = lax.ppermute(own_a, "tiles", swap_a)
         inner = call(
@@ -496,10 +508,13 @@
         )
         axes = "tiles" if step < POWER else ("tiles", "probes")
         operands = [scalars, meta, own_a, own_b, new_a, new_b, inner, weight] + shared
-        basal = call(
+        last = step == POWER
+        shape = (group_size, window)
+        out_shape = [shaped((lax.axis_size(axes), *shape), BF16 if last else F32)]
+        basal, *own = call(
             functools.partial(adjoint_kernel, tiles, levels),
             "adjoint",
-            shaped((lax.axis_size(axes), group_size, window), F32),
+            out_shape + [shaped(shape, F32)] * last,
             operands,
             [smem] + [vmem] * (len(operands) - 1),
             [
@@ -515,13 +530,13 @@
         functools.partial(gram_kernel, POWER % 2 == 1, tiles, groups),
         "gram",
         [
-            shaped((cell_count, group_size), F32),
+            shaped((group_size, cell_count), F32),
             shaped((tiles, group_size, groups * group_size), F32),
         ],
-        [scalars, meta, gathered],
-        [smem, vmem, vmem],
+        [scalars, meta, gathered, own[0]],
+        [smem, vmem, vmem, vmem],
     )
-    return (samples, refined, gram)
+    return (samples, refined.T, gram)
 
 
 def solution(mesh):

time: 115 us -> 107 us (0.930)
  blocking collectives: 26 us -> 42.9 us
  waiting for transfers between devices: 15.6 us -> 1 us
  starting transfers between devices: 17.4 us -> 12.2 us
  local copies, waits for them, and re-layouts: 16.5 us -> 11.5 us
    all_to_all x2 -> x3, blocking collectives: 26 us -> 42.9 us  [shards(): gathered = lax.all_to_all(basal, axes, 0, 0)]
    all_to_all x1 -> x0, waiting for transfers between devices: 12.5 us -> none  [shards(): gathered = lax.all_to_all(basal, axes, 0, 0)]
    all_to_all x1 -> x0, starting transfers between devices: 6.09 us -> none  [shards(): gathered = lax.all_to_all(basal, axes, 0, 0)]
    unnamed x28 -> x24, local copies, waits for them, and re-layouts: 16.4 us -> 11.5 us
    all_to_all x1, waiting for transfers between devices: 2.08 us -> 0.01 us  [shards(): meta = lax.all_to_all(meta, 'tiles', 0, 0)]
  transfers between devices with their start and end apart: 8 -> 7, of which waited for: 4 -> 2; matrix products, arithmetic and copies ran while one was open for 1% -> 0% of each run, Pallas kernels for 9% -> 10%
where the time goes in v4:
time: 107 us; the launch traced here: 106 us
  blocking collectives  42.9 us (40%)
  Pallas kernels  37 us (35%)
  starting transfers between devices  12.2 us (11%)
  local copies, waits for them, and re-layouts  11.5 us (11%)
  between operations  1.49 us (1%)
    all_to_all x3, blocking collectives, shards(): gathered = lax.all_to_all(basal, axes, 0, 0)  42.9 us
    pallas_call x12, Pallas kernels, call(): pl.pallas_call(kernel, out_shape=out_shape, in_specs=in_specs or [vmem] *...  37 us
    unnamed x24, local copies, waits for them, and re-layouts  11.5 us
    all_to_all x1, starting transfers between devices, shards(): meta = lax.all_to_all(meta, 'tiles', 0, 0)  7.28 us
    ppermute x3, starting transfers between devices, shards(): new_a = lax.ppermute(own_a, 'tiles', swap_a)  2.77 us
    ppermute x3, starting transfers between devices, shards(): new_b = lax.ppermute(own_b, 'tiles', swap_b)  2.18 us
  transfers between devices with their start and end apart: 7, of which 2 were waited for; matrix products, arithmetic and copies ran while one was open for 0% of the time, Pallas kernels for 10%

profile of v4, /device:TPU:0, one launch (start us, length us, event | category | flops | bytes accessed | tf_op | source)
XLA Modules:
  0.0 106.2 jit_solution(15148637622958252813)
XLA Ops:
  0.6 0.0 copy-start.5
  0.6 0.8 copy-done.5
  1.5 0.0 copy-start.10
  1.5 0.7 copy-done.10
  2.2 0.0 copy-start.11
  2.2 0.7 copy-done.11
  2.9 0.7 announce.1
  3.6 7.3 %all-to-all-start = ((f32[8,24,256]{2,1,0:T(8,128)}), f32[8,24,256]{2,1,0:T(8,128)S(1)}, u32[]{:S(2)}, u32[]{:S(2)}) async-start(f32[8,24,256]{2,1,0:T(8,128)} %announce.1), calls=%async_computation | async-start | bytes 393216 | tf_op jit(solution)/shard_map/all_to_all | solution.py:450
  10.8 0.0 copy-start.6
  11.5 0.0 copy-start.7
  11.5 0.9 copy-done.7
  12.4 0.8 copy-done.8
  13.2 0.8 copy-done.9
  13.9 2.9 %setup.1 = (s32[32,128]{1,0:T(8,128)S(1)}, s32[32,128]{1,0:T(8,128)S(1)}, f32[64,256]{1,0:T(8,128)S(1)}, bf16[512,4096]{1,0:T(8,128)(2,1)S(1)}, bf16[128,4096]{1...) custom-call(s32[64,64]{1,0:T(8,128)S(1)} %copy-done.8, s32[64,64]{1,0:T(8,128)S(1)} %copy-done.9, ...), custom_call_target="tpu_custom_call" | custom-call | tf_op jit(solution)/shard_map/setup/pallas_call | solution.py:433
  16.8 0.0 copy-start
  16.8 1.9 %copy-done = bf16[512,4096]{1,0:T(8,128)(2,1)} copy-done((bf16[512,4096]{1,0:T(8,128)(2,1)}, bf16[512,4096]{1,0:T(8,128)(2,1)S(1)}, u32[]{:S(2)}) %copy-start) | copy-done | bytes 4194328
  18.8 0.1 pad_add_fusion.refs_0_.scalars
  18.9 0.0 all-to-all-done.refs_1_.meta_ref
  18.9 2.2 %copy-done.1 = bf16[512,4096]{1,0:T(8,128)(2,1)S(1)} copy-done((bf16[512,4096]{1,0:T(8,128)(2,1)S(1)}, bf16[512,4096]{1,0:T(8,128)(2,1)}, u32[]{:S(2)}) %copy-start.1) | copy-done | bytes 4194328
  21.0 2.8 %copy-done.3 = bf16[64,192,192]{2,1,0:T(8,128)(2,1)S(1)} copy-done((bf16[64,192,192]{2,1,0:T(8,128)(2,1)S(1)}, bf16[64,192,192]{2,1,0:T(8,128)(2,1)}, u32[]{:S(2)}) %copy-start.3) | copy-done | bytes 4718616
  23.8 4.3 %forward.3 = (f32[512,384]{1,0:T(8,128)S(1)}, f32[24,512]{1,0:T(8,128)S(1)}, f32[24,512]{1,0:T(8,128)S(1)}) custom-call(s32[3]{0:T(128)S(1)} %pad_add_fusion.refs_0_.scalars, f32[8,24,256]{2,1,0:T(8,128)S(1)} %all-to-all-done.refs_1_.meta_ref, s32[32,128]{1,0:T(8,128)S(1)} %get-tuple-element.24.refs_2_.conn_ref.refs_3_, ...), custom_call_target="tpu_custom_call" | custom-call | tf_op jit(solution)/shard_map/forward/pallas_call | solution.py:433
  28.1 2.1 %collective-permute-start = (f32[24,512]{1,0:T(8,128)S(1)}, f32[24,512]{1,0:T(8,128)S(1)}, u32[]{:S(2)}, u32[]{:S(2)}) collective-permute-start(f32[24,512]{1,0:T(8,128)S(1)} %get-tuple-element.31.own_a), channel_id=1, source_target_pairs={{0,4},{8,12},{16,20},{24,28},{4,0},{12,8},{20,16},{28,24},{1,5},{9... | collective-permute-start | bytes 147464 | tf_op jit(solution)/shard_map/ppermute | solution.py:501
  30.2 0.7 collective-permute-start.1
  30.9 0.0 copy-done.6
  30.9 0.0 copy-done.2
  30.9 2.5 %inner.3.inner_ref = f32[256,384]{1,0:T(8,128)S(1)} custom-call(f32[512,384]{1,0:T(8,128)S(1)} %get-tuple-element.33.ordered_ref, f32[3,4096]{1,0:T(4,128)S(1)} %bitcast.10, s32[32,128]{1,0:T(8,128)S(1)} %get-tuple-element.24.refs_2_.conn_ref.refs_3_, bf16[512,4096]{1,0:T(8,128)(2,1)S(1)} %copy-done.2), custom_call_target="tpu_custom_call" | custom-call | tf_op jit(solution)/shard_map/inner/pallas_call | solution.py:433
  33.4 0.0 collective-permute-done.new_a
  33.4 0.0 collective-permute-done.1.new_b
  33.5 0.0 copy-done.4
  33.5 3.5 %adjoint.3 = f32[8,8,384]{2,1,0:T(8,128)S(1)} custom-call(s32[3]{0:T(128)S(1)} %pad_add_fusion.refs_0_.scalars, f32[8,24,256]{2,1,0:T(8,128)S(1)} %all-to-all-done.refs_1_.meta_ref, f32[24,512]{1,0:T(8,128)S(1)} %get-tuple-element.31.own_a, f32[24,512]{1,0:T(8,128)S(1)} %get-tuple-element.32.own_b, f32[24,512]{1,0:T(8,128)S(1)} %collective-permute-done.new_a, ...), custom_call_target="tpu_custom_call" | custom-call | tf_op jit(solution)/shard_map/adjoint/pallas_call | solution.py:433
  37.0 15.1 %all_to_all.20.refs_2_ = f32[8,8,384]{2,1,0:T(8,128)S(1)} all-to-all(f32[8,8,384]{2,1,0:T(8,128)S(1)} %adjoint.3), channel_id=1, replica_groups=mesh['tiles'=8,'probes'=4] {'tiles'}, dimensions={0} | all-to-all | bytes 196608 | tf_op jit(solution)/shard_map/all_to_all | solution.py:526
  52.0 4.9 %forward.4 = (f32[512,384]{1,0:T(8,128)S(1)}, f32[24,512]{1,0:T(8,128)S(1)}, f32[24,512]{1,0:T(8,128)S(1)}, f32[8,256]{1,0:T(8,128)}) custom-call(s32[3]{0:T(128)S(1)} %pad_add_fusion.refs_0_.scalars, f32[8,24,256]{2,1,0:T(8,128)S(1)} %all-to-all-done.refs_1_.meta_ref, f32[8,8,384]{2,1,0:T(8,128)S(1)} %all_to_all.20.refs_2_, ...), custom_call_target="tpu_custom_call" | custom-call | tf_op jit(solution)/shard_map/forward/pallas_call | solution.py:433
  56.9 0.3 collective-permute-start.2
  57.2 0.7 collective-permute-start.3
  57.9 2.5 %inner.4.inner_ref = f32[256,384]{1,0:T(8,128)S(1)} custom-call(f32[512,384]{1,0:T(8,128)S(1)} %get-tuple-element.37.ordered_ref, f32[3,4096]{1,0:T(4,128)S(1)} %bitcast.12, s32[32,128]{1,0:T(8,128)S(1)} %get-tuple-element.24.refs_2_.conn_ref.refs_3_, bf16[512,4096]{1,0:T(8,128)(2,1)S(1)} %copy-done.2), custom_call_target="tpu_custom_call" | custom-call | tf_op jit(solution)/shard_map/inner/pallas_call | solution.py:433
  60.4 0.6 collective-permute-done.2.new_a
  61.0 0.0 collective-permute-done.3.new_b
  61.0 3.5 %adjoint.4 = f32[8,8,384]{2,1,0:T(8,128)S(1)} custom-call(s32[3]{0:T(128)S(1)} %pad_add_fusion.refs_0_.scalars, f32[8,24,256]{2,1,0:T(8,128)S(1)} %all-to-all-done.refs_1_.meta_ref, f32[24,512]{1,0:T(8,128)S(1)} %get-tuple-element.35.own_a, f32[24,512]{1,0:T(8,128)S(1)} %get-tuple-element.36.own_b, f32[24,512]{1,0:T(8,128)S(1)} %collective-permute-done.2.new_a, ...), custom_call_target="tpu_custom_call" | custom-call | tf_op jit(solution)/shard_map/adjoint/pallas_call | solution.py:433
  64.5 13.0 %all_to_all.21.refs_2_ = f32[8,8,384]{2,1,0:T(8,128)S(1)} all-to-all(f32[8,8,384]{2,1,0:T(8,128)S(1)} %adjoint.4), channel_id=1, replica_groups=mesh['tiles'=8,'probes'=4] {'tiles'}, dimensions={0} | all-to-all | bytes 196608 | tf_op jit(solution)/shard_map/all_to_all | solution.py:526
  77.5 4.5 %forward.5 = (f32[512,384]{1,0:T(8,128)S(1)}, f32[24,512]{1,0:T(8,128)S(1)}, f32[24,512]{1,0:T(8,128)S(1)}) custom-call(s32[3]{0:T(128)S(1)} %pad_add_fusion.refs_0_.scalars, f32[8,24,256]{2,1,0:T(8,128)S(1)} %all-to-all-done.refs_1_.meta_ref, f32[8,8,384]{2,1,0:T(8,128)S(1)} %all_to_all.21.refs_2_, ...), custom_call_target="tpu_custom_call" | custom-call | tf_op jit(solution)/shard_map/forward/pallas_call | solution.py:433
  82.0 0.4 collective-permute-start.4
  82.4 0.9 collective-permute-start.5
  83.3 2.5 %inner.5.inner_ref = f32[256,384]{1,0:T(8,128)S(1)} custom-call(f32[512,384]{1,0:T(8,128)S(1)} %get-tuple-element.40.ordered_ref, f32[3,4096]{1,0:T(4,128)S(1)} %bitcast.14, s32[32,128]{1,0:T(8,128)S(1)} %get-tuple-element.24.refs_2_.conn_ref.refs_3_, bf16[512,4096]{1,0:T(8,128)(2,1)S(1)} %copy-done.2), custom_call_target="tpu_custom_call" | custom-call | tf_op jit(solution)/shard_map/inner/pallas_call | solution.py:433
  85.8 0.4 collective-permute-done.4.new_a
  86.2 0.0 collective-permute-done.5.new_b
  86.2 3.5 %adjoint.5 = (bf16[32,8,384]{2,1,0:T(8,128)(2,1)S(1)}, f32[8,384]{1,0:T(8,128)S(1)}) custom-call(s32[3]{0:T(128)S(1)} %pad_add_fusion.refs_0_.scalars, f32[8,24,256]{2,1,0:T(8,128)S(1)} %all-to-all-done.refs_1_.meta_ref, f32[24,512]{1,0:T(8,128)S(1)} %get-tuple-element.38.own_a, f32[24,512]{1,0:T(8,128)S(1)} %get-tuple-element.39.own_b, ...), custom_call_target="tpu_custom_call" | custom-call | tf_op jit(solution)/shard_map/adjoint/pallas_call | solution.py:433
  89.7 14.8 %all_to_all.22 = bf16[32,8,384]{2,1,0:T(8,128)(2,1)S(1)} all-to-all(bf16[32,8,384]{2,1,0:T(8,128)(2,1)S(1)} %get-tuple-element.41), channel_id=1, replica_groups=mesh['tiles'=8,'probes'=4] {'tiles','probes'}, dimensions={0} | all-to-all | bytes 393216 | tf_op jit(solution)/shard_map/all_to_all | solution.py:526
  104.5 1.7 %gram.1 = (f32[8,256]{1,0:T(8,128)}, f32[8,8,32]{2,1,0:T(8,128)}) custom-call(s32[3]{0:T(128)S(1)} %pad_add_fusion.refs_0_.scalars, f32[8,24,256]{2,1,0:T(8,128)S(1)} %all-to-all-done.refs_1_.meta_ref, bf16[8,4,8,384]{3,2,1,0:T(8,128)(2,1)S(1)} %bitcast.16, f32[8,384]{1,0:T(8,128)S(1)} %get-tuple-element.42.own_ref), custom_call_target="tpu_custom_call" | custom-call | tf_op jit(solution)/shard_map/gram/pallas_call | solution.py:433
  (6 shorter events, 0.0 us)
Async XLA Ops:
  0.6 0.8 copy-start.5
  1.5 0.7 copy-start.10
  2.2 0.7 copy-start.11
  3.6 15.3 %all-to-all-start = ((f32[8,24,256]{2,1,0:T(8,128)}), f32[8,24,256]{2,1,0:T(8,128)S(1)}, u32[]{:S(2)}, u32[]{:S(2)}) async-start(f32[8,24,256]{2,1,0:T(8,128)} %announce.1), calls=%async_computation | async-start | bytes 393216 | tf_op jit(solution)/shard_map/all_to_all | solution.py:450
  10.8 20.0 %copy-start.6 = (f32[4096,3]{0,1:T(4,128)S(1)}, f32[4096,3]{0,1:T(4,128)}, u32[]{:S(2)}) copy-start(f32[4096,3]{0,1:T(4,128)} %param.13) | copy-start | bytes 147460
  11.5 0.9 copy-start.7
  12.4 0.8 copy-start.8
  13.2 0.8 copy-start.9
  16.8 1.9 %copy-start = (bf16[512,4096]{1,0:T(8,128)(2,1)}, bf16[512,4096]{1,0:T(8,128)(2,1)S(1)}, u32[]{:S(2)}) copy-start(bf16[512,4096]{1,0:T(8,128)(2,1)S(1)} %get-tuple-element.27.refs_6_.node_hot.refs_7_) | copy-start | bytes 12582916
  18.9 2.2 %copy-start.1 = (bf16[512,4096]{1,0:T(8,128)(2,1)S(1)}, bf16[512,4096]{1,0:T(8,128)(2,1)}, u32[]{:S(2)}) copy-start(bf16[512,4096]{1,0:T(8,128)(2,1)} %copy-done) | copy-start | bytes 12582916
  21.0 2.8 %copy-start.3 = (bf16[64,192,192]{2,1,0:T(8,128)(2,1)S(1)}, bf16[64,192,192]{2,1,0:T(8,128)(2,1)}, u32[]{:S(2)}) copy-start(bf16[64,192,192]{2,1,0:T(8,128)(2,1)} %blocks.5) | copy-start | bytes 14155780
  23.8 7.1 %copy-start.2 = (bf16[512,4096]{1,0:T(8,128)(2,1)S(1)}, bf16[512,4096]{1,0:T(8,128)(2,1)}, u32[]{:S(2)}) copy-start(bf16[512,4096]{1,0:T(8,128)(2,1)} %copy-done) | copy-start | bytes 12582916
  23.8 9.6 %copy-start.4 = (bf16[64,192,192]{2,1,0:T(8,128)(2,1)S(1)}, bf16[64,192,192]{2,1,0:T(8,128)(2,1)}, u32[]{:S(2)}) copy-start(bf16[64,192,192]{2,1,0:T(8,128)(2,1)} %blocks.5) | copy-start | bytes 14155780
  28.1 5.3 %collective-permute-start = (f32[24,512]{1,0:T(8,128)S(1)}, f32[24,512]{1,0:T(8,128)S(1)}, u32[]{:S(2)}, u32[]{:S(2)}) collective-permute-start(f32[24,512]{1,0:T(8,128)S(1)} %get-tuple-element.31.own_a), channel_id=1, source_target_pairs={{0,4},{8,12},{16,20},{24,28},{4,0},{12,8},{20,16},{28,24},{1,5},{9... | collective-permute-start | bytes 147464 | tf_op jit(solution)/shard_map/ppermute | solution.py:501
  30.2 3.2 %collective-permute-start.1 = (f32[24,512]{1,0:T(8,128)S(1)}, f32[24,512]{1,0:T(8,128)S(1)}, u32[]{:S(2)}, u32[]{:S(2)}) collective-permute-start(f32[24,512]{1,0:T(8,128)S(1)} %get-tuple-element.32.own_b), channel_id=1, source_target_pairs={{4,8},{12,16},{20,24},{8,4},{16,12},{24,20},{5,9},{13,17},{21,25},... | collective-permute-start | bytes 147464 | tf_op jit(solution)/shard_map/ppermute | solution.py:500
  56.9 4.1 %collective-permute-start.2 = (f32[24,512]{1,0:T(8,128)S(1)}, f32[24,512]{1,0:T(8,128)S(1)}, u32[]{:S(2)}, u32[]{:S(2)}) collective-permute-start(f32[24,512]{1,0:T(8,128)S(1)} %get-tuple-element.35.own_a), channel_id=1, source_target_pairs={{0,4},{8,12},{16,20},{24,28},{4,0},{12,8},{20,16},{28,24},{1,5},{9... | collective-permute-start | bytes 147464 | tf_op jit(solution)/shard_map/ppermute | solution.py:501
  57.2 3.8 %collective-permute-start.3 = (f32[24,512]{1,0:T(8,128)S(1)}, f32[24,512]{1,0:T(8,128)S(1)}, u32[]{:S(2)}, u32[]{:S(2)}) collective-permute-start(f32[24,512]{1,0:T(8,128)S(1)} %get-tuple-element.36.own_b), channel_id=1, source_target_pairs={{4,8},{12,16},{20,24},{8,4},{16,12},{24,20},{5,9},{13,17},{21,25},... | collective-permute-start | bytes 147464 | tf_op jit(solution)/shard_map/ppermute | solution.py:500
  82.0 4.2 %collective-permute-start.4 = (f32[24,512]{1,0:T(8,128)S(1)}, f32[24,512]{1,0:T(8,128)S(1)}, u32[]{:S(2)}, u32[]{:S(2)}) collective-permute-start(f32[24,512]{1,0:T(8,128)S(1)} %get-tuple-element.38.own_a), channel_id=1, source_target_pairs={{0,4},{8,12},{16,20},{24,28},{4,0},{12,8},{20,16},{28,24},{1,5},{9... | collective-permute-start | bytes 147464 | tf_op jit(solution)/shard_map/ppermute | solution.py:501
  82.4 3.8 %collective-permute-start.5 = (f32[24,512]{1,0:T(8,128)S(1)}, f32[24,512]{1,0:T(8,128)S(1)}, u32[]{:S(2)}, u32[]{:S(2)}) collective-permute-start(f32[24,512]{1,0:T(8,128)S(1)} %get-tuple-element.39.own_b), channel_id=1, source_target_pairs={{4,8},{12,16},{20,24},{8,4},{16,12},{24,20},{5,9},{13,17},{21,25},... | collective-permute-start | bytes 147464 | tf_op jit(solution)/shard_map/ppermute | solution.py:500

commit v5 on v4

v5 whole, which is shorter than its diff:
```python
import functools

import jax
import jax.numpy as jnp
from jax import lax
from jax.experimental import pallas as pl
from jax.experimental.pallas import tpu as pltpu
from jax.sharding import PartitionSpec as P

HALO = 512
POWER = 2
RIM = 64
LANES = 128
RADIX = 256
EDGE = HALO // RADIX
SHRINK = 2.0**-40
VMEM_BYTES = 16 * 1024 * 1024

F32 = jnp.float32
BF16 = jnp.bfloat16


def dot(a, b):
    return lax.dot_general(a, b, (((1,), (0,)), ((), ())), preferred_element_type=F32)


def dot_nt(a, b):
    return lax.dot_general(a, b, (((1,), (1,)), ((), ())), preferred_element_type=F32)


def split(x):
    hi = x.astype(BF16)
    return hi, (x - hi.astype(F32)).astype(BF16)


def rows_iota(shape):
    return lax.broadcasted_iota(jnp.int32, shape, 0)


def lanes_iota(shape):
    return lax.broadcasted_iota(jnp.int32, shape, 1)


def spread_matrix(node_slots, padded_order):
    shape = (2 * node_slots, 2 * padded_order)
    row = rows_iota(shape)
    start = (row // node_slots) * padded_order + 3 * (row % node_slots)
    gap = lanes_iota(shape) - start
    return jnp.where((gap >= 0) & (gap < 3), F32(1), F32(0)).astype(BF16)


def order_matrix(node_slots, padded_order):
    pair = 2 * node_slots
    shape = (2 * padded_order, 3 * pair)
    col = lanes_iota(shape)
    inner = col % pair
    source = (inner // node_slots) * padded_order + 3 * (inner % node_slots) + col // pair
    return jnp.where(rows_iota(shape) == source, F32(1), F32(0)).astype(BF16)


def colour_of(ids):
    return (ids % 2) == (rows_iota(ids.shape) % 2)


def by_side(tile, a, b):
    even = tile % 2 == 0
    return jnp.where(even, a, b), jnp.where(even, b, a)


def to_swaps(tile, for_next, for_previous):
    even = tile % 2 == 0
    return jnp.where(even, for_next, for_previous), jnp.where(even, for_previous, for_next)


def setup_kernel(
    conn_in,
    cell_in,
    friction_ref,
    conn_ref,
    cell_ref,
    fr_ref,
    node_hot_ref,
    cell_hot_ref,
    spread_ref,
    order_ref,
):
    pairs = conn_ref.shape[0]
    slots, padded_order = fr_ref.shape
    node_slots = conn_in.shape[1]
    window = 3 * LANES

    def paired(ref):
        return jnp.concatenate(
            [ref[pl.ds(0, pairs, stride=2), :], ref[pl.ds(1, pairs, stride=2), :]], axis=1
        )

    conn = paired(conn_in)
    cells = paired(cell_in)
    cells = jnp.where(cells < RIM, cells + (window - RIM), cells - RIM)
    conn_ref[...] = conn
    cell_ref[...] = cells
    rows = rows_iota((RADIX, LANES))
    for m in range(pairs):
        at = pl.ds(m * LANES, LANES)
        hot = rows == conn[m : m + 1, :] % RADIX
        node_hot_ref[:, at] = jnp.where(hot, F32(1), F32(0)).astype(BF16)
        hot = rows[:LANES] == cells[m : m + 1, :] % LANES
        cell_hot_ref[:, at] = jnp.where(hot, F32(1), F32(0)).astype(BF16)
    spread_ref[...] = spread_matrix(node_slots, padded_order)
    order_ref[...] = order_matrix(node_slots, padded_order)

    shape = (node_slots, padded_order)
    total = jnp.zeros((slots, padded_order), F32)
    for c in range(3):
        place = lanes_iota(shape) == 3 * rows_iota(shape) + c
        place = jnp.where(place, F32(1), F32(0)).astype(BF16)
        rest = friction_ref[c]
        for _ in range(3):
            part = rest.astype(BF16)
            total = total + dot(part, place)
            rest = rest - part.astype(F32)
    fr_ref[...] = total


def edge_levels(levels):
    return list(range(EDGE)) + list(range(levels - EDGE, levels))


def forward_kernel(step, tiles, levels, *refs):
    scalars, block_ref, block_a, block_b, *refs = refs
    first = step == 0
    if not first:
        basal_ref, rim_a, rim_b, *refs = refs
    conn_ref, cell_ref, fr_ref, blocks, node_hot, cell_hot, spread_ref, order_ref, *refs = refs
    ordered_ref, a_ref, b_ref, *refs = refs
    if not first:
        squares_ref, *refs = refs
    if step == 1:
        field_ref, *refs = refs
    f_ref, v_ref = refs

    order = blocks.shape[1]
    padded_order = f_ref.shape[1] // 2
    pairs = blocks.shape[0] // 2
    tile = scalars[0]
    count = scalars[1]

    lane = lanes_iota((8, LANES))
    low = lane < RIM
    after, before = by_side(tile, block_a[:8, :], block_b[:8, :])
    starts = [
        block_ref[:8, :LANES],
        block_ref[:8, LANES:],
        jnp.where(low, after[:, :LANES], before[:, LANES:]),
    ]
    if first:
        parts = starts
    else:
        after, before = by_side(tile, rim_a[...], rim_b[...])
        parts = [basal_ref[:, i * LANES : (i + 1) * LANES] for i in range(3)]
        parts[0] = parts[0] + jnp.where(low, before, F32(0))
        parts[1] = parts[1] + jnp.where(low, F32(0), after)
        parts[2] = parts[2] + jnp.where(low, after, before)
        there = (low & (tile < tiles - 1)) | (~low & (tile > 0))
        parts[2] = jnp.where(there, parts[2], F32(0))
        kept = [(start != 0) if step % 2 == 0 else (start == 0) for start in starts]
        parts = [jnp.where(keep, part, F32(0)) for keep, part in zip(kept, parts)]
        if step == 1:
            field_ref[:, :LANES] = parts[0]
            field_ref[:, LANES:] = parts[1]
        squares_ref[...] = parts[0] * parts[0] + parts[1] * parts[1]
    window = jnp.concatenate(parts, axis=0)
    if step == 1:
        window = window * F32(SHRINK)

    cells = cell_ref[...]
    hi, lo = split(window)
    picked = dot(jnp.concatenate([hi, lo], axis=0), cell_hot[...])
    tops = []
    rests = []
    for m in range(pairs):
        part = picked[:, m * LANES : (m + 1) * LANES]
        which = cells[m : m + 1, :] // LANES
        for base, out in ((0, tops), (24, rests)):
            chosen = jnp.where(which == 0, part[base : base + 8], F32(0))
            for level in (1, 2):
                at = base + 8 * level
                chosen = jnp.where(which == level, part[at : at + 8], chosen)
            out.append(chosen)
    stacked = jnp.concatenate(tops + rests, axis=0).astype(BF16)
    spread = dot(stacked, spread_ref[...])
    half = 8 * pairs
    spread = spread[:half] + spread[half:]

    f_ref[...] = jnp.zeros_like(f_ref)
    for m in range(pairs):
        for side in range(2):
            at = side * padded_order
            slot = 2 * m + side
            inputs = spread[8 * m : 8 * m + 8, at : at + order] * fr_ref[slot : slot + 1, :order]
            if first:
                out = dot_nt(inputs.astype(BF16), blocks[slot])
            else:
                hi = inputs.astype(BF16).astype(F32)
                both = jnp.concatenate([hi, inputs - hi], axis=0).astype(BF16)
                out = dot_nt(both, blocks[slot])
                out = out[:8] + out[8:]
            out = jnp.where(slot < count, out, F32(0))
            hi = out.astype(BF16).astype(F32)
            f_ref[16 * m : 16 * m + 8, at : at + order] = hi
            f_ref[16 * m + 8 : 16 * m + 16, at : at + order] = out - hi

    ordered = dot(f_ref[...].astype(BF16), order_ref[...])
    ordered_ref[...] = ordered
    conn = conn_ref[...]
    edges = edge_levels(levels)
    for m in range(pairs):
        which = conn[m : m + 1, :] // RADIX
        rows = [
            jnp.where(
                which == level,
                ordered[16 * m : 16 * m + 16, c * LANES : (c + 1) * LANES],
                F32(0),
            )
            for level in edges
            for c in range(3)
        ]
        v_ref[:, m * LANES : (m + 1) * LANES] = jnp.concatenate(rows, axis=0).astype(BF16)
    rim = dot_nt(v_ref[...], node_hot[...])
    sums = [
        rim[16 * i : 16 * i + 8] + rim[16 * i + 8 : 16 * i + 16] for i in range(3 * len(edges))
    ]
    half = len(sums) // 2
    for i in range(half):
        lead, spill = sums[i], sums[half + i]
        a_ref[8 * i : 8 * i + 8, :], b_ref[8 * i : 8 * i + 8, :] = to_swaps(tile, spill, lead)


def inner_kernel(levels, ordered_ref, weight_ref, conn_ref, node_hot, picked_ref, v_ref):
    pairs = conn_ref.shape[0]
    conn = conn_ref[...]
    inside = list(range(EDGE, levels - EDGE))
    for m in range(pairs):
        which = conn[m : m + 1, :] // RADIX
        rows = [
            jnp.where(
                which == level,
                ordered_ref[16 * m : 16 * m + 16, c * LANES : (c + 1) * LANES],
                F32(0),
            )
            for level in inside
            for c in range(3)
        ]
        v_ref[:, m * LANES : (m + 1) * LANES] = jnp.concatenate(rows, axis=0).astype(BF16)
    nodes = dot_nt(v_ref[...], node_hot[...])
    rows = []
    for i in range(3 * len(inside)):
        value = nodes[16 * i : 16 * i + 8] + nodes[16 * i + 8 : 16 * i + 16]
        at = inside[i // 3] * RADIX
        rows.append(value * weight_ref[i % 3 : i % 3 + 1, at : at + RADIX])
    weighted = jnp.concatenate(rows, axis=0).astype(BF16)
    step = 2
    for start in range(0, pairs, step):
        found = dot(weighted, node_hot[:, start * LANES : (start + step) * LANES])
        for i in range(step):
            m = start + i
            which = conn[m : m + 1, :] // RADIX
            part = found[:, i * LANES : (i + 1) * LANES]
            chosen = jnp.zeros((24, LANES), F32)
            for at, level in enumerate(inside):
                chosen = jnp.where(which == level, part[24 * at : 24 * at + 24], chosen)
            for c in range(3):
                picked_ref[8 * m : 8 * m + 8, c * LANES : (c + 1) * LANES] = chosen[8 * c : 8 * c + 8]


def adjoint_kernel(last, levels, *refs):
    scalars, block_a, block_b, own_a, own_b, new_a, new_b, inner_ref, weight_ref, *refs = refs
    conn_ref, cell_ref, fr_ref, blocks, node_hot, cell_hot, spread_ref, order_ref, *refs = refs
    if last:
        squares_1, squares_2, ids_ref, *refs = refs
        basal_ref, out_ref, p_ref, n_ref, v_ref = refs
    else:
        basal_ref, a_ref, b_ref, p_ref, n_ref, v_ref = refs

    order = blocks.shape[1]
    padded_order = p_ref.shape[1] // 2
    pairs = blocks.shape[0] // 2
    tile = scalars[0]
    count = scalars[1]

    spill, lead = by_side(tile, own_a[...] + new_a[...], own_b[...] + new_b[...])
    after, _ = by_side(tile, block_a[8:16, :], block_b[8:16, :])
    rows = []
    for i in range(3 * EDGE):
        at = (i // 3) * RADIX
        rows.append(lead[8 * i : 8 * i + 8] * weight_ref[i % 3 : i % 3 + 1, at : at + RADIX])
    for i in range(3 * EDGE):
        rows.append(spill[8 * i : 8 * i + 8] * after[i : i + 1, :])
    weighted = jnp.concatenate(rows, axis=0).astype(BF16)

    conn = conn_ref[...]
    edges = edge_levels(levels)
    step = 2
    for start in range(0, pairs, step):
        found = dot(weighted, node_hot[:, start * LANES : (start + step) * LANES])
        for i in range(step):
            m = start + i
            which = conn[m : m + 1, :] // RADIX
            part = found[:, i * LANES : (i + 1) * LANES]
            for c in range(3):
                value = inner_ref[8 * m : 8 * m + 8, c * LANES : (c + 1) * LANES]
                for at, level in enumerate(edges):
                    row = 24 * at + 8 * c
                    value = jnp.where(which == level, part[row : row + 8], value)
                n_ref[8 * m : 8 * m + 8, c * LANES : (c + 1) * LANES] = value
    natural = dot_nt(n_ref[...].astype(BF16), order_ref[...])
    p_ref[...] = jnp.zeros_like(p_ref)
    for m in range(pairs):
        for side in range(2):
            at = side * padded_order
            slot = 2 * m + side
            out = dot(natural[8 * m : 8 * m + 8, at : at + order].astype(BF16), blocks[slot])
            out = out * fr_ref[slot : slot + 1, :order]
            p_ref[8 * m : 8 * m + 8, at : at + order] = jnp.where(slot < count, out, F32(0))

    hi, lo = split(p_ref[...])
    partial = dot_nt(jnp.concatenate([hi, lo], axis=0), spread_ref[...])
    half = 8 * pairs
    partial = partial[:half] + partial[half:]
    cells = cell_ref[...]
    for m in range(pairs):
        which = cells[m : m + 1, :] // LANES
        value = partial[8 * m : 8 * m + 8, :]
        rows = jnp.concatenate([jnp.where(which == level, value, F32(0)) for level in range(3)], axis=0)
        hi = rows.astype(BF16).astype(F32)
        both = jnp.concatenate([hi, rows - hi], axis=0)
        v_ref[:, m * LANES : (m + 1) * LANES] = both.astype(BF16)
    basal = dot_nt(v_ref[...], cell_hot[...])
    basal = basal[:24] + basal[24:]
    parts = [basal[8 * i : 8 * i + 8] for i in range(3)]
    for i in range(3):
        basal_ref[:, i * LANES : (i + 1) * LANES] = parts[i]
    lane = lanes_iota((8, LANES))
    if not last:
        for_next = jnp.where(lane < RIM, parts[2], parts[1])
        for_previous = jnp.where(lane < RIM, parts[0], parts[2])
        a_ref[...], b_ref[...] = to_swaps(tile, for_next, for_previous)
        return

    ids = ids_ref[...].astype(F32)
    row = rows_iota((8, LANES))
    ids = jnp.where(row == 0, ids[:, :LANES], jnp.where(row == 1, ids[:, LANES:], F32(0)))
    extra = jnp.zeros((8, LANES), F32)
    for i, ref in enumerate((squares_1, squares_2)):
        rest = jnp.sum(ref[...], axis=1, keepdims=True)
        for j in range(3):
            piece = rest.astype(BF16).astype(F32)
            extra = jnp.where(lane == 3 * i + j, piece, extra)
            rest = rest - piece
    message = jnp.concatenate(parts + [ids, extra], axis=1).astype(BF16)
    for t in range(out_ref.shape[0]):
        out_ref[t] = message


def gram_kernel(keep_same, tiles, groups, scalars, g_ref, own_ref, field_ref, gram_ref):
    tile = scalars[0]
    group = scalars[2]
    clusters = gram_ref.shape[0]
    cell_count = tiles * 2 * LANES
    low = lanes_iota((8, LANES)) < RIM

    def factor_of(p):
        def add(t, acc):
            return acc + g_ref[t, p][:, 4 * LANES :].astype(F32)

        sums = lax.fori_loop(0, tiles, add, jnp.zeros((8, LANES), F32), unroll=tiles <= 8)
        first = jnp.sum(sums[:, :3], axis=1, keepdims=True)
        second = jnp.sum(sums[:, 3:6], axis=1, keepdims=True)
        scale = jnp.sqrt(first / cell_count + F32(1e-06))
        size = jnp.sqrt(second / cell_count) * F32(1 / SHRINK) / scale
        return F32(1 / SHRINK) / (scale * jnp.sqrt(size * size + F32(1e-06)))

    def ids_of(t):
        rows = g_ref[t, 0][:, 3 * LANES : 4 * LANES].astype(F32).astype(jnp.int32)
        return [jnp.broadcast_to(rows[i : i + 1, :], (8, LANES)) for i in range(2)]

    def field(t, p, ids, own=None):
        before = g_ref[jnp.maximum(t - 1, 0), p][:, 2 * LANES : 3 * LANES].astype(F32)
        after = g_ref[jnp.minimum(t + 1, tiles - 1), p][:, 2 * LANES : 3 * LANES].astype(F32)
        if own is None:
            own = g_ref[t, p][:, : 2 * LANES].astype(F32)
        parts = [
            own[:, :LANES] + jnp.where(low & (t > 0), before, F32(0)),
            own[:, LANES : 2 * LANES] + jnp.where(~low & (t < tiles - 1), after, F32(0)),
        ]
        return [
            jnp.where(colour_of(i) if keep_same else ~colour_of(i), part, F32(0))
            for i, part in zip(ids, parts)
        ]

    factors = [factor_of(p) for p in range(groups)]
    mine_factor = factors[0]
    for p in range(1, groups):
        mine_factor = jnp.where(group == p, factors[p], mine_factor)
    own = field(tile, group, ids_of(tile), own_ref[...])
    field_ref[:, :LANES] = own[0] * mine_factor
    field_ref[:, LANES:] = own[1] * mine_factor

    def add_tile(t, acc):
        ids = ids_of(t)
        every = [
            jnp.concatenate(field(t, p, ids), axis=1) * factors[p] for p in range(groups)
        ]
        mine = every[0]
        for p in range(1, groups):
            mine = jnp.where(group == p, every[p], mine)
        ids = jnp.concatenate(ids, axis=1)
        left = jnp.concatenate([jnp.where(ids == k, mine, F32(0)) for k in range(clusters)], axis=0)
        return acc + lax.dot_general(
            left,
            jnp.concatenate(every, axis=0),
            (((1,), (1,)), ((), ())),
            precision=lax.Precision.HIGHEST,
            preferred_element_type=F32,
        )

    acc = jnp.zeros((8 * clusters, 8 * groups), F32)
    acc = lax.fori_loop(0, tiles, add_tile, acc, unroll=tiles <= 8)
    gram_ref[...] = acc.reshape(gram_ref.shape)


def shards(
    blocks, connectivity, basal_map, friction, elem_counts, obs_weight, sign_bits, cluster_ids
):
    slots = blocks.shape[0]
    node_slots = connectivity.shape[1]
    node_count = obs_weight.shape[0]
    cell_count, group_size = sign_bits.shape
    tiles = lax.axis_size("tiles")
    groups = lax.axis_size("probes")
    pairs = slots * node_slots // LANES
    refs = pairs * LANES
    levels = (node_count + HALO) // RADIX
    padded_order = 2 * LANES
    window = cell_count + 2 * RIM

    smem = pl.BlockSpec(memory_space=pltpu.SMEM)
    vmem = pl.BlockSpec(memory_space=pltpu.VMEM)
    params = pltpu.CompilerParams(vmem_limit_bytes=VMEM_BYTES)
    shaped = jax.ShapeDtypeStruct

    def call(kernel, name, out_shape, operands, scratch=(), scalar=True):
        return pl.pallas_call(
            kernel,
            out_shape=out_shape,
            in_specs=[smem] * scalar + [vmem] * (len(operands) - scalar),
            out_specs=jax.tree.map(lambda _: vmem, out_shape),
            scratch_shapes=list(scratch),
            compiler_params=params,
            name=name,
        )(*operands)

    evens = range(0, tiles - 1, 2)
    odds = range(1, tiles - 1, 2)
    pairs_a = [(i, i + 1) for i in evens] + [(i + 1, i) for i in evens]
    pairs_b = [(i, i + 1) for i in odds] + [(i + 1, i) for i in odds]

    def swapped(a, b):
        return lax.ppermute(a, "tiles", pairs_a), lax.ppermute(b, "tiles", pairs_b)

    weight = obs_weight.T
    parity = jnp.arange(group_size, dtype=jnp.int32) % 2
    same = (cluster_ids % 2)[None, :] == parity[:, None]
    probes = jnp.where(same, (2 * sign_bits.T - 1).astype(F32), F32(0))
    lead = [weight[:, i * RADIX : (i + 1) * RADIX] for i in range(EDGE)]
    spare = jnp.zeros((8 - 3 * EDGE, RADIX), F32)
    block = jnp.concatenate([probes, *lead, spare], axis=0)
    block_a, block_b = swapped(block, block)

    conn, cells, fr, node_hot, cell_hot, spread, order_map = call(
        setup_kernel,
        "setup",
        [
            shaped((pairs, LANES), jnp.int32),
            shaped((pairs, LANES), jnp.int32),
            shaped((slots, padded_order), F32),
            shaped((RADIX, refs), BF16),
            shaped((LANES, refs), BF16),
            shaped((LANES, 2 * padded_order), BF16),
            shaped((2 * padded_order, 3 * LANES), BF16),
        ],
        [connectivity, basal_map, friction.transpose(2, 0, 1)],
        scalar=False,
    )
    scalars = jnp.stack(
        [lax.axis_index("tiles"), elem_counts[0], lax.axis_index("probes")]
    ).astype(jnp.int32)
    shared = [conn, cells, fr, blocks, node_hot, cell_hot, spread, order_map]

    edge = shaped((24 * EDGE, RADIX), F32)
    rim = shaped((group_size, LANES), F32)
    whole = shaped((group_size, window), F32)
    field = shaped((group_size, cell_count), F32)
    everyone = ("tiles", "probes")

    carried = []
    squares = []
    samples = None
    for step in range(POWER + 1):
        last = step == POWER
        out_shape = [shaped((16 * pairs, 3 * LANES), F32), edge, edge]
        out_shape += [rim] * (step > 0) + [field] * (step == 1)
        ordered, own_a, own_b, *extra = call(
            functools.partial(forward_kernel, step, tiles, levels),
            "forward",
            out_shape,
            [scalars, block, block_a, block_b] + carried + shared,
            [
                pltpu.VMEM((16 * pairs, 2 * padded_order), F32),
                pltpu.VMEM((96 * EDGE, refs), BF16),
            ],
        )
        squares += extra[:1]
        if step == 1:
            samples = extra[1].T
        new_a, new_b = swapped(own_a, own_b)
        inner = call(
            functools.partial(inner_kernel, levels),
            "inner",
            shaped((8 * pairs, 3 * LANES), F32),
            [ordered, weight, conn, node_hot],
            [pltpu.VMEM((48 * (levels - 2 * EDGE), refs), BF16)],
            scalar=False,
        )
        operands = [scalars, block_a, block_b, own_a, own_b, new_a, new_b, inner, weight] + shared
        if last:
            operands += squares + [cluster_ids.reshape(1, cell_count)]
            message = shaped((lax.axis_size(everyone), group_size, window + 2 * LANES), BF16)
            out_shape = [whole, message]
        else:
            out_shape = [whole, rim, rim]
        basal, *messages = call(
            functools.partial(adjoint_kernel, last, levels),
            "adjoint",
            out_shape,
            operands,
            [
                pltpu.VMEM((8 * pairs, 2 * padded_order), F32),
                pltpu.VMEM((8 * pairs, 3 * LANES), F32),
                pltpu.VMEM((48, refs), BF16),
            ],
        )
        if not last:
            carried = [basal, *swapped(*messages)]

    gathered = lax.all_to_all(messages[0], everyone, 0, 0)
    gathered = gathered.reshape(tiles, groups, *gathered.shape[1:])
    refined, gram = call(
        functools.partial(gram_kernel, POWER % 2 == 1, tiles, groups),
        "gram",
        [field, shaped((tiles, group_size, groups * group_size), F32)],
        [scalars, gathered, basal],
    )
    return (samples, refined.T, gram)


def solution(mesh):
    in_specs = (
        P("tiles", None, None),
        P("tiles", None),
        P("tiles", None),
        P("tiles", None, None),
        P("tiles"),
        P("tiles", None),
        P("tiles", "probes"),
        P("tiles"),
    )
    out_specs = (P("tiles", "probes"), P("tiles", "probes"), P(None, "probes", None))
    return jax.shard_map(shards, mesh=mesh, in_specs=in_specs, out_specs=out_specs, check_vma=False)
```

time: 107 us -> 99.6 us (0.931)
  blocking collectives: 42.9 us -> 19.2 us
  starting transfers between devices: 12.2 us -> 30 us
  local copies, waits for them, and re-layouts: 11.5 us -> 6.03 us
  Pallas kernels: 37 us -> 38.9 us
  other arithmetic: 0.08 us -> 1.61 us
    ppermute x6 -> x12, starting transfers between devices: 4.95 us -> 30 us  [the longest x6 25.7 us: swapped(): lax.ppermute(a, 'tiles', pairs_a)]
    all_to_all x3 -> x1, blocking collectives: 42.9 us -> 19.2 us  [shards(): gathered = lax.all_to_all(messages[0], everyone, 0, 0)]
    all_to_all x1 -> x0, starting transfers between devices: 7.28 us -> none  [shards(): meta = lax.all_to_all(meta, 'tiles', 0, 0)]
    unnamed x24 -> x14, local copies, waits for them, and re-layouts: 11.5 us -> 5.2 us
    pallas_call x12 -> x11, Pallas kernels: 37 us -> 38.9 us  [call(): pl.pallas_call(kernel, out_shape=out_shape, in_specs=[smem] * scalar + [v...]
    select_n x0 -> x3, other arithmetic: none -> 1.46 us  [the longest x1 0.77 us: shards(): probes = jnp.where(same, (2 * sign_bits.T - 1).astype(F32), F32(0))]
  transfers between devices with their start and end apart: 7 -> 12, of which waited for: 2 -> 2; matrix products, arithmetic and copies ran while one was open for 0% -> 0% of each run, Pallas kernels for 10% -> 14%
where the time goes in v5:
time: 99.6 us; the launch traced here: 99 us
  Pallas kernels  38.9 us (39%)
  starting transfers between devices  30 us (30%)
  blocking collectives  19.2 us (19%)
  local copies, waits for them, and re-layouts  6.03 us (6%)
  waiting for transfers between devices  1.7 us (2%)
  other arithmetic  1.61 us (2%)
  between operations  1.5 us (2%)
    pallas_call x11, Pallas kernels, call(): pl.pallas_call(kernel, out_shape=out_shape, in_specs=[smem] * scalar + [v...  38.9 us
    ppermute x6, starting transfers between devices, swapped(): lax.ppermute(a, 'tiles', pairs_a)  25.7 us
    all_to_all x1, blocking collectives, shards(): gathered = lax.all_to_all(messages[0], everyone, 0, 0)  19.2 us
    unnamed x14, local copies, waits for them, and re-layouts  5.2 us
    ppermute x6, starting transfers between devices, swapped(): lax.ppermute(b, 'tiles', pairs_b)  4.3 us
  transfers between devices with their start and end apart: 12, of which 2 were waited for; matrix products, arithmetic and copies ran while one was open for 0% of the time, Pallas kernels for 14%

profile of v5, /device:TPU:0, one launch (start us, length us, event | category | flops | bytes accessed | tf_op | source)
XLA Modules:
  0.0 99.0 jit_solution(2712393866804254232)
XLA Ops:
  0.6 0.0 copy-start.2
  0.7 0.7 fusion.1
  1.4 0.7 and_select_fusion.1
  2.1 0.1 pad.3.clone
  2.2 0.8 bitcast_select_fusion
  2.9 0.1 maximum_maximum_fusion.refs_1_
  3.0 3.0 %collective-permute-start = (f32[16,256]{1,0:T(8,128)S(1)}, f32[16,256]{1,0:T(8,128)S(1)}, u32[]{:S(2)}, u32[]{:S(2)}) collective-permute-start(f32[16,256]{1,0:T(8,128)S(1)} %maximum_maximum_fusion.refs_1_), channel_id=1, source_target_pairs={{0,4},{8,12},{16,20},{24,28},{4,0},{12,8},{20,16},{28,24},{1,5},{9... | collective-permute-start | bytes 49160 | tf_op jit(solution)/shard_map/ppermute | solution.py:469
  6.0 0.7 collective-permute-start.1
  7.3 0.1 pad_add_fusion.refs_0_.scalars
  7.4 0.9 copy-done.3
  8.3 0.8 copy-done.4
  9.0 0.8 copy-done.5
  9.8 1.7 %setup.1 = (s32[32,128]{1,0:T(8,128)S(1)}, s32[32,128]{1,0:T(8,128)S(1)}, f32[64,256]{1,0:T(8,128)S(1)}, bf16[256,4096]{1,0:T(8,128)(2,1)S(1)}, bf16[128,4096]{1...) custom-call(s32[64,64]{1,0:T(8,128)S(1)} %copy-done.4, s32[64,64]{1,0:T(8,128)S(1)} %copy-done.5, ...), custom_call_target="tpu_custom_call" | custom-call | tf_op jit(solution)/shard_map/setup/pallas_call | solution.py:453
  11.5 0.0 collective-permute-done.refs_2_.refs_1_
  11.5 0.0 collective-permute-done.1.refs_3_.refs_2_
  11.5 0.0 copy-start
  11.5 2.8 %copy-done = bf16[64,192,192]{2,1,0:T(8,128)(2,1)S(1)} copy-done((bf16[64,192,192]{2,1,0:T(8,128)(2,1)S(1)}, bf16[64,192,192]{2,1,0:T(8,128)(2,1)}, u32[]{:S(2)}) %copy-start) | copy-done | bytes 4718616
  14.3 4.5 %forward.3 = (f32[512,384]{1,0:T(8,128)S(1)}, f32[48,256]{1,0:T(8,128)S(1)}, f32[48,256]{1,0:T(8,128)S(1)}) custom-call(s32[3]{0:T(128)S(1)} %pad_add_fusion.refs_0_.scalars, f32[16,256]{1,0:T(8,128)S(1)} %maximum_maximum_fusion.refs_1_, f32[16,256]{1,0:T(8,128)S(1)} %collective-permute-done.refs_2_.refs_1_, ...), custom_call_target="tpu_custom_call" | custom-call | tf_op jit(solution)/shard_map/forward/pallas_call | solution.py:453
  18.8 4.3 %collective-permute-start.2 = (f32[48,256]{1,0:T(8,128)S(1)}, f32[48,256]{1,0:T(8,128)S(1)}, u32[]{:S(2)}, u32[]{:S(2)}) collective-permute-start(f32[48,256]{1,0:T(8,128)S(1)} %get-tuple-element.39.refs_3_), channel_id=1, source_target_pairs={{0,4},{8,12},{16,20},{24,28},{4,0},{12,8},{20,16},{28,24},{1,5},{9... | collective-permute-start | bytes 147464 | tf_op jit(solution)/shard_map/ppermute | solution.py:469
  23.1 0.7 collective-permute-start.3
  23.8 4.1 %inner.3.refs_7_ = f32[256,384]{1,0:T(8,128)S(1)} custom-call(f32[512,384]{1,0:T(8,128)S(1)} %get-tuple-element.41.ordered_ref, f32[3,4096]{1,0:T(4,128)S(1)} %bitcast.11, s32[32,128]{1,0:T(8,128)S(1)} %get-tuple-element.32.refs_4_.conn_ref.refs_9_.refs_7_, bf16[256,4096]{1,0:T(8,128)(2,1)S(1)} %get-tuple-element.35.refs_8_.node_hot.refs_13_.refs_11_), custom_call_target="tpu_custom_call" | custom-call | tf_op jit(solution)/shard_map/inner/pallas_call | solution.py:453
  27.9 0.0 collective-permute-done.2.refs_5_
  27.9 0.0 collective-permute-done.3.refs_6_
  27.9 3.1 %adjoint.3 = (f32[8,384]{1,0:T(8,128)S(1)}, f32[8,128]{1,0:T(8,128)S(1)}, f32[8,128]{1,0:T(8,128)S(1)}) custom-call(s32[3]{0:T(128)S(1)} %pad_add_fusion.refs_0_.scalars, f32[16,256]{1,0:T(8,128)S(1)} %collective-permute-done.refs_2_.refs_1_, f32[16,256]{1,0:T(8,128)S(1)} %collective-permute-done.1.refs_3_.refs_2_, f32[48,256]{1,0:T(8,128)S(1)} %get-tuple-element.39.refs_3_, ...), custom_call_target="tpu_custom_call" | custom-call | tf_op jit(solution)/shard_map/adjoint/pallas_call | solution.py:453
  31.0 4.4 %collective-permute-start.4 = (f32[8,128]{1,0:T(8,128)S(1)}, f32[8,128]{1,0:T(8,128)S(1)}, u32[]{:S(2)}, u32[]{:S(2)}) collective-permute-start(f32[8,128]{1,0:T(8,128)S(1)} %get-tuple-element.43), channel_id=1, source_target_pairs={{0,4},{8,12},{16,20},{24,28},{4,0},{12,8},{20,16},{28,24},{1,5},{9... | collective-permute-start | bytes 12296 | tf_op jit(solution)/shard_map/ppermute | solution.py:469
  35.4 0.8 collective-permute-start.5
  36.2 0.7 collective-permute-done.4.refs_5_
  36.9 0.0 collective-permute-done.5.refs_6_
  36.9 4.8 %forward.4 = (f32[512,384]{1,0:T(8,128)S(1)}, f32[48,256]{1,0:T(8,128)S(1)}, f32[48,256]{1,0:T(8,128)S(1)}, f32[8,128]{1,0:T(8,128)S(1)}, f32[8,256]{1,0:T(8,128)}) custom-call(s32[3]{0:T(128)S(1)} %pad_add_fusion.refs_0_.scalars, f32[16,256]{1,0:T(8,128)S(1)} %maximum_maximum_fusion.refs_1_, f32[16,256]{1,0:T(8,128)S(1)} %collective-permute-done.refs_2_.refs_1_, ...), custom_call_target="tpu_custom_call" | custom-call | tf_op jit(solution)/shard_map/forward/pallas_call | solution.py:453
  41.8 4.9 %collective-permute-start.6 = (f32[48,256]{1,0:T(8,128)S(1)}, f32[48,256]{1,0:T(8,128)S(1)}, u32[]{:S(2)}, u32[]{:S(2)}) collective-permute-start(f32[48,256]{1,0:T(8,128)S(1)} %get-tuple-element.46.refs_3_), channel_id=1, source_target_pairs={{0,4},{8,12},{16,20},{24,28},{4,0},{12,8},{20,16},{28,24},{1,5},{9... | collective-permute-start | bytes 147464 | tf_op jit(solution)/shard_map/ppermute | solution.py:469
  46.7 0.7 collective-permute-start.7
  47.4 4.1 %inner.4.refs_7_ = f32[256,384]{1,0:T(8,128)S(1)} custom-call(f32[512,384]{1,0:T(8,128)S(1)} %get-tuple-element.48.ordered_ref, f32[3,4096]{1,0:T(4,128)S(1)} %bitcast.13, s32[32,128]{1,0:T(8,128)S(1)} %get-tuple-element.32.refs_4_.conn_ref.refs_9_.refs_7_, bf16[256,4096]{1,0:T(8,128)(2,1)S(1)} %get-tuple-element.35.refs_8_.node_hot.refs_13_.refs_11_), custom_call_target="tpu_custom_call" | custom-call | tf_op jit(solution)/shard_map/inner/pallas_call | solution.py:453
  51.4 0.0 collective-permute-done.6.refs_5_
  51.4 0.0 collective-permute-done.7.refs_6_
  51.5 3.1 %adjoint.4 = (f32[8,384]{1,0:T(8,128)S(1)}, f32[8,128]{1,0:T(8,128)S(1)}, f32[8,128]{1,0:T(8,128)S(1)}) custom-call(s32[3]{0:T(128)S(1)} %pad_add_fusion.refs_0_.scalars, f32[16,256]{1,0:T(8,128)S(1)} %collective-permute-done.refs_2_.refs_1_, f32[16,256]{1,0:T(8,128)S(1)} %collective-permute-done.1.refs_3_.refs_2_, f32[48,256]{1,0:T(8,128)S(1)} %get-tuple-element.46.refs_3_, ...), custom_call_target="tpu_custom_call" | custom-call | tf_op jit(solution)/shard_map/adjoint/pallas_call | solution.py:453
  54.6 4.3 %collective-permute-start.8 = (f32[8,128]{1,0:T(8,128)S(1)}, f32[8,128]{1,0:T(8,128)S(1)}, u32[]{:S(2)}, u32[]{:S(2)}) collective-permute-start(f32[8,128]{1,0:T(8,128)S(1)} %get-tuple-element.50), channel_id=1, source_target_pairs={{0,4},{8,12},{16,20},{24,28},{4,0},{12,8},{20,16},{28,24},{1,5},{9... | collective-permute-start | bytes 12296 | tf_op jit(solution)/shard_map/ppermute | solution.py:469
  58.8 0.6 collective-permute-start.9
  59.5 0.9 collective-permute-done.8.refs_5_
  60.4 0.0 collective-permute-done.9.refs_6_
  60.4 4.5 %forward.5 = (f32[512,384]{1,0:T(8,128)S(1)}, f32[48,256]{1,0:T(8,128)S(1)}, f32[48,256]{1,0:T(8,128)S(1)}, f32[8,128]{1,0:T(8,128)S(1)}) custom-call(s32[3]{0:T(128)S(1)} %pad_add_fusion.refs_0_.scalars, f32[16,256]{1,0:T(8,128)S(1)} %maximum_maximum_fusion.refs_1_, f32[16,256]{1,0:T(8,128)S(1)} %collective-permute-done.refs_2_.refs_1_, ...), custom_call_target="tpu_custom_call" | custom-call | tf_op jit(solution)/shard_map/forward/pallas_call | solution.py:453
  64.9 4.9 %collective-permute-start.10 = (f32[48,256]{1,0:T(8,128)S(1)}, f32[48,256]{1,0:T(8,128)S(1)}, u32[]{:S(2)}, u32[]{:S(2)}) collective-permute-start(f32[48,256]{1,0:T(8,128)S(1)} %get-tuple-element.52.refs_3_), channel_id=1, source_target_pairs={{0,4},{8,12},{16,20},{24,28},{4,0},{12,8},{20,16},{28,24},{1,5},{9... | collective-permute-start | bytes 147464 | tf_op jit(solution)/shard_map/ppermute | solution.py:469
  69.8 0.9 collective-permute-start.11
  70.6 4.1 %inner.5.refs_7_ = f32[256,384]{1,0:T(8,128)S(1)} custom-call(f32[512,384]{1,0:T(8,128)S(1)} %get-tuple-element.54.ordered_ref, f32[3,4096]{1,0:T(4,128)S(1)} %bitcast.15, s32[32,128]{1,0:T(8,128)S(1)} %get-tuple-element.32.refs_4_.conn_ref.refs_9_.refs_7_, bf16[256,4096]{1,0:T(8,128)(2,1)S(1)} %get-tuple-element.35.refs_8_.node_hot.refs_13_.refs_11_), custom_call_target="tpu_custom_call" | custom-call | tf_op jit(solution)/shard_map/inner/pallas_call | solution.py:453
  74.7 0.0 collective-permute-done.10.refs_5_
  74.7 0.0 collective-permute-done.11.refs_6_
  74.7 3.1 %adjoint.5 = (f32[8,384]{1,0:T(8,128)S(1)}, bf16[32,8,640]{2,1,0:T(8,128)(2,1)S(1)}) custom-call(s32[3]{0:T(128)S(1)} %pad_add_fusion.refs_0_.scalars, f32[16,256]{1,0:T(8,128)S(1)} %collective-permute-done.refs_2_.refs_1_, f32[16,256]{1,0:T(8,128)S(1)} %collective-permute-done.1.refs_3_.refs_2_, f32[48,256]{1,0:T(8,128)S(1)} %get-tuple-element.52.refs_3_, ...), custom_call_target="tpu_custom_call" | custom-call | tf_op jit(solution)/shard_map/adjoint/pallas_call | solution.py:453
  77.9 19.2 %all_to_all.5 = bf16[32,8,640]{2,1,0:T(8,128)(2,1)S(1)} all-to-all(bf16[32,8,640]{2,1,0:T(8,128)(2,1)S(1)} %get-tuple-element.57), channel_id=1, replica_groups=mesh['tiles'=8,'probes'=4] {'tiles','probes'}, dimensions={0} | all-to-all | bytes 655360 | tf_op jit(solution)/shard_map/all_to_all | solution.py:556
  97.1 1.9 %gram.1 = (f32[8,256]{1,0:T(8,128)}, f32[8,8,32]{2,1,0:T(8,128)}) custom-call(s32[3]{0:T(128)S(1)} %pad_add_fusion.refs_0_.scalars, bf16[8,4,8,640]{3,2,1,0:T(8,128)(2,1)S(1)} %bitcast.17, f32[8,384]{1,0:T(8,128)S(1)} %get-tuple-element.58.own_ref), custom_call_target="tpu_custom_call" | custom-call | tf_op jit(solution)/shard_map/gram/pallas_call | solution.py:453
  (10 shorter events, 0.0 us)
Async XLA Ops:
  0.6 23.1 %copy-start.2 = (f32[4096,3]{0,1:T(4,128)S(1)}, f32[4096,3]{0,1:T(4,128)}, u32[]{:S(2)}) copy-start(f32[4096,3]{0,1:T(4,128)} %param.13) | copy-start | bytes 147460
  3.0 8.5 %collective-permute-start = (f32[16,256]{1,0:T(8,128)S(1)}, f32[16,256]{1,0:T(8,128)S(1)}, u32[]{:S(2)}, u32[]{:S(2)}) collective-permute-start(f32[16,256]{1,0:T(8,128)S(1)} %maximum_maximum_fusion.refs_1_), channel_id=1, source_target_pairs={{0,4},{8,12},{16,20},{24,28},{4,0},{12,8},{20,16},{28,24},{1,5},{9... | collective-permute-start | bytes 49160 | tf_op jit(solution)/shard_map/ppermute | solution.py:469
  6.0 5.5 %collective-permute-start.1 = (f32[16,256]{1,0:T(8,128)S(1)}, f32[16,256]{1,0:T(8,128)S(1)}, u32[]{:S(2)}, u32[]{:S(2)}) collective-permute-start(f32[16,256]{1,0:T(8,128)S(1)} %maximum_maximum_fusion.refs_1_), channel_id=1, source_target_pairs={{4,8},{12,16},{20,24},{8,4},{16,12},{24,20},{5,9},{13,17},{21,25},... | collective-permute-start | bytes 49160 | tf_op jit(solution)/shard_map/ppermute | solution.py:469
  7.4 0.9 copy-start.3
  8.3 0.8 copy-start.4
  9.0 0.8 copy-start.5
  11.5 2.8 %copy-start = (bf16[64,192,192]{2,1,0:T(8,128)(2,1)S(1)}, bf16[64,192,192]{2,1,0:T(8,128)(2,1)}, u32[]{:S(2)}) copy-start(bf16[64,192,192]{2,1,0:T(8,128)(2,1)} %refs_12_.5) | copy-start | bytes 14155780
  14.3 13.6 %copy-start.1 = (bf16[64,192,192]{2,1,0:T(8,128)(2,1)S(1)}, bf16[64,192,192]{2,1,0:T(8,128)(2,1)}, u32[]{:S(2)}) copy-start(bf16[64,192,192]{2,1,0:T(8,128)(2,1)} %refs_12_.5) | copy-start | bytes 14155780
  18.8 9.1 %collective-permute-start.2 = (f32[48,256]{1,0:T(8,128)S(1)}, f32[48,256]{1,0:T(8,128)S(1)}, u32[]{:S(2)}, u32[]{:S(2)}) collective-permute-start(f32[48,256]{1,0:T(8,128)S(1)} %get-tuple-element.39.refs_3_), channel_id=1, source_target_pairs={{0,4},{8,12},{16,20},{24,28},{4,0},{12,8},{20,16},{28,24},{1,5},{9... | collective-permute-start | bytes 147464 | tf_op jit(solution)/shard_map/ppermute | solution.py:469
  23.1 4.8 %collective-permute-start.3 = (f32[48,256]{1,0:T(8,128)S(1)}, f32[48,256]{1,0:T(8,128)S(1)}, u32[]{:S(2)}, u32[]{:S(2)}) collective-permute-start(f32[48,256]{1,0:T(8,128)S(1)} %get-tuple-element.40.refs_4_), channel_id=1, source_target_pairs={{4,8},{12,16},{20,24},{8,4},{16,12},{24,20},{5,9},{13,17},{21,25},... | collective-permute-start | bytes 147464 | tf_op jit(solution)/shard_map/ppermute | solution.py:469
  31.0 5.9 %collective-permute-start.4 = (f32[8,128]{1,0:T(8,128)S(1)}, f32[8,128]{1,0:T(8,128)S(1)}, u32[]{:S(2)}, u32[]{:S(2)}) collective-permute-start(f32[8,128]{1,0:T(8,128)S(1)} %get-tuple-element.43), channel_id=1, source_target_pairs={{0,4},{8,12},{16,20},{24,28},{4,0},{12,8},{20,16},{28,24},{1,5},{9... | collective-permute-start | bytes 12296 | tf_op jit(solution)/shard_map/ppermute | solution.py:469
  35.4 1.6 %collective-permute-start.5 = (f32[8,128]{1,0:T(8,128)S(1)}, f32[8,128]{1,0:T(8,128)S(1)}, u32[]{:S(2)}, u32[]{:S(2)}) collective-permute-start(f32[8,128]{1,0:T(8,128)S(1)} %get-tuple-element.44), channel_id=1, source_target_pairs={{4,8},{12,16},{20,24},{8,4},{16,12},{24,20},{5,9},{13,17},{21,25},... | collective-permute-start | bytes 12296 | tf_op jit(solution)/shard_map/ppermute | solution.py:469
  41.8 9.7 %collective-permute-start.6 = (f32[48,256]{1,0:T(8,128)S(1)}, f32[48,256]{1,0:T(8,128)S(1)}, u32[]{:S(2)}, u32[]{:S(2)}) collective-permute-start(f32[48,256]{1,0:T(8,128)S(1)} %get-tuple-element.46.refs_3_), channel_id=1, source_target_pairs={{0,4},{8,12},{16,20},{24,28},{4,0},{12,8},{20,16},{28,24},{1,5},{9... | collective-permute-start | bytes 147464 | tf_op jit(solution)/shard_map/ppermute | solution.py:469
  46.7 4.7 %collective-permute-start.7 = (f32[48,256]{1,0:T(8,128)S(1)}, f32[48,256]{1,0:T(8,128)S(1)}, u32[]{:S(2)}, u32[]{:S(2)}) collective-permute-start(f32[48,256]{1,0:T(8,128)S(1)} %get-tuple-element.47.refs_4_), channel_id=1, source_target_pairs={{4,8},{12,16},{20,24},{8,4},{16,12},{24,20},{5,9},{13,17},{21,25},... | collective-permute-start | bytes 147464 | tf_op jit(solution)/shard_map/ppermute | solution.py:469
  54.6 5.8 %collective-permute-start.8 = (f32[8,128]{1,0:T(8,128)S(1)}, f32[8,128]{1,0:T(8,128)S(1)}, u32[]{:S(2)}, u32[]{:S(2)}) collective-permute-start(f32[8,128]{1,0:T(8,128)S(1)} %get-tuple-element.50), channel_id=1, source_target_pairs={{0,4},{8,12},{16,20},{24,28},{4,0},{12,8},{20,16},{28,24},{1,5},{9... | collective-permute-start | bytes 12296 | tf_op jit(solution)/shard_map/ppermute | solution.py:469
  58.8 1.6 %collective-permute-start.9 = (f32[8,128]{1,0:T(8,128)S(1)}, f32[8,128]{1,0:T(8,128)S(1)}, u32[]{:S(2)}, u32[]{:S(2)}) collective-permute-start(f32[8,128]{1,0:T(8,128)S(1)} %get-tuple-element.51), channel_id=1, source_target_pairs={{4,8},{12,16},{20,24},{8,4},{16,12},{24,20},{5,9},{13,17},{21,25},... | collective-permute-start | bytes 12296 | tf_op jit(solution)/shard_map/ppermute | solution.py:469
  60.4 14.3 %copy-start.6 = (s32[256]{0:T(256)S(1)}, s32[256]{0:T(256)}, u32[]{:S(2)}) copy-start(s32[256]{0:T(256)} %param.15) | copy-start | bytes 3076
  64.9 9.8 %collective-permute-start.10 = (f32[48,256]{1,0:T(8,128)S(1)}, f32[48,256]{1,0:T(8,128)S(1)}, u32[]{:S(2)}, u32[]{:S(2)}) collective-permute-start(f32[48,256]{1,0:T(8,128)S(1)} %get-tuple-element.52.refs_3_), channel_id=1, source_target_pairs={{0,4},{8,12},{16,20},{24,28},{4,0},{12,8},{20,16},{28,24},{1,5},{9... | collective-permute-start | bytes 147464 | tf_op jit(solution)/shard_map/ppermute | solution.py:469
  69.8 5.0 %collective-permute-start.11 = (f32[48,256]{1,0:T(8,128)S(1)}, f32[48,256]{1,0:T(8,128)S(1)}, u32[]{:S(2)}, u32[]{:S(2)}) collective-permute-start(f32[48,256]{1,0:T(8,128)S(1)} %get-tuple-element.53.refs_4_), channel_id=1, source_target_pairs={{4,8},{12,16},{20,24},{8,4},{16,12},{24,20},{5,9},{13,17},{21,25},... | collective-permute-start | bytes 147464 | tf_op jit(solution)/shard_map/ppermute | solution.py:469

commit v6 on v5

--- a/solution.py
+++ b/solution.py
@@ -64,62 +64,116 @@
 
 def by_side(tile, a, b):
     even = tile % 2 == 0
-    return jnp.where(even, a, b), jnp.where(even, b, a)
+    return jnp.where(even, b, a), jnp.where(even, a, b)
 
 
 def to_swaps(tile, for_next, for_previous):
     even = tile % 2 == 0
-    return jnp.where(even, for_next, for_previous), jnp.where(even, for_previous, for_next)
+    return jnp.where(even, for_previous, for_next), jnp.where(even, for_next, for_previous)
+
+
+def announce_kernel(signs_hbm, ids_hbm, weight_hbm, out_ref, signs, ids, lead, sems):
+    loads = [
+        pltpu.make_async_copy(signs_hbm, signs, sems.at[0]),
+        pltpu.make_async_copy(ids_hbm, ids, sems.at[1]),
+        pltpu.make_async_copy(weight_hbm.at[:, pl.ds(0, HALO)], lead, sems.at[2]),
+    ]
+    for load in loads:
+        load.start()
+    for load in loads:
+        load.wait()
+    colours = jnp.broadcast_to(ids[...], signs.shape)
+    probes = jnp.where(colour_of(colours), (2 * signs[...] - 1).astype(F32), F32(0))
+    out_ref[:8, :] = probes
+    out_ref[8:, :] = jnp.zeros((8, RADIX), F32)
+    for i in range(EDGE):
+        out_ref[8 + 3 * i : 11 + 3 * i, :] = lead[:, i * RADIX : (i + 1) * RADIX]
 
 
 def setup_kernel(
-    conn_in,
-    cell_in,
-    friction_ref,
+    conn_hbm,
+    cell_hbm,
+    friction_hbm,
+    blocks_hbm,
     conn_ref,
     cell_ref,
     fr_ref,
+    blocks_ref,
     node_hot_ref,
+    level_hot_ref,
     cell_hot_ref,
     spread_ref,
     order_ref,
+    conn_in,
+    cell_in,
+    friction_in,
+    sems,
 ):
+    loads = [
+        pltpu.make_async_copy(conn_hbm, conn_in, sems.at[0]),
+        pltpu.make_async_copy(cell_hbm, cell_in, sems.at[1]),
+        pltpu.make_async_copy(friction_hbm, friction_in, sems.at[2]),
+        pltpu.make_async_copy(blocks_hbm, blocks_ref, sems.at[3]),
+    ]
+    for load in loads:
+        load.start()
     pairs = conn_ref.shape[0]
     slots, padded_order = fr_ref.shape
     node_slots = conn_in.shape[1]
+    levels = level_hot_ref.shape[0] // 16
     window = 3 * LANES
+
+    spread_ref[...] = spread_matrix(node_slots, padded_order)
+    order_ref[...] = order_matrix(node_slots, padded_order)
 
     def paired(ref):
         return jnp.concatenate(
             [ref[pl.ds(0, pairs, stride=2), :], ref[pl.ds(1, pairs, stride=2), :]], axis=1
         )
 
+    loads[0].wait()
     conn = paired(conn_in)
+    conn_ref[...] = conn
+    loads[1].wait()
     cells = paired(cell_in)
     cells = jnp.where(cells < RIM, cells + (window - RIM), cells - RIM)
-    conn_ref[...] = conn
     cell_ref[...] = cells
     rows = rows_iota((RADIX, LANES))
     for m in range(pairs):
         at = pl.ds(m * LANES, LANES)
         hot = rows == conn[m : m + 1, :] % RADIX
         node_hot_ref[:, at] = jnp.where(hot, F32(1), F32(0)).astype(BF16)
+        which = jnp.broadcast_to(conn[m : m + 1, :] // RADIX, (16, LANES))
+        for level in range(levels):
+            hot = jnp.where(which == level, F32(1), F32(0)).astype(BF16)
+            level_hot_ref[16 * level : 16 * level + 16, at] = hot
         hot = rows[:LANES] == cells[m : m + 1, :] % LANES
         cell_hot_ref[:, at] = jnp.where(hot, F32(1), F32(0)).astype(BF16)
-    spread_ref[...] = spread_matrix(node_slots, padded_order)
-    order_ref[...] = order_matrix(node_slots, padded_order)
-
+
+    loads[2].wait()
     shape = (node_slots, padded_order)
     total = jnp.zeros((slots, padded_order), F32)
     for c in range(3):
         place = lanes_iota(shape) == 3 * rows_iota(shape) + c
         place = jnp.where(place, F32(1), F32(0)).astype(BF16)
-        rest = friction_ref[c]
+        rest = friction_in[c]
         for _ in range(3):
             part = rest.astype(BF16)
             total = total + dot(part, place)
             rest = rest - part.astype(F32)
     fr_ref[...] = total
+    loads[3].wait()
+
+
+def spread_levels(v_ref, ordered, level_hot, levels, pairs):
+    for m in range(pairs):
+        at = pl.ds(m * LANES, LANES)
+        values = [ordered[16 * m : 16 * m + 16, c * LANES : (c + 1) * LANES] for c in range(3)]
+        for i, level in enumerate(levels):
+            mask = level_hot[16 * level : 16 * level + 16, at]
+            for c in range(3):
+                row = 48 * i + 16 * c
+                v_ref[row : row + 16, at] = values[c] * mask
 
 
 def edge_levels(levels):
@@ -131,7 +185,8 @@
     first = step == 0
     if not first:
         basal_ref, rim_a, rim_b, *refs = refs
-    conn_ref, cell_ref, fr_ref, blocks, node_hot, cell_hot, spread_ref, order_ref, *refs = refs
+    conn_ref, cell_ref, fr_ref, blocks, node_hot, level_hot, cell_hot, *refs = refs
+    spread_ref, order_ref, *refs = refs
     ordered_ref, a_ref, b_ref, *refs = refs
     if not first:
         squares_ref, *refs = refs
@@ -210,22 +265,10 @@
             f_ref[16 * m : 16 * m + 8, at : at + order] = hi
             f_ref[16 * m + 8 : 16 * m + 16, at : at + order] = out - hi
 
-    ordered = dot(f_ref[...].astype(BF16), order_ref[...])
+    ordered = dot(f_ref[...].astype(BF16), order_ref[...]).astype(BF16)
     ordered_ref[...] = ordered
-    conn = conn_ref[...]
     edges = edge_levels(levels)
-    for m in range(pairs):
-        which = conn[m : m + 1, :] // RADIX
-        rows = [
-            jnp.where(
-                which == level,
-                ordered[16 * m : 16 * m + 16, c * LANES : (c + 1) * LANES],
-                F32(0),
-            )
-            for level in edges
-            for c in range(3)
-        ]
-        v_ref[:, m * LANES : (m + 1) * LANES] = jnp.concatenate(rows, axis=0).astype(BF16)
+    spread_levels(v_ref, ordered, level_hot, edges, pairs)
     rim = dot_nt(v_ref[...], node_hot[...])
     sums = [
         rim[16 * i : 16 * i + 8] + rim[16 * i + 8 : 16 * i + 16] for i in range(3 * len(edges))
@@ -236,22 +279,13 @@
         a_ref[8 * i : 8 * i + 8, :], b_ref[8 * i : 8 * i + 8, :] = to_swaps(tile, spill, lead)
 
 
-def inner_kernel(levels, ordered_ref, weight_ref, conn_ref, node_hot, picked_ref, v_ref):
+def inner_kernel(
+    levels, ordered_ref, weight_ref, conn_ref, node_hot, level_hot, picked_ref, v_ref
+):
     pairs = conn_ref.shape[0]
     conn = conn_ref[...]
     inside = list(range(EDGE, levels - EDGE))
-    for m in range(pairs):
-        which = conn[m : m + 1, :] // RADIX
-        rows = [
-            jnp.where(
-                which == level,
-                ordered_ref[16 * m : 16 * m + 16, c * LANES : (c + 1) * LANES],
-                F32(0),
-            )
-            for level in inside
-            for c in range(3)
-        ]
-        v_ref[:, m * LANES : (m + 1) * LANES] = jnp.concatenate(rows, axis=0).astype(BF16)
+    spread_levels(v_ref, ordered_ref, level_hot, inside, pairs)
     nodes = dot_nt(v_ref[...], node_hot[...])
     rows = []
     for i in range(3 * len(inside)):
@@ -273,9 +307,9 @@
                 picked_ref[8 * m : 8 * m + 8, c * LANES : (c + 1) * LANES] = chosen[8 * c : 8 * c + 8]
 
 
-def adjoint_kernel(last, levels, *refs):
+def adjoint_kernel(last, clusters, levels, *refs):
     scalars, block_a, block_b, own_a, own_b, new_a, new_b, inner_ref, weight_ref, *refs = refs
-    conn_ref, cell_ref, fr_ref, blocks, node_hot, cell_hot, spread_ref, order_ref, *refs = refs
+    conn_ref, cell_ref, fr_ref, blocks, node_hot, _, cell_hot, spread_ref, order_ref, *refs = refs
     if last:
         squares_1, squares_2, ids_ref, *refs = refs
         basal_ref, out_ref, p_ref, n_ref, v_ref = refs
@@ -347,9 +381,7 @@
         a_ref[...], b_ref[...] = to_swaps(tile, for_next, for_previous)
         return
 
-    ids = ids_ref[...].astype(F32)
-    row = rows_iota((8, LANES))
-    ids = jnp.where(row == 0, ids[:, :LANES], jnp.where(row == 1, ids[:, LANES:], F32(0)))
+    ids = ids_ref[...]
     extra = jnp.zeros((8, LANES), F32)
     for i, ref in enumerate((squares_1, squares_2)):
         rest = jnp.sum(ref[...], axis=1, keepdims=True)
@@ -357,7 +389,10 @@
             piece = rest.astype(BF16).astype(F32)
             extra = jnp.where(lane == 3 * i + j, piece, extra)
             rest = rest - piece
-    message = jnp.concatenate(parts + [ids, extra], axis=1).astype(BF16)
+    for k in range(1, clusters):
+        below = jnp.sum((ids < k).astype(F32), axis=1, keepdims=True)
+        extra = jnp.where(lane == 8 + k, below, extra)
+    message = jnp.concatenate(parts + [extra], axis=1).astype(BF16)
     for t in range(out_ref.shape[0]):
         out_ref[t] = message
 
@@ -371,7 +406,7 @@
 
     def factor_of(p):
         def add(t, acc):
-            return acc + g_ref[t, p][:, 4 * LANES :].astype(F32)
+            return acc + g_ref[t, p][:, 3 * LANES :].astype(F32)
 
         sums = lax.fori_loop(0, tiles, add, jnp.zeros((8, LANES), F32), unroll=tiles <= 8)
         first = jnp.sum(sums[:, :3], axis=1, keepdims=True)
@@ -381,8 +416,12 @@
         return F32(1 / SHRINK) / (scale * jnp.sqrt(size * size + F32(1e-06)))
 
     def ids_of(t):
-        rows = g_ref[t, 0][:, 3 * LANES : 4 * LANES].astype(F32).astype(jnp.int32)
-        return [jnp.broadcast_to(rows[i : i + 1, :], (8, LANES)) for i in range(2)]
+        starts = g_ref[t, 0][:, 3 * LANES :].astype(F32)
+        cell = lanes_iota((8, 2 * LANES)).astype(F32)
+        ids = jnp.zeros(cell.shape, jnp.int32)
+        for k in range(1, clusters):
+            ids = ids + (cell >= starts[:, 8 + k : 9 + k]).astype(jnp.int32)
+        return [ids[:, :LANES], ids[:, LANES:]]
 
     def field(t, p, ids, own=None):
         before = g_ref[jnp.maximum(t - 1, 0), p][:, 2 * LANES : 3 * LANES].astype(F32)
@@ -449,11 +488,15 @@
     params = pltpu.CompilerParams(vmem_limit_bytes=VMEM_BYTES)
     shaped = jax.ShapeDtypeStruct
 
-    def call(kernel, name, out_shape, operands, scratch=(), scalar=True):
+    hbm = pl.BlockSpec(memory_space=pltpu.HBM)
+
+    def call(kernel, name, out_shape, operands, scratch=(), in_specs=None):
+        if in_specs and in_specs[0] is hbm:
+            operands = [pltpu.with_memory_space_constraint(x, pltpu.HBM) for x in operands]
         return pl.pallas_call(
             kernel,
             out_shape=out_shape,
-            in_specs=[smem] * scalar + [vmem] * (len(operands) - scalar),
+            in_specs=in_specs or [smem] + [vmem] * (len(operands) - 1),
             out_specs=jax.tree.map(lambda _: vmem, out_shape),
             scratch_shapes=list(scratch),
             compiler_params=params,
@@ -462,40 +505,55 @@
 
     evens = range(0, tiles - 1, 2)
     odds = range(1, tiles - 1, 2)
-    pairs_a = [(i, i + 1) for i in evens] + [(i + 1, i) for i in evens]
-    pairs_b = [(i, i + 1) for i in odds] + [(i + 1, i) for i in odds]
+    pairs_a = [(i, i + 1) for i in odds] + [(i + 1, i) for i in odds]
+    pairs_b = [(i, i + 1) for i in evens] + [(i + 1, i) for i in evens]
 
     def swapped(a, b):
         return lax.ppermute(a, "tiles", pairs_a), lax.ppermute(b, "tiles", pairs_b)
 
     weight = obs_weight.T
-    parity = jnp.arange(group_size, dtype=jnp.int32) % 2
-    same = (cluster_ids % 2)[None, :] == parity[:, None]
-    probes = jnp.where(same, (2 * sign_bits.T - 1).astype(F32), F32(0))
-    lead = [weight[:, i * RADIX : (i + 1) * RADIX] for i in range(EDGE)]
-    spare = jnp.zeros((8 - 3 * EDGE, RADIX), F32)
-    block = jnp.concatenate([probes, *lead, spare], axis=0)
+    block = call(
+        announce_kernel,
+        "announce",
+        shaped((16, cell_count), F32),
+        [sign_bits.T, cluster_ids.reshape(1, cell_count), weight],
+        [
+            pltpu.VMEM((group_size, cell_count), jnp.int32),
+            pltpu.VMEM((1, cell_count), jnp.int32),
+            pltpu.VMEM((3, HALO), F32),
+            pltpu.SemaphoreType.DMA((3,)),
+        ],
+        [hbm] * 3,
+    )
     block_a, block_b = swapped(block, block)
 
-    conn, cells, fr, node_hot, cell_hot, spread, order_map = call(
+    shared = call(
         setup_kernel,
         "setup",
         [
             shaped((pairs, LANES), jnp.int32),
             shaped((pairs, LANES), jnp.int32),
             shaped((slots, padded_order), F32),
+            shaped(blocks.shape, BF16),
             shaped((RADIX, refs), BF16),
+            shaped((16 * levels, refs), BF16),
             shaped((LANES, refs), BF16),
             shaped((LANES, 2 * padded_order), BF16),
             shaped((2 * padded_order, 3 * LANES), BF16),
         ],
-        [connectivity, basal_map, friction.transpose(2, 0, 1)],
-        scalar=False,
+        [connectivity, basal_map, friction.transpose(2, 0, 1), blocks],
+        [
+            pltpu.VMEM(connectivity.shape, jnp.int32),
+            pltpu.VMEM(basal_map.shape, jnp.int32),
+            pltpu.VMEM((3, slots, node_slots), F32),
+            pltpu.SemaphoreType.DMA((4,)),
+        ],
+        [hbm] * 4,
     )
     scalars = jnp.stack(
         [lax.axis_index("tiles"), elem_counts[0], lax.axis_index("probes")]
     ).astype(jnp.int32)
-    shared = [conn, cells, fr, blocks, node_hot, cell_hot, spread, order_map]
+    conn, node_hot, level_hot = shared[0], shared[4], shared[5]
 
     edge = shaped((24 * EDGE, RADIX), F32)
     rim = shaped((group_size, LANES), F32)
@@ -508,13 +566,13 @@
     samples = None
     for step in range(POWER + 1):
         last = step == POWER
-        out_shape = [shaped((16 * pairs, 3 * LANES), F32), edge, edge]
+        out_shape = [shaped((16 * pairs, 3 * LANES), BF16), edge, edge]
         out_shape += [rim] * (step > 0) + [field] * (step == 1)
         ordered, own_a, own_b, *extra = call(
             functools.partial(forward_kernel, step, tiles, levels),
             "forward",
             out_shape,
-            [scalars, block, block_a, block_b] + carried + shared,
+            [scalars, block, block_a, block_b] + carried + [*shared],
             [
                 pltpu.VMEM((16 * pairs, 2 * padded_order), F32),
                 pltpu.VMEM((96 * EDGE, refs), BF16),
@@ -528,19 +586,19 @@
             functools.partial(inner_kernel, levels),
             "inner",
             shaped((8 * pairs, 3 * LANES), F32),
-            [ordered, weight, conn, node_hot],
+            [ordered, weight, conn, node_hot, level_hot],
             [pltpu.VMEM((48 * (levels - 2 * EDGE), refs), BF16)],
-            scalar=False,
+            [vmem] * 5,
         )
-        operands = [scalars, block_a, block_b, own_a, own_b, new_a, new_b, inner, weight] + shared
+        operands = [scalars, block_a, block_b, own_a, own_b, new_a, new_b, inner, weight, *shared]
         if last:
             operands += squares + [cluster_ids.reshape(1, cell_count)]
-            message = shaped((lax.axis_size(everyone), group_size, window + 2 * LANES), BF16)
+            message = shaped((lax.axis_size(everyone), group_size, window + LANES), BF16)
             out_shape = [whole, message]
         else:
             out_shape = [whole, rim, rim]
         basal, *messages = call(
-            functools.partial(adjoint_kernel, last, levels),
+            functools.partial(adjoint_kernel, last, tiles, levels),
             "adjoint",
             out_shape,
             operands,

time: 99.6 us -> 91.3 us (0.917)
  local copies, waits for them, and re-layouts: 6.03 us -> 0.01 us
  blocking collectives: 19.2 us -> 14.4 us
  Pallas kernels: 38.9 us -> 40.8 us
  other arithmetic: 1.61 us -> 0.08 us
  waiting for transfers between devices: 1.7 us -> 3.19 us
  starting transfers between devices: 30 us -> 31 us
    ppermute x6, starting transfers between devices: 4.3 us -> 26.6 us  [swapped(): lax.ppermute(b, 'tiles', pairs_b)]
    ppermute x6, starting transfers between devices: 25.7 us -> 4.42 us  [swapped(): lax.ppermute(a, 'tiles', pairs_a)]
    unnamed x14 -> x4, local copies, waits for them, and re-layouts: 5.2 us -> 0.01 us
    all_to_all x1, blocking collectives: 19.2 us -> 14.4 us  [shards(): gathered = lax.all_to_all(messages[0], everyone, 0, 0)]
    ppermute x6, waiting for transfers between devices: 0.02 us -> 3.18 us  [swapped(): lax.ppermute(b, 'tiles', pairs_b)]
    pallas_call x11 -> x12, Pallas kernels: 38.9 us -> 40.8 us  [call(): pl.pallas_call(kernel, out_shape=out_shape, in_specs=in_specs or [smem] +...]
    ppermute x6, waiting for transfers between devices: 1.69 us -> 0.02 us  [swapped(): lax.ppermute(a, 'tiles', pairs_a)]
    select_n x3 -> x0, other arithmetic: 1.46 us -> none  [the longest x1 0.77 us: shards(): probes = jnp.where(same, (2 * sign_bits.T - 1).astype(F32), F32(0))]
  transfers between devices with their start and end apart: 12 -> 12, of which waited for: 2 -> 2; matrix products, arithmetic and copies ran while one was open for 0% -> 0% of each run, Pallas kernels for 14% -> 17%
where the time goes in v6:
time: 91.3 us; the launch traced here: 90.9 us
  Pallas kernels  40.8 us (45%)
  starting transfers between devices  31 us (34%)
  blocking collectives  14.4 us (16%)
  waiting for transfers between devices  3.19 us (3%)
  between operations  1.47 us (2%)
    pallas_call x12, Pallas kernels, call(): pl.pallas_call(kernel, out_shape=out_shape, in_specs=in_specs or [smem] +...  40.8 us
    ppermute x6, starting transfers between devices, swapped(): lax.ppermute(b, 'tiles', pairs_b)  26.6 us
    all_to_all x1, blocking collectives, shards(): gathered = lax.all_to_all(messages[0], everyone, 0, 0)  14.4 us
    ppermute x6, starting transfers between devices, swapped(): lax.ppermute(a, 'tiles', pairs_a)  4.42 us
    ppermute x6, waiting for transfers between devices, swapped(): lax.ppermute(b, 'tiles', pairs_b)  3.18 us
  transfers between devices with their start and end apart: 12, of which 2 were waited for; matrix products, arithmetic and copies ran while one was open for 0% of the time, Pallas kernels for 17%

profile of v6, /device:TPU:0, one launch (start us, length us, event | category | flops | bytes accessed | tf_op | source)
XLA Modules:
  0.0 90.9 jit_solution(1556435580039917161)
XLA Ops:
  0.6 0.8 announce.1.refs_1_
  1.4 0.7 collective-permute-start
  2.1 5.8 %collective-permute-start.1 = (f32[16,256]{1,0:T(8,128)S(1)}, f32[16,256]{1,0:T(8,128)S(1)}, u32[]{:S(2)}, u32[]{:S(2)}) collective-permute-start(f32[16,256]{1,0:T(8,128)S(1)} %announce.1.refs_1_), channel_id=1, source_target_pairs={{0,4},{8,12},{16,20},{24,28},{4,0},{12,8},{20,16},{28,24},{1,5},{9... | collective-permute-start | bytes 49160 | tf_op jit(solution)/shard_map/ppermute | solution.py:512
  8.5 0.1 pad_add_fusion.refs_0_.scalars
  8.6 2.9 %setup.1 = (s32[32,128]{1,0:T(8,128)S(1)}, s32[32,128]{1,0:T(8,128)S(1)}, f32[64,256]{1,0:T(8,128)S(1)}, bf16[64,192,192]{2,1,0:T(8,128)(2,1)S(1)}, bf16[256,409...) custom-call(s32[64,64]{1,0:T(8,128)} %conn_hbm.1, ...), custom_call_target="tpu_custom_call" | custom-call | tf_op jit(solution)/shard_map/setup/pallas_call | solution.py:496
  11.5 0.0 copy-start
  11.5 0.0 collective-permute-done.refs_2_.refs_1_
  11.5 0.0 collective-permute-done.1.refs_3_.refs_2_
  11.6 4.5 %forward.3 = (bf16[512,384]{1,0:T(8,128)(2,1)S(1)}, f32[48,256]{1,0:T(8,128)S(1)}, f32[48,256]{1,0:T(8,128)S(1)}) custom-call(s32[3]{0:T(128)S(1)} %pad_add_fusion.refs_0_.scalars, f32[16,256]{1,0:T(8,128)S(1)} %announce.1.refs_1_, f32[16,256]{1,0:T(8,128)S(1)} %collective-permute-done.refs_2_.refs_1_, f32[16,256]{1,0:T(8,128)S(1)} %collective-permute-done.1.refs_3_.refs_2_, ...), custom_call_target="tpu_custom_call" | custom-call | tf_op jit(solution)/shard_map/forward/pallas_call | solution.py:496
  16.0 0.7 collective-permute-start.2
  16.7 4.3 %collective-permute-start.3 = (f32[48,256]{1,0:T(8,128)S(1)}, f32[48,256]{1,0:T(8,128)S(1)}, u32[]{:S(2)}, u32[]{:S(2)}) collective-permute-start(f32[48,256]{1,0:T(8,128)S(1)} %get-tuple-element.44.refs_4_), channel_id=1, source_target_pairs={{0,4},{8,12},{16,20},{24,28},{4,0},{12,8},{20,16},{28,24},{1,5},{9... | collective-permute-start | bytes 147464 | tf_op jit(solution)/shard_map/ppermute | solution.py:512
  21.0 0.0 copy-done
  21.0 4.0 %inner.3.refs_7_ = f32[256,384]{1,0:T(8,128)S(1)} custom-call(bf16[512,384]{1,0:T(8,128)(2,1)S(1)} %get-tuple-element.45.ordered_ref, f32[3,4096]{1,0:T(4,128)S(1)} %bitcast.10, s32[32,128]{1,0:T(8,128)S(1)} %get-tuple-element.34.refs_4_.conn_ref.refs_9_.refs_7_, bf16[256,4096]{1,0:T(8,128)(2,1)S(1)} %get-tuple-element.38.refs_8_.node_hot.refs_13_.refs_11_, ...), custom_call_target="tpu_custom_call" | custom-call | tf_op jit(solution)/shard_map/inner/pallas_call | solution.py:496
  25.1 0.0 collective-permute-done.2.refs_5_
  25.1 0.0 collective-permute-done.3.refs_6_
  25.1 3.1 %adjoint.3 = (f32[8,384]{1,0:T(8,128)S(1)}, f32[8,128]{1,0:T(8,128)S(1)}, f32[8,128]{1,0:T(8,128)S(1)}) custom-call(s32[3]{0:T(128)S(1)} %pad_add_fusion.refs_0_.scalars, f32[16,256]{1,0:T(8,128)S(1)} %collective-permute-done.refs_2_.refs_1_, f32[16,256]{1,0:T(8,128)S(1)} %collective-permute-done.1.refs_3_.refs_2_, f32[48,256]{1,0:T(8,128)S(1)} %get-tuple-element.43.refs_3_, ...), custom_call_target="tpu_custom_call" | custom-call | tf_op jit(solution)/shard_map/adjoint/pallas_call | solution.py:496
  28.2 0.9 collective-permute-start.4
  29.1 4.4 %collective-permute-start.5 = (f32[8,128]{1,0:T(8,128)S(1)}, f32[8,128]{1,0:T(8,128)S(1)}, u32[]{:S(2)}, u32[]{:S(2)}) collective-permute-start(f32[8,128]{1,0:T(8,128)S(1)} %get-tuple-element.48), channel_id=1, source_target_pairs={{0,4},{8,12},{16,20},{24,28},{4,0},{12,8},{20,16},{28,24},{1,5},{9... | collective-permute-start | bytes 12296 | tf_op jit(solution)/shard_map/ppermute | solution.py:512
  33.4 0.0 collective-permute-done.4.refs_5_
  33.4 1.6 %collective-permute-done.5.refs_6_ = f32[8,128]{1,0:T(8,128)S(1)} collective-permute-done((f32[8,128]{1,0:T(8,128)S(1)}, f32[8,128]{1,0:T(8,128)S(1)}, u32[]{:S(2)}, u32[]{:S(2)}) %collective-permute-start.5) | collective-permute-done | bytes 4128 | tf_op jit(solution)/shard_map/ppermute | solution.py:512
  35.0 4.8 %forward.4 = (bf16[512,384]{1,0:T(8,128)(2,1)S(1)}, f32[48,256]{1,0:T(8,128)S(1)}, f32[48,256]{1,0:T(8,128)S(1)}, f32[8,128]{1,0:T(8,128)S(1)}, f32[8,256]{1,0:T(8,128)}) custom-call(s32[3]{0:T(128)S(1)} %pad_add_fusion.refs_0_.scalars, f32[16,256]{1,0:T(8,128)S(1)} %announce.1.refs_1_, f32[16,256]{1,0:T(8,128)S(1)} %collective-permute-done.refs_2_.refs_1_, ...), custom_call_target="tpu_custom_call" | custom-call | tf_op jit(solution)/shard_map/forward/pallas_call | solution.py:496
  39.8 0.7 collective-permute-start.6
  40.5 4.0 %collective-permute-start.7 = (f32[48,256]{1,0:T(8,128)S(1)}, f32[48,256]{1,0:T(8,128)S(1)}, u32[]{:S(2)}, u32[]{:S(2)}) collective-permute-start(f32[48,256]{1,0:T(8,128)S(1)} %get-tuple-element.51.refs_4_), channel_id=1, source_target_pairs={{0,4},{8,12},{16,20},{24,28},{4,0},{12,8},{20,16},{28,24},{1,5},{9... | collective-permute-start | bytes 147464 | tf_op jit(solution)/shard_map/ppermute | solution.py:512
  44.5 4.1 %inner.4.refs_7_ = f32[256,384]{1,0:T(8,128)S(1)} custom-call(bf16[512,384]{1,0:T(8,128)(2,1)S(1)} %get-tuple-element.52.ordered_ref, f32[3,4096]{1,0:T(4,128)S(1)} %bitcast.12, s32[32,128]{1,0:T(8,128)S(1)} %get-tuple-element.34.refs_4_.conn_ref.refs_9_.refs_7_, bf16[256,4096]{1,0:T(8,128)(2,1)S(1)} %get-tuple-element.38.refs_8_.node_hot.refs_13_.refs_11_, ...), custom_call_target="tpu_custom_call" | custom-call | tf_op jit(solution)/shard_map/inner/pallas_call | solution.py:496
  48.5 0.0 collective-permute-done.6.refs_5_
  48.5 0.0 collective-permute-done.7.refs_6_
  48.5 3.1 %adjoint.4 = (f32[8,384]{1,0:T(8,128)S(1)}, f32[8,128]{1,0:T(8,128)S(1)}, f32[8,128]{1,0:T(8,128)S(1)}) custom-call(s32[3]{0:T(128)S(1)} %pad_add_fusion.refs_0_.scalars, f32[16,256]{1,0:T(8,128)S(1)} %collective-permute-done.refs_2_.refs_1_, f32[16,256]{1,0:T(8,128)S(1)} %collective-permute-done.1.refs_3_.refs_2_, f32[48,256]{1,0:T(8,128)S(1)} %get-tuple-element.50.refs_3_, ...), custom_call_target="tpu_custom_call" | custom-call | tf_op jit(solution)/shard_map/adjoint/pallas_call | solution.py:496
  51.6 0.7 collective-permute-start.8
  52.3 3.6 %collective-permute-start.9 = (f32[8,128]{1,0:T(8,128)S(1)}, f32[8,128]{1,0:T(8,128)S(1)}, u32[]{:S(2)}, u32[]{:S(2)}) collective-permute-start(f32[8,128]{1,0:T(8,128)S(1)} %get-tuple-element.55), channel_id=1, source_target_pairs={{0,4},{8,12},{16,20},{24,28},{4,0},{12,8},{20,16},{28,24},{1,5},{9... | collective-permute-start | bytes 12296 | tf_op jit(solution)/shard_map/ppermute | solution.py:512
  56.0 0.0 collective-permute-done.8.refs_5_
  56.0 1.6 %collective-permute-done.9.refs_6_ = f32[8,128]{1,0:T(8,128)S(1)} collective-permute-done((f32[8,128]{1,0:T(8,128)S(1)}, f32[8,128]{1,0:T(8,128)S(1)}, u32[]{:S(2)}, u32[]{:S(2)}) %collective-permute-start.9) | collective-permute-done | bytes 4128 | tf_op jit(solution)/shard_map/ppermute | solution.py:512
  57.5 0.0 copy-start.1
  57.5 4.4 %forward.5 = (bf16[512,384]{1,0:T(8,128)(2,1)S(1)}, f32[48,256]{1,0:T(8,128)S(1)}, f32[48,256]{1,0:T(8,128)S(1)}, f32[8,128]{1,0:T(8,128)S(1)}) custom-call(s32[3]{0:T(128)S(1)} %pad_add_fusion.refs_0_.scalars, f32[16,256]{1,0:T(8,128)S(1)} %announce.1.refs_1_, f32[16,256]{1,0:T(8,128)S(1)} %collective-permute-done.refs_2_.refs_1_, ...), custom_call_target="tpu_custom_call" | custom-call | tf_op jit(solution)/shard_map/forward/pallas_call | solution.py:496
  62.0 0.9 collective-permute-start.10
  62.9 4.5 %collective-permute-start.11 = (f32[48,256]{1,0:T(8,128)S(1)}, f32[48,256]{1,0:T(8,128)S(1)}, u32[]{:S(2)}, u32[]{:S(2)}) collective-permute-start(f32[48,256]{1,0:T(8,128)S(1)} %get-tuple-element.57.refs_4_), channel_id=1, source_target_pairs={{0,4},{8,12},{16,20},{24,28},{4,0},{12,8},{20,16},{28,24},{1,5},{9... | collective-permute-start | bytes 147464 | tf_op jit(solution)/shard_map/ppermute | solution.py:512
  67.4 4.1 %inner.5.refs_7_ = f32[256,384]{1,0:T(8,128)S(1)} custom-call(bf16[512,384]{1,0:T(8,128)(2,1)S(1)} %get-tuple-element.58.ordered_ref, f32[3,4096]{1,0:T(4,128)S(1)} %bitcast.14, s32[32,128]{1,0:T(8,128)S(1)} %get-tuple-element.34.refs_4_.conn_ref.refs_9_.refs_7_, bf16[256,4096]{1,0:T(8,128)(2,1)S(1)} %get-tuple-element.38.refs_8_.node_hot.refs_13_.refs_11_, ...), custom_call_target="tpu_custom_call" | custom-call | tf_op jit(solution)/shard_map/inner/pallas_call | solution.py:496
  71.4 0.0 collective-permute-done.10.refs_5_
  71.4 0.0 collective-permute-done.11.refs_6_
  71.5 0.0 copy-done.1
  71.5 3.2 %adjoint.5 = (f32[8,384]{1,0:T(8,128)S(1)}, bf16[32,8,512]{2,1,0:T(8,128)(2,1)S(1)}) custom-call(s32[3]{0:T(128)S(1)} %pad_add_fusion.refs_0_.scalars, f32[16,256]{1,0:T(8,128)S(1)} %collective-permute-done.refs_2_.refs_1_, f32[16,256]{1,0:T(8,128)S(1)} %collective-permute-done.1.refs_3_.refs_2_, f32[48,256]{1,0:T(8,128)S(1)} %get-tuple-element.56.refs_3_, ...), custom_call_target="tpu_custom_call" | custom-call | tf_op jit(solution)/shard_map/adjoint/pallas_call | solution.py:496
  74.6 14.4 %all_to_all.5 = bf16[32,8,512]{2,1,0:T(8,128)(2,1)S(1)} all-to-all(bf16[32,8,512]{2,1,0:T(8,128)(2,1)S(1)} %get-tuple-element.61), channel_id=1, replica_groups=mesh['tiles'=8,'probes'=4] {'tiles','probes'}, dimensions={0} | all-to-all | bytes 524288 | tf_op jit(solution)/shard_map/all_to_all | solution.py:614
  89.0 2.0 %gram.1 = (f32[8,256]{1,0:T(8,128)}, f32[8,8,32]{2,1,0:T(8,128)}) custom-call(s32[3]{0:T(128)S(1)} %pad_add_fusion.refs_0_.scalars, bf16[8,4,8,512]{3,2,1,0:T(8,128)(2,1)S(1)} %bitcast.16, f32[8,384]{1,0:T(8,128)S(1)} %get-tuple-element.62.own_ref), custom_call_target="tpu_custom_call" | custom-call | tf_op jit(solution)/shard_map/gram/pallas_call | solution.py:496
Async XLA Ops:
  1.4 10.1 %collective-permute-start = (f32[16,256]{1,0:T(8,128)S(1)}, f32[16,256]{1,0:T(8,128)S(1)}, u32[]{:S(2)}, u32[]{:S(2)}) collective-permute-start(f32[16,256]{1,0:T(8,128)S(1)} %announce.1.refs_1_), channel_id=1, source_target_pairs={{4,8},{12,16},{20,24},{8,4},{16,12},{24,20},{5,9},{13,17},{21,25},... | collective-permute-start | bytes 49160 | tf_op jit(solution)/shard_map/ppermute | solution.py:512
  2.1 9.5 %collective-permute-start.1 = (f32[16,256]{1,0:T(8,128)S(1)}, f32[16,256]{1,0:T(8,128)S(1)}, u32[]{:S(2)}, u32[]{:S(2)}) collective-permute-start(f32[16,256]{1,0:T(8,128)S(1)} %announce.1.refs_1_), channel_id=1, source_target_pairs={{0,4},{8,12},{16,20},{24,28},{4,0},{12,8},{20,16},{28,24},{1,5},{9... | collective-permute-start | bytes 49160 | tf_op jit(solution)/shard_map/ppermute | solution.py:512
  11.5 9.5 %copy-start = (f32[4096,3]{0,1:T(4,128)S(1)}, f32[4096,3]{0,1:T(4,128)}, u32[]{:S(2)}) copy-start(f32[4096,3]{0,1:T(4,128)} %param.13) | copy-start | bytes 147460
  16.0 9.1 %collective-permute-start.2 = (f32[48,256]{1,0:T(8,128)S(1)}, f32[48,256]{1,0:T(8,128)S(1)}, u32[]{:S(2)}, u32[]{:S(2)}) collective-permute-start(f32[48,256]{1,0:T(8,128)S(1)} %get-tuple-element.43.refs_3_), channel_id=1, source_target_pairs={{4,8},{12,16},{20,24},{8,4},{16,12},{24,20},{5,9},{13,17},{21,25},... | collective-permute-start | bytes 147464 | tf_op jit(solution)/shard_map/ppermute | solution.py:512
  16.7 8.4 %collective-permute-start.3 = (f32[48,256]{1,0:T(8,128)S(1)}, f32[48,256]{1,0:T(8,128)S(1)}, u32[]{:S(2)}, u32[]{:S(2)}) collective-permute-start(f32[48,256]{1,0:T(8,128)S(1)} %get-tuple-element.44.refs_4_), channel_id=1, source_target_pairs={{0,4},{8,12},{16,20},{24,28},{4,0},{12,8},{20,16},{28,24},{1,5},{9... | collective-permute-start | bytes 147464 | tf_op jit(solution)/shard_map/ppermute | solution.py:512
  28.2 5.2 %collective-permute-start.4 = (f32[8,128]{1,0:T(8,128)S(1)}, f32[8,128]{1,0:T(8,128)S(1)}, u32[]{:S(2)}, u32[]{:S(2)}) collective-permute-start(f32[8,128]{1,0:T(8,128)S(1)} %get-tuple-element.47), channel_id=1, source_target_pairs={{4,8},{12,16},{20,24},{8,4},{16,12},{24,20},{5,9},{13,17},{21,25},... | collective-permute-start | bytes 12296 | tf_op jit(solution)/shard_map/ppermute | solution.py:512
  29.1 5.9 %collective-permute-start.5 = (f32[8,128]{1,0:T(8,128)S(1)}, f32[8,128]{1,0:T(8,128)S(1)}, u32[]{:S(2)}, u32[]{:S(2)}) collective-permute-start(f32[8,128]{1,0:T(8,128)S(1)} %get-tuple-element.48), channel_id=1, source_target_pairs={{0,4},{8,12},{16,20},{24,28},{4,0},{12,8},{20,16},{28,24},{1,5},{9... | collective-permute-start | bytes 12296 | tf_op jit(solution)/shard_map/ppermute | solution.py:512
  39.8 8.7 %collective-permute-start.6 = (f32[48,256]{1,0:T(8,128)S(1)}, f32[48,256]{1,0:T(8,128)S(1)}, u32[]{:S(2)}, u32[]{:S(2)}) collective-permute-start(f32[48,256]{1,0:T(8,128)S(1)} %get-tuple-element.50.refs_3_), channel_id=1, source_target_pairs={{4,8},{12,16},{20,24},{8,4},{16,12},{24,20},{5,9},{13,17},{21,25},... | collective-permute-start | bytes 147464 | tf_op jit(solution)/shard_map/ppermute | solution.py:512
  40.5 8.0 %collective-permute-start.7 = (f32[48,256]{1,0:T(8,128)S(1)}, f32[48,256]{1,0:T(8,128)S(1)}, u32[]{:S(2)}, u32[]{:S(2)}) collective-permute-start(f32[48,256]{1,0:T(8,128)S(1)} %get-tuple-element.51.refs_4_), channel_id=1, source_target_pairs={{0,4},{8,12},{16,20},{24,28},{4,0},{12,8},{20,16},{28,24},{1,5},{9... | collective-permute-start | bytes 147464 | tf_op jit(solution)/shard_map/ppermute | solution.py:512
  51.6 4.3 %collective-permute-start.8 = (f32[8,128]{1,0:T(8,128)S(1)}, f32[8,128]{1,0:T(8,128)S(1)}, u32[]{:S(2)}, u32[]{:S(2)}) collective-permute-start(f32[8,128]{1,0:T(8,128)S(1)} %get-tuple-element.54), channel_id=1, source_target_pairs={{4,8},{12,16},{20,24},{8,4},{16,12},{24,20},{5,9},{13,17},{21,25},... | collective-permute-start | bytes 12296 | tf_op jit(solution)/shard_map/ppermute | solution.py:512
  52.3 5.2 %collective-permute-start.9 = (f32[8,128]{1,0:T(8,128)S(1)}, f32[8,128]{1,0:T(8,128)S(1)}, u32[]{:S(2)}, u32[]{:S(2)}) collective-permute-start(f32[8,128]{1,0:T(8,128)S(1)} %get-tuple-element.55), channel_id=1, source_target_pairs={{0,4},{8,12},{16,20},{24,28},{4,0},{12,8},{20,16},{28,24},{1,5},{9... | collective-permute-start | bytes 12296 | tf_op jit(solution)/shard_map/ppermute | solution.py:512
  57.5 13.9 %copy-start.1 = (s32[256]{0:T(256)S(1)}, s32[256]{0:T(256)}, u32[]{:S(2)}) copy-start(s32[256]{0:T(256)} %param.15) | copy-start | bytes 3076
  62.0 9.4 %collective-permute-start.10 = (f32[48,256]{1,0:T(8,128)S(1)}, f32[48,256]{1,0:T(8,128)S(1)}, u32[]{:S(2)}, u32[]{:S(2)}) collective-permute-start(f32[48,256]{1,0:T(8,128)S(1)} %get-tuple-element.56.refs_3_), channel_id=1, source_target_pairs={{4,8},{12,16},{20,24},{8,4},{16,12},{24,20},{5,9},{13,17},{21,25},... | collective-permute-start | bytes 147464 | tf_op jit(solution)/shard_map/ppermute | solution.py:512
  62.9 8.6 %collective-permute-start.11 = (f32[48,256]{1,0:T(8,128)S(1)}, f32[48,256]{1,0:T(8,128)S(1)}, u32[]{:S(2)}, u32[]{:S(2)}) collective-permute-start(f32[48,256]{1,0:T(8,128)S(1)} %get-tuple-element.57.refs_4_), channel_id=1, source_target_pairs={{0,4},{8,12},{16,20},{24,28},{4,0},{12,8},{20,16},{28,24},{1,5},{9... | collective-permute-start | bytes 147464 | tf_op jit(solution)/shard_map/ppermute | solution.py:512

commit v7 on v6

--- a/solution.py
+++ b/solution.py
@@ -11,7 +11,7 @@
 POWER = 2
 RIM = 64
 LANES = 128
-RADIX = 256
+RADIX = 512
 EDGE = HALO // RADIX
 SHRINK = 2.0**-40
 VMEM_BYTES = 16 * 1024 * 1024
@@ -85,12 +85,14 @@
     colours = jnp.broadcast_to(ids[...], signs.shape)
     probes = jnp.where(colour_of(colours), (2 * signs[...] - 1).astype(F32), F32(0))
     out_ref[:8, :] = probes
-    out_ref[8:, :] = jnp.zeros((8, RADIX), F32)
-    for i in range(EDGE):
-        out_ref[8 + 3 * i : 11 + 3 * i, :] = lead[:, i * RADIX : (i + 1) * RADIX]
+    out_ref[8:, :] = jnp.zeros_like(probes)
+    half = HALO // 2
+    out_ref[8:11, :] = lead[:, :half]
+    out_ref[11:14, :] = lead[:, half:]
 
 
 def setup_kernel(
+    counts,
     conn_hbm,
     cell_hbm,
     friction_hbm,
@@ -99,6 +101,7 @@
     cell_ref,
     fr_ref,
     blocks_ref,
+    turned_ref,
     node_hot_ref,
     level_hot_ref,
     cell_hot_ref,
@@ -161,8 +164,10 @@
             part = rest.astype(BF16)
             total = total + dot(part, place)
             rest = rest - part.astype(F32)
-    fr_ref[...] = total
+    fr_ref[...] = jnp.where(rows_iota(total.shape) < counts[0], total, F32(0))
     loads[3].wait()
+    for slot in range(slots):
+        turned_ref[slot] = blocks_ref[slot].T
 
 
 def spread_levels(v_ref, ordered, level_hot, levels, pairs):
@@ -181,11 +186,11 @@
 
 
 def forward_kernel(step, tiles, levels, *refs):
-    scalars, block_ref, block_a, block_b, *refs = refs
+    block_ref, block_a, block_b, *refs = refs
     first = step == 0
     if not first:
         basal_ref, rim_a, rim_b, *refs = refs
-    conn_ref, cell_ref, fr_ref, blocks, node_hot, level_hot, cell_hot, *refs = refs
+    conn_ref, cell_ref, fr_ref, _, turned, node_hot, level_hot, cell_hot, *refs = refs
     spread_ref, order_ref, *refs = refs
     ordered_ref, a_ref, b_ref, *refs = refs
     if not first:
@@ -194,11 +199,10 @@
         field_ref, *refs = refs
     f_ref, v_ref = refs
 
-    order = blocks.shape[1]
+    order = turned.shape[1]
     padded_order = f_ref.shape[1] // 2
-    pairs = blocks.shape[0] // 2
-    tile = scalars[0]
-    count = scalars[1]
+    pairs = turned.shape[0] // 2
+    tile = lax.axis_index("tiles")
 
     lane = lanes_iota((8, LANES))
     low = lane < RIM
@@ -254,13 +258,12 @@
             slot = 2 * m + side
             inputs = spread[8 * m : 8 * m + 8, at : at + order] * fr_ref[slot : slot + 1, :order]
             if first:
-                out = dot_nt(inputs.astype(BF16), blocks[slot])
+                out = dot(inputs.astype(BF16), turned[slot])
             else:
                 hi = inputs.astype(BF16).astype(F32)
                 both = jnp.concatenate([hi, inputs - hi], axis=0).astype(BF16)
-                out = dot_nt(both, blocks[slot])
+                out = dot(both, turned[slot])
                 out = out[:8] + out[8:]
-            out = jnp.where(slot < count, out, F32(0))
             hi = out.astype(BF16).astype(F32)
             f_ref[16 * m : 16 * m + 8, at : at + order] = hi
             f_ref[16 * m + 8 : 16 * m + 16, at : at + order] = out - hi
@@ -308,8 +311,9 @@
 
 
 def adjoint_kernel(last, clusters, levels, *refs):
-    scalars, block_a, block_b, own_a, own_b, new_a, new_b, inner_ref, weight_ref, *refs = refs
-    conn_ref, cell_ref, fr_ref, blocks, node_hot, _, cell_hot, spread_ref, order_ref, *refs = refs
+    block_ref, block_a, block_b, own_a, own_b, new_a, new_b, inner_ref, weight_ref, *refs = refs
+    conn_ref, cell_ref, fr_ref, blocks, _, node_hot, _, cell_hot, *refs = refs
+    spread_ref, order_ref, *refs = refs
     if last:
         squares_1, squares_2, ids_ref, *refs = refs
         basal_ref, out_ref, p_ref, n_ref, v_ref = refs
@@ -319,17 +323,14 @@
     order = blocks.shape[1]
     padded_order = p_ref.shape[1] // 2
     pairs = blocks.shape[0] // 2
-    tile = scalars[0]
-    count = scalars[1]
+    tile = lax.axis_index("tiles")
 
     spill, lead = by_side(tile, own_a[...] + new_a[...], own_b[...] + new_b[...])
-    after, _ = by_side(tile, block_a[8:16, :], block_b[8:16, :])
-    rows = []
-    for i in range(3 * EDGE):
-        at = (i // 3) * RADIX
-        rows.append(lead[8 * i : 8 * i + 8] * weight_ref[i % 3 : i % 3 + 1, at : at + RADIX])
-    for i in range(3 * EDGE):
-        rows.append(spill[8 * i : 8 * i + 8] * after[i : i + 1, :])
+    after, before = by_side(tile, block_a[...], block_b[...])
+    rows = [lead[8 * c : 8 * c + 8] * weight_ref[c : c + 1, :HALO] for c in range(3)]
+    for c in range(3):
+        weight = jnp.concatenate([after[8 + c : 9 + c, :], after[11 + c : 12 + c, :]], axis=1)
+        rows.append(spill[8 * c : 8 * c + 8] * weight)
     weighted = jnp.concatenate(rows, axis=0).astype(BF16)
 
     conn = conn_ref[...]
@@ -355,7 +356,7 @@
             slot = 2 * m + side
             out = dot(natural[8 * m : 8 * m + 8, at : at + order].astype(BF16), blocks[slot])
             out = out * fr_ref[slot : slot + 1, :order]
-            p_ref[8 * m : 8 * m + 8, at : at + order] = jnp.where(slot < count, out, F32(0))
+            p_ref[8 * m : 8 * m + 8, at : at + order] = out
 
     hi, lo = split(p_ref[...])
     partial = dot_nt(jnp.concatenate([hi, lo], axis=0), spread_ref[...])
@@ -381,7 +382,16 @@
         a_ref[...], b_ref[...] = to_swaps(tile, for_next, for_previous)
         return
 
-    ids = ids_ref[...]
+    starts = [
+        block_ref[:1, :LANES],
+        block_ref[:1, LANES:],
+        jnp.where(lane[:1] < RIM, after[:1, :LANES], before[:1, LANES:]),
+    ]
+    packed = []
+    for start, part in zip(starts, parts):
+        even = start != 0
+        rows = [jnp.where(even, part[r + 1 : r + 2], part[r : r + 1]) for r in range(0, 8, 2)]
+        packed.append(jnp.concatenate(rows, axis=0))
     extra = jnp.zeros((8, LANES), F32)
     for i, ref in enumerate((squares_1, squares_2)):
         rest = jnp.sum(ref[...], axis=1, keepdims=True)
@@ -389,26 +399,45 @@
             piece = rest.astype(BF16).astype(F32)
             extra = jnp.where(lane == 3 * i + j, piece, extra)
             rest = rest - piece
+    moved = pltpu.roll(extra, 8, 1)
+    rows = [extra[r : r + 1] + moved[r + 1 : r + 2] for r in range(0, 8, 2)]
+    extra = jnp.concatenate(rows, axis=0)
+    ids = ids_ref[...]
     for k in range(1, clusters):
         below = jnp.sum((ids < k).astype(F32), axis=1, keepdims=True)
-        extra = jnp.where(lane == 8 + k, below, extra)
-    message = jnp.concatenate(parts + [extra], axis=1).astype(BF16)
+        extra = jnp.where(lane[:4] == 16 + k, below, extra)
+    top = jnp.concatenate([packed[0], packed[1]], axis=1)
+    message = jnp.concatenate([top, jnp.concatenate([packed[2], extra], axis=1)], axis=0)
+    message = message.astype(BF16)
     for t in range(out_ref.shape[0]):
         out_ref[t] = message
 
 
-def gram_kernel(keep_same, tiles, groups, scalars, g_ref, own_ref, field_ref, gram_ref):
-    tile = scalars[0]
-    group = scalars[2]
+def gram_kernel(keep_same, tiles, groups, g_ref, own_ref, field_ref, gram_ref):
+    tile = lax.axis_index("tiles")
+    group = lax.axis_index("probes")
     clusters = gram_ref.shape[0]
     cell_count = tiles * 2 * LANES
     low = lanes_iota((8, LANES)) < RIM
+    row = rows_iota((8, LANES))
+
+    def twice(x):
+        out = jnp.broadcast_to(x[:1], (8, LANES))
+        for r in range(1, 4):
+            out = jnp.where(row >= 2 * r, jnp.broadcast_to(x[r : r + 1], (8, LANES)), out)
+        return out
+
+    def piece_of(t, p, lower, at):
+        part = g_ref[t, p].astype(F32)
+        return twice(part[4 * lower : 4 * lower + 4, at * LANES : (at + 1) * LANES])
 
     def factor_of(p):
         def add(t, acc):
-            return acc + g_ref[t, p][:, 3 * LANES :].astype(F32)
-
-        sums = lax.fori_loop(0, tiles, add, jnp.zeros((8, LANES), F32), unroll=tiles <= 8)
+            return acc + g_ref[t, p].astype(F32)[4:, LANES:]
+
+        sums = lax.fori_loop(0, tiles, add, jnp.zeros((4, LANES), F32), unroll=tiles <= 8)
+        sums = twice(sums)
+        sums = jnp.where(row % 2 == 0, sums, pltpu.roll(sums, LANES - 8, 1))
         first = jnp.sum(sums[:, :3], axis=1, keepdims=True)
         second = jnp.sum(sums[:, 3:6], axis=1, keepdims=True)
         scale = jnp.sqrt(first / cell_count + F32(1e-06))
@@ -416,21 +445,21 @@
         return F32(1 / SHRINK) / (scale * jnp.sqrt(size * size + F32(1e-06)))
 
     def ids_of(t):
-        starts = g_ref[t, 0][:, 3 * LANES :].astype(F32)
+        starts = piece_of(t, 0, 1, 1)
         cell = lanes_iota((8, 2 * LANES)).astype(F32)
         ids = jnp.zeros(cell.shape, jnp.int32)
         for k in range(1, clusters):
-            ids = ids + (cell >= starts[:, 8 + k : 9 + k]).astype(jnp.int32)
+            ids = ids + (cell >= starts[:, 16 + k : 17 + k]).astype(jnp.int32)
         return [ids[:, :LANES], ids[:, LANES:]]
 
     def field(t, p, ids, own=None):
-        before = g_ref[jnp.maximum(t - 1, 0), p][:, 2 * LANES : 3 * LANES].astype(F32)
-        after = g_ref[jnp.minimum(t + 1, tiles - 1), p][:, 2 * LANES : 3 * LANES].astype(F32)
+        before = piece_of(jnp.maximum(t - 1, 0), p, 1, 0)
+        after = piece_of(jnp.minimum(t + 1, tiles - 1), p, 1, 0)
         if own is None:
-            own = g_ref[t, p][:, : 2 * LANES].astype(F32)
+            own = [piece_of(t, p, 0, at) for at in range(2)]
         parts = [
-            own[:, :LANES] + jnp.where(low & (t > 0), before, F32(0)),
-            own[:, LANES : 2 * LANES] + jnp.where(~low & (t < tiles - 1), after, F32(0)),
+            own[0] + jnp.where(low & (t > 0), before, F32(0)),
+            own[1] + jnp.where(~low & (t < tiles - 1), after, F32(0)),
         ]
         return [
             jnp.where(colour_of(i) if keep_same else ~colour_of(i), part, F32(0))
@@ -441,7 +470,8 @@
     mine_factor = factors[0]
     for p in range(1, groups):
         mine_factor = jnp.where(group == p, factors[p], mine_factor)
-    own = field(tile, group, ids_of(tile), own_ref[...])
+    own = [own_ref[:, at * LANES : (at + 1) * LANES] for at in range(2)]
+    own = field(tile, group, ids_of(tile), own)
     field_ref[:, :LANES] = own[0] * mine_factor
     field_ref[:, LANES:] = own[1] * mine_factor
 
@@ -491,12 +521,15 @@
     hbm = pl.BlockSpec(memory_space=pltpu.HBM)
 
     def call(kernel, name, out_shape, operands, scratch=(), in_specs=None):
-        if in_specs and in_specs[0] is hbm:
-            operands = [pltpu.with_memory_space_constraint(x, pltpu.HBM) for x in operands]
+        in_specs = in_specs or [vmem] * len(operands)
+        operands = [
+            pltpu.with_memory_space_constraint(x, pltpu.HBM) if spec is hbm else x
+            for x, spec in zip(operands, in_specs)
+        ]
         return pl.pallas_call(
             kernel,
             out_shape=out_shape,
-            in_specs=in_specs or [smem] + [vmem] * (len(operands) - 1),
+            in_specs=in_specs,
             out_specs=jax.tree.map(lambda _: vmem, out_shape),
             scratch_shapes=list(scratch),
             compiler_params=params,
@@ -535,25 +568,23 @@
             shaped((pairs, LANES), jnp.int32),
             shaped((slots, padded_order), F32),
             shaped(blocks.shape, BF16),
+            shaped(blocks.shape, BF16),
             shaped((RADIX, refs), BF16),
             shaped((16 * levels, refs), BF16),
             shaped((LANES, refs), BF16),
             shaped((LANES, 2 * padded_order), BF16),
             shaped((2 * padded_order, 3 * LANES), BF16),
         ],
-        [connectivity, basal_map, friction.transpose(2, 0, 1), blocks],
+        [elem_counts, connectivity, basal_map, friction.transpose(2, 0, 1), blocks],
         [
             pltpu.VMEM(connectivity.shape, jnp.int32),
             pltpu.VMEM(basal_map.shape, jnp.int32),
             pltpu.VMEM((3, slots, node_slots), F32),
             pltpu.SemaphoreType.DMA((4,)),
         ],
-        [hbm] * 4,
+        [smem] + [hbm] * 4,
     )
-    scalars = jnp.stack(
-        [lax.axis_index("tiles"), elem_counts[0], lax.axis_index("probes")]
-    ).astype(jnp.int32)
-    conn, node_hot, level_hot = shared[0], shared[4], shared[5]
+    conn, node_hot, level_hot = shared[0], shared[5], shared[6]
 
     edge = shaped((24 * EDGE, RADIX), F32)
     rim = shaped((group_size, LANES), F32)
@@ -572,7 +603,7 @@
             functools.partial(forward_kernel, step, tiles, levels),
             "forward",
             out_shape,
-            [scalars, block, block_a, block_b] + carried + [*shared],
+            [block, block_a, block_b] + carried + [*shared],
             [
                 pltpu.VMEM((16 * pairs, 2 * padded_order), F32),
                 pltpu.VMEM((96 * EDGE, refs), BF16),
@@ -588,12 +619,11 @@
             shaped((8 * pairs, 3 * LANES), F32),
             [ordered, weight, conn, node_hot, level_hot],
             [pltpu.VMEM((48 * (levels - 2 * EDGE), refs), BF16)],
-            [vmem] * 5,
         )
-        operands = [scalars, block_a, block_b, own_a, own_b, new_a, new_b, inner, weight, *shared]
+        operands = [block, block_a, block_b, own_a, own_b, new_a, new_b, inner, weight, *shared]
         if last:
             operands += squares + [cluster_ids.reshape(1, cell_count)]
-            message = shaped((lax.axis_size(everyone), group_size, window + LANES), BF16)
+            message = shaped((lax.axis_size(everyone), group_size, 2 * LANES), BF16)
             out_shape = [whole, message]
         else:
             out_shape = [whole, rim, rim]
@@ -617,7 +647,7 @@
         functools.partial(gram_kernel, POWER % 2 == 1, tiles, groups),
         "gram",
         [field, shaped((tiles, group_size, groups * group_size), F32)],
-        [scalars, gathered, basal],
+        [gathered, basal],
     )
     return (samples, refined.T, gram)
 

time: 91.3 us -> 83.5 us (0.915)
  Pallas kernels: 40.8 us -> 33.9 us
  blocking collectives: 14.4 us -> 11.9 us
  starting transfers between devices: 31 us -> 32.7 us
    pallas_call x12, Pallas kernels: 40.8 us -> 33.9 us  [call(): pl.pallas_call(kernel, out_shape=out_shape, in_specs=in_specs, out_specs=...]
    all_to_all x1, blocking collectives: 14.4 us -> 11.9 us  [shards(): gathered = lax.all_to_all(messages[0], everyone, 0, 0)]
    ppermute x6, starting transfers between devices: 26.6 us -> 28.3 us  [swapped(): lax.ppermute(b, 'tiles', pairs_b)]
  transfers between devices with their start and end apart: 12 -> 12, of which waited for: 2 -> 2; matrix products, arithmetic and copies ran while one was open for 0% -> 0% of each run, Pallas kernels for 17% -> 16%
where the time goes in v7:
time: 83.5 us; the launch traced here: 83.2 us
  Pallas kernels  33.9 us (41%)
  starting transfers between devices  32.7 us (39%)
  blocking collectives  11.9 us (14%)
  waiting for transfers between devices  3.19 us (4%)
  between operations  1.47 us (2%)
    pallas_call x12, Pallas kernels, call(): pl.pallas_call(kernel, out_shape=out_shape, in_specs=in_specs, out_specs=...  33.9 us
    ppermute x6, starting transfers between devices, swapped(): lax.ppermute(b, 'tiles', pairs_b)  28.3 us
    all_to_all x1, blocking collectives, shards(): gathered = lax.all_to_all(messages[0], everyone, 0, 0)  11.9 us
    ppermute x6, starting transfers between devices, swapped(): lax.ppermute(a, 'tiles', pairs_a)  4.42 us
    ppermute x6, waiting for transfers between devices, swapped(): lax.ppermute(b, 'tiles', pairs_b)  3.18 us
  transfers between devices with their start and end apart: 12, of which 2 were waited for; matrix products, arithmetic and copies ran while one was open for 0% of the time, Pallas kernels for 16%

profile of v7, /device:TPU:0, one launch (start us, length us, event | category | flops | bytes accessed | tf_op | source)
XLA Modules:
  0.0 83.2 jit_solution(11519515035826576361)
XLA Ops:
  0.6 0.8 announce.1.refs_0_
  1.4 0.7 collective-permute-start
  2.1 5.8 %collective-permute-start.1 = (f32[16,256]{1,0:T(8,128)S(1)}, f32[16,256]{1,0:T(8,128)S(1)}, u32[]{:S(2)}, u32[]{:S(2)}) collective-permute-start(f32[16,256]{1,0:T(8,128)S(1)} %announce.1.refs_0_), channel_id=1, source_target_pairs={{0,4},{8,12},{16,20},{24,28},{4,0},{12,8},{20,16},{28,24},{1,5},{9... | collective-permute-start | bytes 49160 | tf_op jit(solution)/shard_map/ppermute | solution.py:545
  8.5 5.9 %setup.1 = (s32[32,128]{1,0:T(8,128)S(1)}, s32[32,128]{1,0:T(8,128)S(1)}, f32[64,256]{1,0:T(8,128)S(1)}, bf16[64,192,192]{2,1,0:T(8,128)(2,1)S(1)}, bf16[64,192,...) custom-call(s32[1]{0:T(128)S(6)} %copy.11.counts, ...), custom_call_target="tpu_custom_call" | custom-call | tf_op jit(solution)/shard_map/setup/pallas_call | solution.py:529
  14.5 0.0 collective-permute-done.refs_1_
  14.5 0.0 collective-permute-done.1.refs_2_
  14.5 0.0 copy-start
  14.5 3.0 %forward.3 = (bf16[512,384]{1,0:T(8,128)(2,1)S(1)}, f32[24,512]{1,0:T(8,128)S(1)}, f32[24,512]{1,0:T(8,128)S(1)}) custom-call(f32[16,256]{1,0:T(8,128)S(1)} %announce.1.refs_0_, f32[16,256]{1,0:T(8,128)S(1)} %collective-permute-done.refs_1_, f32[16,256]{1,0:T(8,128)S(1)} %collective-permute-done.1.refs_2_, ...), custom_call_target="tpu_custom_call" | custom-call | tf_op jit(solution)/shard_map/forward/pallas_call | solution.py:529
  17.5 0.7 collective-permute-start.2
  18.2 4.3 %collective-permute-start.3 = (f32[24,512]{1,0:T(8,128)S(1)}, f32[24,512]{1,0:T(8,128)S(1)}, u32[]{:S(2)}, u32[]{:S(2)}) collective-permute-start(f32[24,512]{1,0:T(8,128)S(1)} %get-tuple-element.46.refs_4_), channel_id=1, source_target_pairs={{0,4},{8,12},{16,20},{24,28},{4,0},{12,8},{20,16},{28,24},{1,5},{9... | collective-permute-start | bytes 147464 | tf_op jit(solution)/shard_map/ppermute | solution.py:545
  22.5 0.0 copy-done
  22.5 2.5 %inner.3.refs_7_ = f32[256,384]{1,0:T(8,128)S(1)} custom-call(bf16[512,384]{1,0:T(8,128)(2,1)S(1)} %get-tuple-element.47.ordered_ref, f32[3,4096]{1,0:T(4,128)S(1)} %bitcast.8, s32[32,128]{1,0:T(8,128)S(1)} %get-tuple-element.35.refs_3_.conn_ref.refs_9_.refs_6_, bf16[512,4096]{1,0:T(8,128)(2,1)S(1)} %get-tuple-element.40.refs_8_.node_hot.refs_14_.refs_11_, ...), custom_call_target="tpu_custom_call" | custom-call | tf_op jit(solution)/shard_map/inner/pallas_call | solution.py:529
  25.0 0.0 collective-permute-done.2.refs_5_
  25.0 0.0 collective-permute-done.3.refs_6_
  25.1 2.9 %adjoint.3 = (f32[8,384]{1,0:T(8,128)S(1)}, f32[8,128]{1,0:T(8,128)S(1)}, f32[8,128]{1,0:T(8,128)S(1)}) custom-call(f32[16,256]{1,0:T(8,128)S(1)} %announce.1.refs_0_, f32[16,256]{1,0:T(8,128)S(1)} %collective-permute-done.refs_1_, f32[16,256]{1,0:T(8,128)S(1)} %collective-permute-done.1.refs_2_, f32[24,512]{1,0:T(8,128)S(1)} %get-tuple-element.45.refs_3_, ...), custom_call_target="tpu_custom_call" | custom-call | tf_op jit(solution)/shard_map/adjoint/pallas_call | solution.py:529
  28.0 0.9 %collective-permute-start.4 = (f32[8,128]{1,0:T(8,128)S(1)}, f32[8,128]{1,0:T(8,128)S(1)}, u32[]{:S(2)}, u32[]{:S(2)}) collective-permute-start(f32[8,128]{1,0:T(8,128)S(1)} %get-tuple-element.49), channel_id=1, source_target_pairs={{4,8},{12,16},{20,24},{8,4},{16,12},{24,20},{5,9},{13,17},{21,25},... | collective-permute-start | bytes 12296 | tf_op jit(solution)/shard_map/ppermute | solution.py:545
  28.8 4.4 %collective-permute-start.5 = (f32[8,128]{1,0:T(8,128)S(1)}, f32[8,128]{1,0:T(8,128)S(1)}, u32[]{:S(2)}, u32[]{:S(2)}) collective-permute-start(f32[8,128]{1,0:T(8,128)S(1)} %get-tuple-element.50), channel_id=1, source_target_pairs={{0,4},{8,12},{16,20},{24,28},{4,0},{12,8},{20,16},{28,24},{1,5},{9... | collective-permute-start | bytes 12296 | tf_op jit(solution)/shard_map/ppermute | solution.py:545
  33.2 0.0 collective-permute-done.4.refs_4_
  33.2 1.6 %collective-permute-done.5.refs_5_ = f32[8,128]{1,0:T(8,128)S(1)} collective-permute-done((f32[8,128]{1,0:T(8,128)S(1)}, f32[8,128]{1,0:T(8,128)S(1)}, u32[]{:S(2)}, u32[]{:S(2)}) %collective-permute-start.5) | collective-permute-done | bytes 4128 | tf_op jit(solution)/shard_map/ppermute | solution.py:545
  34.8 3.4 %forward.4 = (bf16[512,384]{1,0:T(8,128)(2,1)S(1)}, f32[24,512]{1,0:T(8,128)S(1)}, f32[24,512]{1,0:T(8,128)S(1)}, f32[8,128]{1,0:T(8,128)S(1)}, f32[8,256]{1,0:T(8,128)}) custom-call(f32[16,256]{1,0:T(8,128)S(1)} %announce.1.refs_0_, f32[16,256]{1,0:T(8,128)S(1)} %collective-permute-done.refs_1_, f32[16,256]{1,0:T(8,128)S(1)} %collective-permute-done.1.refs_2_, ...), custom_call_target="tpu_custom_call" | custom-call | tf_op jit(solution)/shard_map/forward/pallas_call | solution.py:529
  38.2 0.7 collective-permute-start.6
  38.8 4.7 %collective-permute-start.7 = (f32[24,512]{1,0:T(8,128)S(1)}, f32[24,512]{1,0:T(8,128)S(1)}, u32[]{:S(2)}, u32[]{:S(2)}) collective-permute-start(f32[24,512]{1,0:T(8,128)S(1)} %get-tuple-element.53.refs_4_), channel_id=1, source_target_pairs={{0,4},{8,12},{16,20},{24,28},{4,0},{12,8},{20,16},{28,24},{1,5},{9... | collective-permute-start | bytes 147464 | tf_op jit(solution)/shard_map/ppermute | solution.py:545
  43.6 2.5 %inner.4.refs_7_ = f32[256,384]{1,0:T(8,128)S(1)} custom-call(bf16[512,384]{1,0:T(8,128)(2,1)S(1)} %get-tuple-element.54.ordered_ref, f32[3,4096]{1,0:T(4,128)S(1)} %bitcast.10, s32[32,128]{1,0:T(8,128)S(1)} %get-tuple-element.35.refs_3_.conn_ref.refs_9_.refs_6_, bf16[512,4096]{1,0:T(8,128)(2,1)S(1)} %get-tuple-element.40.refs_8_.node_hot.refs_14_.refs_11_, ...), custom_call_target="tpu_custom_call" | custom-call | tf_op jit(solution)/shard_map/inner/pallas_call | solution.py:529
  46.1 0.0 collective-permute-done.6.refs_5_
  46.1 0.0 collective-permute-done.7.refs_6_
  46.1 2.9 %adjoint.4 = (f32[8,384]{1,0:T(8,128)S(1)}, f32[8,128]{1,0:T(8,128)S(1)}, f32[8,128]{1,0:T(8,128)S(1)}) custom-call(f32[16,256]{1,0:T(8,128)S(1)} %announce.1.refs_0_, f32[16,256]{1,0:T(8,128)S(1)} %collective-permute-done.refs_1_, f32[16,256]{1,0:T(8,128)S(1)} %collective-permute-done.1.refs_2_, f32[24,512]{1,0:T(8,128)S(1)} %get-tuple-element.52.refs_3_, ...), custom_call_target="tpu_custom_call" | custom-call | tf_op jit(solution)/shard_map/adjoint/pallas_call | solution.py:529
  49.0 0.7 collective-permute-start.8
  49.7 4.4 %collective-permute-start.9 = (f32[8,128]{1,0:T(8,128)S(1)}, f32[8,128]{1,0:T(8,128)S(1)}, u32[]{:S(2)}, u32[]{:S(2)}) collective-permute-start(f32[8,128]{1,0:T(8,128)S(1)} %get-tuple-element.57), channel_id=1, source_target_pairs={{0,4},{8,12},{16,20},{24,28},{4,0},{12,8},{20,16},{28,24},{1,5},{9... | collective-permute-start | bytes 12296 | tf_op jit(solution)/shard_map/ppermute | solution.py:545
  54.1 0.0 collective-permute-done.8.refs_4_
  54.1 1.6 %collective-permute-done.9.refs_5_ = f32[8,128]{1,0:T(8,128)S(1)} collective-permute-done((f32[8,128]{1,0:T(8,128)S(1)}, f32[8,128]{1,0:T(8,128)S(1)}, u32[]{:S(2)}, u32[]{:S(2)}) %collective-permute-start.9) | collective-permute-done | bytes 4128 | tf_op jit(solution)/shard_map/ppermute | solution.py:545
  55.6 0.0 copy-start.1
  55.7 3.0 %forward.5 = (bf16[512,384]{1,0:T(8,128)(2,1)S(1)}, f32[24,512]{1,0:T(8,128)S(1)}, f32[24,512]{1,0:T(8,128)S(1)}, f32[8,128]{1,0:T(8,128)S(1)}) custom-call(f32[16,256]{1,0:T(8,128)S(1)} %announce.1.refs_0_, f32[16,256]{1,0:T(8,128)S(1)} %collective-permute-done.refs_1_, f32[16,256]{1,0:T(8,128)S(1)} %collective-permute-done.1.refs_2_, ...), custom_call_target="tpu_custom_call" | custom-call | tf_op jit(solution)/shard_map/forward/pallas_call | solution.py:529
  58.6 0.9 %collective-permute-start.10 = (f32[24,512]{1,0:T(8,128)S(1)}, f32[24,512]{1,0:T(8,128)S(1)}, u32[]{:S(2)}, u32[]{:S(2)}) collective-permute-start(f32[24,512]{1,0:T(8,128)S(1)} %get-tuple-element.58.refs_3_), channel_id=1, source_target_pairs={{4,8},{12,16},{20,24},{8,4},{16,12},{24,20},{5,9},{13,17},{21,25},... | collective-permute-start | bytes 147464 | tf_op jit(solution)/shard_map/ppermute | solution.py:545
  59.5 4.7 %collective-permute-start.11 = (f32[24,512]{1,0:T(8,128)S(1)}, f32[24,512]{1,0:T(8,128)S(1)}, u32[]{:S(2)}, u32[]{:S(2)}) collective-permute-start(f32[24,512]{1,0:T(8,128)S(1)} %get-tuple-element.59.refs_4_), channel_id=1, source_target_pairs={{0,4},{8,12},{16,20},{24,28},{4,0},{12,8},{20,16},{28,24},{1,5},{9... | collective-permute-start | bytes 147464 | tf_op jit(solution)/shard_map/ppermute | solution.py:545
  64.3 2.5 %inner.5.refs_7_ = f32[256,384]{1,0:T(8,128)S(1)} custom-call(bf16[512,384]{1,0:T(8,128)(2,1)S(1)} %get-tuple-element.60.ordered_ref, f32[3,4096]{1,0:T(4,128)S(1)} %bitcast.12, s32[32,128]{1,0:T(8,128)S(1)} %get-tuple-element.35.refs_3_.conn_ref.refs_9_.refs_6_, bf16[512,4096]{1,0:T(8,128)(2,1)S(1)} %get-tuple-element.40.refs_8_.node_hot.refs_14_.refs_11_, ...), custom_call_target="tpu_custom_call" | custom-call | tf_op jit(solution)/shard_map/inner/pallas_call | solution.py:529
  66.8 0.0 collective-permute-done.10.refs_5_
  66.8 0.0 collective-permute-done.11.refs_6_
  66.8 0.0 copy-done.1
  66.8 2.9 %adjoint.5 = (f32[8,384]{1,0:T(8,128)S(1)}, bf16[32,8,256]{2,1,0:T(8,128)(2,1)S(1)}) custom-call(f32[16,256]{1,0:T(8,128)S(1)} %announce.1.refs_0_, f32[16,256]{1,0:T(8,128)S(1)} %collective-permute-done.refs_1_, f32[16,256]{1,0:T(8,128)S(1)} %collective-permute-done.1.refs_2_, f32[24,512]{1,0:T(8,128)S(1)} %get-tuple-element.58.refs_3_, ...), custom_call_target="tpu_custom_call" | custom-call | tf_op jit(solution)/shard_map/adjoint/pallas_call | solution.py:529
  69.8 11.9 %all_to_all.5 = bf16[32,8,256]{2,1,0:T(8,128)(2,1)S(1)} all-to-all(bf16[32,8,256]{2,1,0:T(8,128)(2,1)S(1)} %get-tuple-element.63), channel_id=1, replica_groups=mesh['tiles'=8,'probes'=4] {'tiles','probes'}, dimensions={0} | all-to-all | bytes 262144 | tf_op jit(solution)/shard_map/all_to_all | solution.py:644
  81.7 1.5 %gram.1 = (f32[8,256]{1,0:T(8,128)}, f32[8,8,32]{2,1,0:T(8,128)}) custom-call(bf16[8,4,8,256]{3,2,1,0:T(8,128)(2,1)S(1)} %bitcast.14, f32[8,384]{1,0:T(8,128)S(1)} %get-tuple-element.64.own_ref), custom_call_target="tpu_custom_call" | custom-call | tf_op jit(solution)/shard_map/gram/pallas_call | solution.py:529
Async XLA Ops:
  1.4 13.1 %collective-permute-start = (f32[16,256]{1,0:T(8,128)S(1)}, f32[16,256]{1,0:T(8,128)S(1)}, u32[]{:S(2)}, u32[]{:S(2)}) collective-permute-start(f32[16,256]{1,0:T(8,128)S(1)} %announce.1.refs_0_), channel_id=1, source_target_pairs={{4,8},{12,16},{20,24},{8,4},{16,12},{24,20},{5,9},{13,17},{21,25},... | collective-permute-start | bytes 49160 | tf_op jit(solution)/shard_map/ppermute | solution.py:545
  2.1 12.4 %collective-permute-start.1 = (f32[16,256]{1,0:T(8,128)S(1)}, f32[16,256]{1,0:T(8,128)S(1)}, u32[]{:S(2)}, u32[]{:S(2)}) collective-permute-start(f32[16,256]{1,0:T(8,128)S(1)} %announce.1.refs_0_), channel_id=1, source_target_pairs={{0,4},{8,12},{16,20},{24,28},{4,0},{12,8},{20,16},{28,24},{1,5},{9... | collective-permute-start | bytes 49160 | tf_op jit(solution)/shard_map/ppermute | solution.py:545
  14.5 8.0 %copy-start = (f32[4096,3]{0,1:T(4,128)S(1)}, f32[4096,3]{0,1:T(4,128)}, u32[]{:S(2)}) copy-start(f32[4096,3]{0,1:T(4,128)} %param.13) | copy-start | bytes 147460
  17.5 7.5 %collective-permute-start.2 = (f32[24,512]{1,0:T(8,128)S(1)}, f32[24,512]{1,0:T(8,128)S(1)}, u32[]{:S(2)}, u32[]{:S(2)}) collective-permute-start(f32[24,512]{1,0:T(8,128)S(1)} %get-tuple-element.45.refs_3_), channel_id=1, source_target_pairs={{4,8},{12,16},{20,24},{8,4},{16,12},{24,20},{5,9},{13,17},{21,25},... | collective-permute-start | bytes 147464 | tf_op jit(solution)/shard_map/ppermute | solution.py:545
  18.2 6.9 %collective-permute-start.3 = (f32[24,512]{1,0:T(8,128)S(1)}, f32[24,512]{1,0:T(8,128)S(1)}, u32[]{:S(2)}, u32[]{:S(2)}) collective-permute-start(f32[24,512]{1,0:T(8,128)S(1)} %get-tuple-element.46.refs_4_), channel_id=1, source_target_pairs={{0,4},{8,12},{16,20},{24,28},{4,0},{12,8},{20,16},{28,24},{1,5},{9... | collective-permute-start | bytes 147464 | tf_op jit(solution)/shard_map/ppermute | solution.py:545
  28.0 5.2 %collective-permute-start.4 = (f32[8,128]{1,0:T(8,128)S(1)}, f32[8,128]{1,0:T(8,128)S(1)}, u32[]{:S(2)}, u32[]{:S(2)}) collective-permute-start(f32[8,128]{1,0:T(8,128)S(1)} %get-tuple-element.49), channel_id=1, source_target_pairs={{4,8},{12,16},{20,24},{8,4},{16,12},{24,20},{5,9},{13,17},{21,25},... | collective-permute-start | bytes 12296 | tf_op jit(solution)/shard_map/ppermute | solution.py:545
  28.8 5.9 %collective-permute-start.5 = (f32[8,128]{1,0:T(8,128)S(1)}, f32[8,128]{1,0:T(8,128)S(1)}, u32[]{:S(2)}, u32[]{:S(2)}) collective-permute-start(f32[8,128]{1,0:T(8,128)S(1)} %get-tuple-element.50), channel_id=1, source_target_pairs={{0,4},{8,12},{16,20},{24,28},{4,0},{12,8},{20,16},{28,24},{1,5},{9... | collective-permute-start | bytes 12296 | tf_op jit(solution)/shard_map/ppermute | solution.py:545
  38.2 7.9 %collective-permute-start.6 = (f32[24,512]{1,0:T(8,128)S(1)}, f32[24,512]{1,0:T(8,128)S(1)}, u32[]{:S(2)}, u32[]{:S(2)}) collective-permute-start(f32[24,512]{1,0:T(8,128)S(1)} %get-tuple-element.52.refs_3_), channel_id=1, source_target_pairs={{4,8},{12,16},{20,24},{8,4},{16,12},{24,20},{5,9},{13,17},{21,25},... | collective-permute-start | bytes 147464 | tf_op jit(solution)/shard_map/ppermute | solution.py:545
  38.8 7.3 %collective-permute-start.7 = (f32[24,512]{1,0:T(8,128)S(1)}, f32[24,512]{1,0:T(8,128)S(1)}, u32[]{:S(2)}, u32[]{:S(2)}) collective-permute-start(f32[24,512]{1,0:T(8,128)S(1)} %get-tuple-element.53.refs_4_), channel_id=1, source_target_pairs={{0,4},{8,12},{16,20},{24,28},{4,0},{12,8},{20,16},{28,24},{1,5},{9... | collective-permute-start | bytes 147464 | tf_op jit(solution)/shard_map/ppermute | solution.py:545
  49.0 5.1 %collective-permute-start.8 = (f32[8,128]{1,0:T(8,128)S(1)}, f32[8,128]{1,0:T(8,128)S(1)}, u32[]{:S(2)}, u32[]{:S(2)}) collective-permute-start(f32[8,128]{1,0:T(8,128)S(1)} %get-tuple-element.56), channel_id=1, source_target_pairs={{4,8},{12,16},{20,24},{8,4},{16,12},{24,20},{5,9},{13,17},{21,25},... | collective-permute-start | bytes 12296 | tf_op jit(solution)/shard_map/ppermute | solution.py:545
  49.7 5.9 %collective-permute-start.9 = (f32[8,128]{1,0:T(8,128)S(1)}, f32[8,128]{1,0:T(8,128)S(1)}, u32[]{:S(2)}, u32[]{:S(2)}) collective-permute-start(f32[8,128]{1,0:T(8,128)S(1)} %get-tuple-element.57), channel_id=1, source_target_pairs={{0,4},{8,12},{16,20},{24,28},{4,0},{12,8},{20,16},{28,24},{1,5},{9... | collective-permute-start | bytes 12296 | tf_op jit(solution)/shard_map/ppermute | solution.py:545
  55.6 11.2 %copy-start.1 = (s32[256]{0:T(256)S(1)}, s32[256]{0:T(256)}, u32[]{:S(2)}) copy-start(s32[256]{0:T(256)} %param.15) | copy-start | bytes 3076
  58.6 8.1 %collective-permute-start.10 = (f32[24,512]{1,0:T(8,128)S(1)}, f32[24,512]{1,0:T(8,128)S(1)}, u32[]{:S(2)}, u32[]{:S(2)}) collective-permute-start(f32[24,512]{1,0:T(8,128)S(1)} %get-tuple-element.58.refs_3_), channel_id=1, source_target_pairs={{4,8},{12,16},{20,24},{8,4},{16,12},{24,20},{5,9},{13,17},{21,25},... | collective-permute-start | bytes 147464 | tf_op jit(solution)/shard_map/ppermute | solution.py:545
  59.5 7.3 %collective-permute-start.11 = (f32[24,512]{1,0:T(8,128)S(1)}, f32[24,512]{1,0:T(8,128)S(1)}, u32[]{:S(2)}, u32[]{:S(2)}) collective-permute-start(f32[24,512]{1,0:T(8,128)S(1)} %get-tuple-element.59.refs_4_), channel_id=1, source_target_pairs={{0,4},{8,12},{16,20},{24,28},{4,0},{12,8},{20,16},{28,24},{1,5},{9... | collective-permute-start | bytes 147464 | tf_op jit(solution)/shard_map/ppermute | solution.py:545

commit v8 on v7

--- a/solution.py
+++ b/solution.py
@@ -189,7 +189,7 @@
     block_ref, block_a, block_b, *refs = refs
     first = step == 0
     if not first:
-        basal_ref, rim_a, rim_b, *refs = refs
+        basal_ref, rims, *refs = refs
     conn_ref, cell_ref, fr_ref, _, turned, node_hot, level_hot, cell_hot, *refs = refs
     spread_ref, order_ref, *refs = refs
     ordered_ref, a_ref, b_ref, *refs = refs
@@ -215,7 +215,7 @@
     if first:
         parts = starts
     else:
-        after, before = by_side(tile, rim_a[...], rim_b[...])
+        after, before = by_side(tile, rims[8:, :], rims[:8, :])
         parts = [basal_ref[:, i * LANES : (i + 1) * LANES] for i in range(3)]
         parts[0] = parts[0] + jnp.where(low, before, F32(0))
         parts[1] = parts[1] + jnp.where(low, F32(0), after)
@@ -282,11 +282,10 @@
         a_ref[8 * i : 8 * i + 8, :], b_ref[8 * i : 8 * i + 8, :] = to_swaps(tile, spill, lead)
 
 
-def inner_kernel(
-    levels, ordered_ref, weight_ref, conn_ref, node_hot, level_hot, picked_ref, v_ref
+def inner_scatter_kernel(
+    levels, ordered_ref, weight_ref, node_hot, level_hot, weighted_ref, v_ref
 ):
-    pairs = conn_ref.shape[0]
-    conn = conn_ref[...]
+    pairs = v_ref.shape[1] // LANES
     inside = list(range(EDGE, levels - EDGE))
     spread_levels(v_ref, ordered_ref, level_hot, inside, pairs)
     nodes = dot_nt(v_ref[...], node_hot[...])
@@ -295,7 +294,14 @@
         value = nodes[16 * i : 16 * i + 8] + nodes[16 * i + 8 : 16 * i + 16]
         at = inside[i // 3] * RADIX
         rows.append(value * weight_ref[i % 3 : i % 3 + 1, at : at + RADIX])
-    weighted = jnp.concatenate(rows, axis=0).astype(BF16)
+    weighted_ref[...] = jnp.concatenate(rows, axis=0).astype(BF16)
+
+
+def inner_gather_kernel(levels, weighted_ref, conn_ref, node_hot, picked_ref):
+    pairs = conn_ref.shape[0]
+    conn = conn_ref[...]
+    inside = list(range(EDGE, levels - EDGE))
+    weighted = weighted_ref[...]
     step = 2
     for start in range(0, pairs, step):
         found = dot(weighted, node_hot[:, start * LANES : (start + step) * LANES])
@@ -311,7 +317,7 @@
 
 
 def adjoint_kernel(last, clusters, levels, *refs):
-    block_ref, block_a, block_b, own_a, own_b, new_a, new_b, inner_ref, weight_ref, *refs = refs
+    block_ref, block_a, block_b, own_a, own_b, new, inner_ref, weight_ref, *refs = refs
     conn_ref, cell_ref, fr_ref, blocks, _, node_hot, _, cell_hot, *refs = refs
     spread_ref, order_ref, *refs = refs
     if last:
@@ -325,7 +331,7 @@
     pairs = blocks.shape[0] // 2
     tile = lax.axis_index("tiles")
 
-    spill, lead = by_side(tile, own_a[...] + new_a[...], own_b[...] + new_b[...])
+    spill, lead = by_side(tile, own_a[...] + new[24 * EDGE :, :], own_b[...] + new[: 24 * EDGE, :])
     after, before = by_side(tile, block_a[...], block_b[...])
     rows = [lead[8 * c : 8 * c + 8] * weight_ref[c : c + 1, :HALO] for c in range(3)]
     for c in range(3):
@@ -544,6 +550,15 @@
     def swapped(a, b):
         return lax.ppermute(a, "tiles", pairs_a), lax.ppermute(b, "tiles", pairs_b)
 
+    relay = [(i, i + 2) for i in range(1, tiles - 2, 2)]
+    relay += [(i, i - 2) for i in range(2, tiles, 2)]
+
+    def passed(far):
+        return lax.ppermute(far, "tiles", relay)
+
+    def arrived(near, far):
+        return lax.ppermute(jnp.concatenate([near, far], axis=0), "tiles", pairs_b)
+
     weight = obs_weight.T
     block = call(
         announce_kernel,
@@ -612,15 +627,23 @@
         squares += extra[:1]
         if step == 1:
             samples = extra[1].T
-        new_a, new_b = swapped(own_a, own_b)
-        inner = call(
-            functools.partial(inner_kernel, levels),
-            "inner",
-            shaped((8 * pairs, 3 * LANES), F32),
-            [ordered, weight, conn, node_hot, level_hot],
+        far = passed(own_a)
+        weighted = call(
+            functools.partial(inner_scatter_kernel, levels),
+            "inner_scatter",
+            shaped((24 * (levels - 2 * EDGE), RADIX), BF16),
+            [ordered, weight, node_hot, level_hot],
             [pltpu.VMEM((48 * (levels - 2 * EDGE), refs), BF16)],
         )
-        operands = [block, block_a, block_b, own_a, own_b, new_a, new_b, inner, weight, *shared]
+        far, weighted = lax.optimization_barrier((far, weighted))
+        new = arrived(own_b, far)
+        inner = call(
+            functools.partial(inner_gather_kernel, levels),
+            "inner_gather",
+            shaped((8 * pairs, 3 * LANES), F32),
+            [weighted, conn, node_hot],
+        )
+        operands = [block, block_a, block_b, own_a, own_b, new, inner, weight, *shared]
         if last:
             operands += squares + [cluster_ids.reshape(1, cell_count)]
             message = shaped((lax.axis_size(everyone), group_size, 2 * LANES), BF16)
@@ -639,7 +662,7 @@
             ],
         )
         if not last:
-            carried = [basal, *swapped(*messages)]
+            carried = [basal, arrived(messages[1], passed(messages[0]))]
 
     gathered = lax.all_to_all(messages[0], everyone, 0, 0)
     gathered = gathered.reshape(tiles, groups, *gathered.shape[1:])

time: 83.5 us -> 97.6 us (1.17)
  waiting for transfers between devices: 3.19 us -> 35.4 us
  starting transfers between devices: 32.7 us -> 13.6 us
    ppermute x0 -> x10, waiting for transfers between devices: none -> 35.4 us  [the longest x5 18.3 us: arrived(): return lax.ppermute(jnp.concatenate([near, far], axis=0), 'tiles', pairs_b)]
    ppermute x6 -> x1, starting transfers between devices: 28.3 us -> 5.8 us  [swapped(): lax.ppermute(b, 'tiles', pairs_b)]
    ppermute x0 -> x10, starting transfers between devices: none -> 7.12 us  [the longest x5 6.9 us: passed(): return lax.ppermute(far, 'tiles', relay)]
    ppermute x6 -> x1, starting transfers between devices: 4.42 us -> 0.66 us  [swapped(): lax.ppermute(a, 'tiles', pairs_a)]
    ppermute x6 -> x1, waiting for transfers between devices: 3.18 us -> 0.01 us  [swapped(): lax.ppermute(b, 'tiles', pairs_b)]
    pallas_call x12 -> x15, Pallas kernels: 33.9 us -> 34 us  [call(): pl.pallas_call(kernel, out_shape=out_shape, in_specs=in_specs, out_specs=...]
  transfers between devices with their start and end apart: 12 -> 12, of which waited for: 2 -> 10; matrix products, arithmetic and copies ran while one was open for 0% -> 0% of each run, Pallas kernels for 16% -> 14%
where the time goes in v8:
time: 97.6 us; the launch traced here: 97.2 us
  waiting for transfers between devices  35.4 us (36%)
  Pallas kernels  34 us (35%)
  starting transfers between devices  13.6 us (14%)
  blocking collectives  12.8 us (13%)
  between operations  1.48 us (2%)
    pallas_call x15, Pallas kernels, call(): pl.pallas_call(kernel, out_shape=out_shape, in_specs=in_specs, out_specs=...  34 us
    ppermute x5, waiting for transfers between devices, arrived(): return lax.ppermute(jnp.concatenate([near, far], axis=0), 'tiles', pairs_b)  18.3 us
    ppermute x5, waiting for transfers between devices, passed(): return lax.ppermute(far, 'tiles', relay)  17.1 us
    all_to_all x1, blocking collectives, shards(): gathered = lax.all_to_all(messages[0], everyone, 0, 0)  12.8 us
    ppermute x5, starting transfers between devices, passed(): return lax.ppermute(far, 'tiles', relay)  6.9 us
    ppermute x1, starting transfers between devices, swapped(): lax.ppermute(b, 'tiles', pairs_b)  5.8 us
  transfers between devices with their start and end apart: 12, of which 10 were waited for; matrix products, arithmetic and copies ran while one was open for 0% of the time, Pallas kernels for 14%

profile of v8, /device:TPU:0, one launch (start us, length us, event | category | flops | bytes accessed | tf_op | source)
XLA Modules:
  0.0 97.2 jit_solution(15623768227186688858)
XLA Ops:
  0.6 0.8 announce.1.refs_0_
  1.4 0.7 collective-permute-start
  2.1 5.8 %collective-permute-start.1 = (f32[16,256]{1,0:T(8,128)S(1)}, f32[16,256]{1,0:T(8,128)S(1)}, u32[]{:S(2)}, u32[]{:S(2)}) collective-permute-start(f32[16,256]{1,0:T(8,128)S(1)} %announce.1.refs_0_), channel_id=1, source_target_pairs={{0,4},{8,12},{16,20},{24,28},{4,0},{12,8},{20,16},{28,24},{1,5},{9... | collective-permute-start | bytes 49160 | tf_op jit(solution)/shard_map/ppermute | solution.py:551
  8.5 5.9 %setup.1 = (s32[32,128]{1,0:T(8,128)S(1)}, s32[32,128]{1,0:T(8,128)S(1)}, f32[64,256]{1,0:T(8,128)S(1)}, bf16[64,192,192]{2,1,0:T(8,128)(2,1)S(1)}, bf16[64,192,...) custom-call(s32[1]{0:T(128)S(6)} %copy.11.counts, ...), custom_call_target="tpu_custom_call" | custom-call | tf_op jit(solution)/shard_map/setup/pallas_call | solution.py:535
  14.5 0.0 collective-permute-done.refs_1_
  14.5 0.0 collective-permute-done.1.refs_2_
  14.5 0.0 copy-start
  14.5 3.0 %forward.3 = (bf16[512,384]{1,0:T(8,128)(2,1)S(1)}, f32[24,512]{1,0:T(8,128)S(1)}, f32[24,512]{1,0:T(8,128)S(1)}) custom-call(f32[16,256]{1,0:T(8,128)S(1)} %announce.1.refs_0_, f32[16,256]{1,0:T(8,128)S(1)} %collective-permute-done.refs_1_, f32[16,256]{1,0:T(8,128)S(1)} %collective-permute-done.1.refs_2_, ...), custom_call_target="tpu_custom_call" | custom-call | tf_op jit(solution)/shard_map/forward/pallas_call | solution.py:535
  17.5 1.3 %collective-permute-start.2 = (f32[24,512]{1,0:T(8,128)S(1)}, f32[24,512]{1,0:T(8,128)S(1)}, u32[]{:S(2)}, u32[]{:S(2)}) collective-permute-start(f32[24,512]{1,0:T(8,128)S(1)} %get-tuple-element.51.refs_3_), channel_id=1, source_target_pairs={{4,12},{12,20},{20,28},{8,0},{16,8},{24,16},{5,13},{13,21},{21,29}... | collective-permute-start | bytes 147464 | tf_op jit(solution)/shard_map/ppermute | solution.py:557
  18.8 0.0 copy-done
  18.8 1.7 %inner_scatter.3.weighted_ref = bf16[168,512]{1,0:T(8,128)(2,1)S(1)} custom-call(bf16[512,384]{1,0:T(8,128)(2,1)S(1)} %get-tuple-element.53.ordered_ref, f32[3,4096]{1,0:T(4,128)S(1)} %bitcast.8, bf16[512,4096]{1,0:T(8,128)(2,1)S(1)} %get-tuple-element.46.refs_8_.node_hot.refs_13_.refs_10_, ...), custom_call_target="tpu_custom_call" | custom-call | tf_op jit(solution)/shard_map/inner_scatter/pallas_call | solution.py:535
  20.5 3.0 %collective-permute-done.2 = f32[24,512]{1,0:T(8,128)S(1)} collective-permute-done((f32[24,512]{1,0:T(8,128)S(1)}, f32[24,512]{1,0:T(8,128)S(1)}, u32[]{:S(2)}, u32[]{:S(2)}) %collective-permute-start.2) | collective-permute-done | bytes 49184 | tf_op jit(solution)/shard_map/ppermute | solution.py:557
  23.5 0.1 collective-permute-start.3
  23.6 0.9 inner_gather.3.refs_6_
  24.5 3.7 %collective-permute-done.3.refs_5_ = f32[48,512]{1,0:T(8,128)S(1)} collective-permute-done((f32[48,512]{1,0:T(8,128)S(1)}, f32[48,512]{1,0:T(8,128)S(1)}, u32[]{:S(2)}, u32[]{:S(2)}) %collective-permute-start.3) | collective-permute-done | bytes 98336 | tf_op jit(solution)/shard_map/ppermute | solution.py:560
  28.2 2.9 %adjoint.3 = (f32[8,384]{1,0:T(8,128)S(1)}, f32[8,128]{1,0:T(8,128)S(1)}, f32[8,128]{1,0:T(8,128)S(1)}) custom-call(f32[16,256]{1,0:T(8,128)S(1)} %announce.1.refs_0_, f32[16,256]{1,0:T(8,128)S(1)} %collective-permute-done.refs_1_, f32[16,256]{1,0:T(8,128)S(1)} %collective-permute-done.1.refs_2_, f32[24,512]{1,0:T(8,128)S(1)} %get-tuple-element.51.refs_3_, ...), custom_call_target="tpu_custom_call" | custom-call | tf_op jit(solution)/shard_map/adjoint/pallas_call | solution.py:535
  31.1 1.5 %collective-permute-start.4 = (f32[8,128]{1,0:T(8,128)S(1)}, f32[8,128]{1,0:T(8,128)S(1)}, u32[]{:S(2)}, u32[]{:S(2)}) collective-permute-start(f32[8,128]{1,0:T(8,128)S(1)} %get-tuple-element.58), channel_id=1, source_target_pairs={{4,12},{12,20},{20,28},{8,0},{16,8},{24,16},{5,13},{13,21},{21,29}... | collective-permute-start | bytes 12296 | tf_op jit(solution)/shard_map/ppermute | solution.py:557
  32.6 4.0 %collective-permute-done.4 = f32[8,128]{1,0:T(8,128)S(1)} collective-permute-done((f32[8,128]{1,0:T(8,128)S(1)}, f32[8,128]{1,0:T(8,128)S(1)}, u32[]{:S(2)}, u32[]{:S(2)}) %collective-permute-start.4) | collective-permute-done | bytes 4128 | tf_op jit(solution)/shard_map/ppermute | solution.py:557
  36.6 0.0 collective-permute-start.5
  36.6 3.6 %collective-permute-done.5.refs_4_ = f32[16,128]{1,0:T(8,128)S(1)} collective-permute-done((f32[16,128]{1,0:T(8,128)S(1)}, f32[16,128]{1,0:T(8,128)S(1)}, u32[]{:S(2)}, u32[]{:S(2)}) %collective-permute-start.5) | collective-permute-done | bytes 8224 | tf_op jit(solution)/shard_map/ppermute | solution.py:560
  40.2 3.4 %forward.4 = (bf16[512,384]{1,0:T(8,128)(2,1)S(1)}, f32[24,512]{1,0:T(8,128)S(1)}, f32[24,512]{1,0:T(8,128)S(1)}, f32[8,128]{1,0:T(8,128)S(1)}, f32[8,256]{1,0:T(8,128)}) custom-call(f32[16,256]{1,0:T(8,128)S(1)} %announce.1.refs_0_, f32[16,256]{1,0:T(8,128)S(1)} %collective-permute-done.refs_1_, f32[16,256]{1,0:T(8,128)S(1)} %collective-permute-done.1.refs_2_, ...), custom_call_target="tpu_custom_call" | custom-call | tf_op jit(solution)/shard_map/forward/pallas_call | solution.py:535
  43.6 1.3 %collective-permute-start.6 = (f32[24,512]{1,0:T(8,128)S(1)}, f32[24,512]{1,0:T(8,128)S(1)}, u32[]{:S(2)}, u32[]{:S(2)}) collective-permute-start(f32[24,512]{1,0:T(8,128)S(1)} %get-tuple-element.60.refs_3_), channel_id=1, source_target_pairs={{4,12},{12,20},{20,28},{8,0},{16,8},{24,16},{5,13},{13,21},{21,29}... | collective-permute-start | bytes 147464 | tf_op jit(solution)/shard_map/ppermute | solution.py:557
  44.9 1.7 %inner_scatter.4.weighted_ref = bf16[168,512]{1,0:T(8,128)(2,1)S(1)} custom-call(bf16[512,384]{1,0:T(8,128)(2,1)S(1)} %get-tuple-element.62.ordered_ref, f32[3,4096]{1,0:T(4,128)S(1)} %bitcast.10, bf16[512,4096]{1,0:T(8,128)(2,1)S(1)} %get-tuple-element.46.refs_8_.node_hot.refs_13_.refs_10_, ...), custom_call_target="tpu_custom_call" | custom-call | tf_op jit(solution)/shard_map/inner_scatter/pallas_call | solution.py:535
  46.6 3.0 %collective-permute-done.6 = f32[24,512]{1,0:T(8,128)S(1)} collective-permute-done((f32[24,512]{1,0:T(8,128)S(1)}, f32[24,512]{1,0:T(8,128)S(1)}, u32[]{:S(2)}, u32[]{:S(2)}) %collective-permute-start.6) | collective-permute-done | bytes 49184 | tf_op jit(solution)/shard_map/ppermute | solution.py:557
  49.6 0.1 collective-permute-start.7
  49.7 0.9 inner_gather.4.refs_6_
  50.6 3.7 %collective-permute-done.7.refs_5_ = f32[48,512]{1,0:T(8,128)S(1)} collective-permute-done((f32[48,512]{1,0:T(8,128)S(1)}, f32[48,512]{1,0:T(8,128)S(1)}, u32[]{:S(2)}, u32[]{:S(2)}) %collective-permute-start.7) | collective-permute-done | bytes 98336 | tf_op jit(solution)/shard_map/ppermute | solution.py:560
  54.3 2.9 %adjoint.4 = (f32[8,384]{1,0:T(8,128)S(1)}, f32[8,128]{1,0:T(8,128)S(1)}, f32[8,128]{1,0:T(8,128)S(1)}) custom-call(f32[16,256]{1,0:T(8,128)S(1)} %announce.1.refs_0_, f32[16,256]{1,0:T(8,128)S(1)} %collective-permute-done.refs_1_, f32[16,256]{1,0:T(8,128)S(1)} %collective-permute-done.1.refs_2_, f32[24,512]{1,0:T(8,128)S(1)} %get-tuple-element.60.refs_3_, ...), custom_call_target="tpu_custom_call" | custom-call | tf_op jit(solution)/shard_map/adjoint/pallas_call | solution.py:535
  57.2 1.3 %collective-permute-start.8 = (f32[8,128]{1,0:T(8,128)S(1)}, f32[8,128]{1,0:T(8,128)S(1)}, u32[]{:S(2)}, u32[]{:S(2)}) collective-permute-start(f32[8,128]{1,0:T(8,128)S(1)} %get-tuple-element.67), channel_id=1, source_target_pairs={{4,12},{12,20},{20,28},{8,0},{16,8},{24,16},{5,13},{13,21},{21,29}... | collective-permute-start | bytes 12296 | tf_op jit(solution)/shard_map/ppermute | solution.py:557
  58.5 4.2 %collective-permute-done.8 = f32[8,128]{1,0:T(8,128)S(1)} collective-permute-done((f32[8,128]{1,0:T(8,128)S(1)}, f32[8,128]{1,0:T(8,128)S(1)}, u32[]{:S(2)}, u32[]{:S(2)}) %collective-permute-start.8) | collective-permute-done | bytes 4128 | tf_op jit(solution)/shard_map/ppermute | solution.py:557
  62.7 0.0 collective-permute-start.9
  62.7 3.6 %collective-permute-done.9.refs_4_ = f32[16,128]{1,0:T(8,128)S(1)} collective-permute-done((f32[16,128]{1,0:T(8,128)S(1)}, f32[16,128]{1,0:T(8,128)S(1)}, u32[]{:S(2)}, u32[]{:S(2)}) %collective-permute-start.9) | collective-permute-done | bytes 8224 | tf_op jit(solution)/shard_map/ppermute | solution.py:560
  66.3 3.0 %forward.5 = (bf16[512,384]{1,0:T(8,128)(2,1)S(1)}, f32[24,512]{1,0:T(8,128)S(1)}, f32[24,512]{1,0:T(8,128)S(1)}, f32[8,128]{1,0:T(8,128)S(1)}) custom-call(f32[16,256]{1,0:T(8,128)S(1)} %announce.1.refs_0_, f32[16,256]{1,0:T(8,128)S(1)} %collective-permute-done.refs_1_, f32[16,256]{1,0:T(8,128)S(1)} %collective-permute-done.1.refs_2_, ...), custom_call_target="tpu_custom_call" | custom-call | tf_op jit(solution)/shard_map/forward/pallas_call | solution.py:535
  69.3 0.0 copy-start.1
  69.3 1.5 %collective-permute-start.10 = (f32[24,512]{1,0:T(8,128)S(1)}, f32[24,512]{1,0:T(8,128)S(1)}, u32[]{:S(2)}, u32[]{:S(2)}) collective-permute-start(f32[24,512]{1,0:T(8,128)S(1)} %get-tuple-element.68.refs_3_), channel_id=1, source_target_pairs={{4,12},{12,20},{20,28},{8,0},{16,8},{24,16},{5,13},{13,21},{21,29}... | collective-permute-start | bytes 147464 | tf_op jit(solution)/shard_map/ppermute | solution.py:557
  70.9 1.7 %inner_scatter.5.weighted_ref = bf16[168,512]{1,0:T(8,128)(2,1)S(1)} custom-call(bf16[512,384]{1,0:T(8,128)(2,1)S(1)} %get-tuple-element.70.ordered_ref, f32[3,4096]{1,0:T(4,128)S(1)} %bitcast.12, bf16[512,4096]{1,0:T(8,128)(2,1)S(1)} %get-tuple-element.46.refs_8_.node_hot.refs_13_.refs_10_, ...), custom_call_target="tpu_custom_call" | custom-call | tf_op jit(solution)/shard_map/inner_scatter/pallas_call | solution.py:535
  72.5 2.8 %collective-permute-done.10 = f32[24,512]{1,0:T(8,128)S(1)} collective-permute-done((f32[24,512]{1,0:T(8,128)S(1)}, f32[24,512]{1,0:T(8,128)S(1)}, u32[]{:S(2)}, u32[]{:S(2)}) %collective-permute-start.10) | collective-permute-done | bytes 49184 | tf_op jit(solution)/shard_map/ppermute | solution.py:557
  75.3 0.1 collective-permute-start.11
  75.4 0.9 inner_gather.5.refs_6_
  76.3 3.7 %collective-permute-done.11.refs_5_ = f32[48,512]{1,0:T(8,128)S(1)} collective-permute-done((f32[48,512]{1,0:T(8,128)S(1)}, f32[48,512]{1,0:T(8,128)S(1)}, u32[]{:S(2)}, u32[]{:S(2)}) %collective-permute-start.11) | collective-permute-done | bytes 98336 | tf_op jit(solution)/shard_map/ppermute | solution.py:560
  80.0 0.0 copy-done.1
  80.0 2.9 %adjoint.5 = (f32[8,384]{1,0:T(8,128)S(1)}, bf16[32,8,256]{2,1,0:T(8,128)(2,1)S(1)}) custom-call(f32[16,256]{1,0:T(8,128)S(1)} %announce.1.refs_0_, f32[16,256]{1,0:T(8,128)S(1)} %collective-permute-done.refs_1_, f32[16,256]{1,0:T(8,128)S(1)} %collective-permute-done.1.refs_2_, f32[24,512]{1,0:T(8,128)S(1)} %get-tuple-element.68.refs_3_, ...), custom_call_target="tpu_custom_call" | custom-call | tf_op jit(solution)/shard_map/adjoint/pallas_call | solution.py:535
  83.0 12.8 %all_to_all.5 = bf16[32,8,256]{2,1,0:T(8,128)(2,1)S(1)} all-to-all(bf16[32,8,256]{2,1,0:T(8,128)(2,1)S(1)} %get-tuple-element.75), channel_id=1, replica_groups=mesh['tiles'=8,'probes'=4] {'tiles','probes'}, dimensions={0} | all-to-all | bytes 262144 | tf_op jit(solution)/shard_map/all_to_all | solution.py:667
  95.7 1.5 %gram.1 = (f32[8,256]{1,0:T(8,128)}, f32[8,8,32]{2,1,0:T(8,128)}) custom-call(bf16[8,4,8,256]{3,2,1,0:T(8,128)(2,1)S(1)} %bitcast.14, f32[8,384]{1,0:T(8,128)S(1)} %get-tuple-element.76.own_ref), custom_call_target="tpu_custom_call" | custom-call | tf_op jit(solution)/shard_map/gram/pallas_call | solution.py:535
  (5 shorter events, 0.0 us)
Async XLA Ops:
  1.4 13.1 %collective-permute-start = (f32[16,256]{1,0:T(8,128)S(1)}, f32[16,256]{1,0:T(8,128)S(1)}, u32[]{:S(2)}, u32[]{:S(2)}) collective-permute-start(f32[16,256]{1,0:T(8,128)S(1)} %announce.1.refs_0_), channel_id=1, source_target_pairs={{4,8},{12,16},{20,24},{8,4},{16,12},{24,20},{5,9},{13,17},{21,25},... | collective-permute-start | bytes 49160 | tf_op jit(solution)/shard_map/ppermute | solution.py:551
  2.1 12.4 %collective-permute-start.1 = (f32[16,256]{1,0:T(8,128)S(1)}, f32[16,256]{1,0:T(8,128)S(1)}, u32[]{:S(2)}, u32[]{:S(2)}) collective-permute-start(f32[16,256]{1,0:T(8,128)S(1)} %announce.1.refs_0_), channel_id=1, source_target_pairs={{0,4},{8,12},{16,20},{24,28},{4,0},{12,8},{20,16},{28,24},{1,5},{9... | collective-permute-start | bytes 49160 | tf_op jit(solution)/shard_map/ppermute | solution.py:551
  14.5 4.3 %copy-start = (f32[4096,3]{0,1:T(4,128)S(1)}, f32[4096,3]{0,1:T(4,128)}, u32[]{:S(2)}) copy-start(f32[4096,3]{0,1:T(4,128)} %param.13) | copy-start | bytes 147460
  17.5 6.0 %collective-permute-start.2 = (f32[24,512]{1,0:T(8,128)S(1)}, f32[24,512]{1,0:T(8,128)S(1)}, u32[]{:S(2)}, u32[]{:S(2)}) collective-permute-start(f32[24,512]{1,0:T(8,128)S(1)} %get-tuple-element.51.refs_3_), channel_id=1, source_target_pairs={{4,12},{12,20},{20,28},{8,0},{16,8},{24,16},{5,13},{13,21},{21,29}... | collective-permute-start | bytes 147464 | tf_op jit(solution)/shard_map/ppermute | solution.py:557
  23.5 4.7 %collective-permute-start.3 = (f32[48,512]{1,0:T(8,128)S(1)}, f32[48,512]{1,0:T(8,128)S(1)}, u32[]{:S(2)}, u32[]{:S(2)}) collective-permute-start(f32[48,512]{1,0:T(8,128)S(1)} %pad_maximum_fusion), channel_id=1, source_target_pairs={{0,4},{8,12},{16,20},{24,28},{4,0},{12,8},{20,16},{28,24},{1,5},{9... | collective-permute-start | bytes 294920 | tf_op jit(solution)/shard_map/ppermute | solution.py:560
  31.1 5.5 %collective-permute-start.4 = (f32[8,128]{1,0:T(8,128)S(1)}, f32[8,128]{1,0:T(8,128)S(1)}, u32[]{:S(2)}, u32[]{:S(2)}) collective-permute-start(f32[8,128]{1,0:T(8,128)S(1)} %get-tuple-element.58), channel_id=1, source_target_pairs={{4,12},{12,20},{20,28},{8,0},{16,8},{24,16},{5,13},{13,21},{21,29}... | collective-permute-start | bytes 12296 | tf_op jit(solution)/shard_map/ppermute | solution.py:557
  36.6 3.7 %collective-permute-start.5 = (f32[16,128]{1,0:T(8,128)S(1)}, f32[16,128]{1,0:T(8,128)S(1)}, u32[]{:S(2)}, u32[]{:S(2)}) collective-permute-start(f32[16,128]{1,0:T(8,128)S(1)} %pad_maximum_fusion.3), channel_id=1, source_target_pairs={{0,4},{8,12},{16,20},{24,28},{4,0},{12,8},{20,16},{28,24},{1,5},{9... | collective-permute-start | bytes 24584 | tf_op jit(solution)/shard_map/ppermute | solution.py:560
  43.6 6.0 %collective-permute-start.6 = (f32[24,512]{1,0:T(8,128)S(1)}, f32[24,512]{1,0:T(8,128)S(1)}, u32[]{:S(2)}, u32[]{:S(2)}) collective-permute-start(f32[24,512]{1,0:T(8,128)S(1)} %get-tuple-element.60.refs_3_), channel_id=1, source_target_pairs={{4,12},{12,20},{20,28},{8,0},{16,8},{24,16},{5,13},{13,21},{21,29}... | collective-permute-start | bytes 147464 | tf_op jit(solution)/shard_map/ppermute | solution.py:557
  49.6 4.7 %collective-permute-start.7 = (f32[48,512]{1,0:T(8,128)S(1)}, f32[48,512]{1,0:T(8,128)S(1)}, u32[]{:S(2)}, u32[]{:S(2)}) collective-permute-start(f32[48,512]{1,0:T(8,128)S(1)} %pad_maximum_fusion.1), channel_id=1, source_target_pairs={{0,4},{8,12},{16,20},{24,28},{4,0},{12,8},{20,16},{28,24},{1,5},{9... | collective-permute-start | bytes 294920 | tf_op jit(solution)/shard_map/ppermute | solution.py:560
  57.2 5.5 %collective-permute-start.8 = (f32[8,128]{1,0:T(8,128)S(1)}, f32[8,128]{1,0:T(8,128)S(1)}, u32[]{:S(2)}, u32[]{:S(2)}) collective-permute-start(f32[8,128]{1,0:T(8,128)S(1)} %get-tuple-element.67), channel_id=1, source_target_pairs={{4,12},{12,20},{20,28},{8,0},{16,8},{24,16},{5,13},{13,21},{21,29}... | collective-permute-start | bytes 12296 | tf_op jit(solution)/shard_map/ppermute | solution.py:557
  62.7 3.7 %collective-permute-start.9 = (f32[16,128]{1,0:T(8,128)S(1)}, f32[16,128]{1,0:T(8,128)S(1)}, u32[]{:S(2)}, u32[]{:S(2)}) collective-permute-start(f32[16,128]{1,0:T(8,128)S(1)} %pad_maximum_fusion.4), channel_id=1, source_target_pairs={{0,4},{8,12},{16,20},{24,28},{4,0},{12,8},{20,16},{28,24},{1,5},{9... | collective-permute-start | bytes 24584 | tf_op jit(solution)/shard_map/ppermute | solution.py:560
  69.3 10.7 %copy-start.1 = (s32[256]{0:T(256)S(1)}, s32[256]{0:T(256)}, u32[]{:S(2)}) copy-start(s32[256]{0:T(256)} %param.15) | copy-start | bytes 3076
  69.3 6.0 %collective-permute-start.10 = (f32[24,512]{1,0:T(8,128)S(1)}, f32[24,512]{1,0:T(8,128)S(1)}, u32[]{:S(2)}, u32[]{:S(2)}) collective-permute-start(f32[24,512]{1,0:T(8,128)S(1)} %get-tuple-element.68.refs_3_), channel_id=1, source_target_pairs={{4,12},{12,20},{20,28},{8,0},{16,8},{24,16},{5,13},{13,21},{21,29}... | collective-permute-start | bytes 147464 | tf_op jit(solution)/shard_map/ppermute | solution.py:557
  75.3 4.7 %collective-permute-start.11 = (f32[48,512]{1,0:T(8,128)S(1)}, f32[48,512]{1,0:T(8,128)S(1)}, u32[]{:S(2)}, u32[]{:S(2)}) collective-permute-start(f32[48,512]{1,0:T(8,128)S(1)} %pad_maximum_fusion.2), channel_id=1, source_target_pairs={{0,4},{8,12},{16,20},{24,28},{4,0},{12,8},{20,16},{28,24},{1,5},{9... | collective-permute-start | bytes 294920 | tf_op jit(solution)/shard_map/ppermute | solution.py:560

commit v9 on v7

--- a/solution.py
+++ b/solution.py
@@ -12,6 +12,7 @@
 RIM = 64
 LANES = 128
 RADIX = 512
+CHUNKS = 4
 EDGE = HALO // RADIX
 SHRINK = 2.0**-40
 VMEM_BYTES = 16 * 1024 * 1024
@@ -24,10 +25,6 @@
     return lax.dot_general(a, b, (((1,), (0,)), ((), ())), preferred_element_type=F32)
 
 
-def dot_nt(a, b):
-    return lax.dot_general(a, b, (((1,), (1,)), ((), ())), preferred_element_type=F32)
-
-
 def split(x):
     hi = x.astype(BF16)
     return hi, (x - hi.astype(F32)).astype(BF16)
@@ -41,21 +38,28 @@
     return lax.broadcasted_iota(jnp.int32, shape, 1)
 
 
-def spread_matrix(node_slots, padded_order):
+def hot(mask):
+    return jnp.where(mask, F32(1), F32(0)).astype(BF16)
+
+
+def spread_matrix(node_slots, padded_order, turned=False):
     shape = (2 * node_slots, 2 * padded_order)
-    row = rows_iota(shape)
-    start = (row // node_slots) * padded_order + 3 * (row % node_slots)
-    gap = lanes_iota(shape) - start
-    return jnp.where((gap >= 0) & (gap < 3), F32(1), F32(0)).astype(BF16)
-
-
-def order_matrix(node_slots, padded_order):
+    row, col = rows_iota(shape), lanes_iota(shape)
+    if turned:
+        row, col = lanes_iota(shape[::-1]), rows_iota(shape[::-1])
+    gap = col - ((row // node_slots) * padded_order + 3 * (row % node_slots))
+    return hot((gap >= 0) & (gap < 3))
+
+
+def order_matrix(node_slots, padded_order, turned=False):
     pair = 2 * node_slots
     shape = (2 * padded_order, 3 * pair)
-    col = lanes_iota(shape)
+    row, col = rows_iota(shape), lanes_iota(shape)
+    if turned:
+        row, col = lanes_iota(shape[::-1]), rows_iota(shape[::-1])
     inner = col % pair
     source = (inner // node_slots) * padded_order + 3 * (inner % node_slots) + col // pair
-    return jnp.where(rows_iota(shape) == source, F32(1), F32(0)).astype(BF16)
+    return hot(row == source)
 
 
 def colour_of(ids):
@@ -103,71 +107,94 @@
     blocks_ref,
     turned_ref,
     node_hot_ref,
+    node_turn_ref,
     level_hot_ref,
     cell_hot_ref,
+    cell_turn_ref,
     spread_ref,
+    spread_turn_ref,
     order_ref,
+    order_turn_ref,
     conn_in,
     cell_in,
     friction_in,
     sems,
 ):
-    loads = [
-        pltpu.make_async_copy(conn_hbm, conn_in, sems.at[0]),
-        pltpu.make_async_copy(cell_hbm, cell_in, sems.at[1]),
-        pltpu.make_async_copy(friction_hbm, friction_in, sems.at[2]),
-        pltpu.make_async_copy(blocks_hbm, blocks_ref, sems.at[3]),
-    ]
-    for load in loads:
-        load.start()
     pairs = conn_ref.shape[0]
     slots, padded_order = fr_ref.shape
     node_slots = conn_in.shape[1]
     levels = level_hot_ref.shape[0] // 16
     window = 3 * LANES
+    chunks = sems.shape[0] - 3
+    chunk = slots // chunks
+
+    loads = [
+        pltpu.make_async_copy(source, target, sems.at[i])
+        for i, (source, target) in enumerate(
+            [
+                (conn_hbm, conn_in),
+                (cell_hbm, cell_in),
+                (friction_hbm, friction_in),
+            ]
+        )
+    ]
+    for i in range(chunks):
+        at = pl.ds(i * chunk, chunk)
+        loads.append(pltpu.make_async_copy(blocks_hbm.at[at], blocks_ref.at[at], sems.at[3 + i]))
+    for load in loads:
+        load.start()
 
     spread_ref[...] = spread_matrix(node_slots, padded_order)
+    spread_turn_ref[...] = spread_matrix(node_slots, padded_order, True)
     order_ref[...] = order_matrix(node_slots, padded_order)
+    order_turn_ref[...] = order_matrix(node_slots, padded_order, True)
 
     def paired(ref):
         return jnp.concatenate(
             [ref[pl.ds(0, pairs, stride=2), :], ref[pl.ds(1, pairs, stride=2), :]], axis=1
         )
 
-    loads[0].wait()
+    for load in loads[:3]:
+        load.wait()
     conn = paired(conn_in)
     conn_ref[...] = conn
-    loads[1].wait()
     cells = paired(cell_in)
     cells = jnp.where(cells < RIM, cells + (window - RIM), cells - RIM)
     cell_ref[...] = cells
-    rows = rows_iota((RADIX, LANES))
-    for m in range(pairs):
-        at = pl.ds(m * LANES, LANES)
-        hot = rows == conn[m : m + 1, :] % RADIX
-        node_hot_ref[:, at] = jnp.where(hot, F32(1), F32(0)).astype(BF16)
-        which = jnp.broadcast_to(conn[m : m + 1, :] // RADIX, (16, LANES))
-        for level in range(levels):
-            hot = jnp.where(which == level, F32(1), F32(0)).astype(BF16)
-            level_hot_ref[16 * level : 16 * level + 16, at] = hot
-        hot = rows[:LANES] == cells[m : m + 1, :] % LANES
-        cell_hot_ref[:, at] = jnp.where(hot, F32(1), F32(0)).astype(BF16)
-
-    loads[2].wait()
+    node_low = conn % RADIX
+    cell_low = cells % LANES
+    node_column = node_low.astype(F32).T
+    cell_column = cell_low.astype(F32).T
+
     shape = (node_slots, padded_order)
     total = jnp.zeros((slots, padded_order), F32)
     for c in range(3):
-        place = lanes_iota(shape) == 3 * rows_iota(shape) + c
-        place = jnp.where(place, F32(1), F32(0)).astype(BF16)
+        place = hot(lanes_iota(shape) == 3 * rows_iota(shape) + c)
         rest = friction_in[c]
         for _ in range(3):
             part = rest.astype(BF16)
             total = total + dot(part, place)
             rest = rest - part.astype(F32)
-    fr_ref[...] = jnp.where(rows_iota(total.shape) < counts[0], total, F32(0))
-    loads[3].wait()
-    for slot in range(slots):
-        turned_ref[slot] = blocks_ref[slot].T
+    live = rows_iota(total.shape) < counts[0]
+    fr_ref[...] = jnp.where(live, total, F32(0))
+
+    rows = rows_iota((RADIX, LANES))
+    lanes = lanes_iota((LANES, RADIX)).astype(F32)
+    for i in range(chunks):
+        loads[3 + i].wait()
+        for slot in range(i * chunk, (i + 1) * chunk):
+            turned_ref[slot] = blocks_ref[slot].T
+            if slot % 2:
+                continue
+            m = slot // 2
+            at = pl.ds(m * LANES, LANES)
+            node_hot_ref[:, at] = hot(rows == node_low[m : m + 1, :])
+            node_turn_ref[at, :] = hot(lanes == node_column[:, m : m + 1])
+            which = jnp.broadcast_to(conn[m : m + 1, :] // RADIX, (16, LANES))
+            for level in range(levels):
+                level_hot_ref[16 * level : 16 * level + 16, at] = hot(which == level)
+            cell_hot_ref[:, at] = hot(rows[:LANES] == cell_low[m : m + 1, :])
+            cell_turn_ref[at, :] = hot(lanes[:, :LANES] == cell_column[:, m : m + 1])
 
 
 def spread_levels(v_ref, ordered, level_hot, levels, pairs):
@@ -190,8 +217,8 @@
     first = step == 0
     if not first:
         basal_ref, rim_a, rim_b, *refs = refs
-    conn_ref, cell_ref, fr_ref, _, turned, node_hot, level_hot, cell_hot, *refs = refs
-    spread_ref, order_ref, *refs = refs
+    _, cell_ref, fr_ref, _, turned, _, node_turn, level_hot, cell_hot, _, *refs = refs
+    spread_ref, _, order_ref, _, *refs = refs
     ordered_ref, a_ref, b_ref, *refs = refs
     if not first:
         squares_ref, *refs = refs
@@ -272,7 +299,7 @@
     ordered_ref[...] = ordered
     edges = edge_levels(levels)
     spread_levels(v_ref, ordered, level_hot, edges, pairs)
-    rim = dot_nt(v_ref[...], node_hot[...])
+    rim = dot(v_ref[...], node_turn[...])
     sums = [
         rim[16 * i : 16 * i + 8] + rim[16 * i + 8 : 16 * i + 16] for i in range(3 * len(edges))
     ]
@@ -283,13 +310,13 @@
 
 
 def inner_kernel(
-    levels, ordered_ref, weight_ref, conn_ref, node_hot, level_hot, picked_ref, v_ref
+    levels, ordered_ref, weight_ref, conn_ref, node_hot, node_turn, level_hot, picked_ref, v_ref
 ):
     pairs = conn_ref.shape[0]
     conn = conn_ref[...]
     inside = list(range(EDGE, levels - EDGE))
     spread_levels(v_ref, ordered_ref, level_hot, inside, pairs)
-    nodes = dot_nt(v_ref[...], node_hot[...])
+    nodes = dot(v_ref[...], node_turn[...])
     rows = []
     for i in range(3 * len(inside)):
         value = nodes[16 * i : 16 * i + 8] + nodes[16 * i + 8 : 16 * i + 16]
@@ -312,8 +339,8 @@
 
 def adjoint_kernel(last, clusters, levels, *refs):
     block_ref, block_a, block_b, own_a, own_b, new_a, new_b, inner_ref, weight_ref, *refs = refs
-    conn_ref, cell_ref, fr_ref, blocks, _, node_hot, _, cell_hot, *refs = refs
-    spread_ref, order_ref, *refs = refs
+    conn_ref, cell_ref, fr_ref, blocks, _, node_hot, _, _, _, cell_turn, *refs = refs
+    _, spread_turn, _, order_turn, *refs = refs
     if last:
         squares_1, squares_2, ids_ref, *refs = refs
         basal_ref, out_ref, p_ref, n_ref, v_ref = refs
@@ -348,7 +375,7 @@
                     row = 24 * at + 8 * c
                     value = jnp.where(which == level, part[row : row + 8], value)
                 n_ref[8 * m : 8 * m + 8, c * LANES : (c + 1) * LANES] = value
-    natural = dot_nt(n_ref[...].astype(BF16), order_ref[...])
+    natural = dot(n_ref[...].astype(BF16), order_turn[...])
     p_ref[...] = jnp.zeros_like(p_ref)
     for m in range(pairs):
         for side in range(2):
@@ -359,7 +386,7 @@
             p_ref[8 * m : 8 * m + 8, at : at + order] = out
 
     hi, lo = split(p_ref[...])
-    partial = dot_nt(jnp.concatenate([hi, lo], axis=0), spread_ref[...])
+    partial = dot(jnp.concatenate([hi, lo], axis=0), spread_turn[...])
     half = 8 * pairs
     partial = partial[:half] + partial[half:]
     cells = cell_ref[...]
@@ -370,7 +397,7 @@
         hi = rows.astype(BF16).astype(F32)
         both = jnp.concatenate([hi, rows - hi], axis=0)
         v_ref[:, m * LANES : (m + 1) * LANES] = both.astype(BF16)
-    basal = dot_nt(v_ref[...], cell_hot[...])
+    basal = dot(v_ref[...], cell_turn[...])
     basal = basal[:24] + basal[24:]
     parts = [basal[8 * i : 8 * i + 8] for i in range(3)]
     for i in range(3):
@@ -413,7 +440,10 @@
         out_ref[t] = message
 
 
-def gram_kernel(keep_same, tiles, groups, g_ref, own_ref, field_ref, gram_ref):
+def gram_kernel(
+    keep_same, tiles, groups, g_ref, own_ref, samples_in, samples_ref, field_ref, gram_ref
+):
+    samples_ref[...] = samples_in[...]
     tile = lax.axis_index("tiles")
     group = lax.axis_index("probes")
     clusters = gram_ref.shape[0]
@@ -513,12 +543,12 @@
     padded_order = 2 * LANES
     window = cell_count + 2 * RIM
 
-    smem = pl.BlockSpec(memory_space=pltpu.SMEM)
     vmem = pl.BlockSpec(memory_space=pltpu.VMEM)
     params = pltpu.CompilerParams(vmem_limit_bytes=VMEM_BYTES)
     shaped = jax.ShapeDtypeStruct
 
     hbm = pl.BlockSpec(memory_space=pltpu.HBM)
+    smem = pl.BlockSpec(memory_space=pltpu.SMEM)
 
     def call(kernel, name, out_shape, operands, scratch=(), in_specs=None):
         in_specs = in_specs or [vmem] * len(operands)
@@ -570,21 +600,31 @@
             shaped(blocks.shape, BF16),
             shaped(blocks.shape, BF16),
             shaped((RADIX, refs), BF16),
+            shaped((refs, RADIX), BF16),
             shaped((16 * levels, refs), BF16),
             shaped((LANES, refs), BF16),
+            shaped((refs, LANES), BF16),
             shaped((LANES, 2 * padded_order), BF16),
+            shaped((2 * padded_order, LANES), BF16),
             shaped((2 * padded_order, 3 * LANES), BF16),
+            shaped((3 * LANES, 2 * padded_order), BF16),
         ],
-        [elem_counts, connectivity, basal_map, friction.transpose(2, 0, 1), blocks],
+        [
+            elem_counts,
+            connectivity,
+            basal_map,
+            friction.transpose(2, 0, 1),
+            blocks,
+        ],
         [
             pltpu.VMEM(connectivity.shape, jnp.int32),
             pltpu.VMEM(basal_map.shape, jnp.int32),
             pltpu.VMEM((3, slots, node_slots), F32),
-            pltpu.SemaphoreType.DMA((4,)),
+            pltpu.SemaphoreType.DMA((3 + CHUNKS,)),
         ],
         [smem] + [hbm] * 4,
     )
-    conn, node_hot, level_hot = shared[0], shared[5], shared[6]
+    conn, node_hot, node_turn, level_hot = shared[0], *shared[5:8]
 
     edge = shaped((24 * EDGE, RADIX), F32)
     rim = shaped((group_size, LANES), F32)
@@ -611,13 +651,13 @@
         )
         squares += extra[:1]
         if step == 1:
-            samples = extra[1].T
+            samples = extra[1]
         new_a, new_b = swapped(own_a, own_b)
         inner = call(
             functools.partial(inner_kernel, levels),
             "inner",
             shaped((8 * pairs, 3 * LANES), F32),
-            [ordered, weight, conn, node_hot, level_hot],
+            [ordered, weight, conn, node_hot, node_turn, level_hot],
             [pltpu.VMEM((48 * (levels - 2 * EDGE), refs), BF16)],
         )
         operands = [block, block_a, block_b, own_a, own_b, new_a, new_b, inner, weight, *shared]
@@ -643,13 +683,13 @@
 
     gathered = lax.all_to_all(messages[0], everyone, 0, 0)
     gathered = gathered.reshape(tiles, groups, *gathered.shape[1:])
-    refined, gram = call(
+    samples, refined, gram = call(
         functools.partial(gram_kernel, POWER % 2 == 1, tiles, groups),
         "gram",
-        [field, shaped((tiles, group_size, groups * group_size), F32)],
-        [gathered, basal],
+        [field, field, shaped((tiles, group_size, groups * group_size), F32)],
+        [gathered, basal, samples],
     )
-    return (samples, refined.T, gram)
+    return (samples.T, refined.T, gram)
 
 
 def solution(mesh):

time: 83.5 us -> 82.7 us (level)
  Pallas kernels: 33.9 us -> 32.2 us
  blocking collectives: 11.9 us -> 13.1 us
    pallas_call x12, Pallas kernels: 33.9 us -> 32.2 us  [call(): pl.pallas_call(kernel, out_shape=out_shape, in_specs=in_specs, out_specs=...]
    all_to_all x1, blocking collectives: 11.9 us -> 13.1 us  [shards(): gathered = lax.all_to_all(messages[0], everyone, 0, 0)]
  transfers between devices with their start and end apart: 12 -> 12, of which waited for: 2 -> 2; matrix products, arithmetic and copies ran while one was open for 0% -> 0% of each run, Pallas kernels for 16% -> 18%
where the time goes in v9:
time: 82.7 us; the launch traced here: 82.3 us
  starting transfers between devices  32.4 us (39%)
  Pallas kernels  32.2 us (39%)
  blocking collectives  13.1 us (16%)
  waiting for transfers between devices  3.19 us (4%)
  between operations  1.48 us (2%)
    pallas_call x12, Pallas kernels, call(): pl.pallas_call(kernel, out_shape=out_shape, in_specs=in_specs, out_specs=...  32.2 us
    ppermute x6, starting transfers between devices, swapped(): lax.ppermute(b, 'tiles', pairs_b)  28.3 us
    all_to_all x1, blocking collectives, shards(): gathered = lax.all_to_all(messages[0], everyone, 0, 0)  13.1 us
    ppermute x6, starting transfers between devices, swapped(): lax.ppermute(a, 'tiles', pairs_a)  4.15 us
    ppermute x6, waiting for transfers between devices, swapped(): lax.ppermute(b, 'tiles', pairs_b)  3.18 us
  transfers between devices with their start and end apart: 12, of which 2 were waited for; matrix products, arithmetic and copies ran while one was open for 0% of the time, Pallas kernels for 18%

profile of v9, /device:TPU:0, one launch (start us, length us, event | category | flops | bytes accessed | tf_op | source)
XLA Modules:
  0.0 82.3 jit_solution(2456766988959062803)
XLA Ops:
  0.6 0.8 announce.1.refs_0_
  1.4 3.0 %collective-permute-start.1 = (f32[16,256]{1,0:T(8,128)S(1)}, f32[16,256]{1,0:T(8,128)S(1)}, u32[]{:S(2)}, u32[]{:S(2)}) collective-permute-start(f32[16,256]{1,0:T(8,128)S(1)} %announce.1.refs_0_), channel_id=1, source_target_pairs={{0,4},{8,12},{16,20},{24,28},{4,0},{12,8},{20,16},{28,24},{1,5},{9... | collective-permute-start | bytes 49160 | tf_op jit(solution)/shard_map/ppermute | solution.py:575
  4.4 0.7 collective-permute-start
  5.7 7.5 %setup.1 = (s32[32,128]{1,0:T(8,128)S(1)}, s32[32,128]{1,0:T(8,128)S(1)}, f32[64,256]{1,0:T(8,128)S(1)}, bf16[64,192,192]{2,1,0:T(8,128)(2,1)S(1)}, bf16[64,192,...) custom-call(s32[1]{0:T(128)S(6)} %copy.11.counts, ...), custom_call_target="tpu_custom_call" | custom-call | tf_op jit(solution)/shard_map/setup/pallas_call | solution.py:559
  13.2 0.0 collective-permute-done.1.refs_2_
  13.2 0.0 collective-permute-done.refs_1_
  13.2 0.0 copy-start
  13.3 2.4 %forward.3 = (bf16[512,384]{1,0:T(8,128)(2,1)S(1)}, f32[24,512]{1,0:T(8,128)S(1)}, f32[24,512]{1,0:T(8,128)S(1)}) custom-call(f32[16,256]{1,0:T(8,128)S(1)} %announce.1.refs_0_, f32[16,256]{1,0:T(8,128)S(1)} %collective-permute-done.refs_1_, f32[16,256]{1,0:T(8,128)S(1)} %collective-permute-done.1.refs_2_, ...), custom_call_target="tpu_custom_call" | custom-call | tf_op jit(solution)/shard_map/forward/pallas_call | solution.py:559
  15.7 0.7 collective-permute-start.2
  16.4 5.6 %collective-permute-start.3 = (f32[24,512]{1,0:T(8,128)S(1)}, f32[24,512]{1,0:T(8,128)S(1)}, u32[]{:S(2)}, u32[]{:S(2)}) collective-permute-start(f32[24,512]{1,0:T(8,128)S(1)} %get-tuple-element.55.refs_4_), channel_id=1, source_target_pairs={{0,4},{8,12},{16,20},{24,28},{4,0},{12,8},{20,16},{28,24},{1,5},{9... | collective-permute-start | bytes 147464 | tf_op jit(solution)/shard_map/ppermute | solution.py:575
  22.0 0.0 copy-done
  22.0 2.5 %inner.3.refs_7_ = f32[256,384]{1,0:T(8,128)S(1)} custom-call(bf16[512,384]{1,0:T(8,128)(2,1)S(1)} %get-tuple-element.56.ordered_ref, f32[3,4096]{1,0:T(4,128)S(1)} %bitcast.8, s32[32,128]{1,0:T(8,128)S(1)} %get-tuple-element.40.refs_3_.conn_ref.refs_9_.refs_6_, bf16[512,4096]{1,0:T(8,128)(2,1)S(1)} %get-tuple-element.45.refs_8_.node_hot.refs_14_.refs_11_, ...), custom_call_target="tpu_custom_call" | custom-call | tf_op jit(solution)/shard_map/inner/pallas_call | solution.py:559
  24.5 0.0 collective-permute-done.2.refs_5_
  24.5 0.0 collective-permute-done.3.refs_6_
  24.5 2.6 %adjoint.3 = (f32[8,384]{1,0:T(8,128)S(1)}, f32[8,128]{1,0:T(8,128)S(1)}, f32[8,128]{1,0:T(8,128)S(1)}) custom-call(f32[16,256]{1,0:T(8,128)S(1)} %announce.1.refs_0_, f32[16,256]{1,0:T(8,128)S(1)} %collective-permute-done.refs_1_, f32[16,256]{1,0:T(8,128)S(1)} %collective-permute-done.1.refs_2_, f32[24,512]{1,0:T(8,128)S(1)} %get-tuple-element.54.refs_3_, ...), custom_call_target="tpu_custom_call" | custom-call | tf_op jit(solution)/shard_map/adjoint/pallas_call | solution.py:559
  27.1 0.8 %collective-permute-start.4 = (f32[8,128]{1,0:T(8,128)S(1)}, f32[8,128]{1,0:T(8,128)S(1)}, u32[]{:S(2)}, u32[]{:S(2)}) collective-permute-start(f32[8,128]{1,0:T(8,128)S(1)} %get-tuple-element.58), channel_id=1, source_target_pairs={{4,8},{12,16},{20,24},{8,4},{16,12},{24,20},{5,9},{13,17},{21,25},... | collective-permute-start | bytes 12296 | tf_op jit(solution)/shard_map/ppermute | solution.py:575
  27.9 5.8 %collective-permute-start.5 = (f32[8,128]{1,0:T(8,128)S(1)}, f32[8,128]{1,0:T(8,128)S(1)}, u32[]{:S(2)}, u32[]{:S(2)}) collective-permute-start(f32[8,128]{1,0:T(8,128)S(1)} %get-tuple-element.59), channel_id=1, source_target_pairs={{0,4},{8,12},{16,20},{24,28},{4,0},{12,8},{20,16},{28,24},{1,5},{9... | collective-permute-start | bytes 12296 | tf_op jit(solution)/shard_map/ppermute | solution.py:575
  33.7 0.0 collective-permute-done.4.refs_4_
  33.7 1.6 %collective-permute-done.5.refs_5_ = f32[8,128]{1,0:T(8,128)S(1)} collective-permute-done((f32[8,128]{1,0:T(8,128)S(1)}, f32[8,128]{1,0:T(8,128)S(1)}, u32[]{:S(2)}, u32[]{:S(2)}) %collective-permute-start.5) | collective-permute-done | bytes 4128 | tf_op jit(solution)/shard_map/ppermute | solution.py:575
  35.3 2.4 %forward.4 = (bf16[512,384]{1,0:T(8,128)(2,1)S(1)}, f32[24,512]{1,0:T(8,128)S(1)}, f32[24,512]{1,0:T(8,128)S(1)}, f32[8,128]{1,0:T(8,128)S(1)}, f32[8,256]{1,0:T(8,128)S(1)}) custom-call(f32[16,256]{1,0:T(8,128)S(1)} %announce.1.refs_0_, f32[16,256]{1,0:T(8,128)S(1)} %collective-permute-done.refs_1_, f32[16,256]{1,0:T(8,128)S(1)} %collective-permute-done.1.refs_2_, ...), custom_call_target="tpu_custom_call" | custom-call | tf_op jit(solution)/shard_map/forward/pallas_call | solution.py:559
  37.7 0.7 collective-permute-start.6
  38.4 4.3 %collective-permute-start.7 = (f32[24,512]{1,0:T(8,128)S(1)}, f32[24,512]{1,0:T(8,128)S(1)}, u32[]{:S(2)}, u32[]{:S(2)}) collective-permute-start(f32[24,512]{1,0:T(8,128)S(1)} %get-tuple-element.61.refs_4_), channel_id=1, source_target_pairs={{0,4},{8,12},{16,20},{24,28},{4,0},{12,8},{20,16},{28,24},{1,5},{9... | collective-permute-start | bytes 147464 | tf_op jit(solution)/shard_map/ppermute | solution.py:575
  42.7 2.5 %inner.4.refs_7_ = f32[256,384]{1,0:T(8,128)S(1)} custom-call(bf16[512,384]{1,0:T(8,128)(2,1)S(1)} %get-tuple-element.62.ordered_ref, f32[3,4096]{1,0:T(4,128)S(1)} %bitcast.10, s32[32,128]{1,0:T(8,128)S(1)} %get-tuple-element.40.refs_3_.conn_ref.refs_9_.refs_6_, bf16[512,4096]{1,0:T(8,128)(2,1)S(1)} %get-tuple-element.45.refs_8_.node_hot.refs_14_.refs_11_, ...), custom_call_target="tpu_custom_call" | custom-call | tf_op jit(solution)/shard_map/inner/pallas_call | solution.py:559
  45.2 0.0 collective-permute-done.6.refs_5_
  45.2 0.0 collective-permute-done.7.refs_6_
  45.2 2.6 %adjoint.4 = (f32[8,384]{1,0:T(8,128)S(1)}, f32[8,128]{1,0:T(8,128)S(1)}, f32[8,128]{1,0:T(8,128)S(1)}) custom-call(f32[16,256]{1,0:T(8,128)S(1)} %announce.1.refs_0_, f32[16,256]{1,0:T(8,128)S(1)} %collective-permute-done.refs_1_, f32[16,256]{1,0:T(8,128)S(1)} %collective-permute-done.1.refs_2_, f32[24,512]{1,0:T(8,128)S(1)} %get-tuple-element.60.refs_3_, ...), custom_call_target="tpu_custom_call" | custom-call | tf_op jit(solution)/shard_map/adjoint/pallas_call | solution.py:559
  47.8 0.7 collective-permute-start.8
  48.5 4.8 %collective-permute-start.9 = (f32[8,128]{1,0:T(8,128)S(1)}, f32[8,128]{1,0:T(8,128)S(1)}, u32[]{:S(2)}, u32[]{:S(2)}) collective-permute-start(f32[8,128]{1,0:T(8,128)S(1)} %get-tuple-element.65), channel_id=1, source_target_pairs={{0,4},{8,12},{16,20},{24,28},{4,0},{12,8},{20,16},{28,24},{1,5},{9... | collective-permute-start | bytes 12296 | tf_op jit(solution)/shard_map/ppermute | solution.py:575
  53.3 0.0 collective-permute-done.8.refs_4_
  53.3 1.6 %collective-permute-done.9.refs_5_ = f32[8,128]{1,0:T(8,128)S(1)} collective-permute-done((f32[8,128]{1,0:T(8,128)S(1)}, f32[8,128]{1,0:T(8,128)S(1)}, u32[]{:S(2)}, u32[]{:S(2)}) %collective-permute-start.9) | collective-permute-done | bytes 4128 | tf_op jit(solution)/shard_map/ppermute | solution.py:575
  54.9 2.4 %forward.5 = (bf16[512,384]{1,0:T(8,128)(2,1)S(1)}, f32[24,512]{1,0:T(8,128)S(1)}, f32[24,512]{1,0:T(8,128)S(1)}, f32[8,128]{1,0:T(8,128)S(1)}) custom-call(f32[16,256]{1,0:T(8,128)S(1)} %announce.1.refs_0_, f32[16,256]{1,0:T(8,128)S(1)} %collective-permute-done.refs_1_, f32[16,256]{1,0:T(8,128)S(1)} %collective-permute-done.1.refs_2_, ...), custom_call_target="tpu_custom_call" | custom-call | tf_op jit(solution)/shard_map/forward/pallas_call | solution.py:559
  57.3 0.0 copy-start.1
  57.3 0.7 collective-permute-start.10
  58.0 4.7 %collective-permute-start.11 = (f32[24,512]{1,0:T(8,128)S(1)}, f32[24,512]{1,0:T(8,128)S(1)}, u32[]{:S(2)}, u32[]{:S(2)}) collective-permute-start(f32[24,512]{1,0:T(8,128)S(1)} %get-tuple-element.67.refs_4_), channel_id=1, source_target_pairs={{0,4},{8,12},{16,20},{24,28},{4,0},{12,8},{20,16},{28,24},{1,5},{9... | collective-permute-start | bytes 147464 | tf_op jit(solution)/shard_map/ppermute | solution.py:575
  62.7 2.5 %inner.5.refs_7_ = f32[256,384]{1,0:T(8,128)S(1)} custom-call(bf16[512,384]{1,0:T(8,128)(2,1)S(1)} %get-tuple-element.68.ordered_ref, f32[3,4096]{1,0:T(4,128)S(1)} %bitcast.12, s32[32,128]{1,0:T(8,128)S(1)} %get-tuple-element.40.refs_3_.conn_ref.refs_9_.refs_6_, bf16[512,4096]{1,0:T(8,128)(2,1)S(1)} %get-tuple-element.45.refs_8_.node_hot.refs_14_.refs_11_, ...), custom_call_target="tpu_custom_call" | custom-call | tf_op jit(solution)/shard_map/inner/pallas_call | solution.py:559
  65.1 0.0 collective-permute-done.10.refs_5_
  65.1 0.0 collective-permute-done.11.refs_6_
  65.1 0.0 copy-done.1
  65.2 2.6 %adjoint.5 = (f32[8,384]{1,0:T(8,128)S(1)}, bf16[32,8,256]{2,1,0:T(8,128)(2,1)S(1)}) custom-call(f32[16,256]{1,0:T(8,128)S(1)} %announce.1.refs_0_, f32[16,256]{1,0:T(8,128)S(1)} %collective-permute-done.refs_1_, f32[16,256]{1,0:T(8,128)S(1)} %collective-permute-done.1.refs_2_, f32[24,512]{1,0:T(8,128)S(1)} %get-tuple-element.66.refs_3_, ...), custom_call_target="tpu_custom_call" | custom-call | tf_op jit(solution)/shard_map/adjoint/pallas_call | solution.py:559
  67.8 13.1 %all_to_all.5 = bf16[32,8,256]{2,1,0:T(8,128)(2,1)S(1)} all-to-all(bf16[32,8,256]{2,1,0:T(8,128)(2,1)S(1)} %get-tuple-element.71), channel_id=1, replica_groups=mesh['tiles'=8,'probes'=4] {'tiles','probes'}, dimensions={0} | all-to-all | bytes 262144 | tf_op jit(solution)/shard_map/all_to_all | solution.py:684
  80.8 1.5 %gram.1 = (f32[8,256]{1,0:T(8,128)}, f32[8,256]{1,0:T(8,128)}, f32[8,8,32]{2,1,0:T(8,128)}) custom-call(bf16[8,4,8,256]{3,2,1,0:T(8,128)(2,1)S(1)} %bitcast.14, f32[8,384]{1,0:T(8,128)S(1)} %get-tuple-element.72.own_ref, f32[8,256]{1,0:T(8,128)S(1)} %get-tuple-element.73.samples_in), custom_call_target="tpu_custom_call" | custom-call | tf_op jit(solution)/shard_map/gram/pallas_call | solution.py:559
Async XLA Ops:
  1.4 11.8 %collective-permute-start.1 = (f32[16,256]{1,0:T(8,128)S(1)}, f32[16,256]{1,0:T(8,128)S(1)}, u32[]{:S(2)}, u32[]{:S(2)}) collective-permute-start(f32[16,256]{1,0:T(8,128)S(1)} %announce.1.refs_0_), channel_id=1, source_target_pairs={{0,4},{8,12},{16,20},{24,28},{4,0},{12,8},{20,16},{28,24},{1,5},{9... | collective-permute-start | bytes 49160 | tf_op jit(solution)/shard_map/ppermute | solution.py:575
  4.4 8.8 %collective-permute-start = (f32[16,256]{1,0:T(8,128)S(1)}, f32[16,256]{1,0:T(8,128)S(1)}, u32[]{:S(2)}, u32[]{:S(2)}) collective-permute-start(f32[16,256]{1,0:T(8,128)S(1)} %announce.1.refs_0_), channel_id=1, source_target_pairs={{4,8},{12,16},{20,24},{8,4},{16,12},{24,20},{5,9},{13,17},{21,25},... | collective-permute-start | bytes 49160 | tf_op jit(solution)/shard_map/ppermute | solution.py:575
  13.2 8.7 %copy-start = (f32[4096,3]{0,1:T(4,128)S(1)}, f32[4096,3]{0,1:T(4,128)}, u32[]{:S(2)}) copy-start(f32[4096,3]{0,1:T(4,128)} %param.13) | copy-start | bytes 147460
  15.7 8.8 %collective-permute-start.2 = (f32[24,512]{1,0:T(8,128)S(1)}, f32[24,512]{1,0:T(8,128)S(1)}, u32[]{:S(2)}, u32[]{:S(2)}) collective-permute-start(f32[24,512]{1,0:T(8,128)S(1)} %get-tuple-element.54.refs_3_), channel_id=1, source_target_pairs={{4,8},{12,16},{20,24},{8,4},{16,12},{24,20},{5,9},{13,17},{21,25},... | collective-permute-start | bytes 147464 | tf_op jit(solution)/shard_map/ppermute | solution.py:575
  16.4 8.1 %collective-permute-start.3 = (f32[24,512]{1,0:T(8,128)S(1)}, f32[24,512]{1,0:T(8,128)S(1)}, u32[]{:S(2)}, u32[]{:S(2)}) collective-permute-start(f32[24,512]{1,0:T(8,128)S(1)} %get-tuple-element.55.refs_4_), channel_id=1, source_target_pairs={{0,4},{8,12},{16,20},{24,28},{4,0},{12,8},{20,16},{28,24},{1,5},{9... | collective-permute-start | bytes 147464 | tf_op jit(solution)/shard_map/ppermute | solution.py:575
  27.1 6.7 %collective-permute-start.4 = (f32[8,128]{1,0:T(8,128)S(1)}, f32[8,128]{1,0:T(8,128)S(1)}, u32[]{:S(2)}, u32[]{:S(2)}) collective-permute-start(f32[8,128]{1,0:T(8,128)S(1)} %get-tuple-element.58), channel_id=1, source_target_pairs={{4,8},{12,16},{20,24},{8,4},{16,12},{24,20},{5,9},{13,17},{21,25},... | collective-permute-start | bytes 12296 | tf_op jit(solution)/shard_map/ppermute | solution.py:575
  27.9 7.4 %collective-permute-start.5 = (f32[8,128]{1,0:T(8,128)S(1)}, f32[8,128]{1,0:T(8,128)S(1)}, u32[]{:S(2)}, u32[]{:S(2)}) collective-permute-start(f32[8,128]{1,0:T(8,128)S(1)} %get-tuple-element.59), channel_id=1, source_target_pairs={{0,4},{8,12},{16,20},{24,28},{4,0},{12,8},{20,16},{28,24},{1,5},{9... | collective-permute-start | bytes 12296 | tf_op jit(solution)/shard_map/ppermute | solution.py:575
  37.7 7.5 %collective-permute-start.6 = (f32[24,512]{1,0:T(8,128)S(1)}, f32[24,512]{1,0:T(8,128)S(1)}, u32[]{:S(2)}, u32[]{:S(2)}) collective-permute-start(f32[24,512]{1,0:T(8,128)S(1)} %get-tuple-element.60.refs_3_), channel_id=1, source_target_pairs={{4,8},{12,16},{20,24},{8,4},{16,12},{24,20},{5,9},{13,17},{21,25},... | collective-permute-start | bytes 147464 | tf_op jit(solution)/shard_map/ppermute | solution.py:575
  38.4 6.8 %collective-permute-start.7 = (f32[24,512]{1,0:T(8,128)S(1)}, f32[24,512]{1,0:T(8,128)S(1)}, u32[]{:S(2)}, u32[]{:S(2)}) collective-permute-start(f32[24,512]{1,0:T(8,128)S(1)} %get-tuple-element.61.refs_4_), channel_id=1, source_target_pairs={{0,4},{8,12},{16,20},{24,28},{4,0},{12,8},{20,16},{28,24},{1,5},{9... | collective-permute-start | bytes 147464 | tf_op jit(solution)/shard_map/ppermute | solution.py:575
  47.8 5.5 %collective-permute-start.8 = (f32[8,128]{1,0:T(8,128)S(1)}, f32[8,128]{1,0:T(8,128)S(1)}, u32[]{:S(2)}, u32[]{:S(2)}) collective-permute-start(f32[8,128]{1,0:T(8,128)S(1)} %get-tuple-element.64), channel_id=1, source_target_pairs={{4,8},{12,16},{20,24},{8,4},{16,12},{24,20},{5,9},{13,17},{21,25},... | collective-permute-start | bytes 12296 | tf_op jit(solution)/shard_map/ppermute | solution.py:575
  48.5 6.4 %collective-permute-start.9 = (f32[8,128]{1,0:T(8,128)S(1)}, f32[8,128]{1,0:T(8,128)S(1)}, u32[]{:S(2)}, u32[]{:S(2)}) collective-permute-start(f32[8,128]{1,0:T(8,128)S(1)} %get-tuple-element.65), channel_id=1, source_target_pairs={{0,4},{8,12},{16,20},{24,28},{4,0},{12,8},{20,16},{28,24},{1,5},{9... | collective-permute-start | bytes 12296 | tf_op jit(solution)/shard_map/ppermute | solution.py:575
  57.3 7.8 %copy-start.1 = (s32[256]{0:T(256)S(1)}, s32[256]{0:T(256)}, u32[]{:S(2)}) copy-start(s32[256]{0:T(256)} %param.15) | copy-start | bytes 3076
  57.3 7.8 %collective-permute-start.10 = (f32[24,512]{1,0:T(8,128)S(1)}, f32[24,512]{1,0:T(8,128)S(1)}, u32[]{:S(2)}, u32[]{:S(2)}) collective-permute-start(f32[24,512]{1,0:T(8,128)S(1)} %get-tuple-element.66.refs_3_), channel_id=1, source_target_pairs={{4,8},{12,16},{20,24},{8,4},{16,12},{24,20},{5,9},{13,17},{21,25},... | collective-permute-start | bytes 147464 | tf_op jit(solution)/shard_map/ppermute | solution.py:575
  58.0 7.2 %collective-permute-start.11 = (f32[24,512]{1,0:T(8,128)S(1)}, f32[24,512]{1,0:T(8,128)S(1)}, u32[]{:S(2)}, u32[]{:S(2)}) collective-permute-start(f32[24,512]{1,0:T(8,128)S(1)} %get-tuple-element.67.refs_4_), channel_id=1, source_target_pairs={{0,4},{8,12},{16,20},{24,28},{4,0},{12,8},{20,16},{28,24},{1,5},{9... | collective-permute-start | bytes 147464 | tf_op jit(solution)/shard_map/ppermute | solution.py:575

commit v10 on v9

--- a/solution.py
+++ b/solution.py
@@ -12,8 +12,8 @@
 RIM = 64
 LANES = 128
 RADIX = 512
-CHUNKS = 4
-EDGE = HALO // RADIX
+EDGE_RADIX = 256
+EDGE = HALO // EDGE_RADIX
 SHRINK = 2.0**-40
 VMEM_BYTES = 16 * 1024 * 1024
 
@@ -23,6 +23,10 @@
 
 def dot(a, b):
     return lax.dot_general(a, b, (((1,), (0,)), ((), ())), preferred_element_type=F32)
+
+
+def dot_nt(a, b):
+    return lax.dot_general(a, b, (((1,), (1,)), ((), ())), preferred_element_type=F32)
 
 
 def split(x):
@@ -76,7 +80,7 @@
     return jnp.where(even, for_previous, for_next), jnp.where(even, for_next, for_previous)
 
 
-def announce_kernel(signs_hbm, ids_hbm, weight_hbm, out_ref, signs, ids, lead, sems):
+def announce_kernel(signs_hbm, ids_hbm, weight_hbm, out_ref, again_ref, signs, ids, lead, sems):
     loads = [
         pltpu.make_async_copy(signs_hbm, signs, sems.at[0]),
         pltpu.make_async_copy(ids_hbm, ids, sems.at[1]),
@@ -93,9 +97,11 @@
     half = HALO // 2
     out_ref[8:11, :] = lead[:, :half]
     out_ref[11:14, :] = lead[:, half:]
+    again_ref[...] = out_ref[...]
 
 
 def setup_kernel(
+    levels,
     counts,
     conn_hbm,
     cell_hbm,
@@ -105,10 +111,11 @@
     cell_ref,
     fr_ref,
     blocks_ref,
-    turned_ref,
     node_hot_ref,
-    node_turn_ref,
-    level_hot_ref,
+    edge_hot_ref,
+    edge_turn_ref,
+    inside_ref,
+    edges_ref,
     cell_hot_ref,
     cell_turn_ref,
     spread_ref,
@@ -123,10 +130,8 @@
     pairs = conn_ref.shape[0]
     slots, padded_order = fr_ref.shape
     node_slots = conn_in.shape[1]
-    levels = level_hot_ref.shape[0] // 16
+    inside, edges = levels_of(levels)
     window = 3 * LANES
-    chunks = sems.shape[0] - 3
-    chunk = slots // chunks
 
     loads = [
         pltpu.make_async_copy(source, target, sems.at[i])
@@ -135,12 +140,10 @@
                 (conn_hbm, conn_in),
                 (cell_hbm, cell_in),
                 (friction_hbm, friction_in),
+                (blocks_hbm, blocks_ref),
             ]
         )
     ]
-    for i in range(chunks):
-        at = pl.ds(i * chunk, chunk)
-        loads.append(pltpu.make_async_copy(blocks_hbm.at[at], blocks_ref.at[at], sems.at[3 + i]))
     for load in loads:
         load.start()
 
@@ -163,7 +166,7 @@
     cell_ref[...] = cells
     node_low = conn % RADIX
     cell_low = cells % LANES
-    node_column = node_low.astype(F32).T
+    edge_column = (conn % EDGE_RADIX).astype(F32).T
     cell_column = cell_low.astype(F32).T
 
     shape = (node_slots, padded_order)
@@ -179,46 +182,51 @@
     fr_ref[...] = jnp.where(live, total, F32(0))
 
     rows = rows_iota((RADIX, LANES))
-    lanes = lanes_iota((LANES, RADIX)).astype(F32)
-    for i in range(chunks):
-        loads[3 + i].wait()
-        for slot in range(i * chunk, (i + 1) * chunk):
-            turned_ref[slot] = blocks_ref[slot].T
-            if slot % 2:
-                continue
-            m = slot // 2
-            at = pl.ds(m * LANES, LANES)
-            node_hot_ref[:, at] = hot(rows == node_low[m : m + 1, :])
-            node_turn_ref[at, :] = hot(lanes == node_column[:, m : m + 1])
-            which = jnp.broadcast_to(conn[m : m + 1, :] // RADIX, (16, LANES))
-            for level in range(levels):
-                level_hot_ref[16 * level : 16 * level + 16, at] = hot(which == level)
-            cell_hot_ref[:, at] = hot(rows[:LANES] == cell_low[m : m + 1, :])
-            cell_turn_ref[at, :] = hot(lanes[:, :LANES] == cell_column[:, m : m + 1])
-
-
-def spread_levels(v_ref, ordered, level_hot, levels, pairs):
+    lanes = lanes_iota((LANES, EDGE_RADIX)).astype(F32)
+    for m in range(pairs):
+        at = pl.ds(m * LANES, LANES)
+        mine = hot(rows == node_low[m : m + 1, :])
+        node_hot_ref[:, at] = mine
+        edge_hot_ref[:, at] = mine[:EDGE_RADIX] + mine[EDGE_RADIX:]
+        edge_turn_ref[at, :] = hot(lanes == edge_column[:, m : m + 1])
+        which = jnp.broadcast_to(conn[m : m + 1, :], (16, LANES))
+        for i, level in enumerate(inside):
+            inside_ref[16 * i : 16 * i + 16, at] = hot(which // RADIX == level)
+        for i, level in enumerate(edges):
+            edges_ref[16 * i : 16 * i + 16, at] = hot(which // EDGE_RADIX == level)
+        cell_hot_ref[:, at] = hot(rows[:LANES] == cell_low[m : m + 1, :])
+        cell_turn_ref[at, :] = hot(lanes[:, :LANES] == cell_column[:, m : m + 1])
+    loads[3].wait()
+
+
+def turn_kernel(blocks, turned_ref):
+    for slot in range(blocks.shape[0]):
+        turned_ref[slot] = blocks[slot].T
+
+
+def spread_levels(v_ref, ordered, level_hot, pairs):
     for m in range(pairs):
         at = pl.ds(m * LANES, LANES)
         values = [ordered[16 * m : 16 * m + 16, c * LANES : (c + 1) * LANES] for c in range(3)]
-        for i, level in enumerate(levels):
-            mask = level_hot[16 * level : 16 * level + 16, at]
+        for i in range(level_hot.shape[0] // 16):
+            mask = level_hot[16 * i : 16 * i + 16, at]
             for c in range(3):
                 row = 48 * i + 16 * c
                 v_ref[row : row + 16, at] = values[c] * mask
 
 
-def edge_levels(levels):
-    return list(range(EDGE)) + list(range(levels - EDGE, levels))
-
-
-def forward_kernel(step, tiles, levels, *refs):
+def levels_of(levels):
+    ratio = RADIX // EDGE_RADIX
+    ends = list(range(EDGE)) + list(range(ratio * levels - EDGE, ratio * levels))
+    return list(range(1, levels - 1)), ends
+
+
+def forward_kernel(step, tiles, *refs):
     block_ref, block_a, block_b, *refs = refs
     first = step == 0
     if not first:
         basal_ref, rim_a, rim_b, *refs = refs
-    _, cell_ref, fr_ref, _, turned, _, node_turn, level_hot, cell_hot, _, *refs = refs
-    spread_ref, _, order_ref, _, *refs = refs
+    cell_ref, fr_ref, factors, edge_turn, edges_ref, cell_hot, spread_ref, order_ref, *refs = refs
     ordered_ref, a_ref, b_ref, *refs = refs
     if not first:
         squares_ref, *refs = refs
@@ -226,9 +234,9 @@
         field_ref, *refs = refs
     f_ref, v_ref = refs
 
-    order = turned.shape[1]
+    order = factors.shape[1]
     padded_order = f_ref.shape[1] // 2
-    pairs = turned.shape[0] // 2
+    pairs = factors.shape[0] // 2
     tile = lax.axis_index("tiles")
 
     lane = lanes_iota((8, LANES))
@@ -285,11 +293,11 @@
             slot = 2 * m + side
             inputs = spread[8 * m : 8 * m + 8, at : at + order] * fr_ref[slot : slot + 1, :order]
             if first:
-                out = dot(inputs.astype(BF16), turned[slot])
+                out = dot_nt(inputs.astype(BF16), factors[slot])
             else:
                 hi = inputs.astype(BF16).astype(F32)
                 both = jnp.concatenate([hi, inputs - hi], axis=0).astype(BF16)
-                out = dot(both, turned[slot])
+                out = dot(both, factors[slot])
                 out = out[:8] + out[8:]
             hi = out.astype(BF16).astype(F32)
             f_ref[16 * m : 16 * m + 8, at : at + order] = hi
@@ -297,11 +305,10 @@
 
     ordered = dot(f_ref[...].astype(BF16), order_ref[...]).astype(BF16)
     ordered_ref[...] = ordered
-    edges = edge_levels(levels)
-    spread_levels(v_ref, ordered, level_hot, edges, pairs)
-    rim = dot(v_ref[...], node_turn[...])
+    spread_levels(v_ref, ordered, edges_ref, pairs)
+    rim = dot(v_ref[...], edge_turn[...])
     sums = [
-        rim[16 * i : 16 * i + 8] + rim[16 * i + 8 : 16 * i + 16] for i in range(3 * len(edges))
+        rim[16 * i : 16 * i + 8] + rim[16 * i + 8 : 16 * i + 16] for i in range(6 * EDGE)
     ]
     half = len(sums) // 2
     for i in range(half):
@@ -309,14 +316,12 @@
         a_ref[8 * i : 8 * i + 8, :], b_ref[8 * i : 8 * i + 8, :] = to_swaps(tile, spill, lead)
 
 
-def inner_kernel(
-    levels, ordered_ref, weight_ref, conn_ref, node_hot, node_turn, level_hot, picked_ref, v_ref
-):
+def inner_kernel(levels, ordered_ref, weight_ref, conn_ref, node_hot, inside_ref, picked_ref, v_ref):
     pairs = conn_ref.shape[0]
     conn = conn_ref[...]
-    inside = list(range(EDGE, levels - EDGE))
-    spread_levels(v_ref, ordered_ref, level_hot, inside, pairs)
-    nodes = dot(v_ref[...], node_turn[...])
+    inside, _ = levels_of(levels)
+    spread_levels(v_ref, ordered_ref, inside_ref, pairs)
+    nodes = dot_nt(v_ref[...], node_hot[...])
     rows = []
     for i in range(3 * len(inside)):
         value = nodes[16 * i : 16 * i + 8] + nodes[16 * i + 8 : 16 * i + 16]
@@ -339,8 +344,7 @@
 
 def adjoint_kernel(last, clusters, levels, *refs):
     block_ref, block_a, block_b, own_a, own_b, new_a, new_b, inner_ref, weight_ref, *refs = refs
-    conn_ref, cell_ref, fr_ref, blocks, _, node_hot, _, _, _, cell_turn, *refs = refs
-    _, spread_turn, _, order_turn, *refs = refs
+    conn_ref, cell_ref, fr_ref, blocks, edge_hot, cell_turn, spread_turn, order_turn, *refs = refs
     if last:
         squares_1, squares_2, ids_ref, *refs = refs
         basal_ref, out_ref, p_ref, n_ref, v_ref = refs
@@ -354,20 +358,22 @@
 
     spill, lead = by_side(tile, own_a[...] + new_a[...], own_b[...] + new_b[...])
     after, before = by_side(tile, block_a[...], block_b[...])
-    rows = [lead[8 * c : 8 * c + 8] * weight_ref[c : c + 1, :HALO] for c in range(3)]
-    for c in range(3):
-        weight = jnp.concatenate([after[8 + c : 9 + c, :], after[11 + c : 12 + c, :]], axis=1)
-        rows.append(spill[8 * c : 8 * c + 8] * weight)
+    rows = []
+    for i in range(3 * EDGE):
+        at = (i // 3) * EDGE_RADIX
+        rows.append(lead[8 * i : 8 * i + 8] * weight_ref[i % 3 : i % 3 + 1, at : at + EDGE_RADIX])
+    for i in range(3 * EDGE):
+        rows.append(spill[8 * i : 8 * i + 8] * after[8 + i : 9 + i, :])
     weighted = jnp.concatenate(rows, axis=0).astype(BF16)
 
     conn = conn_ref[...]
-    edges = edge_levels(levels)
+    _, edges = levels_of(levels)
     step = 2
     for start in range(0, pairs, step):
-        found = dot(weighted, node_hot[:, start * LANES : (start + step) * LANES])
+        found = dot(weighted, edge_hot[:, start * LANES : (start + step) * LANES])
         for i in range(step):
             m = start + i
-            which = conn[m : m + 1, :] // RADIX
+            which = conn[m : m + 1, :] // EDGE_RADIX
             part = found[:, i * LANES : (i + 1) * LANES]
             for c in range(3):
                 value = inner_ref[8 * m : 8 * m + 8, c * LANES : (c + 1) * LANES]
@@ -575,10 +581,10 @@
         return lax.ppermute(a, "tiles", pairs_a), lax.ppermute(b, "tiles", pairs_b)
 
     weight = obs_weight.T
-    block = call(
+    block, again = call(
         announce_kernel,
         "announce",
-        shaped((16, cell_count), F32),
+        [shaped((16, cell_count), F32)] * 2,
         [sign_bits.T, cluster_ids.reshape(1, cell_count), weight],
         [
             pltpu.VMEM((group_size, cell_count), jnp.int32),
@@ -588,20 +594,21 @@
         ],
         [hbm] * 3,
     )
-    block_a, block_b = swapped(block, block)
-
-    shared = call(
-        setup_kernel,
+    block_a, block_b = swapped(again, block)
+
+    conn, cells, fr, loaded, *hots, cell_hot, cell_turn, spread, spread_turn, order, order_turn = call(
+        functools.partial(setup_kernel, levels),
         "setup",
         [
             shaped((pairs, LANES), jnp.int32),
             shaped((pairs, LANES), jnp.int32),
             shaped((slots, padded_order), F32),
             shaped(blocks.shape, BF16),
-            shaped(blocks.shape, BF16),
             shaped((RADIX, refs), BF16),
-            shaped((refs, RADIX), BF16),
-            shaped((16 * levels, refs), BF16),
+            shaped((EDGE_RADIX, refs), BF16),
+            shaped((refs, EDGE_RADIX), BF16),
+            shaped((16 * (levels - 2), refs), BF16),
+            shaped((32 * EDGE, refs), BF16),
             shaped((LANES, refs), BF16),
             shaped((refs, LANES), BF16),
             shaped((LANES, 2 * padded_order), BF16),
@@ -609,30 +616,25 @@
             shaped((2 * padded_order, 3 * LANES), BF16),
             shaped((3 * LANES, 2 * padded_order), BF16),
         ],
-        [
-            elem_counts,
-            connectivity,
-            basal_map,
-            friction.transpose(2, 0, 1),
-            blocks,
-        ],
+        [elem_counts, connectivity, basal_map, friction.transpose(2, 0, 1), blocks],
         [
             pltpu.VMEM(connectivity.shape, jnp.int32),
             pltpu.VMEM(basal_map.shape, jnp.int32),
             pltpu.VMEM((3, slots, node_slots), F32),
-            pltpu.SemaphoreType.DMA((3 + CHUNKS,)),
+            pltpu.SemaphoreType.DMA((4,)),
         ],
         [smem] + [hbm] * 4,
     )
-    conn, node_hot, node_turn, level_hot = shared[0], *shared[5:8]
-
-    edge = shaped((24 * EDGE, RADIX), F32)
+    node_hot, edge_hot, edge_turn, inside, edges = hots
+
+    edge = shaped((24 * EDGE, EDGE_RADIX), F32)
     rim = shaped((group_size, LANES), F32)
     whole = shaped((group_size, window), F32)
     field = shaped((group_size, cell_count), F32)
     everyone = ("tiles", "probes")
 
     carried = []
+    factors = loaded
     squares = []
     samples = None
     for step in range(POWER + 1):
@@ -640,10 +642,11 @@
         out_shape = [shaped((16 * pairs, 3 * LANES), BF16), edge, edge]
         out_shape += [rim] * (step > 0) + [field] * (step == 1)
         ordered, own_a, own_b, *extra = call(
-            functools.partial(forward_kernel, step, tiles, levels),
+            functools.partial(forward_kernel, step, tiles),
             "forward",
             out_shape,
-            [block, block_a, block_b] + carried + [*shared],
+            [block, block_a, block_b, *carried]
+            + [cells, fr, factors, edge_turn, edges, cell_hot, spread, order],
             [
                 pltpu.VMEM((16 * pairs, 2 * padded_order), F32),
                 pltpu.VMEM((96 * EDGE, refs), BF16),
@@ -657,10 +660,11 @@
             functools.partial(inner_kernel, levels),
             "inner",
             shaped((8 * pairs, 3 * LANES), F32),
-            [ordered, weight, conn, node_hot, node_turn, level_hot],
-            [pltpu.VMEM((48 * (levels - 2 * EDGE), refs), BF16)],
+            [ordered, weight, conn, node_hot, inside],
+            [pltpu.VMEM((48 * (levels - 2), refs), BF16)],
         )
-        operands = [block, block_a, block_b, own_a, own_b, new_a, new_b, inner, weight, *shared]
+        operands = [block, block_a, block_b, own_a, own_b, new_a, new_b, inner, weight]
+        operands += [conn, cells, fr, loaded, edge_hot, cell_turn, spread_turn, order_turn]
         if last:
             operands += squares + [cluster_ids.reshape(1, cell_count)]
             message = shaped((lax.axis_size(everyone), group_size, 2 * LANES), BF16)
@@ -679,6 +683,9 @@
             ],
         )
         if not last:
+            if step == 0:
+                *messages, settled = lax.optimization_barrier((*messages, loaded))
+                factors = call(turn_kernel, "turn", shaped(blocks.shape, BF16), [settled])
             carried = [basal, *swapped(*messages)]
 
     gathered = lax.all_to_all(messages[0], everyone, 0, 0)

time: 82.7 us -> 81.9 us (level)
  Pallas kernels: 32.2 us -> 34.2 us
  waiting for transfers between devices: 3.19 us -> 1.61 us
  blocking collectives: 13.1 us -> 11.9 us
    pallas_call x12 -> x13, Pallas kernels: 32.2 us -> 34.2 us  [call(): pl.pallas_call(kernel, out_shape=out_shape, in_specs=in_specs, out_specs=...]
    ppermute x6, waiting for transfers between devices: 3.18 us -> 1.6 us  [swapped(): lax.ppermute(b, 'tiles', pairs_b)]
    all_to_all x1, blocking collectives: 13.1 us -> 11.9 us  [shards(): gathered = lax.all_to_all(messages[0], everyone, 0, 0)]
  transfers between devices with their start and end apart: 12 -> 12, of which waited for: 2 -> 1; matrix products, arithmetic and copies ran while one was open for 0% -> 0% of each run, Pallas kernels for 18% -> 19%
where the time goes in v10:
time: 81.9 us; the launch traced here: 81.6 us
  Pallas kernels  34.2 us (42%)
  starting transfers between devices  32.4 us (40%)
  blocking collectives  11.9 us (15%)
  waiting for transfers between devices  1.61 us (2%)
  between operations  1.51 us (2%)
    pallas_call x13, Pallas kernels, call(): pl.pallas_call(kernel, out_shape=out_shape, in_specs=in_specs, out_specs=...  34.2 us
    ppermute x6, starting transfers between devices, swapped(): lax.ppermute(b, 'tiles', pairs_b)  28 us
    all_to_all x1, blocking collectives, shards(): gathered = lax.all_to_all(messages[0], everyone, 0, 0)  11.9 us
    ppermute x6, starting transfers between devices, swapped(): lax.ppermute(a, 'tiles', pairs_a)  4.38 us
  transfers between devices with their start and end apart: 12, of which 1 were waited for; matrix products, arithmetic and copies ran while one was open for 0% of the time, Pallas kernels for 19%

profile of v10, /device:TPU:0, one launch (start us, length us, event | category | flops | bytes accessed | tf_op | source)
XLA Modules:
  0.0 81.6 jit_solution(32878813531513616)
XLA Ops:
  0.6 0.8 announce.1
  1.4 0.7 collective-permute-start
  2.1 5.8 %collective-permute-start.1 = (f32[16,256]{1,0:T(8,128)S(1)}, f32[16,256]{1,0:T(8,128)S(1)}, u32[]{:S(2)}, u32[]{:S(2)}) collective-permute-start(f32[16,256]{1,0:T(8,128)S(1)} %get-tuple-element.46.refs_0_), channel_id=1, source_target_pairs={{0,4},{8,12},{16,20},{24,28},{4,0},{12,8},{20,16},{28,24},{1,5},{9... | collective-permute-start | bytes 49160 | tf_op jit(solution)/shard_map/ppermute | solution.py:581
  8.5 6.0 %setup.1 = (s32[32,128]{1,0:T(8,128)S(1)}, s32[32,128]{1,0:T(8,128)S(1)}, f32[64,256]{1,0:T(8,128)S(1)}, bf16[64,192,192]{2,1,0:T(8,128)(2,1)S(1)}, bf16[512,409...) custom-call(s32[1]{0:T(128)S(6)} %copy.11.counts, ...), custom_call_target="tpu_custom_call" | custom-call | tf_op jit(solution)/shard_map/setup/pallas_call | solution.py:565
  14.5 0.0 copy-start
  14.5 0.0 collective-permute-done.refs_1_
  14.5 0.0 collective-permute-done.1.refs_2_
  14.5 3.8 %forward.3 = (bf16[512,384]{1,0:T(8,128)(2,1)S(1)}, f32[48,256]{1,0:T(8,128)S(1)}, f32[48,256]{1,0:T(8,128)S(1)}) custom-call(f32[16,256]{1,0:T(8,128)S(1)} %get-tuple-element.46.refs_0_, f32[16,256]{1,0:T(8,128)S(1)} %collective-permute-done.refs_1_, f32[16,256]{1,0:T(8,128)S(1)} %collective-permute-done.1.refs_2_, ...), custom_call_target="tpu_custom_call" | custom-call | tf_op jit(solution)/shard_map/forward/pallas_call | solution.py:565
  18.3 0.7 collective-permute-start.2
  19.0 4.3 %collective-permute-start.3 = (f32[48,256]{1,0:T(8,128)S(1)}, f32[48,256]{1,0:T(8,128)S(1)}, u32[]{:S(2)}, u32[]{:S(2)}) collective-permute-start(f32[48,256]{1,0:T(8,128)S(1)} %get-tuple-element.57.refs_4_), channel_id=1, source_target_pairs={{0,4},{8,12},{16,20},{24,28},{4,0},{12,8},{20,16},{28,24},{1,5},{9... | collective-permute-start | bytes 147464 | tf_op jit(solution)/shard_map/ppermute | solution.py:581
  23.3 0.0 copy-done
  23.3 2.5 %inner.3.refs_7_ = f32[256,384]{1,0:T(8,128)S(1)} custom-call(bf16[512,384]{1,0:T(8,128)(2,1)S(1)} %get-tuple-element.58.ordered_ref, f32[3,4096]{1,0:T(4,128)S(1)} %bitcast.8, s32[32,128]{1,0:T(8,128)S(1)} %get-tuple-element.59.conn_ref.refs_9_, bf16[512,4096]{1,0:T(8,128)(2,1)S(1)} %get-tuple-element.60.node_hot, ...), custom_call_target="tpu_custom_call" | custom-call | tf_op jit(solution)/shard_map/inner/pallas_call | solution.py:565
  25.8 0.0 collective-permute-done.2.refs_5_
  25.9 0.0 collective-permute-done.3.refs_6_
  25.9 2.2 %adjoint.3 = (f32[8,384]{1,0:T(8,128)S(1)}, f32[8,128]{1,0:T(8,128)S(1)}, f32[8,128]{1,0:T(8,128)S(1)}) custom-call(f32[16,256]{1,0:T(8,128)S(1)} %get-tuple-element.46.refs_0_, f32[16,256]{1,0:T(8,128)S(1)} %collective-permute-done.refs_1_, f32[16,256]{1,0:T(8,128)S(1)} %collective-permute-done.1.refs_2_, f32[48,256]{1,0:T(8,128)S(1)} %get-tuple-element.56.refs_3_, ...), custom_call_target="tpu_custom_call" | custom-call | tf_op jit(solution)/shard_map/adjoint/pallas_call | solution.py:565
  28.1 0.8 %collective-permute-start.4 = (f32[8,128]{1,0:T(8,128)S(1)}, f32[8,128]{1,0:T(8,128)S(1)}, u32[]{:S(2)}, u32[]{:S(2)}) collective-permute-start(f32[8,128]{1,0:T(8,128)S(1)} %get-tuple-element.69), channel_id=1, source_target_pairs={{4,8},{12,16},{20,24},{8,4},{16,12},{24,20},{5,9},{13,17},{21,25},... | collective-permute-start | bytes 12296 | tf_op jit(solution)/shard_map/ppermute | solution.py:581
  28.9 4.4 %collective-permute-start.5 = (f32[8,128]{1,0:T(8,128)S(1)}, f32[8,128]{1,0:T(8,128)S(1)}, u32[]{:S(2)}, u32[]{:S(2)}) collective-permute-start(f32[8,128]{1,0:T(8,128)S(1)} %get-tuple-element.70), channel_id=1, source_target_pairs={{0,4},{8,12},{16,20},{24,28},{4,0},{12,8},{20,16},{28,24},{1,5},{9... | collective-permute-start | bytes 12296 | tf_op jit(solution)/shard_map/ppermute | solution.py:581
  33.3 2.0 %turn.1.refs_8_ = bf16[64,192,192]{2,1,0:T(8,128)(2,1)S(1)} custom-call(bf16[64,192,192]{2,1,0:T(8,128)(2,1)S(1)} %get-tuple-element.71.refs_5_.refs_12_.blocks), custom_call_target="tpu_custom_call" | custom-call | tf_op jit(solution)/shard_map/turn/pallas_call | solution.py:565
  35.3 0.0 collective-permute-done.4.refs_4_
  35.3 0.0 collective-permute-done.5.refs_5_
  35.3 3.0 %forward.4 = (bf16[512,384]{1,0:T(8,128)(2,1)S(1)}, f32[48,256]{1,0:T(8,128)S(1)}, f32[48,256]{1,0:T(8,128)S(1)}, f32[8,128]{1,0:T(8,128)S(1)}, f32[8,256]{1,0:T(8,128)S(1)}) custom-call(f32[16,256]{1,0:T(8,128)S(1)} %get-tuple-element.46.refs_0_, f32[16,256]{1,0:T(8,128)S(1)} %collective-permute-done.refs_1_, f32[16,256]{1,0:T(8,128)S(1)} %collective-permute-done.1.refs_2_, ...), custom_call_target="tpu_custom_call" | custom-call | tf_op jit(solution)/shard_map/forward/pallas_call | solution.py:565
  38.3 0.7 collective-permute-start.6
  39.0 4.3 %collective-permute-start.7 = (f32[48,256]{1,0:T(8,128)S(1)}, f32[48,256]{1,0:T(8,128)S(1)}, u32[]{:S(2)}, u32[]{:S(2)}) collective-permute-start(f32[48,256]{1,0:T(8,128)S(1)} %get-tuple-element.73.refs_4_), channel_id=1, source_target_pairs={{0,4},{8,12},{16,20},{24,28},{4,0},{12,8},{20,16},{28,24},{1,5},{9... | collective-permute-start | bytes 147464 | tf_op jit(solution)/shard_map/ppermute | solution.py:581
  43.3 2.5 %inner.4.refs_7_ = f32[256,384]{1,0:T(8,128)S(1)} custom-call(bf16[512,384]{1,0:T(8,128)(2,1)S(1)} %get-tuple-element.74.ordered_ref, f32[3,4096]{1,0:T(4,128)S(1)} %bitcast.10, s32[32,128]{1,0:T(8,128)S(1)} %get-tuple-element.59.conn_ref.refs_9_, bf16[512,4096]{1,0:T(8,128)(2,1)S(1)} %get-tuple-element.60.node_hot, ...), custom_call_target="tpu_custom_call" | custom-call | tf_op jit(solution)/shard_map/inner/pallas_call | solution.py:565
  45.8 0.0 collective-permute-done.6.refs_5_
  45.8 0.0 collective-permute-done.7.refs_6_
  45.9 2.2 %adjoint.4 = (f32[8,384]{1,0:T(8,128)S(1)}, f32[8,128]{1,0:T(8,128)S(1)}, f32[8,128]{1,0:T(8,128)S(1)}) custom-call(f32[16,256]{1,0:T(8,128)S(1)} %get-tuple-element.46.refs_0_, f32[16,256]{1,0:T(8,128)S(1)} %collective-permute-done.refs_1_, f32[16,256]{1,0:T(8,128)S(1)} %collective-permute-done.1.refs_2_, f32[48,256]{1,0:T(8,128)S(1)} %get-tuple-element.72.refs_3_, ...), custom_call_target="tpu_custom_call" | custom-call | tf_op jit(solution)/shard_map/adjoint/pallas_call | solution.py:565
  48.1 0.7 collective-permute-start.8
  48.8 4.4 %collective-permute-start.9 = (f32[8,128]{1,0:T(8,128)S(1)}, f32[8,128]{1,0:T(8,128)S(1)}, u32[]{:S(2)}, u32[]{:S(2)}) collective-permute-start(f32[8,128]{1,0:T(8,128)S(1)} %get-tuple-element.77), channel_id=1, source_target_pairs={{0,4},{8,12},{16,20},{24,28},{4,0},{12,8},{20,16},{28,24},{1,5},{9... | collective-permute-start | bytes 12296 | tf_op jit(solution)/shard_map/ppermute | solution.py:581
  53.1 0.0 collective-permute-done.8.refs_4_
  53.1 1.6 %collective-permute-done.9.refs_5_ = f32[8,128]{1,0:T(8,128)S(1)} collective-permute-done((f32[8,128]{1,0:T(8,128)S(1)}, f32[8,128]{1,0:T(8,128)S(1)}, u32[]{:S(2)}, u32[]{:S(2)}) %collective-permute-start.9) | collective-permute-done | bytes 4128 | tf_op jit(solution)/shard_map/ppermute | solution.py:581
  54.7 0.0 copy-start.1
  54.7 3.0 %forward.5 = (bf16[512,384]{1,0:T(8,128)(2,1)S(1)}, f32[48,256]{1,0:T(8,128)S(1)}, f32[48,256]{1,0:T(8,128)S(1)}, f32[8,128]{1,0:T(8,128)S(1)}) custom-call(f32[16,256]{1,0:T(8,128)S(1)} %get-tuple-element.46.refs_0_, f32[16,256]{1,0:T(8,128)S(1)} %collective-permute-done.refs_1_, f32[16,256]{1,0:T(8,128)S(1)} %collective-permute-done.1.refs_2_, ...), custom_call_target="tpu_custom_call" | custom-call | tf_op jit(solution)/shard_map/forward/pallas_call | solution.py:565
  57.7 0.9 %collective-permute-start.10 = (f32[48,256]{1,0:T(8,128)S(1)}, f32[48,256]{1,0:T(8,128)S(1)}, u32[]{:S(2)}, u32[]{:S(2)}) collective-permute-start(f32[48,256]{1,0:T(8,128)S(1)} %get-tuple-element.78.refs_3_), channel_id=1, source_target_pairs={{4,8},{12,16},{20,24},{8,4},{16,12},{24,20},{5,9},{13,17},{21,25},... | collective-permute-start | bytes 147464 | tf_op jit(solution)/shard_map/ppermute | solution.py:581
  58.6 4.8 %collective-permute-start.11 = (f32[48,256]{1,0:T(8,128)S(1)}, f32[48,256]{1,0:T(8,128)S(1)}, u32[]{:S(2)}, u32[]{:S(2)}) collective-permute-start(f32[48,256]{1,0:T(8,128)S(1)} %get-tuple-element.79.refs_4_), channel_id=1, source_target_pairs={{0,4},{8,12},{16,20},{24,28},{4,0},{12,8},{20,16},{28,24},{1,5},{9... | collective-permute-start | bytes 147464 | tf_op jit(solution)/shard_map/ppermute | solution.py:581
  63.4 2.5 %inner.5.refs_7_ = f32[256,384]{1,0:T(8,128)S(1)} custom-call(bf16[512,384]{1,0:T(8,128)(2,1)S(1)} %get-tuple-element.80.ordered_ref, f32[3,4096]{1,0:T(4,128)S(1)} %bitcast.12, s32[32,128]{1,0:T(8,128)S(1)} %get-tuple-element.59.conn_ref.refs_9_, bf16[512,4096]{1,0:T(8,128)(2,1)S(1)} %get-tuple-element.60.node_hot, ...), custom_call_target="tpu_custom_call" | custom-call | tf_op jit(solution)/shard_map/inner/pallas_call | solution.py:565
  65.9 0.0 collective-permute-done.10.refs_5_
  65.9 0.0 collective-permute-done.11.refs_6_
  65.9 0.0 copy-done.1
  65.9 2.2 %adjoint.5 = (f32[8,384]{1,0:T(8,128)S(1)}, bf16[32,8,256]{2,1,0:T(8,128)(2,1)S(1)}) custom-call(f32[16,256]{1,0:T(8,128)S(1)} %get-tuple-element.46.refs_0_, f32[16,256]{1,0:T(8,128)S(1)} %collective-permute-done.refs_1_, f32[16,256]{1,0:T(8,128)S(1)} %collective-permute-done.1.refs_2_, f32[48,256]{1,0:T(8,128)S(1)} %get-tuple-element.78.refs_3_, ...), custom_call_target="tpu_custom_call" | custom-call | tf_op jit(solution)/shard_map/adjoint/pallas_call | solution.py:565
  68.2 11.9 %all_to_all.5 = bf16[32,8,256]{2,1,0:T(8,128)(2,1)S(1)} all-to-all(bf16[32,8,256]{2,1,0:T(8,128)(2,1)S(1)} %get-tuple-element.83), channel_id=1, replica_groups=mesh['tiles'=8,'probes'=4] {'tiles','probes'}, dimensions={0} | all-to-all | bytes 262144 | tf_op jit(solution)/shard_map/all_to_all | solution.py:691
  80.1 1.5 %gram.1 = (f32[8,256]{1,0:T(8,128)}, f32[8,256]{1,0:T(8,128)}, f32[8,8,32]{2,1,0:T(8,128)}) custom-call(bf16[8,4,8,256]{3,2,1,0:T(8,128)(2,1)S(1)} %bitcast.14, f32[8,384]{1,0:T(8,128)S(1)} %get-tuple-element.84.own_ref, f32[8,256]{1,0:T(8,128)S(1)} %get-tuple-element.85.samples_in), custom_call_target="tpu_custom_call" | custom-call | tf_op jit(solution)/shard_map/gram/pallas_call | solution.py:565
Async XLA Ops:
  1.4 13.1 %collective-permute-start = (f32[16,256]{1,0:T(8,128)S(1)}, f32[16,256]{1,0:T(8,128)S(1)}, u32[]{:S(2)}, u32[]{:S(2)}) collective-permute-start(f32[16,256]{1,0:T(8,128)S(1)} %get-tuple-element.47), channel_id=1, source_target_pairs={{4,8},{12,16},{20,24},{8,4},{16,12},{24,20},{5,9},{13,17},{21,25},... | collective-permute-start | bytes 49160 | tf_op jit(solution)/shard_map/ppermute | solution.py:581
  2.1 12.4 %collective-permute-start.1 = (f32[16,256]{1,0:T(8,128)S(1)}, f32[16,256]{1,0:T(8,128)S(1)}, u32[]{:S(2)}, u32[]{:S(2)}) collective-permute-start(f32[16,256]{1,0:T(8,128)S(1)} %get-tuple-element.46.refs_0_), channel_id=1, source_target_pairs={{0,4},{8,12},{16,20},{24,28},{4,0},{12,8},{20,16},{28,24},{1,5},{9... | collective-permute-start | bytes 49160 | tf_op jit(solution)/shard_map/ppermute | solution.py:581
  14.5 8.8 %copy-start = (f32[4096,3]{0,1:T(4,128)S(1)}, f32[4096,3]{0,1:T(4,128)}, u32[]{:S(2)}) copy-start(f32[4096,3]{0,1:T(4,128)} %param.13) | copy-start | bytes 147460
  18.3 7.5 %collective-permute-start.2 = (f32[48,256]{1,0:T(8,128)S(1)}, f32[48,256]{1,0:T(8,128)S(1)}, u32[]{:S(2)}, u32[]{:S(2)}) collective-permute-start(f32[48,256]{1,0:T(8,128)S(1)} %get-tuple-element.56.refs_3_), channel_id=1, source_target_pairs={{4,8},{12,16},{20,24},{8,4},{16,12},{24,20},{5,9},{13,17},{21,25},... | collective-permute-start | bytes 147464 | tf_op jit(solution)/shard_map/ppermute | solution.py:581
  19.0 6.9 %collective-permute-start.3 = (f32[48,256]{1,0:T(8,128)S(1)}, f32[48,256]{1,0:T(8,128)S(1)}, u32[]{:S(2)}, u32[]{:S(2)}) collective-permute-start(f32[48,256]{1,0:T(8,128)S(1)} %get-tuple-element.57.refs_4_), channel_id=1, source_target_pairs={{0,4},{8,12},{16,20},{24,28},{4,0},{12,8},{20,16},{28,24},{1,5},{9... | collective-permute-start | bytes 147464 | tf_op jit(solution)/shard_map/ppermute | solution.py:581
  28.1 7.2 %collective-permute-start.4 = (f32[8,128]{1,0:T(8,128)S(1)}, f32[8,128]{1,0:T(8,128)S(1)}, u32[]{:S(2)}, u32[]{:S(2)}) collective-permute-start(f32[8,128]{1,0:T(8,128)S(1)} %get-tuple-element.69), channel_id=1, source_target_pairs={{4,8},{12,16},{20,24},{8,4},{16,12},{24,20},{5,9},{13,17},{21,25},... | collective-permute-start | bytes 12296 | tf_op jit(solution)/shard_map/ppermute | solution.py:581
  28.9 6.4 %collective-permute-start.5 = (f32[8,128]{1,0:T(8,128)S(1)}, f32[8,128]{1,0:T(8,128)S(1)}, u32[]{:S(2)}, u32[]{:S(2)}) collective-permute-start(f32[8,128]{1,0:T(8,128)S(1)} %get-tuple-element.70), channel_id=1, source_target_pairs={{0,4},{8,12},{16,20},{24,28},{4,0},{12,8},{20,16},{28,24},{1,5},{9... | collective-permute-start | bytes 12296 | tf_op jit(solution)/shard_map/ppermute | solution.py:581
  38.3 7.5 %collective-permute-start.6 = (f32[48,256]{1,0:T(8,128)S(1)}, f32[48,256]{1,0:T(8,128)S(1)}, u32[]{:S(2)}, u32[]{:S(2)}) collective-permute-start(f32[48,256]{1,0:T(8,128)S(1)} %get-tuple-element.72.refs_3_), channel_id=1, source_target_pairs={{4,8},{12,16},{20,24},{8,4},{16,12},{24,20},{5,9},{13,17},{21,25},... | collective-permute-start | bytes 147464 | tf_op jit(solution)/shard_map/ppermute | solution.py:581
  39.0 6.9 %collective-permute-start.7 = (f32[48,256]{1,0:T(8,128)S(1)}, f32[48,256]{1,0:T(8,128)S(1)}, u32[]{:S(2)}, u32[]{:S(2)}) collective-permute-start(f32[48,256]{1,0:T(8,128)S(1)} %get-tuple-element.73.refs_4_), channel_id=1, source_target_pairs={{0,4},{8,12},{16,20},{24,28},{4,0},{12,8},{20,16},{28,24},{1,5},{9... | collective-permute-start | bytes 147464 | tf_op jit(solution)/shard_map/ppermute | solution.py:581
  48.1 5.0 %collective-permute-start.8 = (f32[8,128]{1,0:T(8,128)S(1)}, f32[8,128]{1,0:T(8,128)S(1)}, u32[]{:S(2)}, u32[]{:S(2)}) collective-permute-start(f32[8,128]{1,0:T(8,128)S(1)} %get-tuple-element.76), channel_id=1, source_target_pairs={{4,8},{12,16},{20,24},{8,4},{16,12},{24,20},{5,9},{13,17},{21,25},... | collective-permute-start | bytes 12296 | tf_op jit(solution)/shard_map/ppermute | solution.py:581
  48.8 5.9 %collective-permute-start.9 = (f32[8,128]{1,0:T(8,128)S(1)}, f32[8,128]{1,0:T(8,128)S(1)}, u32[]{:S(2)}, u32[]{:S(2)}) collective-permute-start(f32[8,128]{1,0:T(8,128)S(1)} %get-tuple-element.77), channel_id=1, source_target_pairs={{0,4},{8,12},{16,20},{24,28},{4,0},{12,8},{20,16},{28,24},{1,5},{9... | collective-permute-start | bytes 12296 | tf_op jit(solution)/shard_map/ppermute | solution.py:581
  54.7 11.2 %copy-start.1 = (s32[256]{0:T(256)S(1)}, s32[256]{0:T(256)}, u32[]{:S(2)}) copy-start(s32[256]{0:T(256)} %param.15) | copy-start | bytes 3076
  57.7 8.2 %collective-permute-start.10 = (f32[48,256]{1,0:T(8,128)S(1)}, f32[48,256]{1,0:T(8,128)S(1)}, u32[]{:S(2)}, u32[]{:S(2)}) collective-permute-start(f32[48,256]{1,0:T(8,128)S(1)} %get-tuple-element.78.refs_3_), channel_id=1, source_target_pairs={{4,8},{12,16},{20,24},{8,4},{16,12},{24,20},{5,9},{13,17},{21,25},... | collective-permute-start | bytes 147464 | tf_op jit(solution)/shard_map/ppermute | solution.py:581
  58.6 7.3 %collective-permute-start.11 = (f32[48,256]{1,0:T(8,128)S(1)}, f32[48,256]{1,0:T(8,128)S(1)}, u32[]{:S(2)}, u32[]{:S(2)}) collective-permute-start(f32[48,256]{1,0:T(8,128)S(1)} %get-tuple-element.79.refs_4_), channel_id=1, source_target_pairs={{0,4},{8,12},{16,20},{24,28},{4,0},{12,8},{20,16},{28,24},{1,5},{9... | collective-permute-start | bytes 147464 | tf_op jit(solution)/shard_map/ppermute | solution.py:581

commit v11 on v10

--- a/solution.py
+++ b/solution.py
@@ -29,6 +29,10 @@
     return lax.dot_general(a, b, (((1,), (1,)), ((), ())), preferred_element_type=F32)
 
 
+def product(turned):
+    return dot if turned else dot_nt
+
+
 def split(x):
     hi = x.astype(BF16)
     return hi, (x - hi.astype(F32)).astype(BF16)
@@ -44,6 +48,10 @@
 
 def hot(mask):
     return jnp.where(mask, F32(1), F32(0)).astype(BF16)
+
+
+def hot16(a, b):
+    return jnp.where(a == b, jnp.ones((), BF16), jnp.zeros((), BF16))
 
 
 def spread_matrix(node_slots, padded_order, turned=False):
@@ -113,15 +121,10 @@
     blocks_ref,
     node_hot_ref,
     edge_hot_ref,
-    edge_turn_ref,
-    inside_ref,
-    edges_ref,
+    level_hot_ref,
     cell_hot_ref,
-    cell_turn_ref,
     spread_ref,
-    spread_turn_ref,
     order_ref,
-    order_turn_ref,
     conn_in,
     cell_in,
     friction_in,
@@ -130,7 +133,6 @@
     pairs = conn_ref.shape[0]
     slots, padded_order = fr_ref.shape
     node_slots = conn_in.shape[1]
-    inside, edges = levels_of(levels)
     window = 3 * LANES
 
     loads = [
@@ -148,9 +150,7 @@
         load.start()
 
     spread_ref[...] = spread_matrix(node_slots, padded_order)
-    spread_turn_ref[...] = spread_matrix(node_slots, padded_order, True)
     order_ref[...] = order_matrix(node_slots, padded_order)
-    order_turn_ref[...] = order_matrix(node_slots, padded_order, True)
 
     def paired(ref):
         return jnp.concatenate(
@@ -164,10 +164,6 @@
     cells = paired(cell_in)
     cells = jnp.where(cells < RIM, cells + (window - RIM), cells - RIM)
     cell_ref[...] = cells
-    node_low = conn % RADIX
-    cell_low = cells % LANES
-    edge_column = (conn % EDGE_RADIX).astype(F32).T
-    cell_column = cell_low.astype(F32).T
 
     shape = (node_slots, padded_order)
     total = jnp.zeros((slots, padded_order), F32)
@@ -181,52 +177,69 @@
     live = rows_iota(total.shape) < counts[0]
     fr_ref[...] = jnp.where(live, total, F32(0))
 
-    rows = rows_iota((RADIX, LANES))
-    lanes = lanes_iota((LANES, EDGE_RADIX)).astype(F32)
+    rows = rows_iota((EDGE_RADIX, LANES)).astype(F32).astype(BF16)
+    low = conn % RADIX
+    halves = []
+    for at in range(0, RADIX, EDGE_RADIX):
+        inside = (low >= at) & (low < at + EDGE_RADIX)
+        halves.append(jnp.where(inside, low - at, -1).astype(F32))
+    which = (conn // RADIX).astype(F32)
+    cell_low = (cells % LANES).astype(F32)
     for m in range(pairs):
         at = pl.ds(m * LANES, LANES)
-        mine = hot(rows == node_low[m : m + 1, :])
-        node_hot_ref[:, at] = mine
-        edge_hot_ref[:, at] = mine[:EDGE_RADIX] + mine[EDGE_RADIX:]
-        edge_turn_ref[at, :] = hot(lanes == edge_column[:, m : m + 1])
-        which = jnp.broadcast_to(conn[m : m + 1, :], (16, LANES))
-        for i, level in enumerate(inside):
-            inside_ref[16 * i : 16 * i + 16, at] = hot(which // RADIX == level)
-        for i, level in enumerate(edges):
-            edges_ref[16 * i : 16 * i + 16, at] = hot(which // EDGE_RADIX == level)
-        cell_hot_ref[:, at] = hot(rows[:LANES] == cell_low[m : m + 1, :])
-        cell_turn_ref[at, :] = hot(lanes[:, :LANES] == cell_column[:, m : m + 1])
+        total = jnp.zeros((EDGE_RADIX, LANES), BF16)
+        for i, half in enumerate(halves):
+            row = jnp.broadcast_to(half[m : m + 1, :], (EDGE_RADIX, LANES)).astype(BF16)
+            mine = hot16(rows, row)
+            node_hot_ref[i * EDGE_RADIX : (i + 1) * EDGE_RADIX, at] = mine
+            total = total + mine
+        edge_hot_ref[:, at] = total
+        row = jnp.broadcast_to(which[m : m + 1, :], (16, LANES)).astype(BF16)
+        for level in range(levels):
+            mine = hot16(row, jnp.full((16, LANES), level, BF16))
+            level_hot_ref[16 * level : 16 * level + 16, at] = mine
+        row = jnp.broadcast_to(cell_low[m : m + 1, :], (LANES, LANES)).astype(BF16)
+        cell_hot_ref[:, at] = hot16(rows[:LANES], row)
     loads[3].wait()
 
 
-def turn_kernel(blocks, turned_ref):
+def turn_kernel(
+    blocks, conn_ref, cell_ref, turned_ref, node_turn_ref, cell_turn_ref, spread_turn_ref, order_turn_ref
+):
+    node_slots = blocks.shape[1] // 3
+    padded_order = order_turn_ref.shape[1] // 2
+    spread_turn_ref[...] = spread_matrix(node_slots, padded_order, True)
+    order_turn_ref[...] = order_matrix(node_slots, padded_order, True)
+    nodes = (conn_ref[...] % RADIX).astype(F32).T
+    cells = (cell_ref[...] % LANES).astype(F32).T
+    lanes = lanes_iota((LANES, RADIX)).astype(F32)
     for slot in range(blocks.shape[0]):
         turned_ref[slot] = blocks[slot].T
-
-
-def spread_levels(v_ref, ordered, level_hot, pairs):
+        if slot % 2:
+            continue
+        m = slot // 2
+        at = pl.ds(m * LANES, LANES)
+        node_turn_ref[at, :] = hot(lanes == nodes[:, m : m + 1])
+        cell_turn_ref[at, :] = hot(lanes[:, :LANES] == cells[:, m : m + 1])
+
+
+def spread_levels(v_ref, ordered, level_hot, levels, pairs):
     for m in range(pairs):
         at = pl.ds(m * LANES, LANES)
         values = [ordered[16 * m : 16 * m + 16, c * LANES : (c + 1) * LANES] for c in range(3)]
-        for i in range(level_hot.shape[0] // 16):
-            mask = level_hot[16 * i : 16 * i + 16, at]
+        for i, level in enumerate(levels):
+            mask = level_hot[16 * level : 16 * level + 16, at]
             for c in range(3):
                 row = 48 * i + 16 * c
                 v_ref[row : row + 16, at] = values[c] * mask
 
 
-def levels_of(levels):
-    ratio = RADIX // EDGE_RADIX
-    ends = list(range(EDGE)) + list(range(ratio * levels - EDGE, ratio * levels))
-    return list(range(1, levels - 1)), ends
-
-
-def forward_kernel(step, tiles, *refs):
+def forward_kernel(step, tiles, levels, *refs):
     block_ref, block_a, block_b, *refs = refs
     first = step == 0
     if not first:
         basal_ref, rim_a, rim_b, *refs = refs
-    cell_ref, fr_ref, factors, edge_turn, edges_ref, cell_hot, spread_ref, order_ref, *refs = refs
+    cell_ref, fr_ref, factors, node_map, level_hot, cell_hot, spread_ref, order_ref, *refs = refs
     ordered_ref, a_ref, b_ref, *refs = refs
     if not first:
         squares_ref, *refs = refs
@@ -293,11 +306,11 @@
             slot = 2 * m + side
             inputs = spread[8 * m : 8 * m + 8, at : at + order] * fr_ref[slot : slot + 1, :order]
             if first:
-                out = dot_nt(inputs.astype(BF16), factors[slot])
+                out = product(step > 0)(inputs.astype(BF16), factors[slot])
             else:
                 hi = inputs.astype(BF16).astype(F32)
                 both = jnp.concatenate([hi, inputs - hi], axis=0).astype(BF16)
-                out = dot(both, factors[slot])
+                out = product(step > 0)(both, factors[slot])
                 out = out[:8] + out[8:]
             hi = out.astype(BF16).astype(F32)
             f_ref[16 * m : 16 * m + 8, at : at + order] = hi
@@ -305,22 +318,20 @@
 
     ordered = dot(f_ref[...].astype(BF16), order_ref[...]).astype(BF16)
     ordered_ref[...] = ordered
-    spread_levels(v_ref, ordered, edges_ref, pairs)
-    rim = dot(v_ref[...], edge_turn[...])
-    sums = [
-        rim[16 * i : 16 * i + 8] + rim[16 * i + 8 : 16 * i + 16] for i in range(6 * EDGE)
-    ]
+    spread_levels(v_ref, ordered, level_hot, (0, levels - 1), pairs)
+    rim = product(step > 0)(v_ref[...], node_map[...])
+    sums = [rim[16 * i : 16 * i + 8] + rim[16 * i + 8 : 16 * i + 16] for i in range(6)]
     half = len(sums) // 2
     for i in range(half):
         lead, spill = sums[i], sums[half + i]
         a_ref[8 * i : 8 * i + 8, :], b_ref[8 * i : 8 * i + 8, :] = to_swaps(tile, spill, lead)
 
 
-def inner_kernel(levels, ordered_ref, weight_ref, conn_ref, node_hot, inside_ref, picked_ref, v_ref):
+def inner_kernel(levels, ordered_ref, weight_ref, conn_ref, node_hot, level_hot, picked_ref, v_ref):
     pairs = conn_ref.shape[0]
     conn = conn_ref[...]
-    inside, _ = levels_of(levels)
-    spread_levels(v_ref, ordered_ref, inside_ref, pairs)
+    inside = range(1, levels - 1)
+    spread_levels(v_ref, ordered_ref, level_hot, inside, pairs)
     nodes = dot_nt(v_ref[...], node_hot[...])
     rows = []
     for i in range(3 * len(inside)):
@@ -342,9 +353,9 @@
                 picked_ref[8 * m : 8 * m + 8, c * LANES : (c + 1) * LANES] = chosen[8 * c : 8 * c + 8]
 
 
-def adjoint_kernel(last, clusters, levels, *refs):
+def adjoint_kernel(step, last, clusters, levels, *refs):
     block_ref, block_a, block_b, own_a, own_b, new_a, new_b, inner_ref, weight_ref, *refs = refs
-    conn_ref, cell_ref, fr_ref, blocks, edge_hot, cell_turn, spread_turn, order_turn, *refs = refs
+    conn_ref, cell_ref, fr_ref, blocks, edge_hot, cell_map, spread_map, order_map, *refs = refs
     if last:
         squares_1, squares_2, ids_ref, *refs = refs
         basal_ref, out_ref, p_ref, n_ref, v_ref = refs
@@ -360,18 +371,22 @@
     after, before = by_side(tile, block_a[...], block_b[...])
     rows = []
     for i in range(3 * EDGE):
-        at = (i // 3) * EDGE_RADIX
-        rows.append(lead[8 * i : 8 * i + 8] * weight_ref[i % 3 : i % 3 + 1, at : at + EDGE_RADIX])
+        c, at = i % 3, (i // 3) * EDGE_RADIX
+        value = lead[8 * c : 8 * c + 8, at : at + EDGE_RADIX]
+        rows.append(value * weight_ref[c : c + 1, at : at + EDGE_RADIX])
     for i in range(3 * EDGE):
-        rows.append(spill[8 * i : 8 * i + 8] * after[8 + i : 9 + i, :])
+        c, at = i % 3, (i // 3) * EDGE_RADIX
+        value = spill[8 * c : 8 * c + 8, at : at + EDGE_RADIX]
+        rows.append(value * after[8 + i : 9 + i, :])
     weighted = jnp.concatenate(rows, axis=0).astype(BF16)
 
     conn = conn_ref[...]
-    _, edges = levels_of(levels)
-    step = 2
-    for start in range(0, pairs, step):
-        found = dot(weighted, edge_hot[:, start * LANES : (start + step) * LANES])
-        for i in range(step):
+    first = levels * RADIX // EDGE_RADIX - EDGE
+    edges = [*range(EDGE), *range(first, first + EDGE)]
+    width = 2
+    for start in range(0, pairs, width):
+        found = dot(weighted, edge_hot[:, start * LANES : (start + width) * LANES])
+        for i in range(width):
             m = start + i
             which = conn[m : m + 1, :] // EDGE_RADIX
             part = found[:, i * LANES : (i + 1) * LANES]
@@ -381,7 +396,7 @@
                     row = 24 * at + 8 * c
                     value = jnp.where(which == level, part[row : row + 8], value)
                 n_ref[8 * m : 8 * m + 8, c * LANES : (c + 1) * LANES] = value
-    natural = dot(n_ref[...].astype(BF16), order_turn[...])
+    natural = product(step > 0)(n_ref[...].astype(BF16), order_map[...])
     p_ref[...] = jnp.zeros_like(p_ref)
     for m in range(pairs):
         for side in range(2):
@@ -392,7 +407,7 @@
             p_ref[8 * m : 8 * m + 8, at : at + order] = out
 
     hi, lo = split(p_ref[...])
-    partial = dot(jnp.concatenate([hi, lo], axis=0), spread_turn[...])
+    partial = product(step > 0)(jnp.concatenate([hi, lo], axis=0), spread_map[...])
     half = 8 * pairs
     partial = partial[:half] + partial[half:]
     cells = cell_ref[...]
@@ -403,7 +418,7 @@
         hi = rows.astype(BF16).astype(F32)
         both = jnp.concatenate([hi, rows - hi], axis=0)
         v_ref[:, m * LANES : (m + 1) * LANES] = both.astype(BF16)
-    basal = dot(v_ref[...], cell_turn[...])
+    basal = product(step > 0)(v_ref[...], cell_map[...])
     basal = basal[:24] + basal[24:]
     parts = [basal[8 * i : 8 * i + 8] for i in range(3)]
     for i in range(3):
@@ -596,7 +611,7 @@
     )
     block_a, block_b = swapped(again, block)
 
-    conn, cells, fr, loaded, *hots, cell_hot, cell_turn, spread, spread_turn, order, order_turn = call(
+    conn, cells, fr, loaded, node_hot, edge_hot, level_hot, cell_hot, spread, order = call(
         functools.partial(setup_kernel, levels),
         "setup",
         [
@@ -606,15 +621,10 @@
             shaped(blocks.shape, BF16),
             shaped((RADIX, refs), BF16),
             shaped((EDGE_RADIX, refs), BF16),
-            shaped((refs, EDGE_RADIX), BF16),
-            shaped((16 * (levels - 2), refs), BF16),
-            shaped((32 * EDGE, refs), BF16),
+            shaped((16 * levels, refs), BF16),
             shaped((LANES, refs), BF16),
-            shaped((refs, LANES), BF16),
             shaped((LANES, 2 * padded_order), BF16),
-            shaped((2 * padded_order, LANES), BF16),
             shaped((2 * padded_order, 3 * LANES), BF16),
-            shaped((3 * LANES, 2 * padded_order), BF16),
         ],
         [elem_counts, connectivity, basal_map, friction.transpose(2, 0, 1), blocks],
         [
@@ -625,9 +635,9 @@
         ],
         [smem] + [hbm] * 4,
     )
-    node_hot, edge_hot, edge_turn, inside, edges = hots
-
-    edge = shaped((24 * EDGE, EDGE_RADIX), F32)
+    factors, node_map, cell_map, spread_map, order_map = loaded, node_hot, cell_hot, spread, order
+
+    edge = shaped((24, HALO), F32)
     rim = shaped((group_size, LANES), F32)
     whole = shaped((group_size, window), F32)
     field = shaped((group_size, cell_count), F32)
@@ -642,14 +652,14 @@
         out_shape = [shaped((16 * pairs, 3 * LANES), BF16), edge, edge]
         out_shape += [rim] * (step > 0) + [field] * (step == 1)
         ordered, own_a, own_b, *extra = call(
-            functools.partial(forward_kernel, step, tiles),
+            functools.partial(forward_kernel, step, tiles, levels),
             "forward",
             out_shape,
             [block, block_a, block_b, *carried]
-            + [cells, fr, factors, edge_turn, edges, cell_hot, spread, order],
+            + [cells, fr, factors, node_map, level_hot, cell_hot, spread, order],
             [
                 pltpu.VMEM((16 * pairs, 2 * padded_order), F32),
-                pltpu.VMEM((96 * EDGE, refs), BF16),
+                pltpu.VMEM((96, refs), BF16),
             ],
         )
         squares += extra[:1]
@@ -660,11 +670,11 @@
             functools.partial(inner_kernel, levels),
             "inner",
             shaped((8 * pairs, 3 * LANES), F32),
-            [ordered, weight, conn, node_hot, inside],
+            [ordered, weight, conn, node_hot, level_hot],
             [pltpu.VMEM((48 * (levels - 2), refs), BF16)],
         )
         operands = [block, block_a, block_b, own_a, own_b, new_a, new_b, inner, weight]
-        operands += [conn, cells, fr, loaded, edge_hot, cell_turn, spread_turn, order_turn]
+        operands += [conn, cells, fr, loaded, edge_hot, cell_map, spread_map, order_map]
         if last:
             operands += squares + [cluster_ids.reshape(1, cell_count)]
             message = shaped((lax.axis_size(everyone), group_size, 2 * LANES), BF16)
@@ -672,7 +682,7 @@
         else:
             out_shape = [whole, rim, rim]
         basal, *messages = call(
-            functools.partial(adjoint_kernel, last, tiles, levels),
+            functools.partial(adjoint_kernel, step, last, tiles, levels),
             "adjoint",
             out_shape,
             operands,
@@ -685,7 +695,18 @@
         if not last:
             if step == 0:
                 *messages, settled = lax.optimization_barrier((*messages, loaded))
-                factors = call(turn_kernel, "turn", shaped(blocks.shape, BF16), [settled])
+                factors, node_map, cell_map, spread_map, order_map = call(
+                    turn_kernel,
+                    "turn",
+                    [
+                        shaped(blocks.shape, BF16),
+                        shaped((refs, RADIX), BF16),
+                        shaped((refs, LANES), BF16),
+                        shaped((2 * padded_order, LANES), BF16),
+                        shaped((3 * LANES, 2 * padded_order), BF16),
+                    ],
+                    [settled, conn, cells],
+                )
             carried = [basal, *swapped(*messages)]
 
     gathered = lax.all_to_all(messages[0], everyone, 0, 0)

time: 81.9 us -> 79.5 us (0.971)
  Pallas kernels: 34.2 us -> 32 us
    pallas_call x13, Pallas kernels: 34.2 us -> 32 us  [call(): pl.pallas_call(kernel, out_shape=out_shape, in_specs=in_specs, out_specs=...]
  transfers between devices with their start and end apart: 12 -> 12, of which waited for: 1 -> 1; matrix products, arithmetic and copies ran while one was open for 0% -> 0% of each run, Pallas kernels for 19% -> 18%
where the time goes in v11:
time: 79.5 us; the launch traced here: 79.1 us
  Pallas kernels  32 us (40%)
  starting transfers between devices  31.6 us (40%)
  blocking collectives  12.3 us (15%)
  waiting for transfers between devices  1.61 us (2%)
  between operations  1.5 us (2%)
    pallas_call x13, Pallas kernels, call(): pl.pallas_call(kernel, out_shape=out_shape, in_specs=in_specs, out_specs=...  32 us
    ppermute x6, starting transfers between devices, swapped(): lax.ppermute(b, 'tiles', pairs_b)  27.2 us
    all_to_all x1, blocking collectives, shards(): gathered = lax.all_to_all(messages[0], everyone, 0, 0)  12.3 us
    ppermute x6, starting transfers between devices, swapped(): lax.ppermute(a, 'tiles', pairs_a)  4.4 us
    ppermute x6, waiting for transfers between devices, swapped(): lax.ppermute(b, 'tiles', pairs_b)  1.6 us
  transfers between devices with their start and end apart: 12, of which 1 were waited for; matrix products, arithmetic and copies ran while one was open for 0% of the time, Pallas kernels for 18%

profile of v11, /device:TPU:0, one launch (start us, length us, event | category | flops | bytes accessed | tf_op | source)
XLA Modules:
  0.0 79.1 jit_solution(12700867150804473206)
XLA Ops:
  0.6 0.8 announce.1
  1.4 0.7 collective-permute-start
  2.1 5.8 %collective-permute-start.1 = (f32[16,256]{1,0:T(8,128)S(1)}, f32[16,256]{1,0:T(8,128)S(1)}, u32[]{:S(2)}, u32[]{:S(2)}) collective-permute-start(f32[16,256]{1,0:T(8,128)S(1)} %get-tuple-element.46.refs_0_), channel_id=1, source_target_pairs={{0,4},{8,12},{16,20},{24,28},{4,0},{12,8},{20,16},{28,24},{1,5},{9... | collective-permute-start | bytes 49160 | tf_op jit(solution)/shard_map/ppermute | solution.py:596
  8.5 3.3 %setup.1 = (s32[32,128]{1,0:T(8,128)S(1)}, s32[32,128]{1,0:T(8,128)S(1)}, f32[64,256]{1,0:T(8,128)S(1)}, bf16[64,192,192]{2,1,0:T(8,128)(2,1)S(1)}, bf16[512,409...) custom-call(s32[1]{0:T(128)S(6)} %copy.11.counts, ...), custom_call_target="tpu_custom_call" | custom-call | tf_op jit(solution)/shard_map/setup/pallas_call | solution.py:580
  11.8 0.0 collective-permute-done.refs_1_
  11.8 0.0 collective-permute-done.1.refs_2_
  11.8 0.0 copy-start
  11.8 3.8 %forward.3 = (bf16[512,384]{1,0:T(8,128)(2,1)S(1)}, f32[24,512]{1,0:T(8,128)S(1)}, f32[24,512]{1,0:T(8,128)S(1)}) custom-call(f32[16,256]{1,0:T(8,128)S(1)} %get-tuple-element.46.refs_0_, f32[16,256]{1,0:T(8,128)S(1)} %collective-permute-done.refs_1_, f32[16,256]{1,0:T(8,128)S(1)} %collective-permute-done.1.refs_2_, ...), custom_call_target="tpu_custom_call" | custom-call | tf_op jit(solution)/shard_map/forward/pallas_call | solution.py:580
  15.6 0.7 collective-permute-start.2
  16.3 4.3 %collective-permute-start.3 = (f32[24,512]{1,0:T(8,128)S(1)}, f32[24,512]{1,0:T(8,128)S(1)}, u32[]{:S(2)}, u32[]{:S(2)}) collective-permute-start(f32[24,512]{1,0:T(8,128)S(1)} %get-tuple-element.57.refs_4_), channel_id=1, source_target_pairs={{0,4},{8,12},{16,20},{24,28},{4,0},{12,8},{20,16},{28,24},{1,5},{9... | collective-permute-start | bytes 147464 | tf_op jit(solution)/shard_map/ppermute | solution.py:596
  20.6 0.0 copy-done
  20.6 2.6 %inner.3.refs_7_ = f32[256,384]{1,0:T(8,128)S(1)} custom-call(bf16[512,384]{1,0:T(8,128)(2,1)S(1)} %get-tuple-element.58.ordered_ref, f32[3,4096]{1,0:T(4,128)S(1)} %bitcast.8, s32[32,128]{1,0:T(8,128)S(1)} %get-tuple-element.59.conn_ref.refs_9_, bf16[512,4096]{1,0:T(8,128)(2,1)S(1)} %get-tuple-element.51.refs_6_.node_hot, ...), custom_call_target="tpu_custom_call" | custom-call | tf_op jit(solution)/shard_map/inner/pallas_call | solution.py:580
  23.2 0.0 collective-permute-done.2.refs_5_
  23.2 0.0 collective-permute-done.3.refs_6_
  23.2 2.5 %adjoint.3 = (f32[8,384]{1,0:T(8,128)S(1)}, f32[8,128]{1,0:T(8,128)S(1)}, f32[8,128]{1,0:T(8,128)S(1)}) custom-call(f32[16,256]{1,0:T(8,128)S(1)} %get-tuple-element.46.refs_0_, f32[16,256]{1,0:T(8,128)S(1)} %collective-permute-done.refs_1_, f32[16,256]{1,0:T(8,128)S(1)} %collective-permute-done.1.refs_2_, f32[24,512]{1,0:T(8,128)S(1)} %get-tuple-element.56.refs_3_, ...), custom_call_target="tpu_custom_call" | custom-call | tf_op jit(solution)/shard_map/adjoint/pallas_call | solution.py:580
  25.7 0.9 %collective-permute-start.4 = (f32[8,128]{1,0:T(8,128)S(1)}, f32[8,128]{1,0:T(8,128)S(1)}, u32[]{:S(2)}, u32[]{:S(2)}) collective-permute-start(f32[8,128]{1,0:T(8,128)S(1)} %get-tuple-element.64), channel_id=1, source_target_pairs={{4,8},{12,16},{20,24},{8,4},{16,12},{24,20},{5,9},{13,17},{21,25},... | collective-permute-start | bytes 12296 | tf_op jit(solution)/shard_map/ppermute | solution.py:596
  26.6 4.4 %collective-permute-start.5 = (f32[8,128]{1,0:T(8,128)S(1)}, f32[8,128]{1,0:T(8,128)S(1)}, u32[]{:S(2)}, u32[]{:S(2)}) collective-permute-start(f32[8,128]{1,0:T(8,128)S(1)} %get-tuple-element.65), channel_id=1, source_target_pairs={{0,4},{8,12},{16,20},{24,28},{4,0},{12,8},{20,16},{28,24},{1,5},{9... | collective-permute-start | bytes 12296 | tf_op jit(solution)/shard_map/ppermute | solution.py:596
  30.9 3.3 %turn.1 = (bf16[64,192,192]{2,1,0:T(8,128)(2,1)S(1)}, bf16[4096,512]{1,0:T(8,128)(2,1)S(1)}, bf16[4096,128]{1,0:T(8,128)(2,1)S(1)}, bf16[512,128]{1,0:T(8,128)(2,1)S(1)}, bf16[384,512]{1,0:T(8,128)(2,1)S(1)}) custom-call(bf16[64,192,192]{2,1,0:T(8,128)(2,1)S(1)} %get-tuple-element.66.refs_5_.refs_12_.blocks, ...), custom_call_target="tpu_custom_call" | custom-call | tf_op jit(solution)/shard_map/turn/pallas_call | solution.py:580
  34.3 0.0 collective-permute-done.4.refs_4_
  34.3 0.0 collective-permute-done.5.refs_5_
  34.3 2.4 %forward.4 = (bf16[512,384]{1,0:T(8,128)(2,1)S(1)}, f32[24,512]{1,0:T(8,128)S(1)}, f32[24,512]{1,0:T(8,128)S(1)}, f32[8,128]{1,0:T(8,128)S(1)}, f32[8,256]{1,0:T(8,128)S(1)}) custom-call(f32[16,256]{1,0:T(8,128)S(1)} %get-tuple-element.46.refs_0_, f32[16,256]{1,0:T(8,128)S(1)} %collective-permute-done.refs_1_, f32[16,256]{1,0:T(8,128)S(1)} %collective-permute-done.1.refs_2_, ...), custom_call_target="tpu_custom_call" | custom-call | tf_op jit(solution)/shard_map/forward/pallas_call | solution.py:580
  36.7 0.7 collective-permute-start.6
  37.4 3.6 %collective-permute-start.7 = (f32[24,512]{1,0:T(8,128)S(1)}, f32[24,512]{1,0:T(8,128)S(1)}, u32[]{:S(2)}, u32[]{:S(2)}) collective-permute-start(f32[24,512]{1,0:T(8,128)S(1)} %get-tuple-element.70.refs_4_), channel_id=1, source_target_pairs={{0,4},{8,12},{16,20},{24,28},{4,0},{12,8},{20,16},{28,24},{1,5},{9... | collective-permute-start | bytes 147464 | tf_op jit(solution)/shard_map/ppermute | solution.py:596
  41.0 2.6 %inner.4.refs_7_ = f32[256,384]{1,0:T(8,128)S(1)} custom-call(bf16[512,384]{1,0:T(8,128)(2,1)S(1)} %get-tuple-element.71.ordered_ref, f32[3,4096]{1,0:T(4,128)S(1)} %bitcast.10, s32[32,128]{1,0:T(8,128)S(1)} %get-tuple-element.59.conn_ref.refs_9_, bf16[512,4096]{1,0:T(8,128)(2,1)S(1)} %get-tuple-element.51.refs_6_.node_hot, ...), custom_call_target="tpu_custom_call" | custom-call | tf_op jit(solution)/shard_map/inner/pallas_call | solution.py:580
  43.5 0.0 collective-permute-done.6.refs_5_
  43.6 0.0 collective-permute-done.7.refs_6_
  43.6 2.2 %adjoint.4 = (f32[8,384]{1,0:T(8,128)S(1)}, f32[8,128]{1,0:T(8,128)S(1)}, f32[8,128]{1,0:T(8,128)S(1)}) custom-call(f32[16,256]{1,0:T(8,128)S(1)} %get-tuple-element.46.refs_0_, f32[16,256]{1,0:T(8,128)S(1)} %collective-permute-done.refs_1_, f32[16,256]{1,0:T(8,128)S(1)} %collective-permute-done.1.refs_2_, f32[24,512]{1,0:T(8,128)S(1)} %get-tuple-element.69.refs_3_, ...), custom_call_target="tpu_custom_call" | custom-call | tf_op jit(solution)/shard_map/adjoint/pallas_call | solution.py:580
  45.8 0.7 collective-permute-start.8
  46.5 4.2 %collective-permute-start.9 = (f32[8,128]{1,0:T(8,128)S(1)}, f32[8,128]{1,0:T(8,128)S(1)}, u32[]{:S(2)}, u32[]{:S(2)}) collective-permute-start(f32[8,128]{1,0:T(8,128)S(1)} %get-tuple-element.77), channel_id=1, source_target_pairs={{0,4},{8,12},{16,20},{24,28},{4,0},{12,8},{20,16},{28,24},{1,5},{9... | collective-permute-start | bytes 12296 | tf_op jit(solution)/shard_map/ppermute | solution.py:596
  50.6 0.0 collective-permute-done.8.refs_4_
  50.6 1.6 %collective-permute-done.9.refs_5_ = f32[8,128]{1,0:T(8,128)S(1)} collective-permute-done((f32[8,128]{1,0:T(8,128)S(1)}, f32[8,128]{1,0:T(8,128)S(1)}, u32[]{:S(2)}, u32[]{:S(2)}) %collective-permute-start.9) | collective-permute-done | bytes 4128 | tf_op jit(solution)/shard_map/ppermute | solution.py:596
  52.2 2.4 %forward.5 = (bf16[512,384]{1,0:T(8,128)(2,1)S(1)}, f32[24,512]{1,0:T(8,128)S(1)}, f32[24,512]{1,0:T(8,128)S(1)}, f32[8,128]{1,0:T(8,128)S(1)}) custom-call(f32[16,256]{1,0:T(8,128)S(1)} %get-tuple-element.46.refs_0_, f32[16,256]{1,0:T(8,128)S(1)} %collective-permute-done.refs_1_, f32[16,256]{1,0:T(8,128)S(1)} %collective-permute-done.1.refs_2_, ...), custom_call_target="tpu_custom_call" | custom-call | tf_op jit(solution)/shard_map/forward/pallas_call | solution.py:580
  54.6 0.0 copy-start.1
  54.6 0.9 %collective-permute-start.10 = (f32[24,512]{1,0:T(8,128)S(1)}, f32[24,512]{1,0:T(8,128)S(1)}, u32[]{:S(2)}, u32[]{:S(2)}) collective-permute-start(f32[24,512]{1,0:T(8,128)S(1)} %get-tuple-element.78.refs_3_), channel_id=1, source_target_pairs={{4,8},{12,16},{20,24},{8,4},{16,12},{24,20},{5,9},{13,17},{21,25},... | collective-permute-start | bytes 147464 | tf_op jit(solution)/shard_map/ppermute | solution.py:596
  55.5 4.9 %collective-permute-start.11 = (f32[24,512]{1,0:T(8,128)S(1)}, f32[24,512]{1,0:T(8,128)S(1)}, u32[]{:S(2)}, u32[]{:S(2)}) collective-permute-start(f32[24,512]{1,0:T(8,128)S(1)} %get-tuple-element.79.refs_4_), channel_id=1, source_target_pairs={{0,4},{8,12},{16,20},{24,28},{4,0},{12,8},{20,16},{28,24},{1,5},{9... | collective-permute-start | bytes 147464 | tf_op jit(solution)/shard_map/ppermute | solution.py:596
  60.4 2.6 %inner.5.refs_7_ = f32[256,384]{1,0:T(8,128)S(1)} custom-call(bf16[512,384]{1,0:T(8,128)(2,1)S(1)} %get-tuple-element.80.ordered_ref, f32[3,4096]{1,0:T(4,128)S(1)} %bitcast.12, s32[32,128]{1,0:T(8,128)S(1)} %get-tuple-element.59.conn_ref.refs_9_, bf16[512,4096]{1,0:T(8,128)(2,1)S(1)} %get-tuple-element.51.refs_6_.node_hot, ...), custom_call_target="tpu_custom_call" | custom-call | tf_op jit(solution)/shard_map/inner/pallas_call | solution.py:580
  63.0 0.0 collective-permute-done.10.refs_5_
  63.0 0.0 collective-permute-done.11.refs_6_
  63.0 0.0 copy-done.1
  63.0 2.3 %adjoint.5 = (f32[8,384]{1,0:T(8,128)S(1)}, bf16[32,8,256]{2,1,0:T(8,128)(2,1)S(1)}) custom-call(f32[16,256]{1,0:T(8,128)S(1)} %get-tuple-element.46.refs_0_, f32[16,256]{1,0:T(8,128)S(1)} %collective-permute-done.refs_1_, f32[16,256]{1,0:T(8,128)S(1)} %collective-permute-done.1.refs_2_, f32[24,512]{1,0:T(8,128)S(1)} %get-tuple-element.78.refs_3_, ...), custom_call_target="tpu_custom_call" | custom-call | tf_op jit(solution)/shard_map/adjoint/pallas_call | solution.py:580
  65.3 12.3 %all_to_all.5 = bf16[32,8,256]{2,1,0:T(8,128)(2,1)S(1)} all-to-all(bf16[32,8,256]{2,1,0:T(8,128)(2,1)S(1)} %get-tuple-element.83), channel_id=1, replica_groups=mesh['tiles'=8,'probes'=4] {'tiles','probes'}, dimensions={0} | all-to-all | bytes 262144 | tf_op jit(solution)/shard_map/all_to_all | solution.py:712
  77.6 1.5 %gram.1 = (f32[8,256]{1,0:T(8,128)}, f32[8,256]{1,0:T(8,128)}, f32[8,8,32]{2,1,0:T(8,128)}) custom-call(bf16[8,4,8,256]{3,2,1,0:T(8,128)(2,1)S(1)} %bitcast.14, f32[8,384]{1,0:T(8,128)S(1)} %get-tuple-element.84.own_ref, f32[8,256]{1,0:T(8,128)S(1)} %get-tuple-element.85.samples_in), custom_call_target="tpu_custom_call" | custom-call | tf_op jit(solution)/shard_map/gram/pallas_call | solution.py:580
Async XLA Ops:
  1.4 10.4 %collective-permute-start = (f32[16,256]{1,0:T(8,128)S(1)}, f32[16,256]{1,0:T(8,128)S(1)}, u32[]{:S(2)}, u32[]{:S(2)}) collective-permute-start(f32[16,256]{1,0:T(8,128)S(1)} %get-tuple-element.47), channel_id=1, source_target_pairs={{4,8},{12,16},{20,24},{8,4},{16,12},{24,20},{5,9},{13,17},{21,25},... | collective-permute-start | bytes 49160 | tf_op jit(solution)/shard_map/ppermute | solution.py:596
  2.1 9.8 %collective-permute-start.1 = (f32[16,256]{1,0:T(8,128)S(1)}, f32[16,256]{1,0:T(8,128)S(1)}, u32[]{:S(2)}, u32[]{:S(2)}) collective-permute-start(f32[16,256]{1,0:T(8,128)S(1)} %get-tuple-element.46.refs_0_), channel_id=1, source_target_pairs={{0,4},{8,12},{16,20},{24,28},{4,0},{12,8},{20,16},{28,24},{1,5},{9... | collective-permute-start | bytes 49160 | tf_op jit(solution)/shard_map/ppermute | solution.py:596
  11.8 8.8 %copy-start = (f32[4096,3]{0,1:T(4,128)S(1)}, f32[4096,3]{0,1:T(4,128)}, u32[]{:S(2)}) copy-start(f32[4096,3]{0,1:T(4,128)} %param.13) | copy-start | bytes 147460
  15.6 7.6 %collective-permute-start.2 = (f32[24,512]{1,0:T(8,128)S(1)}, f32[24,512]{1,0:T(8,128)S(1)}, u32[]{:S(2)}, u32[]{:S(2)}) collective-permute-start(f32[24,512]{1,0:T(8,128)S(1)} %get-tuple-element.56.refs_3_), channel_id=1, source_target_pairs={{4,8},{12,16},{20,24},{8,4},{16,12},{24,20},{5,9},{13,17},{21,25},... | collective-permute-start | bytes 147464 | tf_op jit(solution)/shard_map/ppermute | solution.py:596
  16.3 6.9 %collective-permute-start.3 = (f32[24,512]{1,0:T(8,128)S(1)}, f32[24,512]{1,0:T(8,128)S(1)}, u32[]{:S(2)}, u32[]{:S(2)}) collective-permute-start(f32[24,512]{1,0:T(8,128)S(1)} %get-tuple-element.57.refs_4_), channel_id=1, source_target_pairs={{0,4},{8,12},{16,20},{24,28},{4,0},{12,8},{20,16},{28,24},{1,5},{9... | collective-permute-start | bytes 147464 | tf_op jit(solution)/shard_map/ppermute | solution.py:596
  25.7 8.6 %collective-permute-start.4 = (f32[8,128]{1,0:T(8,128)S(1)}, f32[8,128]{1,0:T(8,128)S(1)}, u32[]{:S(2)}, u32[]{:S(2)}) collective-permute-start(f32[8,128]{1,0:T(8,128)S(1)} %get-tuple-element.64), channel_id=1, source_target_pairs={{4,8},{12,16},{20,24},{8,4},{16,12},{24,20},{5,9},{13,17},{21,25},... | collective-permute-start | bytes 12296 | tf_op jit(solution)/shard_map/ppermute | solution.py:596
  26.6 7.7 %collective-permute-start.5 = (f32[8,128]{1,0:T(8,128)S(1)}, f32[8,128]{1,0:T(8,128)S(1)}, u32[]{:S(2)}, u32[]{:S(2)}) collective-permute-start(f32[8,128]{1,0:T(8,128)S(1)} %get-tuple-element.65), channel_id=1, source_target_pairs={{0,4},{8,12},{16,20},{24,28},{4,0},{12,8},{20,16},{28,24},{1,5},{9... | collective-permute-start | bytes 12296 | tf_op jit(solution)/shard_map/ppermute | solution.py:596
  36.7 6.9 %collective-permute-start.6 = (f32[24,512]{1,0:T(8,128)S(1)}, f32[24,512]{1,0:T(8,128)S(1)}, u32[]{:S(2)}, u32[]{:S(2)}) collective-permute-start(f32[24,512]{1,0:T(8,128)S(1)} %get-tuple-element.69.refs_3_), channel_id=1, source_target_pairs={{4,8},{12,16},{20,24},{8,4},{16,12},{24,20},{5,9},{13,17},{21,25},... | collective-permute-start | bytes 147464 | tf_op jit(solution)/shard_map/ppermute | solution.py:596
  37.4 6.2 %collective-permute-start.7 = (f32[24,512]{1,0:T(8,128)S(1)}, f32[24,512]{1,0:T(8,128)S(1)}, u32[]{:S(2)}, u32[]{:S(2)}) collective-permute-start(f32[24,512]{1,0:T(8,128)S(1)} %get-tuple-element.70.refs_4_), channel_id=1, source_target_pairs={{0,4},{8,12},{16,20},{24,28},{4,0},{12,8},{20,16},{28,24},{1,5},{9... | collective-permute-start | bytes 147464 | tf_op jit(solution)/shard_map/ppermute | solution.py:596
  45.8 4.8 %collective-permute-start.8 = (f32[8,128]{1,0:T(8,128)S(1)}, f32[8,128]{1,0:T(8,128)S(1)}, u32[]{:S(2)}, u32[]{:S(2)}) collective-permute-start(f32[8,128]{1,0:T(8,128)S(1)} %get-tuple-element.76), channel_id=1, source_target_pairs={{4,8},{12,16},{20,24},{8,4},{16,12},{24,20},{5,9},{13,17},{21,25},... | collective-permute-start | bytes 12296 | tf_op jit(solution)/shard_map/ppermute | solution.py:596
  46.5 5.7 %collective-permute-start.9 = (f32[8,128]{1,0:T(8,128)S(1)}, f32[8,128]{1,0:T(8,128)S(1)}, u32[]{:S(2)}, u32[]{:S(2)}) collective-permute-start(f32[8,128]{1,0:T(8,128)S(1)} %get-tuple-element.77), channel_id=1, source_target_pairs={{0,4},{8,12},{16,20},{24,28},{4,0},{12,8},{20,16},{28,24},{1,5},{9... | collective-permute-start | bytes 12296 | tf_op jit(solution)/shard_map/ppermute | solution.py:596
  54.6 8.4 %copy-start.1 = (s32[256]{0:T(256)S(1)}, s32[256]{0:T(256)}, u32[]{:S(2)}) copy-start(s32[256]{0:T(256)} %param.15) | copy-start | bytes 3076
  54.6 8.4 %collective-permute-start.10 = (f32[24,512]{1,0:T(8,128)S(1)}, f32[24,512]{1,0:T(8,128)S(1)}, u32[]{:S(2)}, u32[]{:S(2)}) collective-permute-start(f32[24,512]{1,0:T(8,128)S(1)} %get-tuple-element.78.refs_3_), channel_id=1, source_target_pairs={{4,8},{12,16},{20,24},{8,4},{16,12},{24,20},{5,9},{13,17},{21,25},... | collective-permute-start | bytes 147464 | tf_op jit(solution)/shard_map/ppermute | solution.py:596
  55.5 7.5 %collective-permute-start.11 = (f32[24,512]{1,0:T(8,128)S(1)}, f32[24,512]{1,0:T(8,128)S(1)}, u32[]{:S(2)}, u32[]{:S(2)}) collective-permute-start(f32[24,512]{1,0:T(8,128)S(1)} %get-tuple-element.79.refs_4_), channel_id=1, source_target_pairs={{0,4},{8,12},{16,20},{24,28},{4,0},{12,8},{20,16},{28,24},{1,5},{9... | collective-permute-start | bytes 147464 | tf_op jit(solution)/shard_map/ppermute | solution.py:596

commit v12 on v11

--- a/solution.py
+++ b/solution.py
@@ -54,24 +54,36 @@
     return jnp.where(a == b, jnp.ones((), BF16), jnp.zeros((), BF16))
 
 
+def lane_tiles(count, tile):
+    return jnp.concatenate([tile(i * LANES) for i in range(count)], axis=1)
+
+
 def spread_matrix(node_slots, padded_order, turned=False):
-    shape = (2 * node_slots, 2 * padded_order)
-    row, col = rows_iota(shape), lanes_iota(shape)
+    pair, wide = 2 * node_slots, 2 * padded_order
+
+    def start(at):
+        return (at // node_slots) * padded_order + 3 * (at % node_slots)
+
+    def near(gap):
+        return hot((gap >= 0) & (gap < 3))
+
     if turned:
-        row, col = lanes_iota(shape[::-1]), rows_iota(shape[::-1])
-    gap = col - ((row // node_slots) * padded_order + 3 * (row % node_slots))
-    return hot((gap >= 0) & (gap < 3))
+        return near(rows_iota((wide, pair)) - start(lanes_iota((1, pair))))
+    gap = lanes_iota((pair, LANES)) - start(rows_iota((pair, LANES)))
+    return lane_tiles(wide // LANES, lambda at: near(gap + at))
 
 
 def order_matrix(node_slots, padded_order, turned=False):
-    pair = 2 * node_slots
-    shape = (2 * padded_order, 3 * pair)
-    row, col = rows_iota(shape), lanes_iota(shape)
-    if turned:
-        row, col = lanes_iota(shape[::-1]), rows_iota(shape[::-1])
-    inner = col % pair
-    source = (inner // node_slots) * padded_order + 3 * (inner % node_slots) + col // pair
-    return hot(row == source)
+    pair, wide = 2 * node_slots, 2 * padded_order
+
+    def source(at):
+        inner = at % pair
+        return (inner // node_slots) * padded_order + 3 * (inner % node_slots) + at // pair
+
+    if not turned:
+        return hot(rows_iota((wide, 3 * pair)) == source(lanes_iota((1, 3 * pair))))
+    gap = lanes_iota((3 * pair, LANES)) - source(rows_iota((3 * pair, LANES)))
+    return lane_tiles(wide // LANES, lambda at: hot(gap + at == 0))
 
 
 def colour_of(ids):
@@ -106,6 +118,15 @@
     out_ref[8:11, :] = lead[:, :half]
     out_ref[11:14, :] = lead[:, half:]
     again_ref[...] = out_ref[...]
+
+
+def halves_of(conn):
+    low = conn % RADIX
+    halves = []
+    for at in range(0, RADIX, EDGE_RADIX):
+        inside = (low >= at) & (low < at + EDGE_RADIX)
+        halves.append(jnp.where(inside, low - at, -1).astype(F32))
+    return halves
 
 
 def setup_kernel(
@@ -178,11 +199,7 @@
     fr_ref[...] = jnp.where(live, total, F32(0))
 
     rows = rows_iota((EDGE_RADIX, LANES)).astype(F32).astype(BF16)
-    low = conn % RADIX
-    halves = []
-    for at in range(0, RADIX, EDGE_RADIX):
-        inside = (low >= at) & (low < at + EDGE_RADIX)
-        halves.append(jnp.where(inside, low - at, -1).astype(F32))
+    halves = halves_of(conn)
     which = (conn // RADIX).astype(F32)
     cell_low = (cells % LANES).astype(F32)
     for m in range(pairs):
@@ -203,24 +220,31 @@
     loads[3].wait()
 
 
-def turn_kernel(
-    blocks, conn_ref, cell_ref, turned_ref, node_turn_ref, cell_turn_ref, spread_turn_ref, order_turn_ref
-):
+def turn_nodes_kernel(conn_ref, node_turn_ref):
+    columns = [half.T for half in halves_of(conn_ref[...])]
+    lanes = lanes_iota((LANES, EDGE_RADIX)).astype(F32).astype(BF16)
+    for m in range(conn_ref.shape[0]):
+        for i, column in enumerate(columns):
+            row = jnp.broadcast_to(column[:, m : m + 1], (LANES, LANES)).astype(BF16)
+            row = jnp.concatenate([row] * (EDGE_RADIX // LANES), axis=1)
+            at = pl.ds(i * EDGE_RADIX, EDGE_RADIX)
+            node_turn_ref[m * LANES : (m + 1) * LANES, at] = hot16(lanes, row)
+
+
+def turn_kernel(blocks, cell_ref, turned_ref, cell_turn_ref, spread_turn_ref, order_turn_ref):
     node_slots = blocks.shape[1] // 3
     padded_order = order_turn_ref.shape[1] // 2
     spread_turn_ref[...] = spread_matrix(node_slots, padded_order, True)
     order_turn_ref[...] = order_matrix(node_slots, padded_order, True)
-    nodes = (conn_ref[...] % RADIX).astype(F32).T
     cells = (cell_ref[...] % LANES).astype(F32).T
-    lanes = lanes_iota((LANES, RADIX)).astype(F32)
+    lanes = lanes_iota((LANES, LANES)).astype(F32).astype(BF16)
     for slot in range(blocks.shape[0]):
         turned_ref[slot] = blocks[slot].T
         if slot % 2:
             continue
         m = slot // 2
-        at = pl.ds(m * LANES, LANES)
-        node_turn_ref[at, :] = hot(lanes == nodes[:, m : m + 1])
-        cell_turn_ref[at, :] = hot(lanes[:, :LANES] == cells[:, m : m + 1])
+        row = jnp.broadcast_to(cells[:, m : m + 1], (LANES, LANES)).astype(BF16)
+        cell_turn_ref[m * LANES : (m + 1) * LANES, :] = hot16(lanes, row)
 
 
 def spread_levels(v_ref, ordered, level_hot, levels, pairs):
@@ -665,6 +689,10 @@
         squares += extra[:1]
         if step == 1:
             samples = extra[1]
+        if step == 0:
+            own_a, own_b, settled = lax.optimization_barrier((own_a, own_b, conn))
+            shape = shaped((refs, RADIX), BF16)
+            node_map = call(turn_nodes_kernel, "turn_nodes", shape, [settled])
         new_a, new_b = swapped(own_a, own_b)
         inner = call(
             functools.partial(inner_kernel, levels),
@@ -673,6 +701,8 @@
             [ordered, weight, conn, node_hot, level_hot],
             [pltpu.VMEM((48 * (levels - 2), refs), BF16)],
         )
+        if step == 0:
+            inner, node_map = lax.optimization_barrier((inner, node_map))
         operands = [block, block_a, block_b, own_a, own_b, new_a, new_b, inner, weight]
         operands += [conn, cells, fr, loaded, edge_hot, cell_map, spread_map, order_map]
         if last:
@@ -695,17 +725,16 @@
         if not last:
             if step == 0:
                 *messages, settled = lax.optimization_barrier((*messages, loaded))
-                factors, node_map, cell_map, spread_map, order_map = call(
+                factors, cell_map, spread_map, order_map = call(
                     turn_kernel,
                     "turn",
                     [
                         shaped(blocks.shape, BF16),
-                        shaped((refs, RADIX), BF16),
                         shaped((refs, LANES), BF16),
                         shaped((2 * padded_order, LANES), BF16),
                         shaped((3 * LANES, 2 * padded_order), BF16),
                     ],
-                    [settled, conn, cells],
+                    [settled, cells],
                 )
             carried = [basal, *swapped(*messages)]
 

time: 79.5 us -> 78.7 us (0.990)
    pallas_call x13 -> x14, Pallas kernels: 32 us -> 32 us  [call(): pl.pallas_call(kernel, out_shape=out_shape, in_specs=in_specs, out_specs=...]
where the time goes in v12:
time: 78.7 us; the launch traced here: 78.3 us
  Pallas kernels  32 us (41%)
  starting transfers between devices  31.5 us (40%)
  blocking collectives  11.7 us (15%)
  waiting for transfers between devices  1.61 us (2%)
  between operations  1.5 us (2%)
    pallas_call x14, Pallas kernels, call(): pl.pallas_call(kernel, out_shape=out_shape, in_specs=in_specs, out_specs=...  32 us
    ppermute x6, starting transfers between devices, swapped(): lax.ppermute(b, 'tiles', pairs_b)  27.1 us
    all_to_all x1, blocking collectives, shards(): gathered = lax.all_to_all(messages[0], everyone, 0, 0)  11.7 us
    ppermute x6, starting transfers between devices, swapped(): lax.ppermute(a, 'tiles', pairs_a)  4.4 us
    ppermute x6, waiting for transfers between devices, swapped(): lax.ppermute(b, 'tiles', pairs_b)  1.6 us
  transfers between devices with their start and end apart: 12, of which 1 were waited for; matrix products, arithmetic and copies ran while one was open for 0% of the time, Pallas kernels for 18%

profile of v12, /device:TPU:0, one launch (start us, length us, event | category | flops | bytes accessed | tf_op | source)
XLA Modules:
  0.0 78.3 jit_solution(1278219351999302719)
XLA Ops:
  0.6 0.8 announce.1
  1.4 0.7 collective-permute-start
  2.1 5.8 %collective-permute-start.1 = (f32[16,256]{1,0:T(8,128)S(1)}, f32[16,256]{1,0:T(8,128)S(1)}, u32[]{:S(2)}, u32[]{:S(2)}) collective-permute-start(f32[16,256]{1,0:T(8,128)S(1)} %get-tuple-element.50.refs_0_), channel_id=1, source_target_pairs={{0,4},{8,12},{16,20},{24,28},{4,0},{12,8},{20,16},{28,24},{1,5},{9... | collective-permute-start | bytes 49160 | tf_op jit(solution)/shard_map/ppermute | solution.py:620
  8.5 3.3 %setup.1 = (s32[32,128]{1,0:T(8,128)S(1)}, s32[32,128]{1,0:T(8,128)S(1)}, f32[64,256]{1,0:T(8,128)S(1)}, bf16[64,192,192]{2,1,0:T(8,128)(2,1)S(1)}, bf16[512,409...) custom-call(s32[1]{0:T(128)S(6)} %copy.11.counts, ...), custom_call_target="tpu_custom_call" | custom-call | tf_op jit(solution)/shard_map/setup/pallas_call | solution.py:604
  11.8 0.0 collective-permute-done.refs_1_
  11.8 0.0 collective-permute-done.1.refs_2_
  11.8 0.0 copy-start
  11.8 3.8 %forward.3 = (bf16[512,384]{1,0:T(8,128)(2,1)S(1)}, f32[24,512]{1,0:T(8,128)S(1)}, f32[24,512]{1,0:T(8,128)S(1)}) custom-call(f32[16,256]{1,0:T(8,128)S(1)} %get-tuple-element.50.refs_0_, f32[16,256]{1,0:T(8,128)S(1)} %collective-permute-done.refs_1_, f32[16,256]{1,0:T(8,128)S(1)} %collective-permute-done.1.refs_2_, ...), custom_call_target="tpu_custom_call" | custom-call | tf_op jit(solution)/shard_map/forward/pallas_call | solution.py:604
  15.6 0.7 collective-permute-start.2
  16.3 4.3 %collective-permute-start.3 = (f32[24,512]{1,0:T(8,128)S(1)}, f32[24,512]{1,0:T(8,128)S(1)}, u32[]{:S(2)}, u32[]{:S(2)}) collective-permute-start(f32[24,512]{1,0:T(8,128)S(1)} %get-tuple-element.64.refs_4_), channel_id=1, source_target_pairs={{0,4},{8,12},{16,20},{24,28},{4,0},{12,8},{20,16},{28,24},{1,5},{9... | collective-permute-start | bytes 147464 | tf_op jit(solution)/shard_map/ppermute | solution.py:620
  20.6 0.0 copy-done
  20.6 2.5 %inner.3.refs_7_ = f32[256,384]{1,0:T(8,128)S(1)} custom-call(bf16[512,384]{1,0:T(8,128)(2,1)S(1)} %get-tuple-element.65.ordered_ref, f32[3,4096]{1,0:T(4,128)S(1)} %bitcast.8, s32[32,128]{1,0:T(8,128)S(1)} %get-tuple-element.66.conn_ref.refs_9_, bf16[512,4096]{1,0:T(8,128)(2,1)S(1)} %get-tuple-element.55.refs_6_.node_hot, ...), custom_call_target="tpu_custom_call" | custom-call | tf_op jit(solution)/shard_map/inner/pallas_call | solution.py:604
  23.2 0.8 %turn_nodes.1.refs_9_ = bf16[4096,512]{1,0:T(8,128)(2,1)S(1)} custom-call(s32[32,128]{1,0:T(8,128)S(1)} %get-tuple-element.66.conn_ref.refs_9_), custom_call_target="tpu_custom_call" | custom-call | tf_op jit(solution)/shard_map/turn_nodes/pallas_call | solution.py:604
  24.0 0.0 collective-permute-done.2.refs_5_
  24.0 0.0 collective-permute-done.3.refs_6_
  24.0 2.5 %adjoint.3 = (f32[8,384]{1,0:T(8,128)S(1)}, f32[8,128]{1,0:T(8,128)S(1)}, f32[8,128]{1,0:T(8,128)S(1)}) custom-call(f32[16,256]{1,0:T(8,128)S(1)} %get-tuple-element.50.refs_0_, f32[16,256]{1,0:T(8,128)S(1)} %collective-permute-done.refs_1_, f32[16,256]{1,0:T(8,128)S(1)} %collective-permute-done.1.refs_2_, f32[24,512]{1,0:T(8,128)S(1)} %get-tuple-element.63.refs_3_, ...), custom_call_target="tpu_custom_call" | custom-call | tf_op jit(solution)/shard_map/adjoint/pallas_call | solution.py:604
  26.5 0.9 %collective-permute-start.4 = (f32[8,128]{1,0:T(8,128)S(1)}, f32[8,128]{1,0:T(8,128)S(1)}, u32[]{:S(2)}, u32[]{:S(2)}) collective-permute-start(f32[8,128]{1,0:T(8,128)S(1)} %get-tuple-element.72), channel_id=1, source_target_pairs={{4,8},{12,16},{20,24},{8,4},{16,12},{24,20},{5,9},{13,17},{21,25},... | collective-permute-start | bytes 12296 | tf_op jit(solution)/shard_map/ppermute | solution.py:620
  27.4 4.4 %collective-permute-start.5 = (f32[8,128]{1,0:T(8,128)S(1)}, f32[8,128]{1,0:T(8,128)S(1)}, u32[]{:S(2)}, u32[]{:S(2)}) collective-permute-start(f32[8,128]{1,0:T(8,128)S(1)} %get-tuple-element.73), channel_id=1, source_target_pairs={{0,4},{8,12},{16,20},{24,28},{4,0},{12,8},{20,16},{28,24},{1,5},{9... | collective-permute-start | bytes 12296 | tf_op jit(solution)/shard_map/ppermute | solution.py:620
  31.7 2.6 %turn.1 = (bf16[64,192,192]{2,1,0:T(8,128)(2,1)S(1)}, bf16[4096,128]{1,0:T(8,128)(2,1)S(1)}, bf16[512,128]{1,0:T(8,128)(2,1)S(1)}, bf16[384,512]{1,0:T(8,128)(2,1)S(1)}) custom-call(bf16[64,192,192]{2,1,0:T(8,128)(2,1)S(1)} %get-tuple-element.74.refs_5_.refs_12_.blocks, s32[32,128]{1,0:T(8,128)S(1)} %get-tuple-element.52.refs_3_.refs_10_.cell_ref.refs_6_), custom_call_target="tpu_custom_call" | custom-call | tf_op jit(solution)/shard_map/turn/pallas_call | solution.py:604
  34.3 0.0 collective-permute-done.4.refs_4_
  34.3 0.0 collective-permute-done.5.refs_5_
  34.3 2.4 %forward.4 = (bf16[512,384]{1,0:T(8,128)(2,1)S(1)}, f32[24,512]{1,0:T(8,128)S(1)}, f32[24,512]{1,0:T(8,128)S(1)}, f32[8,128]{1,0:T(8,128)S(1)}, f32[8,256]{1,0:T(8,128)S(1)}) custom-call(f32[16,256]{1,0:T(8,128)S(1)} %get-tuple-element.50.refs_0_, f32[16,256]{1,0:T(8,128)S(1)} %collective-permute-done.refs_1_, f32[16,256]{1,0:T(8,128)S(1)} %collective-permute-done.1.refs_2_, ...), custom_call_target="tpu_custom_call" | custom-call | tf_op jit(solution)/shard_map/forward/pallas_call | solution.py:604
  36.7 0.7 collective-permute-start.6
  37.4 3.0 %collective-permute-start.7 = (f32[24,512]{1,0:T(8,128)S(1)}, f32[24,512]{1,0:T(8,128)S(1)}, u32[]{:S(2)}, u32[]{:S(2)}) collective-permute-start(f32[24,512]{1,0:T(8,128)S(1)} %get-tuple-element.78.refs_4_), channel_id=1, source_target_pairs={{0,4},{8,12},{16,20},{24,28},{4,0},{12,8},{20,16},{28,24},{1,5},{9... | collective-permute-start | bytes 147464 | tf_op jit(solution)/shard_map/ppermute | solution.py:620
  40.3 2.6 %inner.4.refs_7_ = f32[256,384]{1,0:T(8,128)S(1)} custom-call(bf16[512,384]{1,0:T(8,128)(2,1)S(1)} %get-tuple-element.79.ordered_ref, f32[3,4096]{1,0:T(4,128)S(1)} %bitcast.10, s32[32,128]{1,0:T(8,128)S(1)} %get-tuple-element.66.conn_ref.refs_9_, bf16[512,4096]{1,0:T(8,128)(2,1)S(1)} %get-tuple-element.55.refs_6_.node_hot, ...), custom_call_target="tpu_custom_call" | custom-call | tf_op jit(solution)/shard_map/inner/pallas_call | solution.py:604
  42.9 0.0 collective-permute-done.6.refs_5_
  42.9 0.0 collective-permute-done.7.refs_6_
  42.9 2.2 %adjoint.4 = (f32[8,384]{1,0:T(8,128)S(1)}, f32[8,128]{1,0:T(8,128)S(1)}, f32[8,128]{1,0:T(8,128)S(1)}) custom-call(f32[16,256]{1,0:T(8,128)S(1)} %get-tuple-element.50.refs_0_, f32[16,256]{1,0:T(8,128)S(1)} %collective-permute-done.refs_1_, f32[16,256]{1,0:T(8,128)S(1)} %collective-permute-done.1.refs_2_, f32[24,512]{1,0:T(8,128)S(1)} %get-tuple-element.77.refs_3_, ...), custom_call_target="tpu_custom_call" | custom-call | tf_op jit(solution)/shard_map/adjoint/pallas_call | solution.py:604
  45.2 0.7 collective-permute-start.8
  45.8 5.1 %collective-permute-start.9 = (f32[8,128]{1,0:T(8,128)S(1)}, f32[8,128]{1,0:T(8,128)S(1)}, u32[]{:S(2)}, u32[]{:S(2)}) collective-permute-start(f32[8,128]{1,0:T(8,128)S(1)} %get-tuple-element.85), channel_id=1, source_target_pairs={{0,4},{8,12},{16,20},{24,28},{4,0},{12,8},{20,16},{28,24},{1,5},{9... | collective-permute-start | bytes 12296 | tf_op jit(solution)/shard_map/ppermute | solution.py:620
  50.9 0.0 collective-permute-done.8.refs_4_
  50.9 1.6 %collective-permute-done.9.refs_5_ = f32[8,128]{1,0:T(8,128)S(1)} collective-permute-done((f32[8,128]{1,0:T(8,128)S(1)}, f32[8,128]{1,0:T(8,128)S(1)}, u32[]{:S(2)}, u32[]{:S(2)}) %collective-permute-start.9) | collective-permute-done | bytes 4128 | tf_op jit(solution)/shard_map/ppermute | solution.py:620
  52.5 2.4 %forward.5 = (bf16[512,384]{1,0:T(8,128)(2,1)S(1)}, f32[24,512]{1,0:T(8,128)S(1)}, f32[24,512]{1,0:T(8,128)S(1)}, f32[8,128]{1,0:T(8,128)S(1)}) custom-call(f32[16,256]{1,0:T(8,128)S(1)} %get-tuple-element.50.refs_0_, f32[16,256]{1,0:T(8,128)S(1)} %collective-permute-done.refs_1_, f32[16,256]{1,0:T(8,128)S(1)} %collective-permute-done.1.refs_2_, ...), custom_call_target="tpu_custom_call" | custom-call | tf_op jit(solution)/shard_map/forward/pallas_call | solution.py:604
  54.9 0.0 copy-start.1
  54.9 0.9 %collective-permute-start.10 = (f32[24,512]{1,0:T(8,128)S(1)}, f32[24,512]{1,0:T(8,128)S(1)}, u32[]{:S(2)}, u32[]{:S(2)}) collective-permute-start(f32[24,512]{1,0:T(8,128)S(1)} %get-tuple-element.86.refs_3_), channel_id=1, source_target_pairs={{4,8},{12,16},{20,24},{8,4},{16,12},{24,20},{5,9},{13,17},{21,25},... | collective-permute-start | bytes 147464 | tf_op jit(solution)/shard_map/ppermute | solution.py:620
  55.8 4.5 %collective-permute-start.11 = (f32[24,512]{1,0:T(8,128)S(1)}, f32[24,512]{1,0:T(8,128)S(1)}, u32[]{:S(2)}, u32[]{:S(2)}) collective-permute-start(f32[24,512]{1,0:T(8,128)S(1)} %get-tuple-element.87.refs_4_), channel_id=1, source_target_pairs={{0,4},{8,12},{16,20},{24,28},{4,0},{12,8},{20,16},{28,24},{1,5},{9... | collective-permute-start | bytes 147464 | tf_op jit(solution)/shard_map/ppermute | solution.py:620
  60.3 2.6 %inner.5.refs_7_ = f32[256,384]{1,0:T(8,128)S(1)} custom-call(bf16[512,384]{1,0:T(8,128)(2,1)S(1)} %get-tuple-element.88.ordered_ref, f32[3,4096]{1,0:T(4,128)S(1)} %bitcast.12, s32[32,128]{1,0:T(8,128)S(1)} %get-tuple-element.66.conn_ref.refs_9_, bf16[512,4096]{1,0:T(8,128)(2,1)S(1)} %get-tuple-element.55.refs_6_.node_hot, ...), custom_call_target="tpu_custom_call" | custom-call | tf_op jit(solution)/shard_map/inner/pallas_call | solution.py:604
  62.9 0.0 collective-permute-done.10.refs_5_
  62.9 0.0 collective-permute-done.11.refs_6_
  62.9 0.0 copy-done.1
  62.9 2.2 %adjoint.5 = (f32[8,384]{1,0:T(8,128)S(1)}, bf16[32,8,256]{2,1,0:T(8,128)(2,1)S(1)}) custom-call(f32[16,256]{1,0:T(8,128)S(1)} %get-tuple-element.50.refs_0_, f32[16,256]{1,0:T(8,128)S(1)} %collective-permute-done.refs_1_, f32[16,256]{1,0:T(8,128)S(1)} %collective-permute-done.1.refs_2_, f32[24,512]{1,0:T(8,128)S(1)} %get-tuple-element.86.refs_3_, ...), custom_call_target="tpu_custom_call" | custom-call | tf_op jit(solution)/shard_map/adjoint/pallas_call | solution.py:604
  65.1 11.7 %all_to_all.5 = bf16[32,8,256]{2,1,0:T(8,128)(2,1)S(1)} all-to-all(bf16[32,8,256]{2,1,0:T(8,128)(2,1)S(1)} %get-tuple-element.91), channel_id=1, replica_groups=mesh['tiles'=8,'probes'=4] {'tiles','probes'}, dimensions={0} | all-to-all | bytes 262144 | tf_op jit(solution)/shard_map/all_to_all | solution.py:741
  76.8 1.5 %gram.1 = (f32[8,256]{1,0:T(8,128)}, f32[8,256]{1,0:T(8,128)}, f32[8,8,32]{2,1,0:T(8,128)}) custom-call(bf16[8,4,8,256]{3,2,1,0:T(8,128)(2,1)S(1)} %bitcast.14, f32[8,384]{1,0:T(8,128)S(1)} %get-tuple-element.92.own_ref, f32[8,256]{1,0:T(8,128)S(1)} %get-tuple-element.93.samples_in), custom_call_target="tpu_custom_call" | custom-call | tf_op jit(solution)/shard_map/gram/pallas_call | solution.py:604
Async XLA Ops:
  1.4 10.4 %collective-permute-start = (f32[16,256]{1,0:T(8,128)S(1)}, f32[16,256]{1,0:T(8,128)S(1)}, u32[]{:S(2)}, u32[]{:S(2)}) collective-permute-start(f32[16,256]{1,0:T(8,128)S(1)} %get-tuple-element.51), channel_id=1, source_target_pairs={{4,8},{12,16},{20,24},{8,4},{16,12},{24,20},{5,9},{13,17},{21,25},... | collective-permute-start | bytes 49160 | tf_op jit(solution)/shard_map/ppermute | solution.py:620
  2.1 9.8 %collective-permute-start.1 = (f32[16,256]{1,0:T(8,128)S(1)}, f32[16,256]{1,0:T(8,128)S(1)}, u32[]{:S(2)}, u32[]{:S(2)}) collective-permute-start(f32[16,256]{1,0:T(8,128)S(1)} %get-tuple-element.50.refs_0_), channel_id=1, source_target_pairs={{0,4},{8,12},{16,20},{24,28},{4,0},{12,8},{20,16},{28,24},{1,5},{9... | collective-permute-start | bytes 49160 | tf_op jit(solution)/shard_map/ppermute | solution.py:620
  11.8 8.8 %copy-start = (f32[4096,3]{0,1:T(4,128)S(1)}, f32[4096,3]{0,1:T(4,128)}, u32[]{:S(2)}) copy-start(f32[4096,3]{0,1:T(4,128)} %param.13) | copy-start | bytes 147460
  15.6 8.4 %collective-permute-start.2 = (f32[24,512]{1,0:T(8,128)S(1)}, f32[24,512]{1,0:T(8,128)S(1)}, u32[]{:S(2)}, u32[]{:S(2)}) collective-permute-start(f32[24,512]{1,0:T(8,128)S(1)} %get-tuple-element.63.refs_3_), channel_id=1, source_target_pairs={{4,8},{12,16},{20,24},{8,4},{16,12},{24,20},{5,9},{13,17},{21,25},... | collective-permute-start | bytes 147464 | tf_op jit(solution)/shard_map/ppermute | solution.py:620
  16.3 7.7 %collective-permute-start.3 = (f32[24,512]{1,0:T(8,128)S(1)}, f32[24,512]{1,0:T(8,128)S(1)}, u32[]{:S(2)}, u32[]{:S(2)}) collective-permute-start(f32[24,512]{1,0:T(8,128)S(1)} %get-tuple-element.64.refs_4_), channel_id=1, source_target_pairs={{0,4},{8,12},{16,20},{24,28},{4,0},{12,8},{20,16},{28,24},{1,5},{9... | collective-permute-start | bytes 147464 | tf_op jit(solution)/shard_map/ppermute | solution.py:620
  26.5 7.8 %collective-permute-start.4 = (f32[8,128]{1,0:T(8,128)S(1)}, f32[8,128]{1,0:T(8,128)S(1)}, u32[]{:S(2)}, u32[]{:S(2)}) collective-permute-start(f32[8,128]{1,0:T(8,128)S(1)} %get-tuple-element.72), channel_id=1, source_target_pairs={{4,8},{12,16},{20,24},{8,4},{16,12},{24,20},{5,9},{13,17},{21,25},... | collective-permute-start | bytes 12296 | tf_op jit(solution)/shard_map/ppermute | solution.py:620
  27.4 6.9 %collective-permute-start.5 = (f32[8,128]{1,0:T(8,128)S(1)}, f32[8,128]{1,0:T(8,128)S(1)}, u32[]{:S(2)}, u32[]{:S(2)}) collective-permute-start(f32[8,128]{1,0:T(8,128)S(1)} %get-tuple-element.73), channel_id=1, source_target_pairs={{0,4},{8,12},{16,20},{24,28},{4,0},{12,8},{20,16},{28,24},{1,5},{9... | collective-permute-start | bytes 12296 | tf_op jit(solution)/shard_map/ppermute | solution.py:620
  36.7 6.2 %collective-permute-start.6 = (f32[24,512]{1,0:T(8,128)S(1)}, f32[24,512]{1,0:T(8,128)S(1)}, u32[]{:S(2)}, u32[]{:S(2)}) collective-permute-start(f32[24,512]{1,0:T(8,128)S(1)} %get-tuple-element.77.refs_3_), channel_id=1, source_target_pairs={{4,8},{12,16},{20,24},{8,4},{16,12},{24,20},{5,9},{13,17},{21,25},... | collective-permute-start | bytes 147464 | tf_op jit(solution)/shard_map/ppermute | solution.py:620
  37.4 5.5 %collective-permute-start.7 = (f32[24,512]{1,0:T(8,128)S(1)}, f32[24,512]{1,0:T(8,128)S(1)}, u32[]{:S(2)}, u32[]{:S(2)}) collective-permute-start(f32[24,512]{1,0:T(8,128)S(1)} %get-tuple-element.78.refs_4_), channel_id=1, source_target_pairs={{0,4},{8,12},{16,20},{24,28},{4,0},{12,8},{20,16},{28,24},{1,5},{9... | collective-permute-start | bytes 147464 | tf_op jit(solution)/shard_map/ppermute | solution.py:620
  45.2 5.8 %collective-permute-start.8 = (f32[8,128]{1,0:T(8,128)S(1)}, f32[8,128]{1,0:T(8,128)S(1)}, u32[]{:S(2)}, u32[]{:S(2)}) collective-permute-start(f32[8,128]{1,0:T(8,128)S(1)} %get-tuple-element.84), channel_id=1, source_target_pairs={{4,8},{12,16},{20,24},{8,4},{16,12},{24,20},{5,9},{13,17},{21,25},... | collective-permute-start | bytes 12296 | tf_op jit(solution)/shard_map/ppermute | solution.py:620
  45.8 6.7 %collective-permute-start.9 = (f32[8,128]{1,0:T(8,128)S(1)}, f32[8,128]{1,0:T(8,128)S(1)}, u32[]{:S(2)}, u32[]{:S(2)}) collective-permute-start(f32[8,128]{1,0:T(8,128)S(1)} %get-tuple-element.85), channel_id=1, source_target_pairs={{0,4},{8,12},{16,20},{24,28},{4,0},{12,8},{20,16},{28,24},{1,5},{9... | collective-permute-start | bytes 12296 | tf_op jit(solution)/shard_map/ppermute | solution.py:620
  54.9 8.0 %copy-start.1 = (s32[256]{0:T(256)S(1)}, s32[256]{0:T(256)}, u32[]{:S(2)}) copy-start(s32[256]{0:T(256)} %param.15) | copy-start | bytes 3076
  54.9 8.0 %collective-permute-start.10 = (f32[24,512]{1,0:T(8,128)S(1)}, f32[24,512]{1,0:T(8,128)S(1)}, u32[]{:S(2)}, u32[]{:S(2)}) collective-permute-start(f32[24,512]{1,0:T(8,128)S(1)} %get-tuple-element.86.refs_3_), channel_id=1, source_target_pairs={{4,8},{12,16},{20,24},{8,4},{16,12},{24,20},{5,9},{13,17},{21,25},... | collective-permute-start | bytes 147464 | tf_op jit(solution)/shard_map/ppermute | solution.py:620
  55.8 7.1 %collective-permute-start.11 = (f32[24,512]{1,0:T(8,128)S(1)}, f32[24,512]{1,0:T(8,128)S(1)}, u32[]{:S(2)}, u32[]{:S(2)}) collective-permute-start(f32[24,512]{1,0:T(8,128)S(1)} %get-tuple-element.87.refs_4_), channel_id=1, source_target_pairs={{0,4},{8,12},{16,20},{24,28},{4,0},{12,8},{20,16},{28,24},{1,5},{9... | collective-permute-start | bytes 147464 | tf_op jit(solution)/shard_map/ppermute | solution.py:620

commit v13 on v12

--- a/solution.py
+++ b/solution.py
@@ -231,18 +231,18 @@
             node_turn_ref[m * LANES : (m + 1) * LANES, at] = hot16(lanes, row)
 
 
-def turn_kernel(blocks, cell_ref, turned_ref, cell_turn_ref, spread_turn_ref, order_turn_ref):
-    node_slots = blocks.shape[1] // 3
+def turn_blocks_kernel(blocks, turned_ref):
+    for slot in range(blocks.shape[0]):
+        turned_ref[slot] = blocks[slot].T
+
+
+def turn_cells_kernel(node_slots, cell_ref, cell_turn_ref, spread_turn_ref, order_turn_ref):
     padded_order = order_turn_ref.shape[1] // 2
     spread_turn_ref[...] = spread_matrix(node_slots, padded_order, True)
     order_turn_ref[...] = order_matrix(node_slots, padded_order, True)
     cells = (cell_ref[...] % LANES).astype(F32).T
     lanes = lanes_iota((LANES, LANES)).astype(F32).astype(BF16)
-    for slot in range(blocks.shape[0]):
-        turned_ref[slot] = blocks[slot].T
-        if slot % 2:
-            continue
-        m = slot // 2
+    for m in range(cell_ref.shape[0]):
         row = jnp.broadcast_to(cells[:, m : m + 1], (LANES, LANES)).astype(BF16)
         cell_turn_ref[m * LANES : (m + 1) * LANES, :] = hot16(lanes, row)
 
@@ -264,7 +264,7 @@
     if not first:
         basal_ref, rim_a, rim_b, *refs = refs
     cell_ref, fr_ref, factors, node_map, level_hot, cell_hot, spread_ref, order_ref, *refs = refs
-    ordered_ref, a_ref, b_ref, *refs = refs
+    ordered_ref, a_ref, b_ref, far_ref, near_ref, *refs = refs
     if not first:
         squares_ref, *refs = refs
     if step == 1:
@@ -345,10 +345,11 @@
     spread_levels(v_ref, ordered, level_hot, (0, levels - 1), pairs)
     rim = product(step > 0)(v_ref[...], node_map[...])
     sums = [rim[16 * i : 16 * i + 8] + rim[16 * i + 8 : 16 * i + 16] for i in range(6)]
-    half = len(sums) // 2
-    for i in range(half):
-        lead, spill = sums[i], sums[half + i]
-        a_ref[8 * i : 8 * i + 8, :], b_ref[8 * i : 8 * i + 8, :] = to_swaps(tile, spill, lead)
+    lead, spill = (jnp.concatenate(part, axis=0) for part in (sums[:3], sums[3:]))
+    for ref, message, value in zip((a_ref, b_ref), (far_ref, near_ref), to_swaps(tile, spill, lead)):
+        ref[...] = value
+        pieces = [value[:, i * EDGE_RADIX : (i + 1) * EDGE_RADIX] for i in range(EDGE)]
+        message[...] = jnp.concatenate(pieces, axis=0).astype(BF16)
 
 
 def inner_kernel(levels, ordered_ref, weight_ref, conn_ref, node_hot, level_hot, picked_ref, v_ref):
@@ -391,16 +392,17 @@
     pairs = blocks.shape[0] // 2
     tile = lax.axis_index("tiles")
 
-    spill, lead = by_side(tile, own_a[...] + new_a[...], own_b[...] + new_b[...])
+    spill, lead = by_side(tile, own_a[...], own_b[...])
+    new_spill, new_lead = by_side(tile, new_a[...].astype(F32), new_b[...].astype(F32))
     after, before = by_side(tile, block_a[...], block_b[...])
     rows = []
     for i in range(3 * EDGE):
         c, at = i % 3, (i // 3) * EDGE_RADIX
-        value = lead[8 * c : 8 * c + 8, at : at + EDGE_RADIX]
+        value = lead[8 * c : 8 * c + 8, at : at + EDGE_RADIX] + new_lead[8 * i : 8 * i + 8]
         rows.append(value * weight_ref[c : c + 1, at : at + EDGE_RADIX])
     for i in range(3 * EDGE):
         c, at = i % 3, (i // 3) * EDGE_RADIX
-        value = spill[8 * c : 8 * c + 8, at : at + EDGE_RADIX]
+        value = spill[8 * c : 8 * c + 8, at : at + EDGE_RADIX] + new_spill[8 * i : 8 * i + 8]
         rows.append(value * after[8 + i : 9 + i, :])
     weighted = jnp.concatenate(rows, axis=0).astype(BF16)
 
@@ -662,6 +664,7 @@
     factors, node_map, cell_map, spread_map, order_map = loaded, node_hot, cell_hot, spread, order
 
     edge = shaped((24, HALO), F32)
+    message = shaped((24 * EDGE, EDGE_RADIX), BF16)
     rim = shaped((group_size, LANES), F32)
     whole = shaped((group_size, window), F32)
     field = shaped((group_size, cell_count), F32)
@@ -673,9 +676,9 @@
     samples = None
     for step in range(POWER + 1):
         last = step == POWER
-        out_shape = [shaped((16 * pairs, 3 * LANES), BF16), edge, edge]
+        out_shape = [shaped((16 * pairs, 3 * LANES), BF16), edge, edge, message, message]
         out_shape += [rim] * (step > 0) + [field] * (step == 1)
-        ordered, own_a, own_b, *extra = call(
+        ordered, own_a, own_b, far, near, *extra = call(
             functools.partial(forward_kernel, step, tiles, levels),
             "forward",
             out_shape,
@@ -690,10 +693,22 @@
         if step == 1:
             samples = extra[1]
         if step == 0:
-            own_a, own_b, settled = lax.optimization_barrier((own_a, own_b, conn))
+            far, near, settled = lax.optimization_barrier((far, near, conn))
             shape = shaped((refs, RADIX), BF16)
             node_map = call(turn_nodes_kernel, "turn_nodes", shape, [settled])
-        new_a, new_b = swapped(own_a, own_b)
+        if step == 1:
+            far, near, settled = lax.optimization_barrier((far, near, cells))
+            cell_map, spread_map, order_map = call(
+                functools.partial(turn_cells_kernel, node_slots),
+                "turn_cells",
+                [
+                    shaped((refs, LANES), BF16),
+                    shaped((2 * padded_order, LANES), BF16),
+                    shaped((3 * LANES, 2 * padded_order), BF16),
+                ],
+                [settled],
+            )
+        new_a, new_b = swapped(far, near)
         inner = call(
             functools.partial(inner_kernel, levels),
             "inner",
@@ -707,8 +722,8 @@
         operands += [conn, cells, fr, loaded, edge_hot, cell_map, spread_map, order_map]
         if last:
             operands += squares + [cluster_ids.reshape(1, cell_count)]
-            message = shaped((lax.axis_size(everyone), group_size, 2 * LANES), BF16)
-            out_shape = [whole, message]
+            packed = shaped((lax.axis_size(everyone), group_size, 2 * LANES), BF16)
+            out_shape = [whole, packed]
         else:
             out_shape = [whole, rim, rim]
         basal, *messages = call(
@@ -725,17 +740,8 @@
         if not last:
             if step == 0:
                 *messages, settled = lax.optimization_barrier((*messages, loaded))
-                factors, cell_map, spread_map, order_map = call(
-                    turn_kernel,
-                    "turn",
-                    [
-                        shaped(blocks.shape, BF16),
-                        shaped((refs, LANES), BF16),
-                        shaped((2 * padded_order, LANES), BF16),
-                        shaped((3 * LANES, 2 * padded_order), BF16),
-                    ],
-                    [settled, cells],
-                )
+                shape = shaped(blocks.shape, BF16)
+                factors = call(turn_blocks_kernel, "turn_blocks", shape, [settled])
             carried = [basal, *swapped(*messages)]
 
     gathered = lax.all_to_all(messages[0], everyone, 0, 0)

time: 78.7 us -> 78.5 us (level)
  starting transfers between devices: 31.5 us -> 30.7 us
    pallas_call x14 -> x15, Pallas kernels: 32 us -> 32.2 us  [call(): pl.pallas_call(kernel, out_shape=out_shape, in_specs=in_specs, out_specs=...]
where the time goes in v13:
time: 78.5 us; the launch traced here: 78.2 us
  Pallas kernels  32.2 us (41%)
  starting transfers between devices  30.7 us (39%)
  blocking collectives  12.1 us (15%)
  waiting for transfers between devices  1.61 us (2%)
  between operations  1.51 us (2%)
    pallas_call x15, Pallas kernels, call(): pl.pallas_call(kernel, out_shape=out_shape, in_specs=in_specs, out_specs=...  32.2 us
    ppermute x6, starting transfers between devices, swapped(): lax.ppermute(b, 'tiles', pairs_b)  26.3 us
    all_to_all x1, blocking collectives, shards(): gathered = lax.all_to_all(messages[0], everyone, 0, 0)  12.1 us
    ppermute x6, starting transfers between devices, swapped(): lax.ppermute(a, 'tiles', pairs_a)  4.4 us
    ppermute x6, waiting for transfers between devices, swapped(): lax.ppermute(b, 'tiles', pairs_b)  1.6 us
  transfers between devices with their start and end apart: 12, of which 1 were waited for; matrix products, arithmetic and copies ran while one was open for 0% of the time, Pallas kernels for 18%

profile of v13, /device:TPU:0, one launch (start us, length us, event | category | flops | bytes accessed | tf_op | source)
XLA Modules:
  0.0 78.2 jit_solution(17206760977580804718)
XLA Ops:
  0.6 0.8 announce.1
  1.4 0.7 collective-permute-start
  2.1 5.8 %collective-permute-start.1 = (f32[16,256]{1,0:T(8,128)S(1)}, f32[16,256]{1,0:T(8,128)S(1)}, u32[]{:S(2)}, u32[]{:S(2)}) collective-permute-start(f32[16,256]{1,0:T(8,128)S(1)} %get-tuple-element.58.refs_0_), channel_id=1, source_target_pairs={{0,4},{8,12},{16,20},{24,28},{4,0},{12,8},{20,16},{28,24},{1,5},{9... | collective-permute-start | bytes 49160 | tf_op jit(solution)/shard_map/ppermute | solution.py:622
  8.5 3.2 %setup.1 = (s32[32,128]{1,0:T(8,128)S(1)}, s32[32,128]{1,0:T(8,128)S(1)}, f32[64,256]{1,0:T(8,128)S(1)}, bf16[64,192,192]{2,1,0:T(8,128)(2,1)S(1)}, bf16[512,409...) custom-call(s32[1]{0:T(128)S(6)} %copy.11.counts, ...), custom_call_target="tpu_custom_call" | custom-call | tf_op jit(solution)/shard_map/setup/pallas_call | solution.py:606
  11.7 0.0 collective-permute-done.refs_1_
  11.8 0.0 collective-permute-done.1.refs_2_
  11.8 0.0 copy-start
  11.8 3.8 %forward.3 = (bf16[512,384]{1,0:T(8,128)(2,1)S(1)}, f32[24,512]{1,0:T(8,128)S(1)}, f32[24,512]{1,0:T(8,128)S(1)}, bf16[48,256]{1,0:T(8,128)(2,1)S(1)}, bf16[48,256]{1,0:T(8,128)(2,1)S(1)}) custom-call(f32[16,256]{1,0:T(8,128)S(1)} %get-tuple-element.58.refs_0_, f32[16,256]{1,0:T(8,128)S(1)} %collective-permute-done.refs_1_, ...), custom_call_target="tpu_custom_call" | custom-call | tf_op jit(solution)/shard_map/forward/pallas_call | solution.py:606
  15.5 0.7 collective-permute-start.2
  16.2 4.4 %collective-permute-start.3 = (bf16[48,256]{1,0:T(8,128)(2,1)S(1)}, bf16[48,256]{1,0:T(8,128)(2,1)S(1)}, u32[]{:S(2)}, u32[]{:S(2)}) collective-permute-start(bf16[48,256]{1,0:T(8,128)(2,1)S(1)} %get-tuple-element.74), channel_id=1, source_target_pairs={{0,4},{8,12},{16,20},{24,28},{4,0},{12,8},{20,16},{28,24},{1,5},{9... | collective-permute-start | bytes 73736 | tf_op jit(solution)/shard_map/ppermute | solution.py:622
  20.6 0.0 copy-done
  20.6 2.5 %inner.3.refs_7_ = f32[256,384]{1,0:T(8,128)S(1)} custom-call(bf16[512,384]{1,0:T(8,128)(2,1)S(1)} %get-tuple-element.75.ordered_ref, f32[3,4096]{1,0:T(4,128)S(1)} %bitcast.8, s32[32,128]{1,0:T(8,128)S(1)} %get-tuple-element.76.conn_ref.refs_9_, bf16[512,4096]{1,0:T(8,128)(2,1)S(1)} %get-tuple-element.63.refs_6_.node_hot, ...), custom_call_target="tpu_custom_call" | custom-call | tf_op jit(solution)/shard_map/inner/pallas_call | solution.py:606
  23.1 0.8 %turn_nodes.1.refs_9_ = bf16[4096,512]{1,0:T(8,128)(2,1)S(1)} custom-call(s32[32,128]{1,0:T(8,128)S(1)} %get-tuple-element.76.conn_ref.refs_9_), custom_call_target="tpu_custom_call" | custom-call | tf_op jit(solution)/shard_map/turn_nodes/pallas_call | solution.py:606
  23.9 0.0 collective-permute-done.2.refs_5_
  23.9 0.0 collective-permute-done.3.refs_6_
  23.9 2.5 %adjoint.3 = (f32[8,384]{1,0:T(8,128)S(1)}, f32[8,128]{1,0:T(8,128)S(1)}, f32[8,128]{1,0:T(8,128)S(1)}) custom-call(f32[16,256]{1,0:T(8,128)S(1)} %get-tuple-element.58.refs_0_, f32[16,256]{1,0:T(8,128)S(1)} %collective-permute-done.refs_1_, f32[16,256]{1,0:T(8,128)S(1)} %collective-permute-done.1.refs_2_, f32[24,512]{1,0:T(8,128)S(1)} %get-tuple-element.68.refs_3_, ...), custom_call_target="tpu_custom_call" | custom-call | tf_op jit(solution)/shard_map/adjoint/pallas_call | solution.py:606
  26.4 0.9 %collective-permute-start.4 = (f32[8,128]{1,0:T(8,128)S(1)}, f32[8,128]{1,0:T(8,128)S(1)}, u32[]{:S(2)}, u32[]{:S(2)}) collective-permute-start(f32[8,128]{1,0:T(8,128)S(1)} %get-tuple-element.82), channel_id=1, source_target_pairs={{4,8},{12,16},{20,24},{8,4},{16,12},{24,20},{5,9},{13,17},{21,25},... | collective-permute-start | bytes 12296 | tf_op jit(solution)/shard_map/ppermute | solution.py:622
  27.3 4.4 %collective-permute-start.5 = (f32[8,128]{1,0:T(8,128)S(1)}, f32[8,128]{1,0:T(8,128)S(1)}, u32[]{:S(2)}, u32[]{:S(2)}) collective-permute-start(f32[8,128]{1,0:T(8,128)S(1)} %get-tuple-element.83), channel_id=1, source_target_pairs={{0,4},{8,12},{16,20},{24,28},{4,0},{12,8},{20,16},{28,24},{1,5},{9... | collective-permute-start | bytes 12296 | tf_op jit(solution)/shard_map/ppermute | solution.py:622
  31.7 2.0 %turn_blocks.1.refs_8_ = bf16[64,192,192]{2,1,0:T(8,128)(2,1)S(1)} custom-call(bf16[64,192,192]{2,1,0:T(8,128)(2,1)S(1)} %get-tuple-element.84.refs_5_.refs_12_.blocks), custom_call_target="tpu_custom_call" | custom-call | tf_op jit(solution)/shard_map/turn_blocks/pallas_call | solution.py:606
  33.6 0.0 collective-permute-done.4.refs_4_
  33.7 0.0 collective-permute-done.5.refs_5_
  33.7 2.4 %forward.4 = (bf16[512,384]{1,0:T(8,128)(2,1)S(1)}, f32[24,512]{1,0:T(8,128)S(1)}, f32[24,512]{1,0:T(8,128)S(1)}, bf16[48,256]{1,0:T(8,128)(2,1)S(1)}, bf16[48,2...) custom-call(f32[16,256]{1,0:T(8,128)S(1)} %get-tuple-element.58.refs_0_, ...), custom_call_target="tpu_custom_call" | custom-call | tf_op jit(solution)/shard_map/forward/pallas_call | solution.py:606
  36.1 0.7 collective-permute-start.6
  36.7 3.5 %collective-permute-start.7 = (bf16[48,256]{1,0:T(8,128)(2,1)S(1)}, bf16[48,256]{1,0:T(8,128)(2,1)S(1)}, u32[]{:S(2)}, u32[]{:S(2)}) collective-permute-start(bf16[48,256]{1,0:T(8,128)(2,1)S(1)} %get-tuple-element.91), channel_id=1, source_target_pairs={{0,4},{8,12},{16,20},{24,28},{4,0},{12,8},{20,16},{28,24},{1,5},{9... | collective-permute-start | bytes 73736 | tf_op jit(solution)/shard_map/ppermute | solution.py:622
  40.3 2.5 %inner.4.refs_7_ = f32[256,384]{1,0:T(8,128)S(1)} custom-call(bf16[512,384]{1,0:T(8,128)(2,1)S(1)} %get-tuple-element.92.ordered_ref, f32[3,4096]{1,0:T(4,128)S(1)} %bitcast.10, s32[32,128]{1,0:T(8,128)S(1)} %get-tuple-element.76.conn_ref.refs_9_, bf16[512,4096]{1,0:T(8,128)(2,1)S(1)} %get-tuple-element.63.refs_6_.node_hot, ...), custom_call_target="tpu_custom_call" | custom-call | tf_op jit(solution)/shard_map/inner/pallas_call | solution.py:606
  42.8 0.8 %turn_cells.1 = (bf16[4096,128]{1,0:T(8,128)(2,1)S(1)}, bf16[512,128]{1,0:T(8,128)(2,1)S(1)}, bf16[384,512]{1,0:T(8,128)(2,1)S(1)}) custom-call(s32[32,128]{1,0:T(8,128)S(1)} %get-tuple-element.93.refs_3_.refs_10_.refs_6_.cell_ref), custom_call_target="tpu_custom_call" | custom-call | tf_op jit(solution)/shard_map/turn_cells/pallas_call | solution.py:606
  43.6 0.0 collective-permute-done.6.refs_5_
  43.6 0.0 collective-permute-done.7.refs_6_
  43.6 2.2 %adjoint.4 = (f32[8,384]{1,0:T(8,128)S(1)}, f32[8,128]{1,0:T(8,128)S(1)}, f32[8,128]{1,0:T(8,128)S(1)}) custom-call(f32[16,256]{1,0:T(8,128)S(1)} %get-tuple-element.58.refs_0_, f32[16,256]{1,0:T(8,128)S(1)} %collective-permute-done.refs_1_, f32[16,256]{1,0:T(8,128)S(1)} %collective-permute-done.1.refs_2_, f32[24,512]{1,0:T(8,128)S(1)} %get-tuple-element.86.refs_3_, ...), custom_call_target="tpu_custom_call" | custom-call | tf_op jit(solution)/shard_map/adjoint/pallas_call | solution.py:606
  45.9 0.7 collective-permute-start.8
  46.5 4.0 %collective-permute-start.9 = (f32[8,128]{1,0:T(8,128)S(1)}, f32[8,128]{1,0:T(8,128)S(1)}, u32[]{:S(2)}, u32[]{:S(2)}) collective-permute-start(f32[8,128]{1,0:T(8,128)S(1)} %get-tuple-element.99), channel_id=1, source_target_pairs={{0,4},{8,12},{16,20},{24,28},{4,0},{12,8},{20,16},{28,24},{1,5},{9... | collective-permute-start | bytes 12296 | tf_op jit(solution)/shard_map/ppermute | solution.py:622
  50.6 0.0 collective-permute-done.8.refs_4_
  50.6 1.6 %collective-permute-done.9.refs_5_ = f32[8,128]{1,0:T(8,128)S(1)} collective-permute-done((f32[8,128]{1,0:T(8,128)S(1)}, f32[8,128]{1,0:T(8,128)S(1)}, u32[]{:S(2)}, u32[]{:S(2)}) %collective-permute-start.9) | collective-permute-done | bytes 4128 | tf_op jit(solution)/shard_map/ppermute | solution.py:622
  52.2 2.4 %forward.5 = (bf16[512,384]{1,0:T(8,128)(2,1)S(1)}, f32[24,512]{1,0:T(8,128)S(1)}, f32[24,512]{1,0:T(8,128)S(1)}, bf16[48,256]{1,0:T(8,128)(2,1)S(1)}, bf16[48,2...) custom-call(f32[16,256]{1,0:T(8,128)S(1)} %get-tuple-element.58.refs_0_, f32[16,256]{1,0:T(8,128)S(1)} %collective-permute-done.refs_1_, ...), custom_call_target="tpu_custom_call" | custom-call | tf_op jit(solution)/shard_map/forward/pallas_call | solution.py:606
  54.6 0.0 copy-start.1
  54.6 0.9 %collective-permute-start.10 = (bf16[48,256]{1,0:T(8,128)(2,1)S(1)}, bf16[48,256]{1,0:T(8,128)(2,1)S(1)}, u32[]{:S(2)}, u32[]{:S(2)}) collective-permute-start(bf16[48,256]{1,0:T(8,128)(2,1)S(1)} %get-tuple-element.102), channel_id=1, source_target_pairs={{4,8},{12,16},{20,24},{8,4},{16,12},{24,20},{5,9},{13,17},{21,25},... | collective-permute-start | bytes 73736 | tf_op jit(solution)/shard_map/ppermute | solution.py:622
  55.5 4.2 %collective-permute-start.11 = (bf16[48,256]{1,0:T(8,128)(2,1)S(1)}, bf16[48,256]{1,0:T(8,128)(2,1)S(1)}, u32[]{:S(2)}, u32[]{:S(2)}) collective-permute-start(bf16[48,256]{1,0:T(8,128)(2,1)S(1)} %get-tuple-element.103), channel_id=1, source_target_pairs={{0,4},{8,12},{16,20},{24,28},{4,0},{12,8},{20,16},{28,24},{1,5},{9... | collective-permute-start | bytes 73736 | tf_op jit(solution)/shard_map/ppermute | solution.py:622
  59.7 2.6 %inner.5.refs_7_ = f32[256,384]{1,0:T(8,128)S(1)} custom-call(bf16[512,384]{1,0:T(8,128)(2,1)S(1)} %get-tuple-element.104.ordered_ref, f32[3,4096]{1,0:T(4,128)S(1)} %bitcast.12, s32[32,128]{1,0:T(8,128)S(1)} %get-tuple-element.76.conn_ref.refs_9_, bf16[512,4096]{1,0:T(8,128)(2,1)S(1)} %get-tuple-element.63.refs_6_.node_hot, ...), custom_call_target="tpu_custom_call" | custom-call | tf_op jit(solution)/shard_map/inner/pallas_call | solution.py:606
  62.3 0.0 collective-permute-done.10.refs_5_
  62.3 0.0 collective-permute-done.11.refs_6_
  62.3 0.0 copy-done.1
  62.3 2.2 %adjoint.5 = (f32[8,384]{1,0:T(8,128)S(1)}, bf16[32,8,256]{2,1,0:T(8,128)(2,1)S(1)}) custom-call(f32[16,256]{1,0:T(8,128)S(1)} %get-tuple-element.58.refs_0_, f32[16,256]{1,0:T(8,128)S(1)} %collective-permute-done.refs_1_, f32[16,256]{1,0:T(8,128)S(1)} %collective-permute-done.1.refs_2_, f32[24,512]{1,0:T(8,128)S(1)} %get-tuple-element.100.refs_3_, ...), custom_call_target="tpu_custom_call" | custom-call | tf_op jit(solution)/shard_map/adjoint/pallas_call | solution.py:606
  64.6 12.1 %all_to_all.5 = bf16[32,8,256]{2,1,0:T(8,128)(2,1)S(1)} all-to-all(bf16[32,8,256]{2,1,0:T(8,128)(2,1)S(1)} %get-tuple-element.107), channel_id=1, replica_groups=mesh['tiles'=8,'probes'=4] {'tiles','probes'}, dimensions={0} | all-to-all | bytes 262144 | tf_op jit(solution)/shard_map/all_to_all | solution.py:747
  76.7 1.5 %gram.1 = (f32[8,256]{1,0:T(8,128)}, f32[8,256]{1,0:T(8,128)}, f32[8,8,32]{2,1,0:T(8,128)}) custom-call(bf16[8,4,8,256]{3,2,1,0:T(8,128)(2,1)S(1)} %bitcast.14, f32[8,384]{1,0:T(8,128)S(1)} %get-tuple-element.108.own_ref, f32[8,256]{1,0:T(8,128)S(1)} %get-tuple-element.109.samples_in), custom_call_target="tpu_custom_call" | custom-call | tf_op jit(solution)/shard_map/gram/pallas_call | solution.py:606
Async XLA Ops:
  1.4 10.3 %collective-permute-start = (f32[16,256]{1,0:T(8,128)S(1)}, f32[16,256]{1,0:T(8,128)S(1)}, u32[]{:S(2)}, u32[]{:S(2)}) collective-permute-start(f32[16,256]{1,0:T(8,128)S(1)} %get-tuple-element.59), channel_id=1, source_target_pairs={{4,8},{12,16},{20,24},{8,4},{16,12},{24,20},{5,9},{13,17},{21,25},... | collective-permute-start | bytes 49160 | tf_op jit(solution)/shard_map/ppermute | solution.py:622
  2.1 9.7 %collective-permute-start.1 = (f32[16,256]{1,0:T(8,128)S(1)}, f32[16,256]{1,0:T(8,128)S(1)}, u32[]{:S(2)}, u32[]{:S(2)}) collective-permute-start(f32[16,256]{1,0:T(8,128)S(1)} %get-tuple-element.58.refs_0_), channel_id=1, source_target_pairs={{0,4},{8,12},{16,20},{24,28},{4,0},{12,8},{20,16},{28,24},{1,5},{9... | collective-permute-start | bytes 49160 | tf_op jit(solution)/shard_map/ppermute | solution.py:622
  11.8 8.8 %copy-start = (f32[4096,3]{0,1:T(4,128)S(1)}, f32[4096,3]{0,1:T(4,128)}, u32[]{:S(2)}) copy-start(f32[4096,3]{0,1:T(4,128)} %param.13) | copy-start | bytes 147460
  15.5 8.4 %collective-permute-start.2 = (bf16[48,256]{1,0:T(8,128)(2,1)S(1)}, bf16[48,256]{1,0:T(8,128)(2,1)S(1)}, u32[]{:S(2)}, u32[]{:S(2)}) collective-permute-start(bf16[48,256]{1,0:T(8,128)(2,1)S(1)} %get-tuple-element.73), channel_id=1, source_target_pairs={{4,8},{12,16},{20,24},{8,4},{16,12},{24,20},{5,9},{13,17},{21,25},... | collective-permute-start | bytes 73736 | tf_op jit(solution)/shard_map/ppermute | solution.py:622
  16.2 7.7 %collective-permute-start.3 = (bf16[48,256]{1,0:T(8,128)(2,1)S(1)}, bf16[48,256]{1,0:T(8,128)(2,1)S(1)}, u32[]{:S(2)}, u32[]{:S(2)}) collective-permute-start(bf16[48,256]{1,0:T(8,128)(2,1)S(1)} %get-tuple-element.74), channel_id=1, source_target_pairs={{0,4},{8,12},{16,20},{24,28},{4,0},{12,8},{20,16},{28,24},{1,5},{9... | collective-permute-start | bytes 73736 | tf_op jit(solution)/shard_map/ppermute | solution.py:622
  26.4 7.2 %collective-permute-start.4 = (f32[8,128]{1,0:T(8,128)S(1)}, f32[8,128]{1,0:T(8,128)S(1)}, u32[]{:S(2)}, u32[]{:S(2)}) collective-permute-start(f32[8,128]{1,0:T(8,128)S(1)} %get-tuple-element.82), channel_id=1, source_target_pairs={{4,8},{12,16},{20,24},{8,4},{16,12},{24,20},{5,9},{13,17},{21,25},... | collective-permute-start | bytes 12296 | tf_op jit(solution)/shard_map/ppermute | solution.py:622
  27.3 6.4 %collective-permute-start.5 = (f32[8,128]{1,0:T(8,128)S(1)}, f32[8,128]{1,0:T(8,128)S(1)}, u32[]{:S(2)}, u32[]{:S(2)}) collective-permute-start(f32[8,128]{1,0:T(8,128)S(1)} %get-tuple-element.83), channel_id=1, source_target_pairs={{0,4},{8,12},{16,20},{24,28},{4,0},{12,8},{20,16},{28,24},{1,5},{9... | collective-permute-start | bytes 12296 | tf_op jit(solution)/shard_map/ppermute | solution.py:622
  36.1 7.6 %collective-permute-start.6 = (bf16[48,256]{1,0:T(8,128)(2,1)S(1)}, bf16[48,256]{1,0:T(8,128)(2,1)S(1)}, u32[]{:S(2)}, u32[]{:S(2)}) collective-permute-start(bf16[48,256]{1,0:T(8,128)(2,1)S(1)} %get-tuple-element.90), channel_id=1, source_target_pairs={{4,8},{12,16},{20,24},{8,4},{16,12},{24,20},{5,9},{13,17},{21,25},... | collective-permute-start | bytes 73736 | tf_op jit(solution)/shard_map/ppermute | solution.py:622
  36.7 6.9 %collective-permute-start.7 = (bf16[48,256]{1,0:T(8,128)(2,1)S(1)}, bf16[48,256]{1,0:T(8,128)(2,1)S(1)}, u32[]{:S(2)}, u32[]{:S(2)}) collective-permute-start(bf16[48,256]{1,0:T(8,128)(2,1)S(1)} %get-tuple-element.91), channel_id=1, source_target_pairs={{0,4},{8,12},{16,20},{24,28},{4,0},{12,8},{20,16},{28,24},{1,5},{9... | collective-permute-start | bytes 73736 | tf_op jit(solution)/shard_map/ppermute | solution.py:622
  45.9 4.7 %collective-permute-start.8 = (f32[8,128]{1,0:T(8,128)S(1)}, f32[8,128]{1,0:T(8,128)S(1)}, u32[]{:S(2)}, u32[]{:S(2)}) collective-permute-start(f32[8,128]{1,0:T(8,128)S(1)} %get-tuple-element.98), channel_id=1, source_target_pairs={{4,8},{12,16},{20,24},{8,4},{16,12},{24,20},{5,9},{13,17},{21,25},... | collective-permute-start | bytes 12296 | tf_op jit(solution)/shard_map/ppermute | solution.py:622
  46.5 5.6 %collective-permute-start.9 = (f32[8,128]{1,0:T(8,128)S(1)}, f32[8,128]{1,0:T(8,128)S(1)}, u32[]{:S(2)}, u32[]{:S(2)}) collective-permute-start(f32[8,128]{1,0:T(8,128)S(1)} %get-tuple-element.99), channel_id=1, source_target_pairs={{0,4},{8,12},{16,20},{24,28},{4,0},{12,8},{20,16},{28,24},{1,5},{9... | collective-permute-start | bytes 12296 | tf_op jit(solution)/shard_map/ppermute | solution.py:622
  54.6 7.7 %copy-start.1 = (s32[256]{0:T(256)S(1)}, s32[256]{0:T(256)}, u32[]{:S(2)}) copy-start(s32[256]{0:T(256)} %param.15) | copy-start | bytes 3076
  54.6 7.7 %collective-permute-start.10 = (bf16[48,256]{1,0:T(8,128)(2,1)S(1)}, bf16[48,256]{1,0:T(8,128)(2,1)S(1)}, u32[]{:S(2)}, u32[]{:S(2)}) collective-permute-start(bf16[48,256]{1,0:T(8,128)(2,1)S(1)} %get-tuple-element.102), channel_id=1, source_target_pairs={{4,8},{12,16},{20,24},{8,4},{16,12},{24,20},{5,9},{13,17},{21,25},... | collective-permute-start | bytes 73736 | tf_op jit(solution)/shard_map/ppermute | solution.py:622
  55.5 6.8 %collective-permute-start.11 = (bf16[48,256]{1,0:T(8,128)(2,1)S(1)}, bf16[48,256]{1,0:T(8,128)(2,1)S(1)}, u32[]{:S(2)}, u32[]{:S(2)}) collective-permute-start(bf16[48,256]{1,0:T(8,128)(2,1)S(1)} %get-tuple-element.103), channel_id=1, source_target_pairs={{0,4},{8,12},{16,20},{24,28},{4,0},{12,8},{20,16},{28,24},{1,5},{9... | collective-permute-start | bytes 73736 | tf_op jit(solution)/shard_map/ppermute | solution.py:622

commit v14 on v13

--- a/solution.py
+++ b/solution.py
@@ -378,7 +378,7 @@
                 picked_ref[8 * m : 8 * m + 8, c * LANES : (c + 1) * LANES] = chosen[8 * c : 8 * c + 8]
 
 
-def adjoint_kernel(step, last, clusters, levels, *refs):
+def adjoint_kernel(last, clusters, levels, *refs):
     block_ref, block_a, block_b, own_a, own_b, new_a, new_b, inner_ref, weight_ref, *refs = refs
     conn_ref, cell_ref, fr_ref, blocks, edge_hot, cell_map, spread_map, order_map, *refs = refs
     if last:
@@ -422,7 +422,7 @@
                     row = 24 * at + 8 * c
                     value = jnp.where(which == level, part[row : row + 8], value)
                 n_ref[8 * m : 8 * m + 8, c * LANES : (c + 1) * LANES] = value
-    natural = product(step > 0)(n_ref[...].astype(BF16), order_map[...])
+    natural = product(last)(n_ref[...].astype(BF16), order_map[...])
     p_ref[...] = jnp.zeros_like(p_ref)
     for m in range(pairs):
         for side in range(2):
@@ -433,7 +433,7 @@
             p_ref[8 * m : 8 * m + 8, at : at + order] = out
 
     hi, lo = split(p_ref[...])
-    partial = product(step > 0)(jnp.concatenate([hi, lo], axis=0), spread_map[...])
+    partial = product(last)(jnp.concatenate([hi, lo], axis=0), spread_map[...])
     half = 8 * pairs
     partial = partial[:half] + partial[half:]
     cells = cell_ref[...]
@@ -444,7 +444,7 @@
         hi = rows.astype(BF16).astype(F32)
         both = jnp.concatenate([hi, rows - hi], axis=0)
         v_ref[:, m * LANES : (m + 1) * LANES] = both.astype(BF16)
-    basal = product(step > 0)(v_ref[...], cell_map[...])
+    basal = product(last)(v_ref[...], cell_map[...])
     basal = basal[:24] + basal[24:]
     parts = [basal[8 * i : 8 * i + 8] for i in range(3)]
     for i in range(3):
@@ -692,22 +692,6 @@
         squares += extra[:1]
         if step == 1:
             samples = extra[1]
-        if step == 0:
-            far, near, settled = lax.optimization_barrier((far, near, conn))
-            shape = shaped((refs, RADIX), BF16)
-            node_map = call(turn_nodes_kernel, "turn_nodes", shape, [settled])
-        if step == 1:
-            far, near, settled = lax.optimization_barrier((far, near, cells))
-            cell_map, spread_map, order_map = call(
-                functools.partial(turn_cells_kernel, node_slots),
-                "turn_cells",
-                [
-                    shaped((refs, LANES), BF16),
-                    shaped((2 * padded_order, LANES), BF16),
-                    shaped((3 * LANES, 2 * padded_order), BF16),
-                ],
-                [settled],
-            )
         new_a, new_b = swapped(far, near)
         inner = call(
             functools.partial(inner_kernel, levels),
@@ -716,8 +700,6 @@
             [ordered, weight, conn, node_hot, level_hot],
             [pltpu.VMEM((48 * (levels - 2), refs), BF16)],
         )
-        if step == 0:
-            inner, node_map = lax.optimization_barrier((inner, node_map))
         operands = [block, block_a, block_b, own_a, own_b, new_a, new_b, inner, weight]
         operands += [conn, cells, fr, loaded, edge_hot, cell_map, spread_map, order_map]
         if last:
@@ -727,7 +709,7 @@
         else:
             out_shape = [whole, rim, rim]
         basal, *messages = call(
-            functools.partial(adjoint_kernel, step, last, tiles, levels),
+            functools.partial(adjoint_kernel, last, tiles, levels),
             "adjoint",
             out_shape,
             operands,
@@ -739,9 +721,24 @@
         )
         if not last:
             if step == 0:
-                *messages, settled = lax.optimization_barrier((*messages, loaded))
+                *messages, source, ids = lax.optimization_barrier((*messages, loaded, conn))
                 shape = shaped(blocks.shape, BF16)
-                factors = call(turn_blocks_kernel, "turn_blocks", shape, [settled])
+                factors = call(turn_blocks_kernel, "turn_blocks", shape, [source])
+                shape = shaped((refs, RADIX), BF16)
+                node_map = call(turn_nodes_kernel, "turn_nodes", shape, [ids])
+            if step == POWER - 1:
+                *messages, ids = lax.optimization_barrier((*messages, cells))
+                cell_map, spread_map, order_map = call(
+                    functools.partial(turn_cells_kernel, node_slots),
+                    "turn_cells",
+                    [
+                        shaped((refs, LANES), BF16),
+                        shaped((2 * padded_order, LANES), BF16),
+                        shaped((3 * LANES, 2 * padded_order), BF16),
+                    ],
+                    [ids],
+                )
+                basal, cell_map = lax.optimization_barrier((basal, cell_map))
             carried = [basal, *swapped(*messages)]
 
     gathered = lax.all_to_all(messages[0], everyone, 0, 0)

time: 78.5 us -> 78.7 us (level)
  waiting for transfers between devices: 1.61 us -> 0.82 us
    ppermute x6, waiting for transfers between devices: 1.6 us -> 0.8 us  [swapped(): lax.ppermute(b, 'tiles', pairs_b)]
  transfers between devices with their start and end apart: 12 -> 12, of which waited for: 1 -> 1; matrix products, arithmetic and copies ran while one was open for 0% -> 0% of each run, Pallas kernels for 18% -> 19%
where the time goes in v14:
time: 78.7 us; the launch traced here: 78.3 us
  Pallas kernels  32.5 us (41%)
  starting transfers between devices  31.1 us (40%)
  blocking collectives  12.3 us (16%)
  between operations  1.51 us (2%)
  waiting for transfers between devices  0.82 us (1%)
    pallas_call x15, Pallas kernels, call(): pl.pallas_call(kernel, out_shape=out_shape, in_specs=in_specs, out_specs=...  32.5 us
    ppermute x6, starting transfers between devices, swapped(): lax.ppermute(b, 'tiles', pairs_b)  26.7 us
    all_to_all x1, blocking collectives, shards(): gathered = lax.all_to_all(messages[0], everyone, 0, 0)  12.3 us
    ppermute x6, starting transfers between devices, swapped(): lax.ppermute(a, 'tiles', pairs_a)  4.43 us
  transfers between devices with their start and end apart: 12, of which 1 were waited for; matrix products, arithmetic and copies ran while one was open for 0% of the time, Pallas kernels for 19%

profile of v14, /device:TPU:0, one launch (start us, length us, event | category | flops | bytes accessed | tf_op | source)
XLA Modules:
  0.0 78.3 jit_solution(13439046908669424)
XLA Ops:
  0.6 0.8 announce.1
  1.4 0.7 collective-permute-start
  2.1 5.8 %collective-permute-start.1 = (f32[16,256]{1,0:T(8,128)S(1)}, f32[16,256]{1,0:T(8,128)S(1)}, u32[]{:S(2)}, u32[]{:S(2)}) collective-permute-start(f32[16,256]{1,0:T(8,128)S(1)} %get-tuple-element.56.refs_0_), channel_id=1, source_target_pairs={{0,4},{8,12},{16,20},{24,28},{4,0},{12,8},{20,16},{28,24},{1,5},{9... | collective-permute-start | bytes 49160 | tf_op jit(solution)/shard_map/ppermute | solution.py:622
  8.5 3.3 %setup.1 = (s32[32,128]{1,0:T(8,128)S(1)}, s32[32,128]{1,0:T(8,128)S(1)}, f32[64,256]{1,0:T(8,128)S(1)}, bf16[64,192,192]{2,1,0:T(8,128)(2,1)S(1)}, bf16[512,409...) custom-call(s32[1]{0:T(128)S(6)} %copy.11.counts, ...), custom_call_target="tpu_custom_call" | custom-call | tf_op jit(solution)/shard_map/setup/pallas_call | solution.py:606
  11.8 0.0 collective-permute-done.refs_1_
  11.9 0.0 collective-permute-done.1.refs_2_
  11.9 0.0 copy-start
  11.9 3.8 %forward.3 = (bf16[512,384]{1,0:T(8,128)(2,1)S(1)}, f32[24,512]{1,0:T(8,128)S(1)}, f32[24,512]{1,0:T(8,128)S(1)}, bf16[48,256]{1,0:T(8,128)(2,1)S(1)}, bf16[48,256]{1,0:T(8,128)(2,1)S(1)}) custom-call(f32[16,256]{1,0:T(8,128)S(1)} %get-tuple-element.56.refs_0_, f32[16,256]{1,0:T(8,128)S(1)} %collective-permute-done.refs_1_, ...), custom_call_target="tpu_custom_call" | custom-call | tf_op jit(solution)/shard_map/forward/pallas_call | solution.py:606
  15.6 0.7 collective-permute-start.2
  16.3 4.3 %collective-permute-start.3 = (bf16[48,256]{1,0:T(8,128)(2,1)S(1)}, bf16[48,256]{1,0:T(8,128)(2,1)S(1)}, u32[]{:S(2)}, u32[]{:S(2)}) collective-permute-start(bf16[48,256]{1,0:T(8,128)(2,1)S(1)} %get-tuple-element.69), channel_id=1, source_target_pairs={{0,4},{8,12},{16,20},{24,28},{4,0},{12,8},{20,16},{28,24},{1,5},{9... | collective-permute-start | bytes 73736 | tf_op jit(solution)/shard_map/ppermute | solution.py:622
  20.6 0.0 copy-done
  20.6 2.6 %inner.3.refs_7_ = f32[256,384]{1,0:T(8,128)S(1)} custom-call(bf16[512,384]{1,0:T(8,128)(2,1)S(1)} %get-tuple-element.70.ordered_ref, f32[3,4096]{1,0:T(4,128)S(1)} %bitcast.8, s32[32,128]{1,0:T(8,128)S(1)} %get-tuple-element.79.conn_ref.refs_9_, bf16[512,4096]{1,0:T(8,128)(2,1)S(1)} %get-tuple-element.61.refs_6_.node_hot, ...), custom_call_target="tpu_custom_call" | custom-call | tf_op jit(solution)/shard_map/inner/pallas_call | solution.py:606
  23.2 0.0 collective-permute-done.2.refs_5_
  23.2 0.0 collective-permute-done.3.refs_6_
  23.2 2.5 %adjoint.3 = (f32[8,384]{1,0:T(8,128)S(1)}, f32[8,128]{1,0:T(8,128)S(1)}, f32[8,128]{1,0:T(8,128)S(1)}) custom-call(f32[16,256]{1,0:T(8,128)S(1)} %get-tuple-element.56.refs_0_, f32[16,256]{1,0:T(8,128)S(1)} %collective-permute-done.refs_1_, f32[16,256]{1,0:T(8,128)S(1)} %collective-permute-done.1.refs_2_, f32[24,512]{1,0:T(8,128)S(1)} %get-tuple-element.66.refs_3_, ...), custom_call_target="tpu_custom_call" | custom-call | tf_op jit(solution)/shard_map/adjoint/pallas_call | solution.py:606
  25.7 0.9 %collective-permute-start.4 = (f32[8,128]{1,0:T(8,128)S(1)}, f32[8,128]{1,0:T(8,128)S(1)}, u32[]{:S(2)}, u32[]{:S(2)}) collective-permute-start(f32[8,128]{1,0:T(8,128)S(1)} %get-tuple-element.76), channel_id=1, source_target_pairs={{4,8},{12,16},{20,24},{8,4},{16,12},{24,20},{5,9},{13,17},{21,25},... | collective-permute-start | bytes 12296 | tf_op jit(solution)/shard_map/ppermute | solution.py:622
  26.6 4.4 %collective-permute-start.5 = (f32[8,128]{1,0:T(8,128)S(1)}, f32[8,128]{1,0:T(8,128)S(1)}, u32[]{:S(2)}, u32[]{:S(2)}) collective-permute-start(f32[8,128]{1,0:T(8,128)S(1)} %get-tuple-element.77), channel_id=1, source_target_pairs={{0,4},{8,12},{16,20},{24,28},{4,0},{12,8},{20,16},{28,24},{1,5},{9... | collective-permute-start | bytes 12296 | tf_op jit(solution)/shard_map/ppermute | solution.py:622
  30.9 0.8 %turn_nodes.1.refs_9_ = bf16[4096,512]{1,0:T(8,128)(2,1)S(1)} custom-call(s32[32,128]{1,0:T(8,128)S(1)} %get-tuple-element.79.conn_ref.refs_9_), custom_call_target="tpu_custom_call" | custom-call | tf_op jit(solution)/shard_map/turn_nodes/pallas_call | solution.py:606
  31.7 2.0 %turn_blocks.1.refs_8_ = bf16[64,192,192]{2,1,0:T(8,128)(2,1)S(1)} custom-call(bf16[64,192,192]{2,1,0:T(8,128)(2,1)S(1)} %get-tuple-element.78.refs_5_.refs_12_.blocks), custom_call_target="tpu_custom_call" | custom-call | tf_op jit(solution)/shard_map/turn_blocks/pallas_call | solution.py:606
  33.7 0.0 collective-permute-done.4.refs_4_
  33.7 0.0 collective-permute-done.5.refs_5_
  33.8 2.4 %forward.4 = (bf16[512,384]{1,0:T(8,128)(2,1)S(1)}, f32[24,512]{1,0:T(8,128)S(1)}, f32[24,512]{1,0:T(8,128)S(1)}, bf16[48,256]{1,0:T(8,128)(2,1)S(1)}, bf16[48,2...) custom-call(f32[16,256]{1,0:T(8,128)S(1)} %get-tuple-element.56.refs_0_, ...), custom_call_target="tpu_custom_call" | custom-call | tf_op jit(solution)/shard_map/forward/pallas_call | solution.py:606
  36.1 0.7 collective-permute-start.6
  36.8 3.4 %collective-permute-start.7 = (bf16[48,256]{1,0:T(8,128)(2,1)S(1)}, bf16[48,256]{1,0:T(8,128)(2,1)S(1)}, u32[]{:S(2)}, u32[]{:S(2)}) collective-permute-start(bf16[48,256]{1,0:T(8,128)(2,1)S(1)} %get-tuple-element.83), channel_id=1, source_target_pairs={{0,4},{8,12},{16,20},{24,28},{4,0},{12,8},{20,16},{28,24},{1,5},{9... | collective-permute-start | bytes 73736 | tf_op jit(solution)/shard_map/ppermute | solution.py:622
  40.2 2.6 %inner.4.refs_7_ = f32[256,384]{1,0:T(8,128)S(1)} custom-call(bf16[512,384]{1,0:T(8,128)(2,1)S(1)} %get-tuple-element.84.ordered_ref, f32[3,4096]{1,0:T(4,128)S(1)} %bitcast.10, s32[32,128]{1,0:T(8,128)S(1)} %get-tuple-element.79.conn_ref.refs_9_, bf16[512,4096]{1,0:T(8,128)(2,1)S(1)} %get-tuple-element.61.refs_6_.node_hot, ...), custom_call_target="tpu_custom_call" | custom-call | tf_op jit(solution)/shard_map/inner/pallas_call | solution.py:606
  42.7 0.0 collective-permute-done.6.refs_5_
  42.8 0.0 collective-permute-done.7.refs_6_
  42.8 2.5 %adjoint.4 = (f32[8,384]{1,0:T(8,128)S(1)}, f32[8,128]{1,0:T(8,128)S(1)}, f32[8,128]{1,0:T(8,128)S(1)}) custom-call(f32[16,256]{1,0:T(8,128)S(1)} %get-tuple-element.56.refs_0_, f32[16,256]{1,0:T(8,128)S(1)} %collective-permute-done.refs_1_, f32[16,256]{1,0:T(8,128)S(1)} %collective-permute-done.1.refs_2_, f32[24,512]{1,0:T(8,128)S(1)} %get-tuple-element.80.refs_3_, ...), custom_call_target="tpu_custom_call" | custom-call | tf_op jit(solution)/shard_map/adjoint/pallas_call | solution.py:606
  45.3 0.7 collective-permute-start.8
  46.0 4.2 %collective-permute-start.9 = (f32[8,128]{1,0:T(8,128)S(1)}, f32[8,128]{1,0:T(8,128)S(1)}, u32[]{:S(2)}, u32[]{:S(2)}) collective-permute-start(f32[8,128]{1,0:T(8,128)S(1)} %get-tuple-element.92), channel_id=1, source_target_pairs={{0,4},{8,12},{16,20},{24,28},{4,0},{12,8},{20,16},{28,24},{1,5},{9... | collective-permute-start | bytes 12296 | tf_op jit(solution)/shard_map/ppermute | solution.py:622
  50.2 0.8 turn_cells.1
  51.0 0.0 collective-permute-done.8.refs_4_
  51.0 0.8 %collective-permute-done.9.refs_5_ = f32[8,128]{1,0:T(8,128)S(1)} collective-permute-done((f32[8,128]{1,0:T(8,128)S(1)}, f32[8,128]{1,0:T(8,128)S(1)}, u32[]{:S(2)}, u32[]{:S(2)}) %collective-permute-start.9) | collective-permute-done | bytes 4128 | tf_op jit(solution)/shard_map/ppermute | solution.py:622
  51.8 2.4 %forward.5 = (bf16[512,384]{1,0:T(8,128)(2,1)S(1)}, f32[24,512]{1,0:T(8,128)S(1)}, f32[24,512]{1,0:T(8,128)S(1)}, bf16[48,256]{1,0:T(8,128)(2,1)S(1)}, bf16[48,2...) custom-call(f32[16,256]{1,0:T(8,128)S(1)} %get-tuple-element.56.refs_0_, f32[16,256]{1,0:T(8,128)S(1)} %collective-permute-done.refs_1_, ...), custom_call_target="tpu_custom_call" | custom-call | tf_op jit(solution)/shard_map/forward/pallas_call | solution.py:606
  54.1 0.0 copy-start.1
  54.1 0.9 %collective-permute-start.10 = (bf16[48,256]{1,0:T(8,128)(2,1)S(1)}, bf16[48,256]{1,0:T(8,128)(2,1)S(1)}, u32[]{:S(2)}, u32[]{:S(2)}) collective-permute-start(bf16[48,256]{1,0:T(8,128)(2,1)S(1)} %get-tuple-element.95), channel_id=1, source_target_pairs={{4,8},{12,16},{20,24},{8,4},{16,12},{24,20},{5,9},{13,17},{21,25},... | collective-permute-start | bytes 73736 | tf_op jit(solution)/shard_map/ppermute | solution.py:622
  55.0 4.6 %collective-permute-start.11 = (bf16[48,256]{1,0:T(8,128)(2,1)S(1)}, bf16[48,256]{1,0:T(8,128)(2,1)S(1)}, u32[]{:S(2)}, u32[]{:S(2)}) collective-permute-start(bf16[48,256]{1,0:T(8,128)(2,1)S(1)} %get-tuple-element.96), channel_id=1, source_target_pairs={{0,4},{8,12},{16,20},{24,28},{4,0},{12,8},{20,16},{28,24},{1,5},{9... | collective-permute-start | bytes 73736 | tf_op jit(solution)/shard_map/ppermute | solution.py:622
  59.6 2.6 %inner.5.refs_7_ = f32[256,384]{1,0:T(8,128)S(1)} custom-call(bf16[512,384]{1,0:T(8,128)(2,1)S(1)} %get-tuple-element.97.ordered_ref, f32[3,4096]{1,0:T(4,128)S(1)} %bitcast.12, s32[32,128]{1,0:T(8,128)S(1)} %get-tuple-element.79.conn_ref.refs_9_, bf16[512,4096]{1,0:T(8,128)(2,1)S(1)} %get-tuple-element.61.refs_6_.node_hot, ...), custom_call_target="tpu_custom_call" | custom-call | tf_op jit(solution)/shard_map/inner/pallas_call | solution.py:606
  62.2 0.0 collective-permute-done.10.refs_5_
  62.2 0.0 collective-permute-done.11.refs_6_
  62.2 0.0 copy-done.1
  62.2 2.3 %adjoint.5 = (f32[8,384]{1,0:T(8,128)S(1)}, bf16[32,8,256]{2,1,0:T(8,128)(2,1)S(1)}) custom-call(f32[16,256]{1,0:T(8,128)S(1)} %get-tuple-element.56.refs_0_, f32[16,256]{1,0:T(8,128)S(1)} %collective-permute-done.refs_1_, f32[16,256]{1,0:T(8,128)S(1)} %collective-permute-done.1.refs_2_, f32[24,512]{1,0:T(8,128)S(1)} %get-tuple-element.93.refs_3_, ...), custom_call_target="tpu_custom_call" | custom-call | tf_op jit(solution)/shard_map/adjoint/pallas_call | solution.py:606
  64.5 12.3 %all_to_all.5 = bf16[32,8,256]{2,1,0:T(8,128)(2,1)S(1)} all-to-all(bf16[32,8,256]{2,1,0:T(8,128)(2,1)S(1)} %get-tuple-element.103), channel_id=1, replica_groups=mesh['tiles'=8,'probes'=4] {'tiles','probes'}, dimensions={0} | all-to-all | bytes 262144 | tf_op jit(solution)/shard_map/all_to_all | solution.py:744
  76.8 1.5 %gram.1 = (f32[8,256]{1,0:T(8,128)}, f32[8,256]{1,0:T(8,128)}, f32[8,8,32]{2,1,0:T(8,128)}) custom-call(bf16[8,4,8,256]{3,2,1,0:T(8,128)(2,1)S(1)} %bitcast.14, f32[8,384]{1,0:T(8,128)S(1)} %get-tuple-element.104.own_ref, f32[8,256]{1,0:T(8,128)S(1)} %get-tuple-element.105.samples_in), custom_call_target="tpu_custom_call" | custom-call | tf_op jit(solution)/shard_map/gram/pallas_call | solution.py:606
Async XLA Ops:
  1.4 10.4 %collective-permute-start = (f32[16,256]{1,0:T(8,128)S(1)}, f32[16,256]{1,0:T(8,128)S(1)}, u32[]{:S(2)}, u32[]{:S(2)}) collective-permute-start(f32[16,256]{1,0:T(8,128)S(1)} %get-tuple-element.57), channel_id=1, source_target_pairs={{4,8},{12,16},{20,24},{8,4},{16,12},{24,20},{5,9},{13,17},{21,25},... | collective-permute-start | bytes 49160 | tf_op jit(solution)/shard_map/ppermute | solution.py:622
  2.1 9.8 %collective-permute-start.1 = (f32[16,256]{1,0:T(8,128)S(1)}, f32[16,256]{1,0:T(8,128)S(1)}, u32[]{:S(2)}, u32[]{:S(2)}) collective-permute-start(f32[16,256]{1,0:T(8,128)S(1)} %get-tuple-element.56.refs_0_), channel_id=1, source_target_pairs={{0,4},{8,12},{16,20},{24,28},{4,0},{12,8},{20,16},{28,24},{1,5},{9... | collective-permute-start | bytes 49160 | tf_op jit(solution)/shard_map/ppermute | solution.py:622
  11.9 8.8 %copy-start = (f32[4096,3]{0,1:T(4,128)S(1)}, f32[4096,3]{0,1:T(4,128)}, u32[]{:S(2)}) copy-start(f32[4096,3]{0,1:T(4,128)} %param.13) | copy-start | bytes 147460
  15.6 7.6 %collective-permute-start.2 = (bf16[48,256]{1,0:T(8,128)(2,1)S(1)}, bf16[48,256]{1,0:T(8,128)(2,1)S(1)}, u32[]{:S(2)}, u32[]{:S(2)}) collective-permute-start(bf16[48,256]{1,0:T(8,128)(2,1)S(1)} %get-tuple-element.68), channel_id=1, source_target_pairs={{4,8},{12,16},{20,24},{8,4},{16,12},{24,20},{5,9},{13,17},{21,25},... | collective-permute-start | bytes 73736 | tf_op jit(solution)/shard_map/ppermute | solution.py:622
  16.3 6.9 %collective-permute-start.3 = (bf16[48,256]{1,0:T(8,128)(2,1)S(1)}, bf16[48,256]{1,0:T(8,128)(2,1)S(1)}, u32[]{:S(2)}, u32[]{:S(2)}) collective-permute-start(bf16[48,256]{1,0:T(8,128)(2,1)S(1)} %get-tuple-element.69), channel_id=1, source_target_pairs={{0,4},{8,12},{16,20},{24,28},{4,0},{12,8},{20,16},{28,24},{1,5},{9... | collective-permute-start | bytes 73736 | tf_op jit(solution)/shard_map/ppermute | solution.py:622
  25.7 8.0 %collective-permute-start.4 = (f32[8,128]{1,0:T(8,128)S(1)}, f32[8,128]{1,0:T(8,128)S(1)}, u32[]{:S(2)}, u32[]{:S(2)}) collective-permute-start(f32[8,128]{1,0:T(8,128)S(1)} %get-tuple-element.76), channel_id=1, source_target_pairs={{4,8},{12,16},{20,24},{8,4},{16,12},{24,20},{5,9},{13,17},{21,25},... | collective-permute-start | bytes 12296 | tf_op jit(solution)/shard_map/ppermute | solution.py:622
  26.6 7.2 %collective-permute-start.5 = (f32[8,128]{1,0:T(8,128)S(1)}, f32[8,128]{1,0:T(8,128)S(1)}, u32[]{:S(2)}, u32[]{:S(2)}) collective-permute-start(f32[8,128]{1,0:T(8,128)S(1)} %get-tuple-element.77), channel_id=1, source_target_pairs={{0,4},{8,12},{16,20},{24,28},{4,0},{12,8},{20,16},{28,24},{1,5},{9... | collective-permute-start | bytes 12296 | tf_op jit(solution)/shard_map/ppermute | solution.py:622
  36.1 6.6 %collective-permute-start.6 = (bf16[48,256]{1,0:T(8,128)(2,1)S(1)}, bf16[48,256]{1,0:T(8,128)(2,1)S(1)}, u32[]{:S(2)}, u32[]{:S(2)}) collective-permute-start(bf16[48,256]{1,0:T(8,128)(2,1)S(1)} %get-tuple-element.82), channel_id=1, source_target_pairs={{4,8},{12,16},{20,24},{8,4},{16,12},{24,20},{5,9},{13,17},{21,25},... | collective-permute-start | bytes 73736 | tf_op jit(solution)/shard_map/ppermute | solution.py:622
  36.8 5.9 %collective-permute-start.7 = (bf16[48,256]{1,0:T(8,128)(2,1)S(1)}, bf16[48,256]{1,0:T(8,128)(2,1)S(1)}, u32[]{:S(2)}, u32[]{:S(2)}) collective-permute-start(bf16[48,256]{1,0:T(8,128)(2,1)S(1)} %get-tuple-element.83), channel_id=1, source_target_pairs={{0,4},{8,12},{16,20},{24,28},{4,0},{12,8},{20,16},{28,24},{1,5},{9... | collective-permute-start | bytes 73736 | tf_op jit(solution)/shard_map/ppermute | solution.py:622
  45.3 5.7 %collective-permute-start.8 = (f32[8,128]{1,0:T(8,128)S(1)}, f32[8,128]{1,0:T(8,128)S(1)}, u32[]{:S(2)}, u32[]{:S(2)}) collective-permute-start(f32[8,128]{1,0:T(8,128)S(1)} %get-tuple-element.91), channel_id=1, source_target_pairs={{4,8},{12,16},{20,24},{8,4},{16,12},{24,20},{5,9},{13,17},{21,25},... | collective-permute-start | bytes 12296 | tf_op jit(solution)/shard_map/ppermute | solution.py:622
  46.0 5.8 %collective-permute-start.9 = (f32[8,128]{1,0:T(8,128)S(1)}, f32[8,128]{1,0:T(8,128)S(1)}, u32[]{:S(2)}, u32[]{:S(2)}) collective-permute-start(f32[8,128]{1,0:T(8,128)S(1)} %get-tuple-element.92), channel_id=1, source_target_pairs={{0,4},{8,12},{16,20},{24,28},{4,0},{12,8},{20,16},{28,24},{1,5},{9... | collective-permute-start | bytes 12296 | tf_op jit(solution)/shard_map/ppermute | solution.py:622
  54.1 8.1 %copy-start.1 = (s32[256]{0:T(256)S(1)}, s32[256]{0:T(256)}, u32[]{:S(2)}) copy-start(s32[256]{0:T(256)} %param.15) | copy-start | bytes 3076
  54.1 8.0 %collective-permute-start.10 = (bf16[48,256]{1,0:T(8,128)(2,1)S(1)}, bf16[48,256]{1,0:T(8,128)(2,1)S(1)}, u32[]{:S(2)}, u32[]{:S(2)}) collective-permute-start(bf16[48,256]{1,0:T(8,128)(2,1)S(1)} %get-tuple-element.95), channel_id=1, source_target_pairs={{4,8},{12,16},{20,24},{8,4},{16,12},{24,20},{5,9},{13,17},{21,25},... | collective-permute-start | bytes 73736 | tf_op jit(solution)/shard_map/ppermute | solution.py:622
  55.0 7.2 %collective-permute-start.11 = (bf16[48,256]{1,0:T(8,128)(2,1)S(1)}, bf16[48,256]{1,0:T(8,128)(2,1)S(1)}, u32[]{:S(2)}, u32[]{:S(2)}) collective-permute-start(bf16[48,256]{1,0:T(8,128)(2,1)S(1)} %get-tuple-element.96), channel_id=1, source_target_pairs={{0,4},{8,12},{16,20},{24,28},{4,0},{12,8},{20,16},{28,24},{1,5},{9... | collective-permute-start | bytes 73736 | tf_op jit(solution)/shard_map/ppermute | solution.py:622

commit v15 on v14

--- a/solution.py
+++ b/solution.py
@@ -256,6 +256,17 @@
             for c in range(3):
                 row = 48 * i + 16 * c
                 v_ref[row : row + 16, at] = values[c] * mask
+
+
+def both_parts(x):
+    hi = x.astype(BF16).astype(F32)
+    return jnp.concatenate([hi, x - hi], axis=0).astype(BF16)
+
+
+def clear_padding(ref, padded_order):
+    for half in range(2):
+        end = (half + 1) * padded_order
+        ref[:, end - LANES : end] = jnp.zeros((ref.shape[0], LANES), BF16)
 
 
 def forward_kernel(step, tiles, levels, *refs):
@@ -323,7 +334,7 @@
     half = 8 * pairs
     spread = spread[:half] + spread[half:]
 
-    f_ref[...] = jnp.zeros_like(f_ref)
+    clear_padding(f_ref, padded_order)
     for m in range(pairs):
         for side in range(2):
             at = side * padded_order
@@ -332,15 +343,11 @@
             if first:
                 out = product(step > 0)(inputs.astype(BF16), factors[slot])
             else:
-                hi = inputs.astype(BF16).astype(F32)
-                both = jnp.concatenate([hi, inputs - hi], axis=0).astype(BF16)
-                out = product(step > 0)(both, factors[slot])
+                out = product(step > 0)(both_parts(inputs), factors[slot])
                 out = out[:8] + out[8:]
-            hi = out.astype(BF16).astype(F32)
-            f_ref[16 * m : 16 * m + 8, at : at + order] = hi
-            f_ref[16 * m + 8 : 16 * m + 16, at : at + order] = out - hi
-
-    ordered = dot(f_ref[...].astype(BF16), order_ref[...]).astype(BF16)
+            f_ref[16 * m : 16 * m + 16, at : at + order] = both_parts(out)
+
+    ordered = dot(f_ref[...], order_ref[...]).astype(BF16)
     ordered_ref[...] = ordered
     spread_levels(v_ref, ordered, level_hot, (0, levels - 1), pairs)
     rim = product(step > 0)(v_ref[...], node_map[...])
@@ -412,6 +419,7 @@
     width = 2
     for start in range(0, pairs, width):
         found = dot(weighted, edge_hot[:, start * LANES : (start + width) * LANES])
+        values = [[] for _ in range(3)]
         for i in range(width):
             m = start + i
             which = conn[m : m + 1, :] // EDGE_RADIX
@@ -421,25 +429,25 @@
                 for at, level in enumerate(edges):
                     row = 24 * at + 8 * c
                     value = jnp.where(which == level, part[row : row + 8], value)
-                n_ref[8 * m : 8 * m + 8, c * LANES : (c + 1) * LANES] = value
-    natural = product(last)(n_ref[...].astype(BF16), order_map[...])
-    p_ref[...] = jnp.zeros_like(p_ref)
+                values[c].append(value)
+        for c in range(3):
+            rows = jnp.concatenate(values[c], axis=0).astype(BF16)
+            n_ref[8 * start : 8 * (start + width), c * LANES : (c + 1) * LANES] = rows
+    natural = product(last)(n_ref[...], order_map[...])
+    clear_padding(p_ref, padded_order)
     for m in range(pairs):
         for side in range(2):
             at = side * padded_order
             slot = 2 * m + side
             out = dot(natural[8 * m : 8 * m + 8, at : at + order].astype(BF16), blocks[slot])
             out = out * fr_ref[slot : slot + 1, :order]
-            p_ref[8 * m : 8 * m + 8, at : at + order] = out
-
-    hi, lo = split(p_ref[...])
-    partial = product(last)(jnp.concatenate([hi, lo], axis=0), spread_map[...])
-    half = 8 * pairs
-    partial = partial[:half] + partial[half:]
+            p_ref[16 * m : 16 * m + 16, at : at + order] = both_parts(out)
+
+    partial = product(last)(p_ref[...], spread_map[...])
     cells = cell_ref[...]
     for m in range(pairs):
         which = cells[m : m + 1, :] // LANES
-        value = partial[8 * m : 8 * m + 8, :]
+        value = partial[16 * m : 16 * m + 8, :] + partial[16 * m + 8 : 16 * m + 16, :]
         rows = jnp.concatenate([jnp.where(which == level, value, F32(0)) for level in range(3)], axis=0)
         hi = rows.astype(BF16).astype(F32)
         both = jnp.concatenate([hi, rows - hi], axis=0)
@@ -506,7 +514,7 @@
 
     def piece_of(t, p, lower, at):
         part = g_ref[t, p].astype(F32)
-        return twice(part[4 * lower : 4 * lower + 4, at * LANES : (at + 1) * LANES])
+        return part[4 * lower : 4 * lower + 4, at * LANES : (at + 1) * LANES]
 
     def factor_of(p):
         def add(t, acc):
@@ -522,7 +530,7 @@
         return F32(1 / SHRINK) / (scale * jnp.sqrt(size * size + F32(1e-06)))
 
     def ids_of(t):
-        starts = piece_of(t, 0, 1, 1)
+        starts = twice(piece_of(t, 0, 1, 1))
         cell = lanes_iota((8, 2 * LANES)).astype(F32)
         ids = jnp.zeros(cell.shape, jnp.int32)
         for k in range(1, clusters):
@@ -531,13 +539,13 @@
 
     def field(t, p, ids, own=None):
         before = piece_of(jnp.maximum(t - 1, 0), p, 1, 0)
+        before = jnp.where(low[:4] & (t > 0), before, F32(0))
         after = piece_of(jnp.minimum(t + 1, tiles - 1), p, 1, 0)
+        after = jnp.where(~low[:4] & (t < tiles - 1), after, F32(0))
         if own is None:
-            own = [piece_of(t, p, 0, at) for at in range(2)]
-        parts = [
-            own[0] + jnp.where(low & (t > 0), before, F32(0)),
-            own[1] + jnp.where(~low & (t < tiles - 1), after, F32(0)),
-        ]
+            parts = [twice(piece_of(t, p, 0, 0) + before), twice(piece_of(t, p, 0, 1) + after)]
+        else:
+            parts = [own[0] + twice(before), own[1] + twice(after)]
         return [
             jnp.where(colour_of(i) if keep_same else ~colour_of(i), part, F32(0))
             for i, part in zip(ids, parts)
@@ -685,7 +693,7 @@
             [block, block_a, block_b, *carried]
             + [cells, fr, factors, node_map, level_hot, cell_hot, spread, order],
             [
-                pltpu.VMEM((16 * pairs, 2 * padded_order), F32),
+                pltpu.VMEM((16 * pairs, 2 * padded_order), BF16),
                 pltpu.VMEM((96, refs), BF16),
             ],
         )
@@ -714,8 +722,8 @@
             out_shape,
             operands,
             [
-                pltpu.VMEM((8 * pairs, 2 * padded_order), F32),
-                pltpu.VMEM((8 * pairs, 3 * LANES), F32),
+                pltpu.VMEM((16 * pairs, 2 * padded_order), BF16),
+                pltpu.VMEM((8 * pairs, 3 * LANES), BF16),
                 pltpu.VMEM((48, refs), BF16),
             ],
         )

time: 78.7 us -> 78.4 us (level)
  no operation moved by 1% of the time
where the time goes in v15:
time: 78.4 us; the launch traced here: 78.1 us
  Pallas kernels  32.3 us (41%)
  starting transfers between devices  31.1 us (40%)
  blocking collectives  12.3 us (16%)
  between operations  1.52 us (2%)
  waiting for transfers between devices  0.82 us (1%)
    pallas_call x15, Pallas kernels, call(): pl.pallas_call(kernel, out_shape=out_shape, in_specs=in_specs, out_specs=...  32.3 us
    ppermute x6, starting transfers between devices, swapped(): lax.ppermute(b, 'tiles', pairs_b)  26.7 us
    all_to_all x1, blocking collectives, shards(): gathered = lax.all_to_all(messages[0], everyone, 0, 0)  12.3 us
    ppermute x6, starting transfers between devices, swapped(): lax.ppermute(a, 'tiles', pairs_a)  4.43 us
  transfers between devices with their start and end apart: 12, of which 1 were waited for; matrix products, arithmetic and copies ran while one was open for 0% of the time, Pallas kernels for 19%

profile of v15, /device:TPU:0, one launch (start us, length us, event | category | flops | bytes accessed | tf_op | source)
XLA Modules:
  0.0 78.1 jit_solution(8344365795752103022)
XLA Ops:
  0.6 0.8 announce.1
  1.4 0.7 collective-permute-start
  2.1 5.8 %collective-permute-start.1 = (f32[16,256]{1,0:T(8,128)S(1)}, f32[16,256]{1,0:T(8,128)S(1)}, u32[]{:S(2)}, u32[]{:S(2)}) collective-permute-start(f32[16,256]{1,0:T(8,128)S(1)} %get-tuple-element.56.refs_0_), channel_id=1, source_target_pairs={{0,4},{8,12},{16,20},{24,28},{4,0},{12,8},{20,16},{28,24},{1,5},{9... | collective-permute-start | bytes 49160 | tf_op jit(solution)/shard_map/ppermute | solution.py:630
  8.5 3.3 %setup.1 = (s32[32,128]{1,0:T(8,128)S(1)}, s32[32,128]{1,0:T(8,128)S(1)}, f32[64,256]{1,0:T(8,128)S(1)}, bf16[64,192,192]{2,1,0:T(8,128)(2,1)S(1)}, bf16[512,409...) custom-call(s32[1]{0:T(128)S(6)} %copy.11.counts, ...), custom_call_target="tpu_custom_call" | custom-call | tf_op jit(solution)/shard_map/setup/pallas_call | solution.py:614
  11.8 0.0 collective-permute-done.refs_1_
  11.9 0.0 collective-permute-done.1.refs_2_
  11.9 0.0 copy-start
  11.9 3.7 %forward.3 = (bf16[512,384]{1,0:T(8,128)(2,1)S(1)}, f32[24,512]{1,0:T(8,128)S(1)}, f32[24,512]{1,0:T(8,128)S(1)}, bf16[48,256]{1,0:T(8,128)(2,1)S(1)}, bf16[48,256]{1,0:T(8,128)(2,1)S(1)}) custom-call(f32[16,256]{1,0:T(8,128)S(1)} %get-tuple-element.56.refs_0_, f32[16,256]{1,0:T(8,128)S(1)} %collective-permute-done.refs_1_, ...), custom_call_target="tpu_custom_call" | custom-call | tf_op jit(solution)/shard_map/forward/pallas_call | solution.py:614
  15.6 0.7 collective-permute-start.2
  16.3 4.4 %collective-permute-start.3 = (bf16[48,256]{1,0:T(8,128)(2,1)S(1)}, bf16[48,256]{1,0:T(8,128)(2,1)S(1)}, u32[]{:S(2)}, u32[]{:S(2)}) collective-permute-start(bf16[48,256]{1,0:T(8,128)(2,1)S(1)} %get-tuple-element.69), channel_id=1, source_target_pairs={{0,4},{8,12},{16,20},{24,28},{4,0},{12,8},{20,16},{28,24},{1,5},{9... | collective-permute-start | bytes 73736 | tf_op jit(solution)/shard_map/ppermute | solution.py:630
  20.6 0.0 copy-done
  20.6 2.6 %inner.3.refs_7_ = f32[256,384]{1,0:T(8,128)S(1)} custom-call(bf16[512,384]{1,0:T(8,128)(2,1)S(1)} %get-tuple-element.70.ordered_ref, f32[3,4096]{1,0:T(4,128)S(1)} %bitcast.8, s32[32,128]{1,0:T(8,128)S(1)} %get-tuple-element.79.conn_ref.refs_9_, bf16[512,4096]{1,0:T(8,128)(2,1)S(1)} %get-tuple-element.61.refs_6_.node_hot, ...), custom_call_target="tpu_custom_call" | custom-call | tf_op jit(solution)/shard_map/inner/pallas_call | solution.py:614
  23.2 0.0 collective-permute-done.2.refs_5_
  23.2 0.0 collective-permute-done.3.refs_6_
  23.2 2.4 %adjoint.3 = (f32[8,384]{1,0:T(8,128)S(1)}, f32[8,128]{1,0:T(8,128)S(1)}, f32[8,128]{1,0:T(8,128)S(1)}) custom-call(f32[16,256]{1,0:T(8,128)S(1)} %get-tuple-element.56.refs_0_, f32[16,256]{1,0:T(8,128)S(1)} %collective-permute-done.refs_1_, f32[16,256]{1,0:T(8,128)S(1)} %collective-permute-done.1.refs_2_, f32[24,512]{1,0:T(8,128)S(1)} %get-tuple-element.66.refs_3_, ...), custom_call_target="tpu_custom_call" | custom-call | tf_op jit(solution)/shard_map/adjoint/pallas_call | solution.py:614
  25.6 0.9 %collective-permute-start.4 = (f32[8,128]{1,0:T(8,128)S(1)}, f32[8,128]{1,0:T(8,128)S(1)}, u32[]{:S(2)}, u32[]{:S(2)}) collective-permute-start(f32[8,128]{1,0:T(8,128)S(1)} %get-tuple-element.76), channel_id=1, source_target_pairs={{4,8},{12,16},{20,24},{8,4},{16,12},{24,20},{5,9},{13,17},{21,25},... | collective-permute-start | bytes 12296 | tf_op jit(solution)/shard_map/ppermute | solution.py:630
  26.5 4.4 %collective-permute-start.5 = (f32[8,128]{1,0:T(8,128)S(1)}, f32[8,128]{1,0:T(8,128)S(1)}, u32[]{:S(2)}, u32[]{:S(2)}) collective-permute-start(f32[8,128]{1,0:T(8,128)S(1)} %get-tuple-element.77), channel_id=1, source_target_pairs={{0,4},{8,12},{16,20},{24,28},{4,0},{12,8},{20,16},{28,24},{1,5},{9... | collective-permute-start | bytes 12296 | tf_op jit(solution)/shard_map/ppermute | solution.py:630
  30.8 0.8 %turn_nodes.1.refs_9_ = bf16[4096,512]{1,0:T(8,128)(2,1)S(1)} custom-call(s32[32,128]{1,0:T(8,128)S(1)} %get-tuple-element.79.conn_ref.refs_9_), custom_call_target="tpu_custom_call" | custom-call | tf_op jit(solution)/shard_map/turn_nodes/pallas_call | solution.py:614
  31.6 2.0 %turn_blocks.1.refs_8_ = bf16[64,192,192]{2,1,0:T(8,128)(2,1)S(1)} custom-call(bf16[64,192,192]{2,1,0:T(8,128)(2,1)S(1)} %get-tuple-element.78.refs_5_.refs_12_.blocks), custom_call_target="tpu_custom_call" | custom-call | tf_op jit(solution)/shard_map/turn_blocks/pallas_call | solution.py:614
  33.6 0.0 collective-permute-done.4.refs_4_
  33.6 0.0 collective-permute-done.5.refs_5_
  33.7 2.4 %forward.4 = (bf16[512,384]{1,0:T(8,128)(2,1)S(1)}, f32[24,512]{1,0:T(8,128)S(1)}, f32[24,512]{1,0:T(8,128)S(1)}, bf16[48,256]{1,0:T(8,128)(2,1)S(1)}, bf16[48,2...) custom-call(f32[16,256]{1,0:T(8,128)S(1)} %get-tuple-element.56.refs_0_, ...), custom_call_target="tpu_custom_call" | custom-call | tf_op jit(solution)/shard_map/forward/pallas_call | solution.py:614
  36.1 0.7 collective-permute-start.6
  36.7 3.4 %collective-permute-start.7 = (bf16[48,256]{1,0:T(8,128)(2,1)S(1)}, bf16[48,256]{1,0:T(8,128)(2,1)S(1)}, u32[]{:S(2)}, u32[]{:S(2)}) collective-permute-start(bf16[48,256]{1,0:T(8,128)(2,1)S(1)} %get-tuple-element.83), channel_id=1, source_target_pairs={{0,4},{8,12},{16,20},{24,28},{4,0},{12,8},{20,16},{28,24},{1,5},{9... | collective-permute-start | bytes 73736 | tf_op jit(solution)/shard_map/ppermute | solution.py:630
  40.1 2.6 %inner.4.refs_7_ = f32[256,384]{1,0:T(8,128)S(1)} custom-call(bf16[512,384]{1,0:T(8,128)(2,1)S(1)} %get-tuple-element.84.ordered_ref, f32[3,4096]{1,0:T(4,128)S(1)} %bitcast.10, s32[32,128]{1,0:T(8,128)S(1)} %get-tuple-element.79.conn_ref.refs_9_, bf16[512,4096]{1,0:T(8,128)(2,1)S(1)} %get-tuple-element.61.refs_6_.node_hot, ...), custom_call_target="tpu_custom_call" | custom-call | tf_op jit(solution)/shard_map/inner/pallas_call | solution.py:614
  42.7 0.0 collective-permute-done.6.refs_5_
  42.7 0.0 collective-permute-done.7.refs_6_
  42.7 2.4 %adjoint.4 = (f32[8,384]{1,0:T(8,128)S(1)}, f32[8,128]{1,0:T(8,128)S(1)}, f32[8,128]{1,0:T(8,128)S(1)}) custom-call(f32[16,256]{1,0:T(8,128)S(1)} %get-tuple-element.56.refs_0_, f32[16,256]{1,0:T(8,128)S(1)} %collective-permute-done.refs_1_, f32[16,256]{1,0:T(8,128)S(1)} %collective-permute-done.1.refs_2_, f32[24,512]{1,0:T(8,128)S(1)} %get-tuple-element.80.refs_3_, ...), custom_call_target="tpu_custom_call" | custom-call | tf_op jit(solution)/shard_map/adjoint/pallas_call | solution.py:614
  45.1 0.7 collective-permute-start.8
  45.8 4.2 %collective-permute-start.9 = (f32[8,128]{1,0:T(8,128)S(1)}, f32[8,128]{1,0:T(8,128)S(1)}, u32[]{:S(2)}, u32[]{:S(2)}) collective-permute-start(f32[8,128]{1,0:T(8,128)S(1)} %get-tuple-element.92), channel_id=1, source_target_pairs={{0,4},{8,12},{16,20},{24,28},{4,0},{12,8},{20,16},{28,24},{1,5},{9... | collective-permute-start | bytes 12296 | tf_op jit(solution)/shard_map/ppermute | solution.py:630
  50.0 0.8 %turn_cells.1 = (bf16[4096,128]{1,0:T(8,128)(2,1)S(1)}, bf16[512,128]{1,0:T(8,128)(2,1)S(1)}, bf16[384,512]{1,0:T(8,128)(2,1)S(1)}) custom-call(s32[32,128]{1,0:T(8,128)S(1)} %get-tuple-element.88.refs_3_.refs_10_.refs_6_.cell_ref), custom_call_target="tpu_custom_call" | custom-call | tf_op jit(solution)/shard_map/turn_cells/pallas_call | solution.py:614
  50.8 0.0 collective-permute-done.8.refs_4_
  50.8 0.8 %collective-permute-done.9.refs_5_ = f32[8,128]{1,0:T(8,128)S(1)} collective-permute-done((f32[8,128]{1,0:T(8,128)S(1)}, f32[8,128]{1,0:T(8,128)S(1)}, u32[]{:S(2)}, u32[]{:S(2)}) %collective-permute-start.9) | collective-permute-done | bytes 4128 | tf_op jit(solution)/shard_map/ppermute | solution.py:630
  51.6 2.4 %forward.5 = (bf16[512,384]{1,0:T(8,128)(2,1)S(1)}, f32[24,512]{1,0:T(8,128)S(1)}, f32[24,512]{1,0:T(8,128)S(1)}, bf16[48,256]{1,0:T(8,128)(2,1)S(1)}, bf16[48,2...) custom-call(f32[16,256]{1,0:T(8,128)S(1)} %get-tuple-element.56.refs_0_, f32[16,256]{1,0:T(8,128)S(1)} %collective-permute-done.refs_1_, ...), custom_call_target="tpu_custom_call" | custom-call | tf_op jit(solution)/shard_map/forward/pallas_call | solution.py:614
  54.0 0.0 copy-start.1
  54.0 0.9 %collective-permute-start.10 = (bf16[48,256]{1,0:T(8,128)(2,1)S(1)}, bf16[48,256]{1,0:T(8,128)(2,1)S(1)}, u32[]{:S(2)}, u32[]{:S(2)}) collective-permute-start(bf16[48,256]{1,0:T(8,128)(2,1)S(1)} %get-tuple-element.95), channel_id=1, source_target_pairs={{4,8},{12,16},{20,24},{8,4},{16,12},{24,20},{5,9},{13,17},{21,25},... | collective-permute-start | bytes 73736 | tf_op jit(solution)/shard_map/ppermute | solution.py:630
  54.9 4.6 %collective-permute-start.11 = (bf16[48,256]{1,0:T(8,128)(2,1)S(1)}, bf16[48,256]{1,0:T(8,128)(2,1)S(1)}, u32[]{:S(2)}, u32[]{:S(2)}) collective-permute-start(bf16[48,256]{1,0:T(8,128)(2,1)S(1)} %get-tuple-element.96), channel_id=1, source_target_pairs={{0,4},{8,12},{16,20},{24,28},{4,0},{12,8},{20,16},{28,24},{1,5},{9... | collective-permute-start | bytes 73736 | tf_op jit(solution)/shard_map/ppermute | solution.py:630
  59.5 2.6 %inner.5.refs_7_ = f32[256,384]{1,0:T(8,128)S(1)} custom-call(bf16[512,384]{1,0:T(8,128)(2,1)S(1)} %get-tuple-element.97.ordered_ref, f32[3,4096]{1,0:T(4,128)S(1)} %bitcast.12, s32[32,128]{1,0:T(8,128)S(1)} %get-tuple-element.79.conn_ref.refs_9_, bf16[512,4096]{1,0:T(8,128)(2,1)S(1)} %get-tuple-element.61.refs_6_.node_hot, ...), custom_call_target="tpu_custom_call" | custom-call | tf_op jit(solution)/shard_map/inner/pallas_call | solution.py:614
  62.0 0.0 collective-permute-done.10.refs_5_
  62.0 0.0 collective-permute-done.11.refs_6_
  62.1 0.0 copy-done.1
  62.1 2.2 %adjoint.5 = (f32[8,384]{1,0:T(8,128)S(1)}, bf16[32,8,256]{2,1,0:T(8,128)(2,1)S(1)}) custom-call(f32[16,256]{1,0:T(8,128)S(1)} %get-tuple-element.56.refs_0_, f32[16,256]{1,0:T(8,128)S(1)} %collective-permute-done.refs_1_, f32[16,256]{1,0:T(8,128)S(1)} %collective-permute-done.1.refs_2_, f32[24,512]{1,0:T(8,128)S(1)} %get-tuple-element.93.refs_3_, ...), custom_call_target="tpu_custom_call" | custom-call | tf_op jit(solution)/shard_map/adjoint/pallas_call | solution.py:614
  64.2 12.3 %all_to_all.5 = bf16[32,8,256]{2,1,0:T(8,128)(2,1)S(1)} all-to-all(bf16[32,8,256]{2,1,0:T(8,128)(2,1)S(1)} %get-tuple-element.103), channel_id=1, replica_groups=mesh['tiles'=8,'probes'=4] {'tiles','probes'}, dimensions={0} | all-to-all | bytes 262144 | tf_op jit(solution)/shard_map/all_to_all | solution.py:752
  76.6 1.5 %gram.1 = (f32[8,256]{1,0:T(8,128)}, f32[8,256]{1,0:T(8,128)}, f32[8,8,32]{2,1,0:T(8,128)}) custom-call(bf16[8,4,8,256]{3,2,1,0:T(8,128)(2,1)S(1)} %bitcast.14, f32[8,384]{1,0:T(8,128)S(1)} %get-tuple-element.104.own_ref, f32[8,256]{1,0:T(8,128)S(1)} %get-tuple-element.105.samples_in), custom_call_target="tpu_custom_call" | custom-call | tf_op jit(solution)/shard_map/gram/pallas_call | solution.py:614
Async XLA Ops:
  1.4 10.4 %collective-permute-start = (f32[16,256]{1,0:T(8,128)S(1)}, f32[16,256]{1,0:T(8,128)S(1)}, u32[]{:S(2)}, u32[]{:S(2)}) collective-permute-start(f32[16,256]{1,0:T(8,128)S(1)} %get-tuple-element.57), channel_id=1, source_target_pairs={{4,8},{12,16},{20,24},{8,4},{16,12},{24,20},{5,9},{13,17},{21,25},... | collective-permute-start | bytes 49160 | tf_op jit(solution)/shard_map/ppermute | solution.py:630
  2.1 9.8 %collective-permute-start.1 = (f32[16,256]{1,0:T(8,128)S(1)}, f32[16,256]{1,0:T(8,128)S(1)}, u32[]{:S(2)}, u32[]{:S(2)}) collective-permute-start(f32[16,256]{1,0:T(8,128)S(1)} %get-tuple-element.56.refs_0_), channel_id=1, source_target_pairs={{0,4},{8,12},{16,20},{24,28},{4,0},{12,8},{20,16},{28,24},{1,5},{9... | collective-permute-start | bytes 49160 | tf_op jit(solution)/shard_map/ppermute | solution.py:630
  11.9 8.8 %copy-start = (f32[4096,3]{0,1:T(4,128)S(1)}, f32[4096,3]{0,1:T(4,128)}, u32[]{:S(2)}) copy-start(f32[4096,3]{0,1:T(4,128)} %param.13) | copy-start | bytes 147460
  15.6 7.6 %collective-permute-start.2 = (bf16[48,256]{1,0:T(8,128)(2,1)S(1)}, bf16[48,256]{1,0:T(8,128)(2,1)S(1)}, u32[]{:S(2)}, u32[]{:S(2)}) collective-permute-start(bf16[48,256]{1,0:T(8,128)(2,1)S(1)} %get-tuple-element.68), channel_id=1, source_target_pairs={{4,8},{12,16},{20,24},{8,4},{16,12},{24,20},{5,9},{13,17},{21,25},... | collective-permute-start | bytes 73736 | tf_op jit(solution)/shard_map/ppermute | solution.py:630
  16.3 6.9 %collective-permute-start.3 = (bf16[48,256]{1,0:T(8,128)(2,1)S(1)}, bf16[48,256]{1,0:T(8,128)(2,1)S(1)}, u32[]{:S(2)}, u32[]{:S(2)}) collective-permute-start(bf16[48,256]{1,0:T(8,128)(2,1)S(1)} %get-tuple-element.69), channel_id=1, source_target_pairs={{0,4},{8,12},{16,20},{24,28},{4,0},{12,8},{20,16},{28,24},{1,5},{9... | collective-permute-start | bytes 73736 | tf_op jit(solution)/shard_map/ppermute | solution.py:630
  25.6 8.0 %collective-permute-start.4 = (f32[8,128]{1,0:T(8,128)S(1)}, f32[8,128]{1,0:T(8,128)S(1)}, u32[]{:S(2)}, u32[]{:S(2)}) collective-permute-start(f32[8,128]{1,0:T(8,128)S(1)} %get-tuple-element.76), channel_id=1, source_target_pairs={{4,8},{12,16},{20,24},{8,4},{16,12},{24,20},{5,9},{13,17},{21,25},... | collective-permute-start | bytes 12296 | tf_op jit(solution)/shard_map/ppermute | solution.py:630
  26.5 7.2 %collective-permute-start.5 = (f32[8,128]{1,0:T(8,128)S(1)}, f32[8,128]{1,0:T(8,128)S(1)}, u32[]{:S(2)}, u32[]{:S(2)}) collective-permute-start(f32[8,128]{1,0:T(8,128)S(1)} %get-tuple-element.77), channel_id=1, source_target_pairs={{0,4},{8,12},{16,20},{24,28},{4,0},{12,8},{20,16},{28,24},{1,5},{9... | collective-permute-start | bytes 12296 | tf_op jit(solution)/shard_map/ppermute | solution.py:630
  36.1 6.6 %collective-permute-start.6 = (bf16[48,256]{1,0:T(8,128)(2,1)S(1)}, bf16[48,256]{1,0:T(8,128)(2,1)S(1)}, u32[]{:S(2)}, u32[]{:S(2)}) collective-permute-start(bf16[48,256]{1,0:T(8,128)(2,1)S(1)} %get-tuple-element.82), channel_id=1, source_target_pairs={{4,8},{12,16},{20,24},{8,4},{16,12},{24,20},{5,9},{13,17},{21,25},... | collective-permute-start | bytes 73736 | tf_op jit(solution)/shard_map/ppermute | solution.py:630
  36.7 5.9 %collective-permute-start.7 = (bf16[48,256]{1,0:T(8,128)(2,1)S(1)}, bf16[48,256]{1,0:T(8,128)(2,1)S(1)}, u32[]{:S(2)}, u32[]{:S(2)}) collective-permute-start(bf16[48,256]{1,0:T(8,128)(2,1)S(1)} %get-tuple-element.83), channel_id=1, source_target_pairs={{0,4},{8,12},{16,20},{24,28},{4,0},{12,8},{20,16},{28,24},{1,5},{9... | collective-permute-start | bytes 73736 | tf_op jit(solution)/shard_map/ppermute | solution.py:630
  45.1 5.7 %collective-permute-start.8 = (f32[8,128]{1,0:T(8,128)S(1)}, f32[8,128]{1,0:T(8,128)S(1)}, u32[]{:S(2)}, u32[]{:S(2)}) collective-permute-start(f32[8,128]{1,0:T(8,128)S(1)} %get-tuple-element.91), channel_id=1, source_target_pairs={{4,8},{12,16},{20,24},{8,4},{16,12},{24,20},{5,9},{13,17},{21,25},... | collective-permute-start | bytes 12296 | tf_op jit(solution)/shard_map/ppermute | solution.py:630
  45.8 5.8 %collective-permute-start.9 = (f32[8,128]{1,0:T(8,128)S(1)}, f32[8,128]{1,0:T(8,128)S(1)}, u32[]{:S(2)}, u32[]{:S(2)}) collective-permute-start(f32[8,128]{1,0:T(8,128)S(1)} %get-tuple-element.92), channel_id=1, source_target_pairs={{0,4},{8,12},{16,20},{24,28},{4,0},{12,8},{20,16},{28,24},{1,5},{9... | collective-permute-start | bytes 12296 | tf_op jit(solution)/shard_map/ppermute | solution.py:630
  54.0 8.1 %copy-start.1 = (s32[256]{0:T(256)S(1)}, s32[256]{0:T(256)}, u32[]{:S(2)}) copy-start(s32[256]{0:T(256)} %param.15) | copy-start | bytes 3076
  54.0 8.0 %collective-permute-start.10 = (bf16[48,256]{1,0:T(8,128)(2,1)S(1)}, bf16[48,256]{1,0:T(8,128)(2,1)S(1)}, u32[]{:S(2)}, u32[]{:S(2)}) collective-permute-start(bf16[48,256]{1,0:T(8,128)(2,1)S(1)} %get-tuple-element.95), channel_id=1, source_target_pairs={{4,8},{12,16},{20,24},{8,4},{16,12},{24,20},{5,9},{13,17},{21,25},... | collective-permute-start | bytes 73736 | tf_op jit(solution)/shard_map/ppermute | solution.py:630
  54.9 7.2 %collective-permute-start.11 = (bf16[48,256]{1,0:T(8,128)(2,1)S(1)}, bf16[48,256]{1,0:T(8,128)(2,1)S(1)}, u32[]{:S(2)}, u32[]{:S(2)}) collective-permute-start(bf16[48,256]{1,0:T(8,128)(2,1)S(1)} %get-tuple-element.96), channel_id=1, source_target_pairs={{0,4},{8,12},{16,20},{24,28},{4,0},{12,8},{20,16},{28,24},{1,5},{9... | collective-permute-start | bytes 73736 | tf_op jit(solution)/shard_map/ppermute | solution.py:630

commit v16 on v15

--- a/solution.py
+++ b/solution.py
@@ -201,6 +201,7 @@
     rows = rows_iota((EDGE_RADIX, LANES)).astype(F32).astype(BF16)
     halves = halves_of(conn)
     which = (conn // RADIX).astype(F32)
+    ends = jnp.where(rows_iota((16, LANES)) < 8, F32(0), F32(levels - 1)).astype(BF16)
     cell_low = (cells % LANES).astype(F32)
     for m in range(pairs):
         at = pl.ds(m * LANES, LANES)
@@ -215,6 +216,7 @@
         for level in range(levels):
             mine = hot16(row, jnp.full((16, LANES), level, BF16))
             level_hot_ref[16 * level : 16 * level + 16, at] = mine
+        level_hot_ref[16 * levels : 16 * levels + 16, at] = hot16(row, ends)
         row = jnp.broadcast_to(cell_low[m : m + 1, :], (LANES, LANES)).astype(BF16)
         cell_hot_ref[:, at] = hot16(rows[:LANES], row)
     loads[3].wait()
@@ -347,12 +349,18 @@
                 out = out[:8] + out[8:]
             f_ref[16 * m : 16 * m + 16, at : at + order] = both_parts(out)
 
-    ordered = dot(f_ref[...], order_ref[...]).astype(BF16)
-    ordered_ref[...] = ordered
-    spread_levels(v_ref, ordered, level_hot, (0, levels - 1), pairs)
+    ordered = dot(f_ref[...], order_ref[...])
+    ordered_ref[...] = ordered.astype(BF16)
+    for m in range(pairs):
+        at = pl.ds(m * LANES, LANES)
+        mask = level_hot[16 * levels : 16 * levels + 16, at]
+        for c in range(3):
+            value = ordered[16 * m : 16 * m + 8, c * LANES : (c + 1) * LANES]
+            value = jnp.concatenate([value, value], axis=0).astype(BF16)
+            v_ref[16 * c : 16 * c + 16, at] = value * mask
     rim = product(step > 0)(v_ref[...], node_map[...])
-    sums = [rim[16 * i : 16 * i + 8] + rim[16 * i + 8 : 16 * i + 16] for i in range(6)]
-    lead, spill = (jnp.concatenate(part, axis=0) for part in (sums[:3], sums[3:]))
+    lead = jnp.concatenate([rim[16 * c : 16 * c + 8] for c in range(3)], axis=0)
+    spill = jnp.concatenate([rim[16 * c + 8 : 16 * c + 16] for c in range(3)], axis=0)
     for ref, message, value in zip((a_ref, b_ref), (far_ref, near_ref), to_swaps(tile, spill, lead)):
         ref[...] = value
         pieces = [value[:, i * EDGE_RADIX : (i + 1) * EDGE_RADIX] for i in range(EDGE)]
@@ -655,7 +663,7 @@
             shaped(blocks.shape, BF16),
             shaped((RADIX, refs), BF16),
             shaped((EDGE_RADIX, refs), BF16),
-            shaped((16 * levels, refs), BF16),
+            shaped((16 * (levels + 1), refs), BF16),
             shaped((LANES, refs), BF16),
             shaped((LANES, 2 * padded_order), BF16),
             shaped((2 * padded_order, 3 * LANES), BF16),
@@ -694,7 +702,7 @@
             + [cells, fr, factors, node_map, level_hot, cell_hot, spread, order],
             [
                 pltpu.VMEM((16 * pairs, 2 * padded_order), BF16),
-                pltpu.VMEM((96, refs), BF16),
+                pltpu.VMEM((48, refs), BF16),
             ],
         )
         squares += extra[:1]

time: 78.4 us -> 78.3 us (level)
  no operation moved by 1% of the time
where the time goes in v16:
time: 78.3 us; the launch traced here: 77.9 us
  Pallas kernels  32.1 us (41%)
  starting transfers between devices  31.1 us (40%)
  blocking collectives  12.3 us (16%)
  between operations  1.52 us (2%)
  waiting for transfers between devices  0.82 us (1%)
    pallas_call x15, Pallas kernels, call(): pl.pallas_call(kernel, out_shape=out_shape, in_specs=in_specs, out_specs=...  32.1 us
    ppermute x6, starting transfers between devices, swapped(): lax.ppermute(b, 'tiles', pairs_b)  26.7 us
    all_to_all x1, blocking collectives, shards(): gathered = lax.all_to_all(messages[0], everyone, 0, 0)  12.3 us
    ppermute x6, starting transfers between devices, swapped(): lax.ppermute(a, 'tiles', pairs_a)  4.43 us
  transfers between devices with their start and end apart: 12, of which 1 were waited for; matrix products, arithmetic and copies ran while one was open for 0% of the time, Pallas kernels for 19%

profile of v16, /device:TPU:0, one launch (start us, length us, event | category | flops | bytes accessed | tf_op | source)
XLA Modules:
  0.0 77.9 jit_solution(2046004003749399847)
XLA Ops:
  0.6 0.8 announce.1
  1.4 0.7 collective-permute-start
  2.1 5.8 %collective-permute-start.1 = (f32[16,256]{1,0:T(8,128)S(1)}, f32[16,256]{1,0:T(8,128)S(1)}, u32[]{:S(2)}, u32[]{:S(2)}) collective-permute-start(f32[16,256]{1,0:T(8,128)S(1)} %get-tuple-element.56.refs_0_), channel_id=1, source_target_pairs={{0,4},{8,12},{16,20},{24,28},{4,0},{12,8},{20,16},{28,24},{1,5},{9... | collective-permute-start | bytes 49160 | tf_op jit(solution)/shard_map/ppermute | solution.py:638
  8.5 3.4 %setup.1 = (s32[32,128]{1,0:T(8,128)S(1)}, s32[32,128]{1,0:T(8,128)S(1)}, f32[64,256]{1,0:T(8,128)S(1)}, bf16[64,192,192]{2,1,0:T(8,128)(2,1)S(1)}, bf16[512,409...) custom-call(s32[1]{0:T(128)S(6)} %copy.11.counts, ...), custom_call_target="tpu_custom_call" | custom-call | tf_op jit(solution)/shard_map/setup/pallas_call | solution.py:622
  11.9 0.0 collective-permute-done.refs_1_
  11.9 0.0 collective-permute-done.1.refs_2_
  11.9 0.0 copy-start
  11.9 3.6 %forward.3 = (bf16[512,384]{1,0:T(8,128)(2,1)S(1)}, f32[24,512]{1,0:T(8,128)S(1)}, f32[24,512]{1,0:T(8,128)S(1)}, bf16[48,256]{1,0:T(8,128)(2,1)S(1)}, bf16[48,256]{1,0:T(8,128)(2,1)S(1)}) custom-call(f32[16,256]{1,0:T(8,128)S(1)} %get-tuple-element.56.refs_0_, f32[16,256]{1,0:T(8,128)S(1)} %collective-permute-done.refs_1_, ...), custom_call_target="tpu_custom_call" | custom-call | tf_op jit(solution)/shard_map/forward/pallas_call | solution.py:622
  15.6 0.7 collective-permute-start.2
  16.2 4.4 %collective-permute-start.3 = (bf16[48,256]{1,0:T(8,128)(2,1)S(1)}, bf16[48,256]{1,0:T(8,128)(2,1)S(1)}, u32[]{:S(2)}, u32[]{:S(2)}) collective-permute-start(bf16[48,256]{1,0:T(8,128)(2,1)S(1)} %get-tuple-element.69), channel_id=1, source_target_pairs={{0,4},{8,12},{16,20},{24,28},{4,0},{12,8},{20,16},{28,24},{1,5},{9... | collective-permute-start | bytes 73736 | tf_op jit(solution)/shard_map/ppermute | solution.py:638
  20.6 0.0 copy-done
  20.6 2.5 %inner.3.refs_7_ = f32[256,384]{1,0:T(8,128)S(1)} custom-call(bf16[512,384]{1,0:T(8,128)(2,1)S(1)} %get-tuple-element.70.ordered_ref, f32[3,4096]{1,0:T(4,128)S(1)} %bitcast.8, s32[32,128]{1,0:T(8,128)S(1)} %get-tuple-element.79.conn_ref.refs_9_, bf16[512,4096]{1,0:T(8,128)(2,1)S(1)} %get-tuple-element.61.refs_6_.node_hot, ...), custom_call_target="tpu_custom_call" | custom-call | tf_op jit(solution)/shard_map/inner/pallas_call | solution.py:622
  23.1 0.0 collective-permute-done.2.refs_5_
  23.1 0.0 collective-permute-done.3.refs_6_
  23.1 2.4 %adjoint.3 = (f32[8,384]{1,0:T(8,128)S(1)}, f32[8,128]{1,0:T(8,128)S(1)}, f32[8,128]{1,0:T(8,128)S(1)}) custom-call(f32[16,256]{1,0:T(8,128)S(1)} %get-tuple-element.56.refs_0_, f32[16,256]{1,0:T(8,128)S(1)} %collective-permute-done.refs_1_, f32[16,256]{1,0:T(8,128)S(1)} %collective-permute-done.1.refs_2_, f32[24,512]{1,0:T(8,128)S(1)} %get-tuple-element.66.refs_3_, ...), custom_call_target="tpu_custom_call" | custom-call | tf_op jit(solution)/shard_map/adjoint/pallas_call | solution.py:622
  25.5 0.9 %collective-permute-start.4 = (f32[8,128]{1,0:T(8,128)S(1)}, f32[8,128]{1,0:T(8,128)S(1)}, u32[]{:S(2)}, u32[]{:S(2)}) collective-permute-start(f32[8,128]{1,0:T(8,128)S(1)} %get-tuple-element.76), channel_id=1, source_target_pairs={{4,8},{12,16},{20,24},{8,4},{16,12},{24,20},{5,9},{13,17},{21,25},... | collective-permute-start | bytes 12296 | tf_op jit(solution)/shard_map/ppermute | solution.py:638
  26.4 4.3 %collective-permute-start.5 = (f32[8,128]{1,0:T(8,128)S(1)}, f32[8,128]{1,0:T(8,128)S(1)}, u32[]{:S(2)}, u32[]{:S(2)}) collective-permute-start(f32[8,128]{1,0:T(8,128)S(1)} %get-tuple-element.77), channel_id=1, source_target_pairs={{0,4},{8,12},{16,20},{24,28},{4,0},{12,8},{20,16},{28,24},{1,5},{9... | collective-permute-start | bytes 12296 | tf_op jit(solution)/shard_map/ppermute | solution.py:638
  30.8 0.8 %turn_nodes.1.refs_9_ = bf16[4096,512]{1,0:T(8,128)(2,1)S(1)} custom-call(s32[32,128]{1,0:T(8,128)S(1)} %get-tuple-element.79.conn_ref.refs_9_), custom_call_target="tpu_custom_call" | custom-call | tf_op jit(solution)/shard_map/turn_nodes/pallas_call | solution.py:622
  31.6 2.0 %turn_blocks.1.refs_8_ = bf16[64,192,192]{2,1,0:T(8,128)(2,1)S(1)} custom-call(bf16[64,192,192]{2,1,0:T(8,128)(2,1)S(1)} %get-tuple-element.78.refs_5_.refs_12_.blocks), custom_call_target="tpu_custom_call" | custom-call | tf_op jit(solution)/shard_map/turn_blocks/pallas_call | solution.py:622
  33.6 0.0 collective-permute-done.4.refs_4_
  33.6 0.0 collective-permute-done.5.refs_5_
  33.6 2.4 %forward.4 = (bf16[512,384]{1,0:T(8,128)(2,1)S(1)}, f32[24,512]{1,0:T(8,128)S(1)}, f32[24,512]{1,0:T(8,128)S(1)}, bf16[48,256]{1,0:T(8,128)(2,1)S(1)}, bf16[48,2...) custom-call(f32[16,256]{1,0:T(8,128)S(1)} %get-tuple-element.56.refs_0_, ...), custom_call_target="tpu_custom_call" | custom-call | tf_op jit(solution)/shard_map/forward/pallas_call | solution.py:622
  35.9 0.7 collective-permute-start.6
  36.6 3.4 %collective-permute-start.7 = (bf16[48,256]{1,0:T(8,128)(2,1)S(1)}, bf16[48,256]{1,0:T(8,128)(2,1)S(1)}, u32[]{:S(2)}, u32[]{:S(2)}) collective-permute-start(bf16[48,256]{1,0:T(8,128)(2,1)S(1)} %get-tuple-element.83), channel_id=1, source_target_pairs={{0,4},{8,12},{16,20},{24,28},{4,0},{12,8},{20,16},{28,24},{1,5},{9... | collective-permute-start | bytes 73736 | tf_op jit(solution)/shard_map/ppermute | solution.py:638
  40.0 2.6 %inner.4.refs_7_ = f32[256,384]{1,0:T(8,128)S(1)} custom-call(bf16[512,384]{1,0:T(8,128)(2,1)S(1)} %get-tuple-element.84.ordered_ref, f32[3,4096]{1,0:T(4,128)S(1)} %bitcast.10, s32[32,128]{1,0:T(8,128)S(1)} %get-tuple-element.79.conn_ref.refs_9_, bf16[512,4096]{1,0:T(8,128)(2,1)S(1)} %get-tuple-element.61.refs_6_.node_hot, ...), custom_call_target="tpu_custom_call" | custom-call | tf_op jit(solution)/shard_map/inner/pallas_call | solution.py:622
  42.5 0.0 collective-permute-done.6.refs_5_
  42.6 0.0 collective-permute-done.7.refs_6_
  42.6 2.4 %adjoint.4 = (f32[8,384]{1,0:T(8,128)S(1)}, f32[8,128]{1,0:T(8,128)S(1)}, f32[8,128]{1,0:T(8,128)S(1)}) custom-call(f32[16,256]{1,0:T(8,128)S(1)} %get-tuple-element.56.refs_0_, f32[16,256]{1,0:T(8,128)S(1)} %collective-permute-done.refs_1_, f32[16,256]{1,0:T(8,128)S(1)} %collective-permute-done.1.refs_2_, f32[24,512]{1,0:T(8,128)S(1)} %get-tuple-element.80.refs_3_, ...), custom_call_target="tpu_custom_call" | custom-call | tf_op jit(solution)/shard_map/adjoint/pallas_call | solution.py:622
  45.0 0.7 collective-permute-start.8
  45.7 4.2 %collective-permute-start.9 = (f32[8,128]{1,0:T(8,128)S(1)}, f32[8,128]{1,0:T(8,128)S(1)}, u32[]{:S(2)}, u32[]{:S(2)}) collective-permute-start(f32[8,128]{1,0:T(8,128)S(1)} %get-tuple-element.92), channel_id=1, source_target_pairs={{0,4},{8,12},{16,20},{24,28},{4,0},{12,8},{20,16},{28,24},{1,5},{9... | collective-permute-start | bytes 12296 | tf_op jit(solution)/shard_map/ppermute | solution.py:638
  49.9 0.8 %turn_cells.1 = (bf16[4096,128]{1,0:T(8,128)(2,1)S(1)}, bf16[512,128]{1,0:T(8,128)(2,1)S(1)}, bf16[384,512]{1,0:T(8,128)(2,1)S(1)}) custom-call(s32[32,128]{1,0:T(8,128)S(1)} %get-tuple-element.88.refs_3_.refs_10_.refs_6_.cell_ref), custom_call_target="tpu_custom_call" | custom-call | tf_op jit(solution)/shard_map/turn_cells/pallas_call | solution.py:622
  50.7 0.0 collective-permute-done.8.refs_4_
  50.7 0.8 %collective-permute-done.9.refs_5_ = f32[8,128]{1,0:T(8,128)S(1)} collective-permute-done((f32[8,128]{1,0:T(8,128)S(1)}, f32[8,128]{1,0:T(8,128)S(1)}, u32[]{:S(2)}, u32[]{:S(2)}) %collective-permute-start.9) | collective-permute-done | bytes 4128 | tf_op jit(solution)/shard_map/ppermute | solution.py:638
  51.5 2.4 %forward.5 = (bf16[512,384]{1,0:T(8,128)(2,1)S(1)}, f32[24,512]{1,0:T(8,128)S(1)}, f32[24,512]{1,0:T(8,128)S(1)}, bf16[48,256]{1,0:T(8,128)(2,1)S(1)}, bf16[48,2...) custom-call(f32[16,256]{1,0:T(8,128)S(1)} %get-tuple-element.56.refs_0_, f32[16,256]{1,0:T(8,128)S(1)} %collective-permute-done.refs_1_, ...), custom_call_target="tpu_custom_call" | custom-call | tf_op jit(solution)/shard_map/forward/pallas_call | solution.py:622
  53.8 0.0 copy-start.1
  53.8 0.9 %collective-permute-start.10 = (bf16[48,256]{1,0:T(8,128)(2,1)S(1)}, bf16[48,256]{1,0:T(8,128)(2,1)S(1)}, u32[]{:S(2)}, u32[]{:S(2)}) collective-permute-start(bf16[48,256]{1,0:T(8,128)(2,1)S(1)} %get-tuple-element.95), channel_id=1, source_target_pairs={{4,8},{12,16},{20,24},{8,4},{16,12},{24,20},{5,9},{13,17},{21,25},... | collective-permute-start | bytes 73736 | tf_op jit(solution)/shard_map/ppermute | solution.py:638
  54.7 4.6 %collective-permute-start.11 = (bf16[48,256]{1,0:T(8,128)(2,1)S(1)}, bf16[48,256]{1,0:T(8,128)(2,1)S(1)}, u32[]{:S(2)}, u32[]{:S(2)}) collective-permute-start(bf16[48,256]{1,0:T(8,128)(2,1)S(1)} %get-tuple-element.96), channel_id=1, source_target_pairs={{0,4},{8,12},{16,20},{24,28},{4,0},{12,8},{20,16},{28,24},{1,5},{9... | collective-permute-start | bytes 73736 | tf_op jit(solution)/shard_map/ppermute | solution.py:638
  59.3 2.6 %inner.5.refs_7_ = f32[256,384]{1,0:T(8,128)S(1)} custom-call(bf16[512,384]{1,0:T(8,128)(2,1)S(1)} %get-tuple-element.97.ordered_ref, f32[3,4096]{1,0:T(4,128)S(1)} %bitcast.12, s32[32,128]{1,0:T(8,128)S(1)} %get-tuple-element.79.conn_ref.refs_9_, bf16[512,4096]{1,0:T(8,128)(2,1)S(1)} %get-tuple-element.61.refs_6_.node_hot, ...), custom_call_target="tpu_custom_call" | custom-call | tf_op jit(solution)/shard_map/inner/pallas_call | solution.py:622
  61.9 0.0 collective-permute-done.10.refs_5_
  61.9 0.0 collective-permute-done.11.refs_6_
  61.9 0.0 copy-done.1
  61.9 2.2 %adjoint.5 = (f32[8,384]{1,0:T(8,128)S(1)}, bf16[32,8,256]{2,1,0:T(8,128)(2,1)S(1)}) custom-call(f32[16,256]{1,0:T(8,128)S(1)} %get-tuple-element.56.refs_0_, f32[16,256]{1,0:T(8,128)S(1)} %collective-permute-done.refs_1_, f32[16,256]{1,0:T(8,128)S(1)} %collective-permute-done.1.refs_2_, f32[24,512]{1,0:T(8,128)S(1)} %get-tuple-element.93.refs_3_, ...), custom_call_target="tpu_custom_call" | custom-call | tf_op jit(solution)/shard_map/adjoint/pallas_call | solution.py:622
  64.1 12.3 %all_to_all.5 = bf16[32,8,256]{2,1,0:T(8,128)(2,1)S(1)} all-to-all(bf16[32,8,256]{2,1,0:T(8,128)(2,1)S(1)} %get-tuple-element.103), channel_id=1, replica_groups=mesh['tiles'=8,'probes'=4] {'tiles','probes'}, dimensions={0} | all-to-all | bytes 262144 | tf_op jit(solution)/shard_map/all_to_all | solution.py:760
  76.4 1.5 %gram.1 = (f32[8,256]{1,0:T(8,128)}, f32[8,256]{1,0:T(8,128)}, f32[8,8,32]{2,1,0:T(8,128)}) custom-call(bf16[8,4,8,256]{3,2,1,0:T(8,128)(2,1)S(1)} %bitcast.14, f32[8,384]{1,0:T(8,128)S(1)} %get-tuple-element.104.own_ref, f32[8,256]{1,0:T(8,128)S(1)} %get-tuple-element.105.samples_in), custom_call_target="tpu_custom_call" | custom-call | tf_op jit(solution)/shard_map/gram/pallas_call | solution.py:622
Async XLA Ops:
  1.4 10.5 %collective-permute-start = (f32[16,256]{1,0:T(8,128)S(1)}, f32[16,256]{1,0:T(8,128)S(1)}, u32[]{:S(2)}, u32[]{:S(2)}) collective-permute-start(f32[16,256]{1,0:T(8,128)S(1)} %get-tuple-element.57), channel_id=1, source_target_pairs={{4,8},{12,16},{20,24},{8,4},{16,12},{24,20},{5,9},{13,17},{21,25},... | collective-permute-start | bytes 49160 | tf_op jit(solution)/shard_map/ppermute | solution.py:638
  2.1 9.8 %collective-permute-start.1 = (f32[16,256]{1,0:T(8,128)S(1)}, f32[16,256]{1,0:T(8,128)S(1)}, u32[]{:S(2)}, u32[]{:S(2)}) collective-permute-start(f32[16,256]{1,0:T(8,128)S(1)} %get-tuple-element.56.refs_0_), channel_id=1, source_target_pairs={{0,4},{8,12},{16,20},{24,28},{4,0},{12,8},{20,16},{28,24},{1,5},{9... | collective-permute-start | bytes 49160 | tf_op jit(solution)/shard_map/ppermute | solution.py:638
  11.9 8.7 %copy-start = (f32[4096,3]{0,1:T(4,128)S(1)}, f32[4096,3]{0,1:T(4,128)}, u32[]{:S(2)}) copy-start(f32[4096,3]{0,1:T(4,128)} %param.13) | copy-start | bytes 147460
  15.6 7.6 %collective-permute-start.2 = (bf16[48,256]{1,0:T(8,128)(2,1)S(1)}, bf16[48,256]{1,0:T(8,128)(2,1)S(1)}, u32[]{:S(2)}, u32[]{:S(2)}) collective-permute-start(bf16[48,256]{1,0:T(8,128)(2,1)S(1)} %get-tuple-element.68), channel_id=1, source_target_pairs={{4,8},{12,16},{20,24},{8,4},{16,12},{24,20},{5,9},{13,17},{21,25},... | collective-permute-start | bytes 73736 | tf_op jit(solution)/shard_map/ppermute | solution.py:638
  16.2 6.9 %collective-permute-start.3 = (bf16[48,256]{1,0:T(8,128)(2,1)S(1)}, bf16[48,256]{1,0:T(8,128)(2,1)S(1)}, u32[]{:S(2)}, u32[]{:S(2)}) collective-permute-start(bf16[48,256]{1,0:T(8,128)(2,1)S(1)} %get-tuple-element.69), channel_id=1, source_target_pairs={{0,4},{8,12},{16,20},{24,28},{4,0},{12,8},{20,16},{28,24},{1,5},{9... | collective-permute-start | bytes 73736 | tf_op jit(solution)/shard_map/ppermute | solution.py:638
  25.5 8.0 %collective-permute-start.4 = (f32[8,128]{1,0:T(8,128)S(1)}, f32[8,128]{1,0:T(8,128)S(1)}, u32[]{:S(2)}, u32[]{:S(2)}) collective-permute-start(f32[8,128]{1,0:T(8,128)S(1)} %get-tuple-element.76), channel_id=1, source_target_pairs={{4,8},{12,16},{20,24},{8,4},{16,12},{24,20},{5,9},{13,17},{21,25},... | collective-permute-start | bytes 12296 | tf_op jit(solution)/shard_map/ppermute | solution.py:638
  26.4 7.1 %collective-permute-start.5 = (f32[8,128]{1,0:T(8,128)S(1)}, f32[8,128]{1,0:T(8,128)S(1)}, u32[]{:S(2)}, u32[]{:S(2)}) collective-permute-start(f32[8,128]{1,0:T(8,128)S(1)} %get-tuple-element.77), channel_id=1, source_target_pairs={{0,4},{8,12},{16,20},{24,28},{4,0},{12,8},{20,16},{28,24},{1,5},{9... | collective-permute-start | bytes 12296 | tf_op jit(solution)/shard_map/ppermute | solution.py:638
  35.9 6.6 %collective-permute-start.6 = (bf16[48,256]{1,0:T(8,128)(2,1)S(1)}, bf16[48,256]{1,0:T(8,128)(2,1)S(1)}, u32[]{:S(2)}, u32[]{:S(2)}) collective-permute-start(bf16[48,256]{1,0:T(8,128)(2,1)S(1)} %get-tuple-element.82), channel_id=1, source_target_pairs={{4,8},{12,16},{20,24},{8,4},{16,12},{24,20},{5,9},{13,17},{21,25},... | collective-permute-start | bytes 73736 | tf_op jit(solution)/shard_map/ppermute | solution.py:638
  36.6 5.9 %collective-permute-start.7 = (bf16[48,256]{1,0:T(8,128)(2,1)S(1)}, bf16[48,256]{1,0:T(8,128)(2,1)S(1)}, u32[]{:S(2)}, u32[]{:S(2)}) collective-permute-start(bf16[48,256]{1,0:T(8,128)(2,1)S(1)} %get-tuple-element.83), channel_id=1, source_target_pairs={{0,4},{8,12},{16,20},{24,28},{4,0},{12,8},{20,16},{28,24},{1,5},{9... | collective-permute-start | bytes 73736 | tf_op jit(solution)/shard_map/ppermute | solution.py:638
  45.0 5.7 %collective-permute-start.8 = (f32[8,128]{1,0:T(8,128)S(1)}, f32[8,128]{1,0:T(8,128)S(1)}, u32[]{:S(2)}, u32[]{:S(2)}) collective-permute-start(f32[8,128]{1,0:T(8,128)S(1)} %get-tuple-element.91), channel_id=1, source_target_pairs={{4,8},{12,16},{20,24},{8,4},{16,12},{24,20},{5,9},{13,17},{21,25},... | collective-permute-start | bytes 12296 | tf_op jit(solution)/shard_map/ppermute | solution.py:638
  45.7 5.8 %collective-permute-start.9 = (f32[8,128]{1,0:T(8,128)S(1)}, f32[8,128]{1,0:T(8,128)S(1)}, u32[]{:S(2)}, u32[]{:S(2)}) collective-permute-start(f32[8,128]{1,0:T(8,128)S(1)} %get-tuple-element.92), channel_id=1, source_target_pairs={{0,4},{8,12},{16,20},{24,28},{4,0},{12,8},{20,16},{28,24},{1,5},{9... | collective-permute-start | bytes 12296 | tf_op jit(solution)/shard_map/ppermute | solution.py:638
  53.8 8.1 %copy-start.1 = (s32[256]{0:T(256)S(1)}, s32[256]{0:T(256)}, u32[]{:S(2)}) copy-start(s32[256]{0:T(256)} %param.15) | copy-start | bytes 3076
  53.8 8.1 %collective-permute-start.10 = (bf16[48,256]{1,0:T(8,128)(2,1)S(1)}, bf16[48,256]{1,0:T(8,128)(2,1)S(1)}, u32[]{:S(2)}, u32[]{:S(2)}) collective-permute-start(bf16[48,256]{1,0:T(8,128)(2,1)S(1)} %get-tuple-element.95), channel_id=1, source_target_pairs={{4,8},{12,16},{20,24},{8,4},{16,12},{24,20},{5,9},{13,17},{21,25},... | collective-permute-start | bytes 73736 | tf_op jit(solution)/shard_map/ppermute | solution.py:638
  54.7 7.2 %collective-permute-start.11 = (bf16[48,256]{1,0:T(8,128)(2,1)S(1)}, bf16[48,256]{1,0:T(8,128)(2,1)S(1)}, u32[]{:S(2)}, u32[]{:S(2)}) collective-permute-start(bf16[48,256]{1,0:T(8,128)(2,1)S(1)} %get-tuple-element.96), channel_id=1, source_target_pairs={{0,4},{8,12},{16,20},{24,28},{4,0},{12,8},{20,16},{28,24},{1,5},{9... | collective-permute-start | bytes 73736 | tf_op jit(solution)/shard_map/ppermute | solution.py:638

commit v17 on v16

--- a/solution.py
+++ b/solution.py
@@ -222,12 +222,13 @@
     loads[3].wait()
 
 
-def turn_nodes_kernel(conn_ref, node_turn_ref):
+def turn_nodes_kernel(first, conn_ref, node_turn_ref):
     columns = [half.T for half in halves_of(conn_ref[...])]
     lanes = lanes_iota((LANES, EDGE_RADIX)).astype(F32).astype(BF16)
-    for m in range(conn_ref.shape[0]):
+    for m in range(node_turn_ref.shape[0] // LANES):
         for i, column in enumerate(columns):
-            row = jnp.broadcast_to(column[:, m : m + 1], (LANES, LANES)).astype(BF16)
+            row = column[:, first + m : first + m + 1]
+            row = jnp.broadcast_to(row, (LANES, LANES)).astype(BF16)
             row = jnp.concatenate([row] * (EDGE_RADIX // LANES), axis=1)
             at = pl.ds(i * EDGE_RADIX, EDGE_RADIX)
             node_turn_ref[m * LANES : (m + 1) * LANES, at] = hot16(lanes, row)
@@ -276,7 +277,11 @@
     first = step == 0
     if not first:
         basal_ref, rim_a, rim_b, *refs = refs
-    cell_ref, fr_ref, factors, node_map, level_hot, cell_hot, spread_ref, order_ref, *refs = refs
+    cell_ref, fr_ref, factors, level_hot, cell_hot, spread_ref, order_ref, *refs = refs
+    if first:
+        node_hot, *refs = refs
+    else:
+        node_turn, node_turn_rest, *refs = refs
     ordered_ref, a_ref, b_ref, far_ref, near_ref, *refs = refs
     if not first:
         squares_ref, *refs = refs
@@ -358,7 +363,11 @@
             value = ordered[16 * m : 16 * m + 8, c * LANES : (c + 1) * LANES]
             value = jnp.concatenate([value, value], axis=0).astype(BF16)
             v_ref[16 * c : 16 * c + 16, at] = value * mask
-    rim = product(step > 0)(v_ref[...], node_map[...])
+    if first:
+        rim = dot_nt(v_ref[...], node_hot[...])
+    else:
+        half = node_turn.shape[0]
+        rim = dot(v_ref[:, :half], node_turn[...]) + dot(v_ref[:, half:], node_turn_rest[...])
     lead = jnp.concatenate([rim[16 * c : 16 * c + 8] for c in range(3)], axis=0)
     spill = jnp.concatenate([rim[16 * c + 8 : 16 * c + 16] for c in range(3)], axis=0)
     for ref, message, value in zip((a_ref, b_ref), (far_ref, near_ref), to_swaps(tile, spill, lead)):
@@ -677,7 +686,8 @@
         ],
         [smem] + [hbm] * 4,
     )
-    factors, node_map, cell_map, spread_map, order_map = loaded, node_hot, cell_hot, spread, order
+    factors, node_maps = loaded, [node_hot]
+    cell_map, spread_map, order_map = cell_hot, spread, order
 
     edge = shaped((24, HALO), F32)
     message = shaped((24 * EDGE, EDGE_RADIX), BF16)
@@ -686,8 +696,15 @@
     field = shaped((group_size, cell_count), F32)
     everyone = ("tiles", "probes")
 
+    def turned_nodes(first_pair, ids):
+        return call(
+            functools.partial(turn_nodes_kernel, first_pair),
+            "turn_nodes",
+            shaped((refs // 2, RADIX), BF16),
+            [ids],
+        )
+
     carried = []
-    factors = loaded
     squares = []
     samples = None
     for step in range(POWER + 1):
@@ -699,7 +716,7 @@
             "forward",
             out_shape,
             [block, block_a, block_b, *carried]
-            + [cells, fr, factors, node_map, level_hot, cell_hot, spread, order],
+            + [cells, fr, factors, level_hot, cell_hot, spread, order, *node_maps],
             [
                 pltpu.VMEM((16 * pairs, 2 * padded_order), BF16),
                 pltpu.VMEM((48, refs), BF16),
@@ -708,6 +725,9 @@
         squares += extra[:1]
         if step == 1:
             samples = extra[1]
+        if step == 0:
+            far, near, ids = lax.optimization_barrier((far, near, conn))
+            node_maps = [turned_nodes(0, ids)]
         new_a, new_b = swapped(far, near)
         inner = call(
             functools.partial(inner_kernel, levels),
@@ -716,6 +736,8 @@
             [ordered, weight, conn, node_hot, level_hot],
             [pltpu.VMEM((48 * (levels - 2), refs), BF16)],
         )
+        if step == 0:
+            inner, node_maps[0] = lax.optimization_barrier((inner, node_maps[0]))
         operands = [block, block_a, block_b, own_a, own_b, new_a, new_b, inner, weight]
         operands += [conn, cells, fr, loaded, edge_hot, cell_map, spread_map, order_map]
         if last:
@@ -740,8 +762,7 @@
                 *messages, source, ids = lax.optimization_barrier((*messages, loaded, conn))
                 shape = shaped(blocks.shape, BF16)
                 factors = call(turn_blocks_kernel, "turn_blocks", shape, [source])
-                shape = shaped((refs, RADIX), BF16)
-                node_map = call(turn_nodes_kernel, "turn_nodes", shape, [ids])
+                node_maps.append(turned_nodes(pairs // 2, ids))
             if step == POWER - 1:
                 *messages, ids = lax.optimization_barrier((*messages, cells))
                 cell_map, spread_map, order_map = call(

time: 78.3 us -> 78.2 us (level)
    pallas_call x15 -> x16, Pallas kernels: 32.1 us -> 32.5 us  [call(): pl.pallas_call(kernel, out_shape=out_shape, in_specs=in_specs, out_specs=...]
where the time goes in v17:
time: 78.2 us; the launch traced here: 77.8 us
  Pallas kernels  32.5 us (42%)
  starting transfers between devices  31.1 us (40%)
  blocking collectives  11.9 us (15%)
  between operations  1.53 us (2%)
  waiting for transfers between devices  0.82 us (1%)
    pallas_call x16, Pallas kernels, call(): pl.pallas_call(kernel, out_shape=out_shape, in_specs=in_specs, out_specs=...  32.5 us
    ppermute x6, starting transfers between devices, swapped(): lax.ppermute(b, 'tiles', pairs_b)  26.6 us
    all_to_all x1, blocking collectives, shards(): gathered = lax.all_to_all(messages[0], everyone, 0, 0)  11.9 us
    ppermute x6, starting transfers between devices, swapped(): lax.ppermute(a, 'tiles', pairs_a)  4.43 us
  transfers between devices with their start and end apart: 12, of which 1 were waited for; matrix products, arithmetic and copies ran while one was open for 0% of the time, Pallas kernels for 19%

profile of v17, /device:TPU:0, one launch (start us, length us, event | category | flops | bytes accessed | tf_op | source)
XLA Modules:
  0.0 77.8 jit_solution(16569089837369549395)
XLA Ops:
  0.6 0.8 announce.1
  1.4 0.7 collective-permute-start
  2.1 5.8 %collective-permute-start.1 = (f32[16,256]{1,0:T(8,128)S(1)}, f32[16,256]{1,0:T(8,128)S(1)}, u32[]{:S(2)}, u32[]{:S(2)}) collective-permute-start(f32[16,256]{1,0:T(8,128)S(1)} %get-tuple-element.61.refs_0_), channel_id=1, source_target_pairs={{0,4},{8,12},{16,20},{24,28},{4,0},{12,8},{20,16},{28,24},{1,5},{9... | collective-permute-start | bytes 49160 | tf_op jit(solution)/shard_map/ppermute | solution.py:647
  8.5 3.4 %setup.1 = (s32[32,128]{1,0:T(8,128)S(1)}, s32[32,128]{1,0:T(8,128)S(1)}, f32[64,256]{1,0:T(8,128)S(1)}, bf16[64,192,192]{2,1,0:T(8,128)(2,1)S(1)}, bf16[512,409...) custom-call(s32[1]{0:T(128)S(6)} %copy.11.counts, ...), custom_call_target="tpu_custom_call" | custom-call | tf_op jit(solution)/shard_map/setup/pallas_call | solution.py:631
  11.9 0.0 collective-permute-done.refs_1_
  11.9 0.0 collective-permute-done.1.refs_2_
  11.9 0.0 copy-start
  11.9 3.6 %forward.3 = (bf16[512,384]{1,0:T(8,128)(2,1)S(1)}, f32[24,512]{1,0:T(8,128)S(1)}, f32[24,512]{1,0:T(8,128)S(1)}, bf16[48,256]{1,0:T(8,128)(2,1)S(1)}, bf16[48,256]{1,0:T(8,128)(2,1)S(1)}) custom-call(f32[16,256]{1,0:T(8,128)S(1)} %get-tuple-element.61.refs_0_, f32[16,256]{1,0:T(8,128)S(1)} %collective-permute-done.refs_1_, ...), custom_call_target="tpu_custom_call" | custom-call | tf_op jit(solution)/shard_map/forward/pallas_call | solution.py:631
  15.6 0.7 collective-permute-start.2
  16.2 4.4 %collective-permute-start.3 = (bf16[48,256]{1,0:T(8,128)(2,1)S(1)}, bf16[48,256]{1,0:T(8,128)(2,1)S(1)}, u32[]{:S(2)}, u32[]{:S(2)}) collective-permute-start(bf16[48,256]{1,0:T(8,128)(2,1)S(1)} %get-tuple-element.77), channel_id=1, source_target_pairs={{0,4},{8,12},{16,20},{24,28},{4,0},{12,8},{20,16},{28,24},{1,5},{9... | collective-permute-start | bytes 73736 | tf_op jit(solution)/shard_map/ppermute | solution.py:647
  20.6 0.0 copy-done
  20.6 2.5 %inner.3.refs_7_ = f32[256,384]{1,0:T(8,128)S(1)} custom-call(bf16[512,384]{1,0:T(8,128)(2,1)S(1)} %get-tuple-element.78.ordered_ref, f32[3,4096]{1,0:T(4,128)S(1)} %bitcast.8, s32[32,128]{1,0:T(8,128)S(1)} %get-tuple-element.89.conn_ref.refs_9_, bf16[512,4096]{1,0:T(8,128)(2,1)S(1)} %get-tuple-element.70.refs_10_.node_hot, ...), custom_call_target="tpu_custom_call" | custom-call | tf_op jit(solution)/shard_map/inner/pallas_call | solution.py:631
  23.1 0.5 turn_nodes.2.refs_13_
  23.6 0.0 collective-permute-done.2.refs_5_
  23.6 0.0 collective-permute-done.3.refs_6_
  23.6 2.4 %adjoint.3 = (f32[8,384]{1,0:T(8,128)S(1)}, f32[8,128]{1,0:T(8,128)S(1)}, f32[8,128]{1,0:T(8,128)S(1)}) custom-call(f32[16,256]{1,0:T(8,128)S(1)} %get-tuple-element.61.refs_0_, f32[16,256]{1,0:T(8,128)S(1)} %collective-permute-done.refs_1_, f32[16,256]{1,0:T(8,128)S(1)} %collective-permute-done.1.refs_2_, f32[24,512]{1,0:T(8,128)S(1)} %get-tuple-element.71.refs_3_, ...), custom_call_target="tpu_custom_call" | custom-call | tf_op jit(solution)/shard_map/adjoint/pallas_call | solution.py:631
  26.0 0.9 %collective-permute-start.4 = (f32[8,128]{1,0:T(8,128)S(1)}, f32[8,128]{1,0:T(8,128)S(1)}, u32[]{:S(2)}, u32[]{:S(2)}) collective-permute-start(f32[8,128]{1,0:T(8,128)S(1)} %get-tuple-element.85), channel_id=1, source_target_pairs={{4,8},{12,16},{20,24},{8,4},{16,12},{24,20},{5,9},{13,17},{21,25},... | collective-permute-start | bytes 12296 | tf_op jit(solution)/shard_map/ppermute | solution.py:647
  26.9 4.4 %collective-permute-start.5 = (f32[8,128]{1,0:T(8,128)S(1)}, f32[8,128]{1,0:T(8,128)S(1)}, u32[]{:S(2)}, u32[]{:S(2)}) collective-permute-start(f32[8,128]{1,0:T(8,128)S(1)} %get-tuple-element.86), channel_id=1, source_target_pairs={{0,4},{8,12},{16,20},{24,28},{4,0},{12,8},{20,16},{28,24},{1,5},{9... | collective-permute-start | bytes 12296 | tf_op jit(solution)/shard_map/ppermute | solution.py:647
  31.3 0.5 turn_nodes.3.refs_14_
  31.8 2.0 %turn_blocks.1.refs_8_ = bf16[64,192,192]{2,1,0:T(8,128)(2,1)S(1)} custom-call(bf16[64,192,192]{2,1,0:T(8,128)(2,1)S(1)} %get-tuple-element.87.refs_5_.refs_12_.blocks), custom_call_target="tpu_custom_call" | custom-call | tf_op jit(solution)/shard_map/turn_blocks/pallas_call | solution.py:631
  33.8 0.0 collective-permute-done.4.refs_4_
  33.8 0.0 collective-permute-done.5.refs_5_
  33.8 2.4 %forward.4 = (bf16[512,384]{1,0:T(8,128)(2,1)S(1)}, f32[24,512]{1,0:T(8,128)S(1)}, f32[24,512]{1,0:T(8,128)S(1)}, bf16[48,256]{1,0:T(8,128)(2,1)S(1)}, bf16[48,2...) custom-call(f32[16,256]{1,0:T(8,128)S(1)} %get-tuple-element.61.refs_0_, ...), custom_call_target="tpu_custom_call" | custom-call | tf_op jit(solution)/shard_map/forward/pallas_call | solution.py:631
  36.2 0.7 collective-permute-start.6
  36.9 3.1 %collective-permute-start.7 = (bf16[48,256]{1,0:T(8,128)(2,1)S(1)}, bf16[48,256]{1,0:T(8,128)(2,1)S(1)}, u32[]{:S(2)}, u32[]{:S(2)}) collective-permute-start(bf16[48,256]{1,0:T(8,128)(2,1)S(1)} %get-tuple-element.93), channel_id=1, source_target_pairs={{0,4},{8,12},{16,20},{24,28},{4,0},{12,8},{20,16},{28,24},{1,5},{9... | collective-permute-start | bytes 73736 | tf_op jit(solution)/shard_map/ppermute | solution.py:647
  40.0 2.6 %inner.4.refs_7_ = f32[256,384]{1,0:T(8,128)S(1)} custom-call(bf16[512,384]{1,0:T(8,128)(2,1)S(1)} %get-tuple-element.94.ordered_ref, f32[3,4096]{1,0:T(4,128)S(1)} %bitcast.10, s32[32,128]{1,0:T(8,128)S(1)} %get-tuple-element.89.conn_ref.refs_9_, bf16[512,4096]{1,0:T(8,128)(2,1)S(1)} %get-tuple-element.70.refs_10_.node_hot, ...), custom_call_target="tpu_custom_call" | custom-call | tf_op jit(solution)/shard_map/inner/pallas_call | solution.py:631
  42.5 0.0 collective-permute-done.6.refs_5_
  42.5 0.0 collective-permute-done.7.refs_6_
  42.6 2.4 %adjoint.4 = (f32[8,384]{1,0:T(8,128)S(1)}, f32[8,128]{1,0:T(8,128)S(1)}, f32[8,128]{1,0:T(8,128)S(1)}) custom-call(f32[16,256]{1,0:T(8,128)S(1)} %get-tuple-element.61.refs_0_, f32[16,256]{1,0:T(8,128)S(1)} %collective-permute-done.refs_1_, f32[16,256]{1,0:T(8,128)S(1)} %collective-permute-done.1.refs_2_, f32[24,512]{1,0:T(8,128)S(1)} %get-tuple-element.90.refs_3_, ...), custom_call_target="tpu_custom_call" | custom-call | tf_op jit(solution)/shard_map/adjoint/pallas_call | solution.py:631
  45.0 0.7 collective-permute-start.8
  45.7 4.8 %collective-permute-start.9 = (f32[8,128]{1,0:T(8,128)S(1)}, f32[8,128]{1,0:T(8,128)S(1)}, u32[]{:S(2)}, u32[]{:S(2)}) collective-permute-start(f32[8,128]{1,0:T(8,128)S(1)} %get-tuple-element.102), channel_id=1, source_target_pairs={{0,4},{8,12},{16,20},{24,28},{4,0},{12,8},{20,16},{28,24},{1,5},{9... | collective-permute-start | bytes 12296 | tf_op jit(solution)/shard_map/ppermute | solution.py:647
  50.5 0.8 %turn_cells.1 = (bf16[4096,128]{1,0:T(8,128)(2,1)S(1)}, bf16[512,128]{1,0:T(8,128)(2,1)S(1)}, bf16[384,512]{1,0:T(8,128)(2,1)S(1)}) custom-call(s32[32,128]{1,0:T(8,128)S(1)} %get-tuple-element.98.refs_3_.refs_10_.refs_6_.cell_ref), custom_call_target="tpu_custom_call" | custom-call | tf_op jit(solution)/shard_map/turn_cells/pallas_call | solution.py:631
  51.2 0.0 collective-permute-done.8.refs_4_
  51.3 0.8 %collective-permute-done.9.refs_5_ = f32[8,128]{1,0:T(8,128)S(1)} collective-permute-done((f32[8,128]{1,0:T(8,128)S(1)}, f32[8,128]{1,0:T(8,128)S(1)}, u32[]{:S(2)}, u32[]{:S(2)}) %collective-permute-start.9) | collective-permute-done | bytes 4128 | tf_op jit(solution)/shard_map/ppermute | solution.py:647
  52.0 2.4 %forward.5 = (bf16[512,384]{1,0:T(8,128)(2,1)S(1)}, f32[24,512]{1,0:T(8,128)S(1)}, f32[24,512]{1,0:T(8,128)S(1)}, bf16[48,256]{1,0:T(8,128)(2,1)S(1)}, bf16[48,2...) custom-call(f32[16,256]{1,0:T(8,128)S(1)} %get-tuple-element.61.refs_0_, f32[16,256]{1,0:T(8,128)S(1)} %collective-permute-done.refs_1_, ...), custom_call_target="tpu_custom_call" | custom-call | tf_op jit(solution)/shard_map/forward/pallas_call | solution.py:631
  54.5 0.0 copy-start.1
  54.5 0.9 %collective-permute-start.10 = (bf16[48,256]{1,0:T(8,128)(2,1)S(1)}, bf16[48,256]{1,0:T(8,128)(2,1)S(1)}, u32[]{:S(2)}, u32[]{:S(2)}) collective-permute-start(bf16[48,256]{1,0:T(8,128)(2,1)S(1)} %get-tuple-element.105), channel_id=1, source_target_pairs={{4,8},{12,16},{20,24},{8,4},{16,12},{24,20},{5,9},{13,17},{21,25},... | collective-permute-start | bytes 73736 | tf_op jit(solution)/shard_map/ppermute | solution.py:647
  55.4 4.3 %collective-permute-start.11 = (bf16[48,256]{1,0:T(8,128)(2,1)S(1)}, bf16[48,256]{1,0:T(8,128)(2,1)S(1)}, u32[]{:S(2)}, u32[]{:S(2)}) collective-permute-start(bf16[48,256]{1,0:T(8,128)(2,1)S(1)} %get-tuple-element.106), channel_id=1, source_target_pairs={{0,4},{8,12},{16,20},{24,28},{4,0},{12,8},{20,16},{28,24},{1,5},{9... | collective-permute-start | bytes 73736 | tf_op jit(solution)/shard_map/ppermute | solution.py:647
  59.7 2.6 %inner.5.refs_7_ = f32[256,384]{1,0:T(8,128)S(1)} custom-call(bf16[512,384]{1,0:T(8,128)(2,1)S(1)} %get-tuple-element.107.ordered_ref, f32[3,4096]{1,0:T(4,128)S(1)} %bitcast.12, s32[32,128]{1,0:T(8,128)S(1)} %get-tuple-element.89.conn_ref.refs_9_, bf16[512,4096]{1,0:T(8,128)(2,1)S(1)} %get-tuple-element.70.refs_10_.node_hot, ...), custom_call_target="tpu_custom_call" | custom-call | tf_op jit(solution)/shard_map/inner/pallas_call | solution.py:631
  62.2 0.0 collective-permute-done.10.refs_5_
  62.2 0.0 collective-permute-done.11.refs_6_
  62.2 0.0 copy-done.1
  62.3 2.2 %adjoint.5 = (f32[8,384]{1,0:T(8,128)S(1)}, bf16[32,8,256]{2,1,0:T(8,128)(2,1)S(1)}) custom-call(f32[16,256]{1,0:T(8,128)S(1)} %get-tuple-element.61.refs_0_, f32[16,256]{1,0:T(8,128)S(1)} %collective-permute-done.refs_1_, f32[16,256]{1,0:T(8,128)S(1)} %collective-permute-done.1.refs_2_, f32[24,512]{1,0:T(8,128)S(1)} %get-tuple-element.103.refs_3_, ...), custom_call_target="tpu_custom_call" | custom-call | tf_op jit(solution)/shard_map/adjoint/pallas_call | solution.py:631
  64.4 11.9 %all_to_all.5 = bf16[32,8,256]{2,1,0:T(8,128)(2,1)S(1)} all-to-all(bf16[32,8,256]{2,1,0:T(8,128)(2,1)S(1)} %get-tuple-element.113), channel_id=1, replica_groups=mesh['tiles'=8,'probes'=4] {'tiles','probes'}, dimensions={0} | all-to-all | bytes 262144 | tf_op jit(solution)/shard_map/all_to_all | solution.py:781
  76.3 1.5 %gram.1 = (f32[8,256]{1,0:T(8,128)}, f32[8,256]{1,0:T(8,128)}, f32[8,8,32]{2,1,0:T(8,128)}) custom-call(bf16[8,4,8,256]{3,2,1,0:T(8,128)(2,1)S(1)} %bitcast.14, f32[8,384]{1,0:T(8,128)S(1)} %get-tuple-element.114.own_ref, f32[8,256]{1,0:T(8,128)S(1)} %get-tuple-element.115.samples_in), custom_call_target="tpu_custom_call" | custom-call | tf_op jit(solution)/shard_map/gram/pallas_call | solution.py:631
Async XLA Ops:
  1.4 10.5 %collective-permute-start = (f32[16,256]{1,0:T(8,128)S(1)}, f32[16,256]{1,0:T(8,128)S(1)}, u32[]{:S(2)}, u32[]{:S(2)}) collective-permute-start(f32[16,256]{1,0:T(8,128)S(1)} %get-tuple-element.62), channel_id=1, source_target_pairs={{4,8},{12,16},{20,24},{8,4},{16,12},{24,20},{5,9},{13,17},{21,25},... | collective-permute-start | bytes 49160 | tf_op jit(solution)/shard_map/ppermute | solution.py:647
  2.1 9.8 %collective-permute-start.1 = (f32[16,256]{1,0:T(8,128)S(1)}, f32[16,256]{1,0:T(8,128)S(1)}, u32[]{:S(2)}, u32[]{:S(2)}) collective-permute-start(f32[16,256]{1,0:T(8,128)S(1)} %get-tuple-element.61.refs_0_), channel_id=1, source_target_pairs={{0,4},{8,12},{16,20},{24,28},{4,0},{12,8},{20,16},{28,24},{1,5},{9... | collective-permute-start | bytes 49160 | tf_op jit(solution)/shard_map/ppermute | solution.py:647
  11.9 8.7 %copy-start = (f32[4096,3]{0,1:T(4,128)S(1)}, f32[4096,3]{0,1:T(4,128)}, u32[]{:S(2)}) copy-start(f32[4096,3]{0,1:T(4,128)} %param.13) | copy-start | bytes 147460
  15.6 8.1 %collective-permute-start.2 = (bf16[48,256]{1,0:T(8,128)(2,1)S(1)}, bf16[48,256]{1,0:T(8,128)(2,1)S(1)}, u32[]{:S(2)}, u32[]{:S(2)}) collective-permute-start(bf16[48,256]{1,0:T(8,128)(2,1)S(1)} %get-tuple-element.76), channel_id=1, source_target_pairs={{4,8},{12,16},{20,24},{8,4},{16,12},{24,20},{5,9},{13,17},{21,25},... | collective-permute-start | bytes 73736 | tf_op jit(solution)/shard_map/ppermute | solution.py:647
  16.2 7.4 %collective-permute-start.3 = (bf16[48,256]{1,0:T(8,128)(2,1)S(1)}, bf16[48,256]{1,0:T(8,128)(2,1)S(1)}, u32[]{:S(2)}, u32[]{:S(2)}) collective-permute-start(bf16[48,256]{1,0:T(8,128)(2,1)S(1)} %get-tuple-element.77), channel_id=1, source_target_pairs={{0,4},{8,12},{16,20},{24,28},{4,0},{12,8},{20,16},{28,24},{1,5},{9... | collective-permute-start | bytes 73736 | tf_op jit(solution)/shard_map/ppermute | solution.py:647
  26.0 7.7 %collective-permute-start.4 = (f32[8,128]{1,0:T(8,128)S(1)}, f32[8,128]{1,0:T(8,128)S(1)}, u32[]{:S(2)}, u32[]{:S(2)}) collective-permute-start(f32[8,128]{1,0:T(8,128)S(1)} %get-tuple-element.85), channel_id=1, source_target_pairs={{4,8},{12,16},{20,24},{8,4},{16,12},{24,20},{5,9},{13,17},{21,25},... | collective-permute-start | bytes 12296 | tf_op jit(solution)/shard_map/ppermute | solution.py:647
  26.9 6.9 %collective-permute-start.5 = (f32[8,128]{1,0:T(8,128)S(1)}, f32[8,128]{1,0:T(8,128)S(1)}, u32[]{:S(2)}, u32[]{:S(2)}) collective-permute-start(f32[8,128]{1,0:T(8,128)S(1)} %get-tuple-element.86), channel_id=1, source_target_pairs={{0,4},{8,12},{16,20},{24,28},{4,0},{12,8},{20,16},{28,24},{1,5},{9... | collective-permute-start | bytes 12296 | tf_op jit(solution)/shard_map/ppermute | solution.py:647
  36.2 6.3 %collective-permute-start.6 = (bf16[48,256]{1,0:T(8,128)(2,1)S(1)}, bf16[48,256]{1,0:T(8,128)(2,1)S(1)}, u32[]{:S(2)}, u32[]{:S(2)}) collective-permute-start(bf16[48,256]{1,0:T(8,128)(2,1)S(1)} %get-tuple-element.92), channel_id=1, source_target_pairs={{4,8},{12,16},{20,24},{8,4},{16,12},{24,20},{5,9},{13,17},{21,25},... | collective-permute-start | bytes 73736 | tf_op jit(solution)/shard_map/ppermute | solution.py:647
  36.9 5.6 %collective-permute-start.7 = (bf16[48,256]{1,0:T(8,128)(2,1)S(1)}, bf16[48,256]{1,0:T(8,128)(2,1)S(1)}, u32[]{:S(2)}, u32[]{:S(2)}) collective-permute-start(bf16[48,256]{1,0:T(8,128)(2,1)S(1)} %get-tuple-element.93), channel_id=1, source_target_pairs={{0,4},{8,12},{16,20},{24,28},{4,0},{12,8},{20,16},{28,24},{1,5},{9... | collective-permute-start | bytes 73736 | tf_op jit(solution)/shard_map/ppermute | solution.py:647
  45.0 6.3 %collective-permute-start.8 = (f32[8,128]{1,0:T(8,128)S(1)}, f32[8,128]{1,0:T(8,128)S(1)}, u32[]{:S(2)}, u32[]{:S(2)}) collective-permute-start(f32[8,128]{1,0:T(8,128)S(1)} %get-tuple-element.101), channel_id=1, source_target_pairs={{4,8},{12,16},{20,24},{8,4},{16,12},{24,20},{5,9},{13,17},{21,25},... | collective-permute-start | bytes 12296 | tf_op jit(solution)/shard_map/ppermute | solution.py:647
  45.7 6.4 %collective-permute-start.9 = (f32[8,128]{1,0:T(8,128)S(1)}, f32[8,128]{1,0:T(8,128)S(1)}, u32[]{:S(2)}, u32[]{:S(2)}) collective-permute-start(f32[8,128]{1,0:T(8,128)S(1)} %get-tuple-element.102), channel_id=1, source_target_pairs={{0,4},{8,12},{16,20},{24,28},{4,0},{12,8},{20,16},{28,24},{1,5},{9... | collective-permute-start | bytes 12296 | tf_op jit(solution)/shard_map/ppermute | solution.py:647
  54.5 7.7 %copy-start.1 = (s32[256]{0:T(256)S(1)}, s32[256]{0:T(256)}, u32[]{:S(2)}) copy-start(s32[256]{0:T(256)} %param.15) | copy-start | bytes 3076
  54.5 7.7 %collective-permute-start.10 = (bf16[48,256]{1,0:T(8,128)(2,1)S(1)}, bf16[48,256]{1,0:T(8,128)(2,1)S(1)}, u32[]{:S(2)}, u32[]{:S(2)}) collective-permute-start(bf16[48,256]{1,0:T(8,128)(2,1)S(1)} %get-tuple-element.105), channel_id=1, source_target_pairs={{4,8},{12,16},{20,24},{8,4},{16,12},{24,20},{5,9},{13,17},{21,25},... | collective-permute-start | bytes 73736 | tf_op jit(solution)/shard_map/ppermute | solution.py:647
  55.4 6.8 %collective-permute-start.11 = (bf16[48,256]{1,0:T(8,128)(2,1)S(1)}, bf16[48,256]{1,0:T(8,128)(2,1)S(1)}, u32[]{:S(2)}, u32[]{:S(2)}) collective-permute-start(bf16[48,256]{1,0:T(8,128)(2,1)S(1)} %get-tuple-element.106), channel_id=1, source_target_pairs={{0,4},{8,12},{16,20},{24,28},{4,0},{12,8},{20,16},{28,24},{1,5},{9... | collective-permute-start | bytes 73736 | tf_op jit(solution)/shard_map/ppermute | solution.py:647

commit v18 on v16

--- a/solution.py
+++ b/solution.py
@@ -379,7 +379,7 @@
         at = inside[i // 3] * RADIX
         rows.append(value * weight_ref[i % 3 : i % 3 + 1, at : at + RADIX])
     weighted = jnp.concatenate(rows, axis=0).astype(BF16)
-    step = 2
+    step = 4
     for start in range(0, pairs, step):
         found = dot(weighted, node_hot[:, start * LANES : (start + step) * LANES])
         for i in range(step):
@@ -424,7 +424,7 @@
     conn = conn_ref[...]
     first = levels * RADIX // EDGE_RADIX - EDGE
     edges = [*range(EDGE), *range(first, first + EDGE)]
-    width = 2
+    width = 4
     for start in range(0, pairs, width):
         found = dot(weighted, edge_hot[:, start * LANES : (start + width) * LANES])
         values = [[] for _ in range(3)]

time: 78.3 us -> 78.3 us (level)
  no operation moved by 1% of the time
where the time goes in v18:
time: 78.3 us; the launch traced here: 77.9 us
  Pallas kernels  32.1 us (41%)
  starting transfers between devices  31.1 us (40%)
  blocking collectives  12.3 us (16%)
  between operations  1.52 us (2%)
  waiting for transfers between devices  0.82 us (1%)
    pallas_call x15, Pallas kernels, call(): pl.pallas_call(kernel, out_shape=out_shape, in_specs=in_specs, out_specs=...  32.1 us
    ppermute x6, starting transfers between devices, swapped(): lax.ppermute(b, 'tiles', pairs_b)  26.7 us
    all_to_all x1, blocking collectives, shards(): gathered = lax.all_to_all(messages[0], everyone, 0, 0)  12.3 us
    ppermute x6, starting transfers between devices, swapped(): lax.ppermute(a, 'tiles', pairs_a)  4.43 us
  transfers between devices with their start and end apart: 12, of which 1 were waited for; matrix products, arithmetic and copies ran while one was open for 0% of the time, Pallas kernels for 19%

profile of v18, /device:TPU:0, one launch (start us, length us, event | category | flops | bytes accessed | tf_op | source)
XLA Modules:
  0.0 77.9 jit_solution(14554454203848306364)
XLA Ops:
  0.6 0.8 announce.1
  1.4 0.7 collective-permute-start
  2.1 5.8 %collective-permute-start.1 = (f32[16,256]{1,0:T(8,128)S(1)}, f32[16,256]{1,0:T(8,128)S(1)}, u32[]{:S(2)}, u32[]{:S(2)}) collective-permute-start(f32[16,256]{1,0:T(8,128)S(1)} %get-tuple-element.56.refs_0_), channel_id=1, source_target_pairs={{0,4},{8,12},{16,20},{24,28},{4,0},{12,8},{20,16},{28,24},{1,5},{9... | collective-permute-start | bytes 49160 | tf_op jit(solution)/shard_map/ppermute | solution.py:638
  8.5 3.4 %setup.1 = (s32[32,128]{1,0:T(8,128)S(1)}, s32[32,128]{1,0:T(8,128)S(1)}, f32[64,256]{1,0:T(8,128)S(1)}, bf16[64,192,192]{2,1,0:T(8,128)(2,1)S(1)}, bf16[512,409...) custom-call(s32[1]{0:T(128)S(6)} %copy.11.counts, ...), custom_call_target="tpu_custom_call" | custom-call | tf_op jit(solution)/shard_map/setup/pallas_call | solution.py:622
  11.9 0.0 collective-permute-done.refs_1_
  11.9 0.0 collective-permute-done.1.refs_2_
  11.9 0.0 copy-start
  11.9 3.6 %forward.3 = (bf16[512,384]{1,0:T(8,128)(2,1)S(1)}, f32[24,512]{1,0:T(8,128)S(1)}, f32[24,512]{1,0:T(8,128)S(1)}, bf16[48,256]{1,0:T(8,128)(2,1)S(1)}, bf16[48,256]{1,0:T(8,128)(2,1)S(1)}) custom-call(f32[16,256]{1,0:T(8,128)S(1)} %get-tuple-element.56.refs_0_, f32[16,256]{1,0:T(8,128)S(1)} %collective-permute-done.refs_1_, ...), custom_call_target="tpu_custom_call" | custom-call | tf_op jit(solution)/shard_map/forward/pallas_call | solution.py:622
  15.6 0.7 collective-permute-start.2
  16.2 4.4 %collective-permute-start.3 = (bf16[48,256]{1,0:T(8,128)(2,1)S(1)}, bf16[48,256]{1,0:T(8,128)(2,1)S(1)}, u32[]{:S(2)}, u32[]{:S(2)}) collective-permute-start(bf16[48,256]{1,0:T(8,128)(2,1)S(1)} %get-tuple-element.69), channel_id=1, source_target_pairs={{0,4},{8,12},{16,20},{24,28},{4,0},{12,8},{20,16},{28,24},{1,5},{9... | collective-permute-start | bytes 73736 | tf_op jit(solution)/shard_map/ppermute | solution.py:638
  20.6 0.0 copy-done
  20.6 2.5 %inner.3.refs_7_ = f32[256,384]{1,0:T(8,128)S(1)} custom-call(bf16[512,384]{1,0:T(8,128)(2,1)S(1)} %get-tuple-element.70.ordered_ref, f32[3,4096]{1,0:T(4,128)S(1)} %bitcast.8, s32[32,128]{1,0:T(8,128)S(1)} %get-tuple-element.79.conn_ref.refs_9_, bf16[512,4096]{1,0:T(8,128)(2,1)S(1)} %get-tuple-element.61.refs_6_.node_hot, ...), custom_call_target="tpu_custom_call" | custom-call | tf_op jit(solution)/shard_map/inner/pallas_call | solution.py:622
  23.1 0.0 collective-permute-done.2.refs_5_
  23.1 0.0 collective-permute-done.3.refs_6_
  23.1 2.4 %adjoint.3 = (f32[8,384]{1,0:T(8,128)S(1)}, f32[8,128]{1,0:T(8,128)S(1)}, f32[8,128]{1,0:T(8,128)S(1)}) custom-call(f32[16,256]{1,0:T(8,128)S(1)} %get-tuple-element.56.refs_0_, f32[16,256]{1,0:T(8,128)S(1)} %collective-permute-done.refs_1_, f32[16,256]{1,0:T(8,128)S(1)} %collective-permute-done.1.refs_2_, f32[24,512]{1,0:T(8,128)S(1)} %get-tuple-element.66.refs_3_, ...), custom_call_target="tpu_custom_call" | custom-call | tf_op jit(solution)/shard_map/adjoint/pallas_call | solution.py:622
  25.5 0.9 %collective-permute-start.4 = (f32[8,128]{1,0:T(8,128)S(1)}, f32[8,128]{1,0:T(8,128)S(1)}, u32[]{:S(2)}, u32[]{:S(2)}) collective-permute-start(f32[8,128]{1,0:T(8,128)S(1)} %get-tuple-element.76), channel_id=1, source_target_pairs={{4,8},{12,16},{20,24},{8,4},{16,12},{24,20},{5,9},{13,17},{21,25},... | collective-permute-start | bytes 12296 | tf_op jit(solution)/shard_map/ppermute | solution.py:638
  26.4 4.3 %collective-permute-start.5 = (f32[8,128]{1,0:T(8,128)S(1)}, f32[8,128]{1,0:T(8,128)S(1)}, u32[]{:S(2)}, u32[]{:S(2)}) collective-permute-start(f32[8,128]{1,0:T(8,128)S(1)} %get-tuple-element.77), channel_id=1, source_target_pairs={{0,4},{8,12},{16,20},{24,28},{4,0},{12,8},{20,16},{28,24},{1,5},{9... | collective-permute-start | bytes 12296 | tf_op jit(solution)/shard_map/ppermute | solution.py:638
  30.8 0.8 %turn_nodes.1.refs_9_ = bf16[4096,512]{1,0:T(8,128)(2,1)S(1)} custom-call(s32[32,128]{1,0:T(8,128)S(1)} %get-tuple-element.79.conn_ref.refs_9_), custom_call_target="tpu_custom_call" | custom-call | tf_op jit(solution)/shard_map/turn_nodes/pallas_call | solution.py:622
  31.6 2.0 %turn_blocks.1.refs_8_ = bf16[64,192,192]{2,1,0:T(8,128)(2,1)S(1)} custom-call(bf16[64,192,192]{2,1,0:T(8,128)(2,1)S(1)} %get-tuple-element.78.refs_5_.refs_12_.blocks), custom_call_target="tpu_custom_call" | custom-call | tf_op jit(solution)/shard_map/turn_blocks/pallas_call | solution.py:622
  33.6 0.0 collective-permute-done.4.refs_4_
  33.6 0.0 collective-permute-done.5.refs_5_
  33.6 2.3 %forward.4 = (bf16[512,384]{1,0:T(8,128)(2,1)S(1)}, f32[24,512]{1,0:T(8,128)S(1)}, f32[24,512]{1,0:T(8,128)S(1)}, bf16[48,256]{1,0:T(8,128)(2,1)S(1)}, bf16[48,2...) custom-call(f32[16,256]{1,0:T(8,128)S(1)} %get-tuple-element.56.refs_0_, ...), custom_call_target="tpu_custom_call" | custom-call | tf_op jit(solution)/shard_map/forward/pallas_call | solution.py:622
  35.9 0.7 collective-permute-start.6
  36.6 3.4 %collective-permute-start.7 = (bf16[48,256]{1,0:T(8,128)(2,1)S(1)}, bf16[48,256]{1,0:T(8,128)(2,1)S(1)}, u32[]{:S(2)}, u32[]{:S(2)}) collective-permute-start(bf16[48,256]{1,0:T(8,128)(2,1)S(1)} %get-tuple-element.83), channel_id=1, source_target_pairs={{0,4},{8,12},{16,20},{24,28},{4,0},{12,8},{20,16},{28,24},{1,5},{9... | collective-permute-start | bytes 73736 | tf_op jit(solution)/shard_map/ppermute | solution.py:638
  40.0 2.6 %inner.4.refs_7_ = f32[256,384]{1,0:T(8,128)S(1)} custom-call(bf16[512,384]{1,0:T(8,128)(2,1)S(1)} %get-tuple-element.84.ordered_ref, f32[3,4096]{1,0:T(4,128)S(1)} %bitcast.10, s32[32,128]{1,0:T(8,128)S(1)} %get-tuple-element.79.conn_ref.refs_9_, bf16[512,4096]{1,0:T(8,128)(2,1)S(1)} %get-tuple-element.61.refs_6_.node_hot, ...), custom_call_target="tpu_custom_call" | custom-call | tf_op jit(solution)/shard_map/inner/pallas_call | solution.py:622
  42.6 0.0 collective-permute-done.6.refs_5_
  42.6 0.0 collective-permute-done.7.refs_6_
  42.6 2.4 %adjoint.4 = (f32[8,384]{1,0:T(8,128)S(1)}, f32[8,128]{1,0:T(8,128)S(1)}, f32[8,128]{1,0:T(8,128)S(1)}) custom-call(f32[16,256]{1,0:T(8,128)S(1)} %get-tuple-element.56.refs_0_, f32[16,256]{1,0:T(8,128)S(1)} %collective-permute-done.refs_1_, f32[16,256]{1,0:T(8,128)S(1)} %collective-permute-done.1.refs_2_, f32[24,512]{1,0:T(8,128)S(1)} %get-tuple-element.80.refs_3_, ...), custom_call_target="tpu_custom_call" | custom-call | tf_op jit(solution)/shard_map/adjoint/pallas_call | solution.py:622
  45.0 0.7 collective-permute-start.8
  45.7 4.2 %collective-permute-start.9 = (f32[8,128]{1,0:T(8,128)S(1)}, f32[8,128]{1,0:T(8,128)S(1)}, u32[]{:S(2)}, u32[]{:S(2)}) collective-permute-start(f32[8,128]{1,0:T(8,128)S(1)} %get-tuple-element.92), channel_id=1, source_target_pairs={{0,4},{8,12},{16,20},{24,28},{4,0},{12,8},{20,16},{28,24},{1,5},{9... | collective-permute-start | bytes 12296 | tf_op jit(solution)/shard_map/ppermute | solution.py:638
  49.9 0.8 %turn_cells.1 = (bf16[4096,128]{1,0:T(8,128)(2,1)S(1)}, bf16[512,128]{1,0:T(8,128)(2,1)S(1)}, bf16[384,512]{1,0:T(8,128)(2,1)S(1)}) custom-call(s32[32,128]{1,0:T(8,128)S(1)} %get-tuple-element.88.refs_3_.refs_10_.refs_6_.cell_ref), custom_call_target="tpu_custom_call" | custom-call | tf_op jit(solution)/shard_map/turn_cells/pallas_call | solution.py:622
  50.7 0.0 collective-permute-done.8.refs_4_
  50.7 0.8 %collective-permute-done.9.refs_5_ = f32[8,128]{1,0:T(8,128)S(1)} collective-permute-done((f32[8,128]{1,0:T(8,128)S(1)}, f32[8,128]{1,0:T(8,128)S(1)}, u32[]{:S(2)}, u32[]{:S(2)}) %collective-permute-start.9) | collective-permute-done | bytes 4128 | tf_op jit(solution)/shard_map/ppermute | solution.py:638
  51.5 2.4 %forward.5 = (bf16[512,384]{1,0:T(8,128)(2,1)S(1)}, f32[24,512]{1,0:T(8,128)S(1)}, f32[24,512]{1,0:T(8,128)S(1)}, bf16[48,256]{1,0:T(8,128)(2,1)S(1)}, bf16[48,2...) custom-call(f32[16,256]{1,0:T(8,128)S(1)} %get-tuple-element.56.refs_0_, f32[16,256]{1,0:T(8,128)S(1)} %collective-permute-done.refs_1_, ...), custom_call_target="tpu_custom_call" | custom-call | tf_op jit(solution)/shard_map/forward/pallas_call | solution.py:622
  53.8 0.0 copy-start.1
  53.9 0.9 %collective-permute-start.10 = (bf16[48,256]{1,0:T(8,128)(2,1)S(1)}, bf16[48,256]{1,0:T(8,128)(2,1)S(1)}, u32[]{:S(2)}, u32[]{:S(2)}) collective-permute-start(bf16[48,256]{1,0:T(8,128)(2,1)S(1)} %get-tuple-element.95), channel_id=1, source_target_pairs={{4,8},{12,16},{20,24},{8,4},{16,12},{24,20},{5,9},{13,17},{21,25},... | collective-permute-start | bytes 73736 | tf_op jit(solution)/shard_map/ppermute | solution.py:638
  54.7 4.6 %collective-permute-start.11 = (bf16[48,256]{1,0:T(8,128)(2,1)S(1)}, bf16[48,256]{1,0:T(8,128)(2,1)S(1)}, u32[]{:S(2)}, u32[]{:S(2)}) collective-permute-start(bf16[48,256]{1,0:T(8,128)(2,1)S(1)} %get-tuple-element.96), channel_id=1, source_target_pairs={{0,4},{8,12},{16,20},{24,28},{4,0},{12,8},{20,16},{28,24},{1,5},{9... | collective-permute-start | bytes 73736 | tf_op jit(solution)/shard_map/ppermute | solution.py:638
  59.3 2.6 %inner.5.refs_7_ = f32[256,384]{1,0:T(8,128)S(1)} custom-call(bf16[512,384]{1,0:T(8,128)(2,1)S(1)} %get-tuple-element.97.ordered_ref, f32[3,4096]{1,0:T(4,128)S(1)} %bitcast.12, s32[32,128]{1,0:T(8,128)S(1)} %get-tuple-element.79.conn_ref.refs_9_, bf16[512,4096]{1,0:T(8,128)(2,1)S(1)} %get-tuple-element.61.refs_6_.node_hot, ...), custom_call_target="tpu_custom_call" | custom-call | tf_op jit(solution)/shard_map/inner/pallas_call | solution.py:622
  61.9 0.0 collective-permute-done.10.refs_5_
  61.9 0.0 collective-permute-done.11.refs_6_
  61.9 0.0 copy-done.1
  61.9 2.2 %adjoint.5 = (f32[8,384]{1,0:T(8,128)S(1)}, bf16[32,8,256]{2,1,0:T(8,128)(2,1)S(1)}) custom-call(f32[16,256]{1,0:T(8,128)S(1)} %get-tuple-element.56.refs_0_, f32[16,256]{1,0:T(8,128)S(1)} %collective-permute-done.refs_1_, f32[16,256]{1,0:T(8,128)S(1)} %collective-permute-done.1.refs_2_, f32[24,512]{1,0:T(8,128)S(1)} %get-tuple-element.93.refs_3_, ...), custom_call_target="tpu_custom_call" | custom-call | tf_op jit(solution)/shard_map/adjoint/pallas_call | solution.py:622
  64.1 12.3 %all_to_all.5 = bf16[32,8,256]{2,1,0:T(8,128)(2,1)S(1)} all-to-all(bf16[32,8,256]{2,1,0:T(8,128)(2,1)S(1)} %get-tuple-element.103), channel_id=1, replica_groups=mesh['tiles'=8,'probes'=4] {'tiles','probes'}, dimensions={0} | all-to-all | bytes 262144 | tf_op jit(solution)/shard_map/all_to_all | solution.py:760
  76.4 1.5 %gram.1 = (f32[8,256]{1,0:T(8,128)}, f32[8,256]{1,0:T(8,128)}, f32[8,8,32]{2,1,0:T(8,128)}) custom-call(bf16[8,4,8,256]{3,2,1,0:T(8,128)(2,1)S(1)} %bitcast.14, f32[8,384]{1,0:T(8,128)S(1)} %get-tuple-element.104.own_ref, f32[8,256]{1,0:T(8,128)S(1)} %get-tuple-element.105.samples_in), custom_call_target="tpu_custom_call" | custom-call | tf_op jit(solution)/shard_map/gram/pallas_call | solution.py:622
Async XLA Ops:
  1.4 10.5 %collective-permute-start = (f32[16,256]{1,0:T(8,128)S(1)}, f32[16,256]{1,0:T(8,128)S(1)}, u32[]{:S(2)}, u32[]{:S(2)}) collective-permute-start(f32[16,256]{1,0:T(8,128)S(1)} %get-tuple-element.57), channel_id=1, source_target_pairs={{4,8},{12,16},{20,24},{8,4},{16,12},{24,20},{5,9},{13,17},{21,25},... | collective-permute-start | bytes 49160 | tf_op jit(solution)/shard_map/ppermute | solution.py:638
  2.1 9.8 %collective-permute-start.1 = (f32[16,256]{1,0:T(8,128)S(1)}, f32[16,256]{1,0:T(8,128)S(1)}, u32[]{:S(2)}, u32[]{:S(2)}) collective-permute-start(f32[16,256]{1,0:T(8,128)S(1)} %get-tuple-element.56.refs_0_), channel_id=1, source_target_pairs={{0,4},{8,12},{16,20},{24,28},{4,0},{12,8},{20,16},{28,24},{1,5},{9... | collective-permute-start | bytes 49160 | tf_op jit(solution)/shard_map/ppermute | solution.py:638
  11.9 8.7 %copy-start = (f32[4096,3]{0,1:T(4,128)S(1)}, f32[4096,3]{0,1:T(4,128)}, u32[]{:S(2)}) copy-start(f32[4096,3]{0,1:T(4,128)} %param.13) | copy-start | bytes 147460
  15.6 7.6 %collective-permute-start.2 = (bf16[48,256]{1,0:T(8,128)(2,1)S(1)}, bf16[48,256]{1,0:T(8,128)(2,1)S(1)}, u32[]{:S(2)}, u32[]{:S(2)}) collective-permute-start(bf16[48,256]{1,0:T(8,128)(2,1)S(1)} %get-tuple-element.68), channel_id=1, source_target_pairs={{4,8},{12,16},{20,24},{8,4},{16,12},{24,20},{5,9},{13,17},{21,25},... | collective-permute-start | bytes 73736 | tf_op jit(solution)/shard_map/ppermute | solution.py:638
  16.2 6.9 %collective-permute-start.3 = (bf16[48,256]{1,0:T(8,128)(2,1)S(1)}, bf16[48,256]{1,0:T(8,128)(2,1)S(1)}, u32[]{:S(2)}, u32[]{:S(2)}) collective-permute-start(bf16[48,256]{1,0:T(8,128)(2,1)S(1)} %get-tuple-element.69), channel_id=1, source_target_pairs={{0,4},{8,12},{16,20},{24,28},{4,0},{12,8},{20,16},{28,24},{1,5},{9... | collective-permute-start | bytes 73736 | tf_op jit(solution)/shard_map/ppermute | solution.py:638
  25.5 8.0 %collective-permute-start.4 = (f32[8,128]{1,0:T(8,128)S(1)}, f32[8,128]{1,0:T(8,128)S(1)}, u32[]{:S(2)}, u32[]{:S(2)}) collective-permute-start(f32[8,128]{1,0:T(8,128)S(1)} %get-tuple-element.76), channel_id=1, source_target_pairs={{4,8},{12,16},{20,24},{8,4},{16,12},{24,20},{5,9},{13,17},{21,25},... | collective-permute-start | bytes 12296 | tf_op jit(solution)/shard_map/ppermute | solution.py:638
  26.4 7.1 %collective-permute-start.5 = (f32[8,128]{1,0:T(8,128)S(1)}, f32[8,128]{1,0:T(8,128)S(1)}, u32[]{:S(2)}, u32[]{:S(2)}) collective-permute-start(f32[8,128]{1,0:T(8,128)S(1)} %get-tuple-element.77), channel_id=1, source_target_pairs={{0,4},{8,12},{16,20},{24,28},{4,0},{12,8},{20,16},{28,24},{1,5},{9... | collective-permute-start | bytes 12296 | tf_op jit(solution)/shard_map/ppermute | solution.py:638
  35.9 6.6 %collective-permute-start.6 = (bf16[48,256]{1,0:T(8,128)(2,1)S(1)}, bf16[48,256]{1,0:T(8,128)(2,1)S(1)}, u32[]{:S(2)}, u32[]{:S(2)}) collective-permute-start(bf16[48,256]{1,0:T(8,128)(2,1)S(1)} %get-tuple-element.82), channel_id=1, source_target_pairs={{4,8},{12,16},{20,24},{8,4},{16,12},{24,20},{5,9},{13,17},{21,25},... | collective-permute-start | bytes 73736 | tf_op jit(solution)/shard_map/ppermute | solution.py:638
  36.6 6.0 %collective-permute-start.7 = (bf16[48,256]{1,0:T(8,128)(2,1)S(1)}, bf16[48,256]{1,0:T(8,128)(2,1)S(1)}, u32[]{:S(2)}, u32[]{:S(2)}) collective-permute-start(bf16[48,256]{1,0:T(8,128)(2,1)S(1)} %get-tuple-element.83), channel_id=1, source_target_pairs={{0,4},{8,12},{16,20},{24,28},{4,0},{12,8},{20,16},{28,24},{1,5},{9... | collective-permute-start | bytes 73736 | tf_op jit(solution)/shard_map/ppermute | solution.py:638
  45.0 5.7 %collective-permute-start.8 = (f32[8,128]{1,0:T(8,128)S(1)}, f32[8,128]{1,0:T(8,128)S(1)}, u32[]{:S(2)}, u32[]{:S(2)}) collective-permute-start(f32[8,128]{1,0:T(8,128)S(1)} %get-tuple-element.91), channel_id=1, source_target_pairs={{4,8},{12,16},{20,24},{8,4},{16,12},{24,20},{5,9},{13,17},{21,25},... | collective-permute-start | bytes 12296 | tf_op jit(solution)/shard_map/ppermute | solution.py:638
  45.7 5.8 %collective-permute-start.9 = (f32[8,128]{1,0:T(8,128)S(1)}, f32[8,128]{1,0:T(8,128)S(1)}, u32[]{:S(2)}, u32[]{:S(2)}) collective-permute-start(f32[8,128]{1,0:T(8,128)S(1)} %get-tuple-element.92), channel_id=1, source_target_pairs={{0,4},{8,12},{16,20},{24,28},{4,0},{12,8},{20,16},{28,24},{1,5},{9... | collective-permute-start | bytes 12296 | tf_op jit(solution)/shard_map/ppermute | solution.py:638
  53.8 8.1 %copy-start.1 = (s32[256]{0:T(256)S(1)}, s32[256]{0:T(256)}, u32[]{:S(2)}) copy-start(s32[256]{0:T(256)} %param.15) | copy-start | bytes 3076
  53.9 8.1 %collective-permute-start.10 = (bf16[48,256]{1,0:T(8,128)(2,1)S(1)}, bf16[48,256]{1,0:T(8,128)(2,1)S(1)}, u32[]{:S(2)}, u32[]{:S(2)}) collective-permute-start(bf16[48,256]{1,0:T(8,128)(2,1)S(1)} %get-tuple-element.95), channel_id=1, source_target_pairs={{4,8},{12,16},{20,24},{8,4},{16,12},{24,20},{5,9},{13,17},{21,25},... | collective-permute-start | bytes 73736 | tf_op jit(solution)/shard_map/ppermute | solution.py:638
  54.7 7.2 %collective-permute-start.11 = (bf16[48,256]{1,0:T(8,128)(2,1)S(1)}, bf16[48,256]{1,0:T(8,128)(2,1)S(1)}, u32[]{:S(2)}, u32[]{:S(2)}) collective-permute-start(bf16[48,256]{1,0:T(8,128)(2,1)S(1)} %get-tuple-element.96), channel_id=1, source_target_pairs={{0,4},{8,12},{16,20},{24,28},{4,0},{12,8},{20,16},{28,24},{1,5},{9... | collective-permute-start | bytes 73736 | tf_op jit(solution)/shard_map/ppermute | solution.py:638
